TPU v7x, 128 devices: a whole 4x4x4 slice. The times are simulated.
128 devices in a mesh: dp: 32 (over z, x, core), owner: 4 (over y).
Axes of the slice: x: 4, y: 4, z: 4, core: 2. Of those that a mesh axis runs over, the one named last changes fastest.
Arguments:
- grad: bfloat16 [32, 2048, 4096], P('dp', 'owner'), may hold values from -6 to 6
- error: bfloat16 [32, 2048, 4096], P('dp', 'owner'), may hold values from -4 to 4
- warm_right: float32 [4096, 32], replicated, may hold values from -6 to 6
Outputs:
- update: float32 [2048, 4096], P('owner')
- new_error: float32 [32, 2048, 4096], P('dp', 'owner')
- right_factor: float32 [4096, 32], replicated
All inputs are finite; a program needn't handle non-finite values.
Results may differ from a plain program's by a relative error of at most 0.013.
Values may be sent and summed in bfloat16 or wider, within the bound.
No kernel may reach another device: no remote copies, remote signals or barrier semaphores. Data moves between devices by JAX's collectives and lax.ppermute only.
A program may use at most 128 MiB of HBM per device.

v0:
```python
import jax
import jax.numpy as jnp
from jax import lax
from jax.sharding import PartitionSpec as P

ITERS = 4


def orthonormal(left, gram):
    rank = gram.shape[0]
    shifted = gram + 1e-06 * (jnp.trace(gram) / rank) * jnp.eye(rank, dtype=jnp.float32)
    factor = jnp.linalg.cholesky(shifted)
    solved = jax.scipy.linalg.solve_triangular(factor, left.T, lower=True)
    return solved.T.astype(jnp.bfloat16)


def gram_of(left):
    return jnp.dot(
        left.T, left, precision=lax.Precision.HIGHEST, preferred_element_type=jnp.float32
    )


def per_device(grad, error, warm_right):
    replicas = lax.axis_size("dp")
    memory = (grad[0].astype(jnp.float32) + error[0].astype(jnp.float32)).astype(jnp.bfloat16)
    right = warm_right
    ortho = jnp.zeros((memory.shape[0], warm_right.shape[1]), jnp.bfloat16)
    for step in range(ITERS):
        term = jnp.dot(memory, right.astype(jnp.bfloat16), preferred_element_type=jnp.float32)
        left = lax.psum(term, "dp")
        gram = lax.psum(gram_of(left), "owner")
        ortho = orthonormal(left, gram)
        partial_right = lax.dot_general(
            memory, ortho, (((0,), (0,)), ((), ())), preferred_element_type=jnp.float32
        )
        right = lax.psum(partial_right, ("dp", "owner")) / replicas
    update = jnp.dot(
        ortho.astype(jnp.float32),
        right.T,
        precision=lax.Precision.HIGHEST,
        preferred_element_type=jnp.float32,
    )
    new_error = memory.astype(jnp.float32) - update
    return (update, new_error[None], right)


def solution(mesh):
    placed = (P("dp", "owner", None), P("dp", "owner", None), P())
    return jax.shard_map(
        per_device,
        mesh=mesh,
        in_specs=placed,
        out_specs=(P("owner", None), P("dp", "owner", None), P()),
        check_vma=False,
    )
```

profile of v0, /device:TPU:1, one launch (start us, length us, event | category | flops | bytes accessed | tf_op | source)
XLA Modules:
  0.0 1120.2 jit_solution(11661349644887477408)
XLA Ops:
  7.2 5.0 fusion
  12.3 2.0 copy-done
  14.3 2.0 fusion.7
  16.3 0.0 all-reduce.11.cloned.1.call-start
  16.4 99.0 %all-reduce.9.cloned.1.call-done = f32[512,32]{0,1:T(8,128)} async-done(((f32[512,32]{0,1:T(8,128)}), f32[512,32]{0,1:T(8,128)}) %all-reduce.9.cloned.1.call-update) | async-done | bytes 65552 | tf_op jit(solution)/shard_map/psum | solution.py:30
  115.4 1.1 fusion.34
  116.5 13.1 %psum.85 = f32[32,32]{0,1:T(8,128)S(1)} all-reduce(f32[32,32]{0,1:T(8,128)S(1)} %fusion.34), channel_id=1, replica_groups=mesh['dp'=32,'owner'=4] {'owner'}, use_global_device_ids=true, to_apply=%region_1.0 | all-reduce | flops 1024 | bytes 8192 | tf_op jit(solution)/shard_map/psum | solution.py:31
  129.6 0.6 select_reduce_fusion.4
  130.9 0.1 copy.7
  131.0 2.9 cholesky.74
  134.0 0.6 compare_reduce_fusion.3
  134.6 0.7 fusion.13
  135.3 2.4 custom-call.8
  137.7 1.1 convolution_convert_fusion.3
  138.8 3.8 fusion.39
  142.7 0.0 all-reduce.13.cloned.1.call-start
  142.7 145.5 %all-reduce.11.cloned.1.call-done = f32[4096,32]{0,1:T(8,128)} async-done(((f32[4096,32]{0,1:T(8,128)}), f32[4096,32]{0,1:T(8,128)}) %all-reduce.11.cloned.1.call-update) | async-done | bytes 524304 | tf_op jit(solution)/shard_map/psum | solution.py:36
  288.2 4.3 fusion.1
  292.6 0.0 all-reduce.15.cloned.1.call-start
  292.6 94.3 %all-reduce.13.cloned.1.call-done = f32[512,32]{0,1:T(8,128)} async-done(((f32[512,32]{0,1:T(8,128)}), f32[512,32]{0,1:T(8,128)}) %all-reduce.13.cloned.1.call-update) | async-done | bytes 65552 | tf_op jit(solution)/shard_map/psum | solution.py:30
  386.9 1.1 fusion.35
  388.0 13.1 %psum.88 = f32[32,32]{0,1:T(8,128)S(1)} all-reduce(f32[32,32]{0,1:T(8,128)S(1)} %fusion.35), channel_id=1, replica_groups=mesh['dp'=32,'owner'=4] {'owner'}, use_global_device_ids=true, to_apply=%region_7.10 | all-reduce | flops 1024 | bytes 8192 | tf_op jit(solution)/shard_map/psum | solution.py:31
  401.2 0.6 select_reduce_fusion.3
  402.5 0.1 copy.9
  402.6 2.9 cholesky.85
  405.5 0.6 compare_reduce_fusion.2
  406.1 0.7 fusion.14
  406.8 2.4 custom-call.9
  409.2 1.1 convolution_convert_fusion.2
  410.4 3.8 fusion.40
  414.2 0.0 all-reduce.17.cloned.1.call-start
  414.3 145.5 %all-reduce.15.cloned.1.call-done = f32[4096,32]{0,1:T(8,128)} async-done(((f32[4096,32]{0,1:T(8,128)}), f32[4096,32]{0,1:T(8,128)}) %all-reduce.15.cloned.1.call-update) | async-done | bytes 524304 | tf_op jit(solution)/shard_map/psum | solution.py:36
  559.8 4.3 fusion.2
  564.1 0.0 all-reduce.19.cloned.1.call-start
  564.1 94.3 %all-reduce.17.cloned.1.call-done = f32[512,32]{0,1:T(8,128)} async-done(((f32[512,32]{0,1:T(8,128)}), f32[512,32]{0,1:T(8,128)}) %all-reduce.17.cloned.1.call-update) | async-done | bytes 65552 | tf_op jit(solution)/shard_map/psum | solution.py:30
  658.5 1.1 fusion.36
  659.6 13.1 %psum.91 = f32[32,32]{0,1:T(8,128)S(1)} all-reduce(f32[32,32]{0,1:T(8,128)S(1)} %fusion.36), channel_id=1, replica_groups=mesh['dp'=32,'owner'=4] {'owner'}, use_global_device_ids=true, to_apply=%region_11.14 | all-reduce | flops 1024 | bytes 8192 | tf_op jit(solution)/shard_map/psum | solution.py:31
  672.7 0.6 select_reduce_fusion.2
  674.0 0.1 copy.11
  674.1 2.9 cholesky.96
  677.1 0.6 compare_reduce_fusion.1
  677.7 0.7 fusion.15
  678.4 2.4 custom-call.10
  680.8 1.1 convolution_convert_fusion.1
  681.9 3.8 fusion.41
  685.8 145.5 %all-reduce.19.cloned.1.call-done = f32[4096,32]{0,1:T(8,128)} async-done(((f32[4096,32]{0,1:T(8,128)}), f32[4096,32]{0,1:T(8,128)}) %all-reduce.19.cloned.1.call-update) | async-done | bytes 524304 | tf_op jit(solution)/shard_map/psum | solution.py:36
  831.3 4.3 fusion.3
  835.7 0.0 all-reduce.23.cloned.1.call-start
  835.7 94.3 %all-reduce.21.cloned.1.call-done = f32[512,32]{0,1:T(8,128)} async-done(((f32[512,32]{0,1:T(8,128)}), f32[512,32]{0,1:T(8,128)}) %all-reduce.21.cloned.1.call-update) | async-done | bytes 65552 | tf_op jit(solution)/shard_map/psum | solution.py:30
  930.0 1.1 fusion.37
  931.2 13.2 %psum.94 = f32[32,32]{0,1:T(8,128)S(1)} all-reduce(f32[32,32]{0,1:T(8,128)S(1)} %fusion.37), channel_id=1, replica_groups=mesh['dp'=32,'owner'=4] {'owner'}, use_global_device_ids=true, to_apply=%region_15.18 | all-reduce | flops 1024 | bytes 8192 | tf_op jit(solution)/shard_map/psum | solution.py:31
  944.3 0.6 select_reduce_fusion.1
  945.6 0.1 copy.13
  945.7 2.9 cholesky.107
  948.6 0.6 compare_reduce_fusion
  949.3 0.7 fusion.16
  949.9 2.4 custom-call.11
  952.4 1.1 convolution_convert_fusion
  953.5 3.8 fusion.42
  957.3 145.5 %all-reduce.23.cloned.1.call-done = f32[4096,32]{0,1:T(8,128)} async-done(((f32[4096,32]{0,1:T(8,128)}), f32[4096,32]{0,1:T(8,128)}) %all-reduce.23.cloned.1.call-update) | async-done | bytes 524304 | tf_op jit(solution)/shard_map/psum | solution.py:36
  1102.9 1.1 broadcast_multiply_fusion
  1104.0 3.5 fusion.38
  1107.5 5.0 subtract_bitcast_fusion
  1112.4 0.9 copy-done.2
  (30 shorter events, 0.4 us)
Async XLA Ops:
  7.2 7.1 copy-start.4
  7.2 108.2 %all-reduce.9.cloned.1.call-start = ((), (), s32[]{:S(2)}) async-start(), calls=%async_computation | async-start | bytes 131072 | tf_op jit(solution)/shard_map/psum | solution.py:30
  12.3 2.0 copy-start
  16.3 271.9 %all-reduce.11.cloned.1.call-start = ((), (), s32[]{:S(2)}) async-start(), calls=%async_computation.1 | async-start | bytes 1048576 | tf_op jit(solution)/shard_map/psum | solution.py:36
  142.7 244.3 %all-reduce.13.cloned.1.call-start = ((), (), s32[]{:S(2)}) async-start(), calls=%async_computation.2 | async-start | bytes 131072 | tf_op jit(solution)/shard_map/psum | solution.py:30
  292.6 267.2 %all-reduce.15.cloned.1.call-start = ((), (), s32[]{:S(2)}) async-start(), calls=%async_computation.3 | async-start | bytes 1048576 | tf_op jit(solution)/shard_map/psum | solution.py:36
  414.2 244.3 %all-reduce.17.cloned.1.call-start = ((), (), s32[]{:S(2)}) async-start(), calls=%async_computation.4 | async-start | bytes 131072 | tf_op jit(solution)/shard_map/psum | solution.py:30
  564.1 267.2 %all-reduce.19.cloned.1.call-start = ((), (), s32[]{:S(2)}) async-start(), calls=%async_computation.5 | async-start | bytes 1048576 | tf_op jit(solution)/shard_map/psum | solution.py:36
  685.7 244.3 %all-reduce.21.cloned.1.call-start = ((), (), s32[]{:S(2)}) async-start(), calls=%async_computation.6 | async-start | bytes 131072 | tf_op jit(solution)/shard_map/psum | solution.py:30
  835.7 267.2 %all-reduce.23.cloned.1.call-start = ((), (), s32[]{:S(2)}) async-start(), calls=%async_computation.7 | async-start | bytes 1048576 | tf_op jit(solution)/shard_map/psum | solution.py:36
  1103.9 3.5 copy-start.3
  1104.0 3.5 copy-start.1
  1107.5 5.9 copy-start.2
Sparse Core Ops, SparseCore 0:
  16.4 98.9 all-reduce.8
  142.8 145.4 all-reduce.10
  292.7 94.2 all-reduce.12
  414.3 145.4 all-reduce.14
  564.2 94.2 all-reduce.16
  685.9 145.4 all-reduce.18
  835.8 94.2 all-reduce.20
  957.5 145.3 all-reduce.22
where the time goes:
time: 1120 us
  waiting for transfers between devices  964 us (86%)
  blocking collectives  52.6 us (5%)
  matrix products  42.5 us (4%)
  other arithmetic  40.3 us (4%)
  between operations  17 us (2%)
    psum x4, waiting for transfers between devices, per_device(): right = lax.psum(partial_right, ('dp', 'owner')) / replicas  582 us
    psum x4, waiting for transfers between devices, per_device(): left = lax.psum(term, 'dp')  382 us
    psum x4, blocking collectives, per_device(): gram = lax.psum(gram_of(left), 'owner')  52.6 us
  transfers between devices with their start and end apart: 8, of which 8 were waited for; matrix products, arithmetic and copies ran while one was open for 0% of the time, Pallas kernels for 0%

commit v1 on v0

v1 whole, which is shorter than its diff:
```python
import jax
import jax.numpy as jnp
from jax import lax
from jax.experimental import pallas as pl
from jax.experimental.pallas import tpu as pltpu
from jax.sharding import PartitionSpec as P

W = 4096
RANK = 32
ITERS = 4
ROWS = 2048
N_DP = 32
N_OWNER = 4
HALF = W // 2
COLS = HALF // 4
ROWS_OWN = ROWS // N_OWNER
PIECE = ROWS_OWN // 4
MID = ROWS // 2
BF = jnp.bfloat16
F32 = jnp.float32
HIGHEST = lax.Precision.HIGHEST

CORE = [(i, i ^ 1) for i in range(N_DP)]
ZX_GROUPS = [[z * 8 + x * 2 + c for z in range(4) for x in range(4)] for c in range(2)]


def z_shift(k):
    return [(i, i ^ (8 * k)) for i in range(N_DP)]


def xy_groups():
    groups = []
    for z in range(4):
        for c in range(2):
            ys = [(y + 2 * c) % 4 for y in range(4)]
            groups.append([(z * 8 + x * 2 + c) * N_OWNER + y for y in ys for x in range(4)])
    return groups


def params(**kw):
    return pltpu.CompilerParams(vmem_limit_bytes=48 * 1024 * 1024, **kw)


def half_of_memory(grad, error, which):
    def body(which_ref, g_ref, e_ref, o_ref):
        o_ref[...] = (g_ref[...].astype(F32) + e_ref[...].astype(F32)).astype(BF)

    steps = 4
    rows = ROWS_OWN // steps
    spec = pl.BlockSpec((rows, HALF), lambda i, w: (i, w[0]))
    return pl.pallas_call(
        body,
        grid_spec=pltpu.PrefetchScalarGridSpec(
            num_scalar_prefetch=1,
            grid=(steps,),
            in_specs=[spec, spec],
            out_specs=pl.BlockSpec((rows, HALF), lambda i, w: (i, 0)),
        ),
        out_shape=jax.ShapeDtypeStruct((ROWS_OWN, HALF), BF),
        compiler_params=params(),
        name="half_of_memory",
    )(which, grad, error)


def pair_sum(mine, received):
    def body(a_ref, b_ref, o_ref):
        for z in range(4):
            cut = slice(z * COLS, (z + 1) * COLS)
            o_ref[z, 0] = (a_ref[:, cut].astype(F32) + b_ref[:, cut].astype(F32)).astype(BF)

    spec = pl.BlockSpec((PIECE, HALF), lambda x: (x, 0))
    return pl.pallas_call(
        body,
        grid=(4,),
        in_specs=[spec, spec],
        out_specs=pl.BlockSpec((4, 1, PIECE, COLS), lambda x: (0, x, 0, 0)),
        out_shape=jax.ShapeDtypeStruct((4, 4, PIECE, COLS), BF),
        compiler_params=params(),
        name="pair_sum",
    )(mine, received)


def piece_sum(pieces):
    def body(p_ref, o_ref):
        total = p_ref[0].astype(F32)
        for i in range(1, 16):
            total = total + p_ref[i].astype(F32)
        total = total.astype(BF)
        for i in range(16):
            o_ref[i] = total

    rows = 32
    spec = pl.BlockSpec((16, rows, COLS), lambda i: (0, i, 0))
    return pl.pallas_call(
        body,
        grid=(PIECE // rows,),
        in_specs=[spec],
        out_specs=spec,
        out_shape=jax.ShapeDtypeStruct((16, PIECE, COLS), BF),
        compiler_params=params(),
        name="piece_sum",
    )(pieces)


def dot(a, b, dims, precision=None):
    return lax.dot_general(a, b, ((dims[0], dims[1]), ((), ())), precision=precision, preferred_element_type=F32)


def left_from(right_t, m_ref, own_ref, oth_ref):
    left = dot(right_t, m_ref[...], ((1,), (1,)))
    own_ref[...] = left[:, :MID]
    oth_ref[...] = left[:, MID:]


def inverse_factor(gram):
    row = lax.broadcasted_iota(jnp.int32, (RANK, 128), 0)
    lane = lax.broadcasted_iota(jnp.int32, (RANK, 128), 1)
    wide = jnp.concatenate([gram, jnp.zeros((RANK, 128 - RANK), F32)], axis=1)
    trace = jnp.sum(jnp.where(row == lane, wide, 0.0), keepdims=True)
    shift = 1e-06 * (trace / RANK)
    work = wide + jnp.where(row == lane, shift, 0.0) + jnp.where(row + RANK == lane, 1.0, 0.0)
    for k in range(RANK - 1):
        col = jnp.broadcast_to(work[:, k : k + 1], (RANK, 128))
        factor = jnp.where(row > k, col / col[k : k + 1, :], 0.0)
        work = work - factor * work[k : k + 1, :]
    pivot = jnp.sum(jnp.where(row == lane, work, 0.0), axis=1, keepdims=True)
    return work[:, RANK : 2 * RANK] * lax.rsqrt(pivot)


def ortho_from(own_ref, oth_ref):
    left = jnp.concatenate([own_ref[...], oth_ref[...]], axis=1)
    gram = dot(left, left, ((1,), (1,)), HIGHEST)
    return dot(inverse_factor(gram), left, ((1,), (0,)), HIGHEST).astype(BF)


HALVES = (jax.ShapeDtypeStruct((RANK, MID), F32),) * 2


def first_left(right_t, m):
    def body(r_ref, m_ref, own_ref, oth_ref):
        left_from(r_ref[...].astype(BF), m_ref, own_ref, oth_ref)

    return pl.pallas_call(body, out_shape=HALVES, compiler_params=params(), name="first_left")(right_t, m)


def next_left(own, oth, m):
    def body(own_in, oth_in, m_ref, own_ref, oth_ref):
        ortho = ortho_from(own_in, oth_in)
        right = dot(ortho, m_ref[...], ((1,), (0,))) * (1.0 / N_DP)
        left_from(right.astype(BF), m_ref, own_ref, oth_ref)

    return pl.pallas_call(body, out_shape=HALVES, compiler_params=params(), name="next_left")(own, oth, m)


def last_right(own, oth, m):
    def body(own_in, oth_in, m_ref, ortho_ref, right_ref):
        ortho = ortho_from(own_in, oth_in)
        ortho_ref[...] = ortho
        right_ref[...] = dot(ortho, m_ref[...], ((1,), (0,))) * (1.0 / N_DP)

    shapes = (jax.ShapeDtypeStruct((RANK, ROWS), BF), jax.ShapeDtypeStruct((RANK, COLS), F32))
    return pl.pallas_call(body, out_shape=shapes, compiler_params=params(), name="last_right")(own, oth, m)


def sum_over_group(own, oth):
    own = own + lax.ppermute(oth, "dp", CORE)
    a, b, c = [lax.ppermute(own, "dp", z_shift(k)) for k in (1, 3, 2)]
    own = (own + a) + (b + c)
    return own, lax.ppermute(own, "dp", CORE)


def finish(place, ortho, rights, mine, other):
    def body(place_ref, o_ref, r0, r1, r2, r3, mine_ref, other_ref, up_ref, err_ref, right_ref):
        step = pl.program_id(0)
        left = o_ref[...]
        left = jnp.concatenate([left, left, left], axis=0)
        for j in range(2):
            for k, ref in enumerate((r0, r1, r2, r3)):

                @pl.when(step == 4 * j + k)
                def _():
                    right = ref[j * RANK : (j + 1) * RANK, :]
                    right_ref[...] = right
                    high = right.astype(BF)
                    rest = right - high.astype(F32)
                    mid = rest.astype(BF)
                    low = (rest - mid.astype(F32)).astype(BF)
                    update = dot(left, jnp.concatenate([high, mid, low], axis=0), ((0,), (0,)))
                    up_ref[...] = update
                    memory = (mine_ref, other_ref)[j][...].astype(F32)
                    err_ref[...] = memory - update

    def group(s, p):
        return (s % 4) ^ p[0]

    whole = pl.BlockSpec((2 * RANK, COLS), lambda s, p: (0, 0))
    out_block = lambda s, p: (0, ((s // 4) ^ p[1]) * 4 + group(s, p))
    return pl.pallas_call(
        body,
        grid_spec=pltpu.PrefetchScalarGridSpec(
            num_scalar_prefetch=1,
            grid=(8,),
            in_specs=[
                pl.BlockSpec((RANK, ROWS_OWN), lambda s, p: (0, p[2])),
                whole,
                whole,
                whole,
                whole,
                pl.BlockSpec((ROWS_OWN, COLS), lambda s, p: (0, group(jnp.minimum(s, 3), p))),
                pl.BlockSpec((ROWS_OWN, COLS), lambda s, p: (0, group(jnp.maximum(s, 4), p))),
            ],
            out_specs=[
                pl.BlockSpec((ROWS_OWN, COLS), out_block),
                pl.BlockSpec((ROWS_OWN, COLS), out_block),
                pl.BlockSpec((RANK, COLS), out_block),
            ],
        ),
        out_shape=(
            jax.ShapeDtypeStruct((ROWS_OWN, W), F32),
            jax.ShapeDtypeStruct((ROWS_OWN, W), F32),
            jax.ShapeDtypeStruct((RANK, W), F32),
        ),
        compiler_params=params(),
        name="finish",
    )(place, ortho, *rights, mine, other)


def per_device(grad, error, warm_right):
    dp = lax.axis_index("dp")
    owner = lax.axis_index("owner")
    core = dp & 1
    z = dp >> 3

    other = half_of_memory(grad[0], error[0], (1 - core)[None])
    received = lax.ppermute(other, "dp", CORE)
    mine = half_of_memory(grad[0], error[0], core[None])
    blocks = pair_sum(mine, received).reshape(16, PIECE, COLS)
    pieces = lax.all_to_all(blocks, "dp", 0, 0, axis_index_groups=ZX_GROUPS)
    m = lax.all_to_all(piece_sum(pieces), ("dp", "owner"), 0, 0, axis_index_groups=xy_groups())
    m = m.reshape(ROWS, COLS)

    start = core * HALF + z * COLS
    right_t = lax.dynamic_slice(warm_right, (start, 0), (COLS, RANK)).T
    own, oth = first_left(right_t, m)
    for step in range(ITERS - 1):
        own, oth = sum_over_group(own, oth)
        own, oth = next_left(own, oth, m)
    own, oth = sum_over_group(own, oth)
    ortho, right = last_right(own, oth, m)

    pair = jnp.concatenate([right, lax.ppermute(right, "dp", CORE)], axis=0)
    rights = [pair] + [lax.ppermute(pair, "dp", z_shift(k)) for k in (1, 2, 3)]
    row_block = ((owner >> 1) ^ core) * 2 + (owner & 1)
    place = jnp.stack([z, core, row_block]).astype(jnp.int32)
    update, new_error, right_t = finish(place, ortho, rights, mine, other)
    return update, new_error[None], right_t.T


def solution(mesh):
    placed = (P("dp", "owner", None), P("dp", "owner", None), P())
    return jax.shard_map(
        per_device,
        mesh=mesh,
        in_specs=placed,
        out_specs=(P("owner", None), P("dp", "owner", None), P()),
        check_vma=False,
    )
```

time: 1120 us -> 186 us (0.17)
  waiting for transfers between devices: 964 us -> 70.4 us
  matrix products: 42.5 us -> 0 us
  Pallas kernels: 0 us -> 42 us
  other arithmetic: 40.3 us -> 0.31 us
  starting transfers between devices: 0.33 us -> 28 us
  blocking collectives: 52.6 us -> 34.8 us
  between operations: 17 us -> 0.78 us
    psum x8 -> x0, waiting for transfers between devices: 964 us -> none  [the longest x4 582 us: per_device(): right = lax.psum(partial_right, ('dp', 'owner')) / replicas]
    psum x4 -> x0, blocking collectives: 52.6 us -> none  [per_device(): gram = lax.psum(gram_of(left), 'owner')]
    ppermute x0 -> x25, waiting for transfers between devices: none -> 43.6 us  [the longest x12 28.3 us: sum_over_group(): a, b, c = [lax.ppermute(own, 'dp', z_shift(k)) for k in (1, 3, 2)]]
    pallas_call x0 -> x10, Pallas kernels: none -> 42 us  [the longest x3 18.2 us: next_left(): pl.pallas_call(body, out_shape=HALVES, compiler_params=params(), name='ne...]
    dot_general x13 -> x0, matrix products: 38 us -> none  [the longest x4 15.3 us: per_device(): lax.dot_general(memory, ortho, (((0,), (0,)), ((), ())), preferred_elemen...]
    all_to_all x0 -> x1, blocking collectives: none -> 34.8 us  [per_device(): pieces = lax.all_to_all(blocks, 'dp', 0, 0, axis_index_groups=ZX_GROUPS)]
    all_to_all x0 -> x1, waiting for transfers between devices: none -> 26.8 us  [per_device(): lax.all_to_all(piece_sum(pieces), ('dp', 'owner'), 0, 0, axis_index_group...]
    another operation x20 -> x1, other arithmetic: 26.7 us -> 0.08 us  [per_device(): place = jnp.stack([z, core, row_block]).astype(jnp.int32)]
  transfers between devices with their start and end apart: 8 -> 26, of which waited for: 8 -> 21; matrix products, arithmetic and copies ran while one was open for 0% -> 0% of each run, Pallas kernels for 0% -> 2%
where the time goes in v1:
time: 186 us; the launch traced here: 182 us
  waiting for transfers between devices  70.4 us (38%)
  Pallas kernels  42 us (23%)
  blocking collectives  34.8 us (19%)
  starting transfers between devices  28 us (15%)
  local copies, waits for them, and re-layouts  5.86 us (3%)
    all_to_all x1, blocking collectives, per_device(): pieces = lax.all_to_all(blocks, 'dp', 0, 0, axis_index_groups=ZX_GROUPS)  34.8 us
    ppermute x12, waiting for transfers between devices, sum_over_group(): a, b, c = [lax.ppermute(own, 'dp', z_shift(k)) for k in (1, 3, 2)]  28.3 us
    all_to_all x1, waiting for transfers between devices, per_device(): lax.all_to_all(piece_sum(pieces), ('dp', 'owner'), 0, 0, axis_index_group...  26.8 us
    pallas_call x3, Pallas kernels, next_left(): pl.pallas_call(body, out_shape=HALVES, compiler_params=params(), name='ne...  18.2 us
    ppermute x12, starting transfers between devices, sum_over_group(): a, b, c = [lax.ppermute(own, 'dp', z_shift(k)) for k in (1, 3, 2)]  10.9 us
    pallas_call x1, Pallas kernels, finish(): pl.pallas_call(body, grid_spec=pltpu.PrefetchScalarGridSpec(num_scalar_pr...  8.19 us
    all_to_all x1, starting transfers between devices, per_device(): lax.all_to_all(piece_sum(pieces), ('dp', 'owner'), 0, 0, axis_index_group...  6.47 us
    pallas_call x2, Pallas kernels, half_of_memory(): pl.pallas_call(body, grid_spec=pltpu.PrefetchScalarGridSpec(num_scalar_pr...  6.17 us
  transfers between devices with their start and end apart: 26, of which 21 were waited for; matrix products, arithmetic and copies ran while one was open for 0% of the time, Pallas kernels for 2%

profile of v1, /device:TPU:1, one launch (start us, length us, event | category | flops | bytes accessed | tf_op | source)
XLA Modules:
  0.0 182.2 jit_solution(15897539529328666369)
XLA Ops:
  0.6 0.0 copy-start
  0.7 3.1 %half_of_memory.3.other_ref = bf16[512,2048]{1,0:T(8,128)(2,1)S(1)} custom-call(s32[1]{0:T(128)} %bitcast.6.which_ref, bf16[512,4096]{1,0:T(8,128)(2,1)} %bitcast.18, bf16[512,4096]{1,0:T(8,128)(2,1)} %bitcast.20), custom_call_target="tpu_custom_call" | custom-call | tf_op jit(solution)/shard_map/half_of_memory/pallas_call | solution.py:51
  3.8 1.5 collective-permute-start
  5.3 3.1 %half_of_memory.2.a_ref.mine_ref = bf16[512,2048]{1,0:T(8,128)(2,1)S(1)} custom-call(s32[1]{0:T(128)} %bitcast.1.which_ref, bf16[512,4096]{1,0:T(8,128)(2,1)} %bitcast.19, bf16[512,4096]{1,0:T(8,128)(2,1)} %bitcast.21), custom_call_target="tpu_custom_call" | custom-call | tf_op jit(solution)/shard_map/half_of_memory/pallas_call | solution.py:51
  8.4 0.7 collective-permute-done.b_ref
  9.1 1.3 copy-done.6
  10.4 2.6 %pair_sum.1 = bf16[4,4,128,512]{3,2,1,0:T(8,128)(2,1)S(1)} custom-call(bf16[512,2048]{1,0:T(8,128)(2,1)S(1)} %half_of_memory.2.a_ref.mine_ref, bf16[512,2048]{1,0:T(8,128)(2,1)} %copy-done.6), custom_call_target="tpu_custom_call" | custom-call | tf_op jit(solution)/shard_map/pair_sum/pallas_call | solution.py:72
  13.0 34.8 %all_to_all.10.p_ref = bf16[16,128,512]{2,1,0:T(8,128)(2,1)S(1)} all-to-all(bf16[16,128,512]{2,1,0:T(8,128)(2,1)S(1)} %bitcast.17), channel_id=1, replica_groups={{0,8,16,24,32,40,48,56,64,72,80,88,96,104,112,120},{4,12,20,28,36,44,52..., dimensions={0} | all-to-all | bytes 4194304 | tf_op jit(solution)/shard_map/all_to_all | solution.py:238
  47.9 0.7 piece_sum.1
  48.6 1.3 copy-done.5
  49.9 6.5 %all-to-all-start.1 = ((bf16[16,128,512]{2,1,0:T(8,128)(2,1)}), bf16[16,128,512]{2,1,0:T(8,128)(2,1)S(1)}, u32[]{:S(2)}, u32[]{:S(2)}) async-start(bf16[16,128,512]{2,1,0:T(8,128)(2,1)} %copy-done.5), calls=%async_computation.1 | async-start | bytes 4194304 | tf_op jit(solution)/shard_map/all_to_all | solution.py:239
  56.4 26.8 %all-to-all-done.1 = bf16[16,128,512]{2,1,0:T(8,128)(2,1)S(1)} async-done(((bf16[16,128,512]{2,1,0:T(8,128)(2,1)}), bf16[16,128,512]{2,1,0:T(8,128)(2,1)S(1)}, u32[]{:S(2)}, u32[]{:S(2)}) %all-to-all-start.1) | async-done | bytes 2097184 | tf_op jit(solution)/shard_map/all_to_all | solution.py:239
  83.2 0.7 first_left.1
  83.9 2.1 %collective-permute-start.1 = (f32[32,1024]{1,0:T(8,128)S(1)}, f32[32,1024]{1,0:T(8,128)S(1)}, u32[]{:S(2)}, u32[]{:S(2)}) collective-permute-start(f32[32,1024]{1,0:T(8,128)S(1)} %get-tuple-element.17), channel_id=1, source_target_pairs={{0,4},{4,0},{8,12},{12,8},{16,20},{20,16},{24,28},{28,24},{32,36},... | collective-permute-start | bytes 393224 | tf_op jit(solution)/shard_map/ppermute | solution.py:166
  86.0 1.0 collective-permute-done.1
  87.0 1.0 collective-permute-start.4
  88.0 0.7 collective-permute-start.3
  88.7 1.0 collective-permute-start.2
  89.7 3.6 %collective-permute-done.4 = f32[32,1024]{1,0:T(8,128)S(1)} collective-permute-done((f32[32,1024]{1,0:T(8,128)S(1)}, f32[32,1024]{1,0:T(8,128)S(1)}, u32[]{:S(2)}, u32[]{:S(2)}) %collective-permute-start.4) | collective-permute-done | bytes 131104 | tf_op jit(solution)/shard_map/ppermute | solution.py:167
  93.3 3.5 %collective-permute-done.3 = f32[32,1024]{1,0:T(8,128)S(1)} collective-permute-done((f32[32,1024]{1,0:T(8,128)S(1)}, f32[32,1024]{1,0:T(8,128)S(1)}, u32[]{:S(2)}, u32[]{:S(2)}) %collective-permute-start.3) | collective-permute-done | bytes 131104 | tf_op jit(solution)/shard_map/ppermute | solution.py:167
  96.9 0.6 collective-permute-start.5
  97.4 1.0 collective-permute-done.5.oth_in
  98.4 6.1 %next_left.3 = (f32[32,1024]{1,0:T(8,128)S(1)}, f32[32,1024]{1,0:T(8,128)S(1)}) custom-call(f32[32,1024]{1,0:T(8,128)S(1)} %add_add_fusion.3.own_in, f32[32,1024]{1,0:T(8,128)S(1)} %collective-permute-done.5.oth_in, bf16[2048,512]{1,0:T(8,128)(2,1)S(1)} %bitcast.13), custom_call_target="tpu_custom_call" | custom-call | tf_op jit(solution)/shard_map/next_left/pallas_call | solution.py:152
  104.5 0.4 collective-permute-start.6
  104.9 1.0 collective-permute-done.6
  105.9 1.0 collective-permute-start.9
  106.9 0.9 collective-permute-start.8
  107.7 0.8 collective-permute-start.7
  108.6 3.6 %collective-permute-done.9 = f32[32,1024]{1,0:T(8,128)S(1)} collective-permute-done((f32[32,1024]{1,0:T(8,128)S(1)}, f32[32,1024]{1,0:T(8,128)S(1)}, u32[]{:S(2)}, u32[]{:S(2)}) %collective-permute-start.9) | collective-permute-done | bytes 131104 | tf_op jit(solution)/shard_map/ppermute | solution.py:167
  112.2 3.5 %collective-permute-done.8 = f32[32,1024]{1,0:T(8,128)S(1)} collective-permute-done((f32[32,1024]{1,0:T(8,128)S(1)}, f32[32,1024]{1,0:T(8,128)S(1)}, u32[]{:S(2)}, u32[]{:S(2)}) %collective-permute-start.8) | collective-permute-done | bytes 131104 | tf_op jit(solution)/shard_map/ppermute | solution.py:167
  115.7 0.6 collective-permute-start.10
  116.3 1.0 collective-permute-done.10.oth_in
  117.3 6.1 %next_left.4 = (f32[32,1024]{1,0:T(8,128)S(1)}, f32[32,1024]{1,0:T(8,128)S(1)}) custom-call(f32[32,1024]{1,0:T(8,128)S(1)} %add_add_fusion.2.own_in, f32[32,1024]{1,0:T(8,128)S(1)} %collective-permute-done.10.oth_in, bf16[2048,512]{1,0:T(8,128)(2,1)S(1)} %bitcast.14), custom_call_target="tpu_custom_call" | custom-call | tf_op jit(solution)/shard_map/next_left/pallas_call | solution.py:152
  123.3 0.4 collective-permute-start.11
  123.7 1.0 collective-permute-done.11
  124.7 1.0 collective-permute-start.14
  125.7 0.9 collective-permute-start.13
  126.6 0.8 collective-permute-start.12
  127.4 3.6 %collective-permute-done.14 = f32[32,1024]{1,0:T(8,128)S(1)} collective-permute-done((f32[32,1024]{1,0:T(8,128)S(1)}, f32[32,1024]{1,0:T(8,128)S(1)}, u32[]{:S(2)}, u32[]{:S(2)}) %collective-permute-start.14) | collective-permute-done | bytes 131104 | tf_op jit(solution)/shard_map/ppermute | solution.py:167
  131.0 3.5 %collective-permute-done.13 = f32[32,1024]{1,0:T(8,128)S(1)} collective-permute-done((f32[32,1024]{1,0:T(8,128)S(1)}, f32[32,1024]{1,0:T(8,128)S(1)}, u32[]{:S(2)}, u32[]{:S(2)}) %collective-permute-start.13) | collective-permute-done | bytes 131104 | tf_op jit(solution)/shard_map/ppermute | solution.py:167
  134.6 0.6 collective-permute-start.15
  135.1 1.0 collective-permute-done.15.oth_in
  136.1 6.1 %next_left.5 = (f32[32,1024]{1,0:T(8,128)S(1)}, f32[32,1024]{1,0:T(8,128)S(1)}) custom-call(f32[32,1024]{1,0:T(8,128)S(1)} %add_add_fusion.1.own_in, f32[32,1024]{1,0:T(8,128)S(1)} %collective-permute-done.15.oth_in, bf16[2048,512]{1,0:T(8,128)(2,1)S(1)} %bitcast.15), custom_call_target="tpu_custom_call" | custom-call | tf_op jit(solution)/shard_map/next_left/pallas_call | solution.py:152
  142.2 0.4 collective-permute-start.16
  142.6 1.0 collective-permute-done.16
  143.6 1.0 collective-permute-start.19
  144.6 0.9 collective-permute-start.18
  145.5 0.8 collective-permute-start.17
  146.3 3.6 %collective-permute-done.19 = f32[32,1024]{1,0:T(8,128)S(1)} collective-permute-done((f32[32,1024]{1,0:T(8,128)S(1)}, f32[32,1024]{1,0:T(8,128)S(1)}, u32[]{:S(2)}, u32[]{:S(2)}) %collective-permute-start.19) | collective-permute-done | bytes 131104 | tf_op jit(solution)/shard_map/ppermute | solution.py:167
  149.9 3.5 %collective-permute-done.18 = f32[32,1024]{1,0:T(8,128)S(1)} collective-permute-done((f32[32,1024]{1,0:T(8,128)S(1)}, f32[32,1024]{1,0:T(8,128)S(1)}, u32[]{:S(2)}, u32[]{:S(2)}) %collective-permute-start.18) | collective-permute-done | bytes 131104 | tf_op jit(solution)/shard_map/ppermute | solution.py:167
  153.4 0.6 collective-permute-start.20
  154.0 1.0 collective-permute-done.20.oth_in
  155.0 5.4 %last_right.1 = (bf16[32,2048]{1,0:T(8,128)(2,1)S(1)}, f32[32,512]{1,0:T(8,128)S(1)}) custom-call(f32[32,1024]{1,0:T(8,128)S(1)} %add_add_fusion.own_in, f32[32,1024]{1,0:T(8,128)S(1)} %collective-permute-done.20.oth_in, bf16[2048,512]{1,0:T(8,128)(2,1)S(1)} %bitcast.16), custom_call_target="tpu_custom_call" | custom-call | tf_op jit(solution)/shard_map/last_right/pallas_call | solution.py:162
  160.4 0.4 collective-permute-start.21
  160.8 0.9 collective-permute-done.21
  161.7 0.7 collective-permute-start.24
  162.4 0.5 collective-permute-start.23
  162.9 2.1 %collective-permute-start.22 = (f32[64,512]{1,0:T(8,128)S(1)}, f32[64,512]{1,0:T(8,128)S(1)}, u32[]{:S(2)}, u32[]{:S(2)}) collective-permute-start(f32[64,512]{1,0:T(8,128)S(1)} %constant_dynamic-update-slice_fusion.r0), channel_id=1, source_target_pairs={{0,32},{4,36},{8,40},{12,44},{16,48},{20,52},{24,56},{28,60},{32,0... | collective-permute-start | bytes 393224 | tf_op jit(solution)/shard_map/ppermute | solution.py:252
  164.9 0.1 pad_add_fusion.place_ref
  165.0 5.3 %collective-permute-done.24.r3 = f32[64,512]{1,0:T(8,128)S(1)} collective-permute-done((f32[64,512]{1,0:T(8,128)S(1)}, f32[64,512]{1,0:T(8,128)S(1)}, u32[]{:S(2)}, u32[]{:S(2)}) %collective-permute-start.24) | collective-permute-done | bytes 131104 | tf_op jit(solution)/shard_map/ppermute | solution.py:252
  170.3 0.5 collective-permute-done.22.r1
  170.8 1.6 copy-done.2
  172.4 1.6 copy-done.4
  174.0 8.2 %finish.1 = (f32[512,4096]{1,0:T(8,128)}, f32[512,4096]{1,0:T(8,128)}, f32[32,4096]{1,0:T(8,128)}) custom-call(s32[3]{0:T(128)S(1)} %pad_add_fusion.place_ref, bf16[32,2048]{1,0:T(8,128)(2,1)S(1)} %get-tuple-element.24.o_ref, f32[64,512]{1,0:T(8,128)S(1)} %constant_dynamic-update-slice_fusion.r0, f32[64,512]{1,0:T(8,128)S(1)} %collective-permute-done.22.r1, ...), custom_call_target="tpu_custom_call" | custom-call | tf_op jit(solution)/shard_map/finish/pallas_call | solution.py:198
  (25 shorter events, 0.3 us)
Async XLA Ops:
  0.6 55.7 %copy-start = (f32[4096,32]{0,1:T(8,128)S(1)}, f32[4096,32]{0,1:T(8,128)}, u32[]{:S(2)}) copy-start(f32[4096,32]{0,1:T(8,128)} %param.5) | copy-start | bytes 1572868
  3.8 4.6 %copy-start.3 = (bf16[512,2048]{1,0:T(8,128)(2,1)}, bf16[512,2048]{1,0:T(8,128)(2,1)S(1)}, u32[]{:S(2)}) copy-start(bf16[512,2048]{1,0:T(8,128)(2,1)S(1)} %half_of_memory.3.other_ref) | copy-start | bytes 6291460
  3.8 5.3 %collective-permute-start = (bf16[512,2048]{1,0:T(8,128)(2,1)S(1)}, bf16[512,2048]{1,0:T(8,128)(2,1)S(1)}, u32[]{:S(2)}, u32[]{:S(2)}) collective-permute-start(bf16[512,2048]{1,0:T(8,128)(2,1)S(1)} %half_of_memory.3.other_ref), channel_id=1, source_target_pairs={{0,4},{4,0},{8,12},{12,8},{16,20},{20,16},{24,28},{28,24},{32,36},... | collective-permute-start | bytes 6291464 | tf_op jit(solution)/shard_map/ppermute | solution.py:235
  8.4 4.7 %copy-start.1 = (bf16[512,2048]{1,0:T(8,128)(2,1)}, bf16[512,2048]{1,0:T(8,128)(2,1)S(1)}, u32[]{:S(2)}) copy-start(bf16[512,2048]{1,0:T(8,128)(2,1)S(1)} %half_of_memory.2.a_ref.mine_ref) | copy-start | bytes 6291460
  9.1 1.3 copy-start.6
  48.6 1.3 copy-start.5
  49.9 33.3 %all-to-all-start.1 = ((bf16[16,128,512]{2,1,0:T(8,128)(2,1)}), bf16[16,128,512]{2,1,0:T(8,128)(2,1)S(1)}, u32[]{:S(2)}, u32[]{:S(2)}) async-start(bf16[16,128,512]{2,1,0:T(8,128)(2,1)} %copy-done.5), calls=%async_computation.1 | async-start | bytes 4194304 | tf_op jit(solution)/shard_map/all_to_all | solution.py:239
  83.9 3.1 %collective-permute-start.1 = (f32[32,1024]{1,0:T(8,128)S(1)}, f32[32,1024]{1,0:T(8,128)S(1)}, u32[]{:S(2)}, u32[]{:S(2)}) collective-permute-start(f32[32,1024]{1,0:T(8,128)S(1)} %get-tuple-element.17), channel_id=1, source_target_pairs={{0,4},{4,0},{8,12},{12,8},{16,20},{20,16},{24,28},{28,24},{32,36},... | collective-permute-start | bytes 393224 | tf_op jit(solution)/shard_map/ppermute | solution.py:166
  87.0 6.3 %collective-permute-start.4 = (f32[32,1024]{1,0:T(8,128)S(1)}, f32[32,1024]{1,0:T(8,128)S(1)}, u32[]{:S(2)}, u32[]{:S(2)}) collective-permute-start(f32[32,1024]{1,0:T(8,128)S(1)} %add.60), channel_id=1, source_target_pairs={{0,64},{4,68},{8,72},{12,76},{16,80},{20,84},{24,88},{28,92},{32,9... | collective-permute-start | bytes 393224 | tf_op jit(solution)/shard_map/ppermute | solution.py:167
  88.0 8.8 %collective-permute-start.3 = (f32[32,1024]{1,0:T(8,128)S(1)}, f32[32,1024]{1,0:T(8,128)S(1)}, u32[]{:S(2)}, u32[]{:S(2)}) collective-permute-start(f32[32,1024]{1,0:T(8,128)S(1)} %add.60), channel_id=1, source_target_pairs={{0,96},{4,100},{8,104},{12,108},{16,112},{20,116},{24,120},{28,124... | collective-permute-start | bytes 393224 | tf_op jit(solution)/shard_map/ppermute | solution.py:167
  88.7 8.1 %collective-permute-start.2 = (f32[32,1024]{1,0:T(8,128)S(1)}, f32[32,1024]{1,0:T(8,128)S(1)}, u32[]{:S(2)}, u32[]{:S(2)}) collective-permute-start(f32[32,1024]{1,0:T(8,128)S(1)} %add.60), channel_id=1, source_target_pairs={{0,32},{4,36},{8,40},{12,44},{16,48},{20,52},{24,56},{28,60},{32,0... | collective-permute-start | bytes 393224 | tf_op jit(solution)/shard_map/ppermute | solution.py:167
  96.9 1.6 collective-permute-start.5
  104.5 1.4 collective-permute-start.6
  105.9 6.3 %collective-permute-start.9 = (f32[32,1024]{1,0:T(8,128)S(1)}, f32[32,1024]{1,0:T(8,128)S(1)}, u32[]{:S(2)}, u32[]{:S(2)}) collective-permute-start(f32[32,1024]{1,0:T(8,128)S(1)} %add.64), channel_id=1, source_target_pairs={{0,64},{4,68},{8,72},{12,76},{16,80},{20,84},{24,88},{28,92},{32,9... | collective-permute-start | bytes 393224 | tf_op jit(solution)/shard_map/ppermute | solution.py:167
  106.9 8.8 %collective-permute-start.8 = (f32[32,1024]{1,0:T(8,128)S(1)}, f32[32,1024]{1,0:T(8,128)S(1)}, u32[]{:S(2)}, u32[]{:S(2)}) collective-permute-start(f32[32,1024]{1,0:T(8,128)S(1)} %add.64), channel_id=1, source_target_pairs={{0,96},{4,100},{8,104},{12,108},{16,112},{20,116},{24,120},{28,124... | collective-permute-start | bytes 393224 | tf_op jit(solution)/shard_map/ppermute | solution.py:167
  107.7 7.9 %collective-permute-start.7 = (f32[32,1024]{1,0:T(8,128)S(1)}, f32[32,1024]{1,0:T(8,128)S(1)}, u32[]{:S(2)}, u32[]{:S(2)}) collective-permute-start(f32[32,1024]{1,0:T(8,128)S(1)} %add.64), channel_id=1, source_target_pairs={{0,32},{4,36},{8,40},{12,44},{16,48},{20,52},{24,56},{28,60},{32,0... | collective-permute-start | bytes 393224 | tf_op jit(solution)/shard_map/ppermute | solution.py:167
  115.7 1.6 collective-permute-start.10
  123.3 1.4 collective-permute-start.11
  124.7 6.3 %collective-permute-start.14 = (f32[32,1024]{1,0:T(8,128)S(1)}, f32[32,1024]{1,0:T(8,128)S(1)}, u32[]{:S(2)}, u32[]{:S(2)}) collective-permute-start(f32[32,1024]{1,0:T(8,128)S(1)} %add.68), channel_id=1, source_target_pairs={{0,64},{4,68},{8,72},{12,76},{16,80},{20,84},{24,88},{28,92},{32,9... | collective-permute-start | bytes 393224 | tf_op jit(solution)/shard_map/ppermute | solution.py:167
  125.7 8.8 %collective-permute-start.13 = (f32[32,1024]{1,0:T(8,128)S(1)}, f32[32,1024]{1,0:T(8,128)S(1)}, u32[]{:S(2)}, u32[]{:S(2)}) collective-permute-start(f32[32,1024]{1,0:T(8,128)S(1)} %add.68), channel_id=1, source_target_pairs={{0,96},{4,100},{8,104},{12,108},{16,112},{20,116},{24,120},{28,124... | collective-permute-start | bytes 393224 | tf_op jit(solution)/shard_map/ppermute | solution.py:167
  126.6 7.9 %collective-permute-start.12 = (f32[32,1024]{1,0:T(8,128)S(1)}, f32[32,1024]{1,0:T(8,128)S(1)}, u32[]{:S(2)}, u32[]{:S(2)}) collective-permute-start(f32[32,1024]{1,0:T(8,128)S(1)} %add.68), channel_id=1, source_target_pairs={{0,32},{4,36},{8,40},{12,44},{16,48},{20,52},{24,56},{28,60},{32,0... | collective-permute-start | bytes 393224 | tf_op jit(solution)/shard_map/ppermute | solution.py:167
  134.6 1.6 collective-permute-start.15
  142.2 1.4 collective-permute-start.16
  143.6 6.3 %collective-permute-start.19 = (f32[32,1024]{1,0:T(8,128)S(1)}, f32[32,1024]{1,0:T(8,128)S(1)}, u32[]{:S(2)}, u32[]{:S(2)}) collective-permute-start(f32[32,1024]{1,0:T(8,128)S(1)} %add.72), channel_id=1, source_target_pairs={{0,64},{4,68},{8,72},{12,76},{16,80},{20,84},{24,88},{28,92},{32,9... | collective-permute-start | bytes 393224 | tf_op jit(solution)/shard_map/ppermute | solution.py:167
  144.6 8.8 %collective-permute-start.18 = (f32[32,1024]{1,0:T(8,128)S(1)}, f32[32,1024]{1,0:T(8,128)S(1)}, u32[]{:S(2)}, u32[]{:S(2)}) collective-permute-start(f32[32,1024]{1,0:T(8,128)S(1)} %add.72), channel_id=1, source_target_pairs={{0,96},{4,100},{8,104},{12,108},{16,112},{20,116},{24,120},{28,124... | collective-permute-start | bytes 393224 | tf_op jit(solution)/shard_map/ppermute | solution.py:167
  145.5 7.9 %collective-permute-start.17 = (f32[32,1024]{1,0:T(8,128)S(1)}, f32[32,1024]{1,0:T(8,128)S(1)}, u32[]{:S(2)}, u32[]{:S(2)}) collective-permute-start(f32[32,1024]{1,0:T(8,128)S(1)} %add.72), channel_id=1, source_target_pairs={{0,32},{4,36},{8,40},{12,44},{16,48},{20,52},{24,56},{28,60},{32,0... | collective-permute-start | bytes 393224 | tf_op jit(solution)/shard_map/ppermute | solution.py:167
  153.4 1.6 collective-permute-start.20
  160.4 1.3 collective-permute-start.21
  161.7 8.6 %collective-permute-start.24 = (f32[64,512]{1,0:T(8,128)S(1)}, f32[64,512]{1,0:T(8,128)S(1)}, u32[]{:S(2)}, u32[]{:S(2)}) collective-permute-start(f32[64,512]{1,0:T(8,128)S(1)} %constant_dynamic-update-slice_fusion.r0), channel_id=1, source_target_pairs={{0,96},{4,100},{8,104},{12,108},{16,112},{20,116},{24,120},{28,124... | collective-permute-start | bytes 393224 | tf_op jit(solution)/shard_map/ppermute | solution.py:252
  162.4 7.9 %collective-permute-start.23 = (f32[64,512]{1,0:T(8,128)S(1)}, f32[64,512]{1,0:T(8,128)S(1)}, u32[]{:S(2)}, u32[]{:S(2)}) collective-permute-start(f32[64,512]{1,0:T(8,128)S(1)} %constant_dynamic-update-slice_fusion.r0), channel_id=1, source_target_pairs={{0,64},{4,68},{8,72},{12,76},{16,80},{20,84},{24,88},{28,92},{32,9... | collective-permute-start | bytes 393224 | tf_op jit(solution)/shard_map/ppermute | solution.py:252
  162.9 7.9 %collective-permute-start.22 = (f32[64,512]{1,0:T(8,128)S(1)}, f32[64,512]{1,0:T(8,128)S(1)}, u32[]{:S(2)}, u32[]{:S(2)}) collective-permute-start(f32[64,512]{1,0:T(8,128)S(1)} %constant_dynamic-update-slice_fusion.r0), channel_id=1, source_target_pairs={{0,32},{4,36},{8,40},{12,44},{16,48},{20,52},{24,56},{28,60},{32,0... | collective-permute-start | bytes 393224 | tf_op jit(solution)/shard_map/ppermute | solution.py:252
  170.8 1.6 copy-start.2
  172.4 1.6 copy-start.4

commit v2 on v1

v2 whole, which is shorter than its diff:
```python
import jax
import jax.numpy as jnp
from jax import lax
from jax.experimental import pallas as pl
from jax.experimental.pallas import tpu as pltpu
from jax.sharding import PartitionSpec as P

W = 4096
RANK = 32
ITERS = 4
ROWS = 2048
N_DP = 32
N_OWNER = 4
HALF = W // 2
COLS = HALF // 4
ROWS_OWN = ROWS // N_OWNER
PIECE = ROWS_OWN // 4
MID = ROWS // 2
BF = jnp.bfloat16
F32 = jnp.float32
HIGHEST = lax.Precision.HIGHEST

CORE = [(i, i ^ 1) for i in range(N_DP)]
STEP = {"z": 32, "x": 8, "y": 1}


def along(array, first, second, k):
    step = (STEP[first], STEP[second])
    pairs = [(i, i ^ (k * step[(i >> 2) & 1])) for i in range(N_DP * N_OWNER)]
    return lax.ppermute(array, ("dp", "owner"), pairs)


def exchange(arrays, first, second):
    return [arrays[0]] + [along(arrays[k], first, second, k) for k in (1, 2, 3)]


def spread(array, first, second):
    return exchange([array] * 4, first, second)


def params(**kw):
    return pltpu.CompilerParams(vmem_limit_bytes=48 * 1024 * 1024, **kw)


def half_of_memory(grad, error, which):
    def body(which_ref, g_ref, e_ref, o_ref):
        o_ref[...] = (g_ref[...].astype(F32) + e_ref[...].astype(F32)).astype(BF)

    steps = 4
    rows = ROWS_OWN // steps
    spec = pl.BlockSpec((rows, HALF), lambda i, w: (i, w[0]))
    return pl.pallas_call(
        body,
        grid_spec=pltpu.PrefetchScalarGridSpec(
            num_scalar_prefetch=1,
            grid=(steps,),
            in_specs=[spec, spec],
            out_specs=pl.BlockSpec((rows, HALF), lambda i, w: (i, 0)),
        ),
        out_shape=jax.ShapeDtypeStruct((ROWS_OWN, HALF), BF),
        compiler_params=params(),
        name="half_of_memory",
    )(which, grad, error)


def pair_sum(place, mine, received):
    def body(place_ref, *refs):
        for k in range(4):
            refs[8 + k][0] = (refs[k][...].astype(F32) + refs[4 + k][...].astype(F32)).astype(BF)

    def index(j, p, k):
        first = p[2] == 0
        return jnp.where(first, j, p[1] ^ k), jnp.where(first, p[0] ^ k, j)

    cuts = [pl.BlockSpec((PIECE, COLS), lambda j, p, k=k: index(j, p, k)) for k in range(4)]
    return pl.pallas_call(
        body,
        grid_spec=pltpu.PrefetchScalarGridSpec(
            num_scalar_prefetch=1,
            grid=(4,),
            in_specs=cuts + cuts,
            out_specs=[pl.BlockSpec((1, PIECE, COLS), lambda j, p: (j, 0, 0))] * 4,
        ),
        out_shape=[jax.ShapeDtypeStruct((4, PIECE, COLS), BF)] * 4,
        compiler_params=params(),
        name="pair_sum",
    )(place, *[mine] * 4, *[received] * 4)


SCALARS = pl.BlockSpec(memory_space=pltpu.SMEM)
WHOLE = pl.BlockSpec(memory_space=pltpu.VMEM)


def call(body, name, out_shape, place, *arrays):
    return pl.pallas_call(
        body,
        in_specs=[SCALARS] + [WHOLE] * len(arrays),
        out_specs=jax.tree.map(lambda s: WHOLE, out_shape),
        out_shape=out_shape,
        compiler_params=params(),
        name=name,
    )(place, *arrays)


def cut(index, size):
    return pl.ds(pl.multiple_of(index * size, size), size)


def first_sum(place, parts):
    def body(place_ref, *refs):
        own = jnp.where(place_ref[2] == 0, place_ref[1], place_ref[0])
        for k in range(4):
            total = refs[0][own ^ k].astype(F32)
            for ref in refs[1:4]:
                total = total + ref[own ^ k].astype(F32)
            refs[4 + k][...] = total.astype(BF)

    return call(body, "first_sum", [jax.ShapeDtypeStruct((PIECE, COLS), BF)] * 4, place, *parts)


def second_sum(place, parts):
    def body(place_ref, a_ref, b_ref, c_ref, d_ref, o_ref):
        total = a_ref[...].astype(F32) + b_ref[...].astype(F32)
        o_ref[...] = (total + (c_ref[...].astype(F32) + d_ref[...].astype(F32))).astype(BF)

    return call(body, "second_sum", jax.ShapeDtypeStruct((PIECE, COLS), BF), place, *parts)


def thirds(x):
    high = x.astype(BF)
    rest = x - high.astype(F32)
    mid = rest.astype(BF)
    low = (rest - mid.astype(F32)).astype(BF)
    return jnp.concatenate([high, mid, low], axis=0)


def dot(a, b, dims, precision=None):
    return lax.dot_general(a, b, ((dims[0], dims[1]), ((), ())), precision=precision, preferred_element_type=F32)


def thirds(x):
    high = x.astype(BF)
    rest = x - high.astype(F32)
    mid = rest.astype(BF)
    low = (rest - mid.astype(F32)).astype(BF)
    return jnp.concatenate([high, mid, low], axis=0)


def add_thirds(x):
    return x[:RANK] + (x[RANK : 2 * RANK] + x[2 * RANK :])


def reorder(rows, place_ref):
    blocks = [rows[:, i * PIECE : (i + 1) * PIECE] for i in range(16)]
    swapped = jnp.concatenate([blocks[(i % 4) * 4 + i // 4] for i in range(16)], axis=1)
    return jnp.where(place_ref[2] == 0, rows, swapped)


def store_halves(place_ref, left, own_ref, oth_ref):
    left = reorder(left, place_ref)
    low, high = left[:, :MID], left[:, MID:]
    first = place_ref[2] == 0
    own_ref[...] = jnp.where(first, low, high)
    oth_ref[...] = jnp.where(first, high, low)


def load_halves(place_ref, own_ref, oth_ref):
    first = place_ref[2] == 0
    own, oth = own_ref[...], oth_ref[...]
    return jnp.concatenate([jnp.where(first, own, oth), jnp.where(first, oth, own)], axis=1)


def times_m(rows, m_refs):
    parts = [dot(rows[:, i * ROWS_OWN : (i + 1) * ROWS_OWN], ref[...], ((1,), (0,))) for i, ref in enumerate(m_refs)]
    return (parts[0] + parts[1]) + (parts[2] + parts[3])


def times_m_t(rows, m_refs):
    return jnp.concatenate([dot(rows, ref[...], ((1,), (1,))) for ref in m_refs], axis=1)


def inverse_factor(gram):
    row = lax.broadcasted_iota(jnp.int32, (RANK, 128), 0)
    lane = lax.broadcasted_iota(jnp.int32, (RANK, 128), 1)
    wide = jnp.concatenate([gram, jnp.zeros((RANK, 128 - RANK), F32)], axis=1)
    trace = jnp.sum(jnp.where(row == lane, wide, 0.0), keepdims=True)
    shift = 1e-06 * (trace / RANK)
    work = wide + jnp.where(row == lane, shift, 0.0) + jnp.where(row + RANK == lane, 1.0, 0.0)
    for k in range(RANK - 1):
        col = jnp.broadcast_to(work[:, k : k + 1], (RANK, 128))
        factor = jnp.where(row > k, col / col[k : k + 1, :], 0.0)
        work = work - factor * work[k : k + 1, :]
    pivot = jnp.sum(jnp.where(row == lane, work, 0.0), axis=1, keepdims=True)
    return work[:, RANK : 2 * RANK] * lax.rsqrt(pivot)


HALVES = [jax.ShapeDtypeStruct((RANK, MID), F32)] * 2


def first_left(place, right_t, m):
    def body(place_ref, r_ref, m0, m1, m2, m3, own_ref, oth_ref):
        cols = cut(place_ref[2] * 4 + place_ref[0], COLS)
        left = times_m_t(r_ref[:, cols].astype(BF), (m0, m1, m2, m3))
        store_halves(place_ref, left, own_ref, oth_ref)

    return call(body, "first_left", HALVES, place, right_t, *m)


def next_left(place, own, oth, inverse, m):
    def body(place_ref, own_in, oth_in, *refs):
        left = load_halves(place_ref, own_in, oth_in)
        if inverse is not None:
            left = dot(refs[0][...], left, ((1,), (0,)), HIGHEST) * (1.0 / N_DP)
            refs = refs[1:]
        m_refs, (left_ref, own_ref, oth_ref) = refs[:4], refs[4:]
        left_ref[...] = left
        right = add_thirds(times_m(thirds(reorder(left, place_ref)), m_refs))
        following = add_thirds(times_m_t(thirds(right), m_refs))
        store_halves(place_ref, following, own_ref, oth_ref)

    shapes = [jax.ShapeDtypeStruct((RANK, ROWS), F32)] + HALVES
    extra = [] if inverse is None else [inverse]
    return call(body, "next_left", shapes, place, own, oth, *extra, *m)


def inverse_of(place, left):
    def body(place_ref, left_ref, o_ref):
        left = left_ref[...]
        o_ref[...] = inverse_factor(dot(left, left, ((1,), (1,)), HIGHEST))

    return call(body, "inverse_of", jax.ShapeDtypeStruct((RANK, RANK), F32), place, left)


def last_right(place, own, oth, inverse, m):
    def body(place_ref, own_in, oth_in, inv_ref, m0, m1, m2, m3, ortho_ref, right_ref):
        left = load_halves(place_ref, own_in, oth_in)
        left = dot(inv_ref[...], left, ((1,), (0,)), HIGHEST) * (1.0 / N_DP)
        gram = dot(left, left, ((1,), (1,)), HIGHEST)
        ortho = dot(inverse_factor(gram), left, ((1,), (0,)), HIGHEST).astype(BF)
        for k in range(4):
            ortho_ref[:, cut(place_ref[1] ^ k, PIECE)] = ortho[:, k * PIECE : (k + 1) * PIECE]
        right_ref[...] = times_m(reorder(ortho, place_ref), (m0, m1, m2, m3)) * (1.0 / N_DP)

    shapes = [jax.ShapeDtypeStruct((RANK, ROWS_OWN), BF), jax.ShapeDtypeStruct((RANK, COLS), F32)]
    return call(body, "last_right", shapes, place, own, oth, inverse, *m)


def sum_over_group(own, oth, beside=None):
    own = own + lax.ppermute(oth, "dp", CORE)
    parts = spread(own, "z", "z")
    if beside is not None:
        parts, beside = lax.optimization_barrier((parts, beside))
    a, b, c, d = parts
    own = (a + b) + (c + d)
    return own, lax.ppermute(own, "dp", CORE), beside


def finish(place, ortho, rights, mine, other):
    def body(place_ref, o_ref, r0, r1, r2, r3, mine_ref, other_ref, up_ref, err_ref, right_ref):
        step = pl.program_id(0)
        left = jnp.concatenate([o_ref[...]] * 3, axis=0)
        for j in range(2):
            for k, ref in enumerate((r0, r1, r2, r3)):

                @pl.when(step == 4 * j + k)
                def _():
                    right = ref[j * RANK : (j + 1) * RANK, :]
                    right_ref[...] = right
                    update = dot(left, thirds(right), ((0,), (0,)))
                    up_ref[...] = update
                    memory = (mine_ref, other_ref)[j][...].astype(F32)
                    err_ref[...] = memory - update

    def group(s, p):
        return (s % 4) ^ p[0]

    whole = pl.BlockSpec((2 * RANK, COLS), lambda s, p: (0, 0))
    out_block = lambda s, p: (0, ((s // 4) ^ p[2]) * 4 + group(s, p))
    return pl.pallas_call(
        body,
        grid_spec=pltpu.PrefetchScalarGridSpec(
            num_scalar_prefetch=1,
            grid=(8,),
            in_specs=[
                pl.BlockSpec((RANK, ROWS_OWN), lambda s, p: (0, 0)),
                whole,
                whole,
                whole,
                whole,
                pl.BlockSpec((ROWS_OWN, COLS), lambda s, p: (0, group(jnp.minimum(s, 3), p))),
                pl.BlockSpec((ROWS_OWN, COLS), lambda s, p: (0, group(jnp.maximum(s, 4), p))),
            ],
            out_specs=[
                pl.BlockSpec((ROWS_OWN, COLS), out_block),
                pl.BlockSpec((ROWS_OWN, COLS), out_block),
                pl.BlockSpec((RANK, COLS), out_block),
            ],
        ),
        out_shape=(
            jax.ShapeDtypeStruct((ROWS_OWN, W), F32),
            jax.ShapeDtypeStruct((ROWS_OWN, W), F32),
            jax.ShapeDtypeStruct((RANK, W), F32),
        ),
        compiler_params=params(),
        name="finish",
    )(place, ortho, *rights, mine, other)


def per_device(grad, error, warm_right):
    dp = lax.axis_index("dp")
    core = dp & 1
    place = jnp.stack([dp >> 3, (dp >> 1) & 3, core]).astype(jnp.int32)

    other = half_of_memory(grad[0], error[0], (1 - core)[None])
    received = lax.ppermute(other, "dp", CORE)
    mine = half_of_memory(grad[0], error[0], core[None])
    pairs = exchange(pair_sum(place, mine, received), "z", "x")
    piece = second_sum(place, exchange(first_sum(place, pairs), "x", "z"))
    m = spread(jnp.concatenate(spread(piece, "x", "y"), axis=0), "y", "x")

    own, oth, inverse = sum_over_group(*first_left(place, warm_right.T, m))
    for step in range(ITERS - 1):
        left, own, oth = next_left(place, own, oth, inverse, m)
        own, oth, inverse = sum_over_group(own, oth, inverse_of(place, left))
    ortho, right = last_right(place, own, oth, inverse, m)

    pair = jnp.concatenate([right, lax.ppermute(right, "dp", CORE)], axis=0)
    update, new_error, right_t = finish(place, ortho, spread(pair, "z", "z"), mine, other)
    return update, new_error[None], right_t.T


def solution(mesh):
    placed = (P("dp", "owner", None), P("dp", "owner", None), P())
    return jax.shard_map(
        per_device,
        mesh=mesh,
        in_specs=placed,
        out_specs=(P("owner", None), P("dp", "owner", None), P()),
        check_vma=False,
    )
```

time: 186 us -> 157 us (0.84); the launches traced: 182 us -> 157 us
  blocking collectives: 34.8 us -> 0 us
  starting transfers between devices: 28 us -> 46.6 us
  waiting for transfers between devices: 70.4 us -> 61.5 us
  local copies, waits for them, and re-layouts: 5.86 us -> 0.01 us
  Pallas kernels: 42 us -> 47.4 us
    all_to_all x1 -> x0, blocking collectives: 34.8 us -> none  [per_device(): pieces = lax.all_to_all(blocks, 'dp', 0, 0, axis_index_groups=ZX_GROUPS)]
    all_to_all x1 -> x0, waiting for transfers between devices: 26.8 us -> none  [per_device(): lax.all_to_all(piece_sum(pieces), ('dp', 'owner'), 0, 0, axis_index_group...]
    ppermute x19 -> x31, starting transfers between devices: 16.5 us -> 38.4 us  [the longest x27 32.1 us: along(): return lax.ppermute(array, ('dp', 'owner'), pairs)]
    ppermute x19 -> x31, waiting for transfers between devices: 38 us -> 55.9 us  [the longest x27 51.9 us: along(): return lax.ppermute(array, ('dp', 'owner'), pairs)]
    all_to_all x1 -> x0, starting transfers between devices: 6.47 us -> none  [per_device(): lax.all_to_all(piece_sum(pieces), ('dp', 'owner'), 0, 0, axis_index_group...]
    unnamed x15 -> x3, local copies, waits for them, and re-layouts: 5.84 us -> 0.01 us
    pallas_call x7 -> x11, Pallas kernels: 27.6 us -> 33.1 us  [the longest x10 29.5 us: call(): pl.pallas_call(body, in_specs=[SCALARS] + [WHOLE] * len(arrays), out_spec...]
    ppermute x4, starting transfers between devices: 3.22 us -> 6.29 us  [sum_over_group(): own = own + lax.ppermute(oth, 'dp', CORE)]
  transfers between devices with their start and end apart: 26 -> 37, of which waited for: 21 -> 28; matrix products, arithmetic and copies ran while one was open for 0% -> 0% of each run, Pallas kernels for 2% -> 11%
where the time goes in v2:
time: 157 us
  waiting for transfers between devices  61.5 us (39%)
  Pallas kernels  47.4 us (30%)
  starting transfers between devices  46.6 us (30%)
    ppermute x27, waiting for transfers between devices, along(): return lax.ppermute(array, ('dp', 'owner'), pairs)  51.9 us
    ppermute x27, starting transfers between devices, along(): return lax.ppermute(array, ('dp', 'owner'), pairs)  32.1 us
    pallas_call x10, Pallas kernels, call(): pl.pallas_call(body, in_specs=[SCALARS] + [WHOLE] * len(arrays), out_spec...  29.5 us
    pallas_call x1, Pallas kernels, finish(): pl.pallas_call(body, grid_spec=pltpu.PrefetchScalarGridSpec(num_scalar_pr...  8.18 us
    ppermute x4, starting transfers between devices, sum_over_group(): return (own, lax.ppermute(own, 'dp', CORE), beside)  6.32 us
    ppermute x4, starting transfers between devices, sum_over_group(): own = own + lax.ppermute(oth, 'dp', CORE)  6.29 us
    pallas_call x2, Pallas kernels, half_of_memory(): pl.pallas_call(body, grid_spec=pltpu.PrefetchScalarGridSpec(num_scalar_pr...  6.13 us
    ppermute x4, waiting for transfers between devices, sum_over_group(): own = own + lax.ppermute(oth, 'dp', CORE)  3.95 us
  transfers between devices with their start and end apart: 37, of which 28 were waited for; matrix products, arithmetic and copies ran while one was open for 0% of the time, Pallas kernels for 11%

profile of v2, /device:TPU:1, one launch (start us, length us, event | category | flops | bytes accessed | tf_op | source)
XLA Modules:
  0.0 156.6 jit_solution(17056529215114094119)
XLA Ops:
  0.6 3.1 %half_of_memory.3.other_ref = bf16[512,2048]{1,0:T(8,128)(2,1)S(1)} custom-call(s32[1]{0:T(128)} %bitcast.6.which_ref, bf16[512,4096]{1,0:T(8,128)(2,1)} %bitcast.10, bf16[512,4096]{1,0:T(8,128)(2,1)} %bitcast.12), custom_call_target="tpu_custom_call" | custom-call | tf_op jit(solution)/shard_map/half_of_memory/pallas_call | solution.py:52
  3.7 1.5 collective-permute-start
  5.2 3.1 %half_of_memory.2.refs_0_.refs_1_.refs_2_.refs_3_.mine_ref = bf16[512,2048]{1,0:T(8,128)(2,1)S(1)} custom-call(s32[1]{0:T(128)} %bitcast.2.which_ref, bf16[512,4096]{1,0:T(8,128)(2,1)} %bitcast.11, bf16[512,4096]{1,0:T(8,128)(2,1)} %bitcast.13), custom_call_target="tpu_custom_call" | custom-call | tf_op jit(solution)/shard_map/half_of_memory/pallas_call | solution.py:52
  8.4 0.8 collective-permute-done.refs_4_.refs_5_.refs_6_.refs_7_
  9.1 3.6 %pair_sum.1 = (bf16[4,128,512]{2,1,0:T(8,128)(2,1)S(1)}, bf16[4,128,512]{2,1,0:T(8,128)(2,1)S(1)}, bf16[4,128,512]{2,1,0:T(8,128)(2,1)S(1)}, bf16[4,128,512]{2,1,0:T(8,128)(2,1)S(1)}) custom-call(s32[3]{0:T(128)S(1)} %pad_add_fusion.place_ref, bf16[512,2048]{1,0:T(8,128)(2,1)S(1)} %half_of_memory.2.refs_0_.refs_1_.refs_2_.refs_3_.mine_ref, ...), custom_call_target="tpu_custom_call" | custom-call | tf_op jit(solution)/shard_map/pair_sum/pallas_call | solution.py:76
  12.7 1.4 collective-permute-start.1
  14.1 2.5 %collective-permute-start.2 = (bf16[4,128,512]{2,1,0:T(8,128)(2,1)S(1)}, bf16[4,128,512]{2,1,0:T(8,128)(2,1)S(1)}, u32[]{:S(2)}, u32[]{:S(2)}) collective-permute-start(bf16[4,128,512]{2,1,0:T(8,128)(2,1)S(1)} %get-tuple-element.44), channel_id=1, source_target_pairs={{0,64},{1,65},{2,66},{3,67},{4,20},{5,21},{6,22},{7,23},{8,72},{9,... | collective-permute-start | bytes 1572872 | tf_op jit(solution)/shard_map/ppermute | solution.py:30
  16.7 4.5 %collective-permute-done.1.refs_1_ = bf16[4,128,512]{2,1,0:T(8,128)(2,1)S(1)} collective-permute-done((bf16[4,128,512]{2,1,0:T(8,128)(2,1)S(1)}, bf16[4,128,512]{2,1,0:T(8,128)(2,1)S(1)}, u32[]{:S(2)}, u32[]{:S(2)}) %collective-permute-start.1) | collective-permute-done | bytes 524320 | tf_op jit(solution)/shard_map/ppermute | solution.py:30
  21.1 7.9 %collective-permute-done.2.refs_2_ = bf16[4,128,512]{2,1,0:T(8,128)(2,1)S(1)} collective-permute-done((bf16[4,128,512]{2,1,0:T(8,128)(2,1)S(1)}, bf16[4,128,512]{2,1,0:T(8,128)(2,1)S(1)}, u32[]{:S(2)}, u32[]{:S(2)}) %collective-permute-start.2) | collective-permute-done | bytes 524320 | tf_op jit(solution)/shard_map/ppermute | solution.py:30
  29.1 2.6 %collective-permute-done.3.refs_3_ = bf16[4,128,512]{2,1,0:T(8,128)(2,1)S(1)} collective-permute-done((bf16[4,128,512]{2,1,0:T(8,128)(2,1)S(1)}, bf16[4,128,512]{2,1,0:T(8,128)(2,1)S(1)}, u32[]{:S(2)}, u32[]{:S(2)}) %collective-permute-start.3) | collective-permute-done | bytes 524320 | tf_op jit(solution)/shard_map/ppermute | solution.py:30
  31.7 0.8 first_sum.1
  32.5 1.4 collective-permute-start.4
  33.9 3.3 %collective-permute-start.5 = (bf16[128,512]{1,0:T(8,128)(2,1)S(1)}, bf16[128,512]{1,0:T(8,128)(2,1)S(1)}, u32[]{:S(2)}, u32[]{:S(2)}) collective-permute-start(bf16[128,512]{1,0:T(8,128)(2,1)S(1)} %get-tuple-element.48), channel_id=1, source_target_pairs={{0,16},{1,17},{2,18},{3,19},{4,68},{5,69},{6,70},{7,71},{8,24},{9,... | collective-permute-start | bytes 393224 | tf_op jit(solution)/shard_map/ppermute | solution.py:30
  37.3 3.8 %collective-permute-done.5.c_ref = bf16[128,512]{1,0:T(8,128)(2,1)S(1)} collective-permute-done((bf16[128,512]{1,0:T(8,128)(2,1)S(1)}, bf16[128,512]{1,0:T(8,128)(2,1)S(1)}, u32[]{:S(2)}, u32[]{:S(2)}) %collective-permute-start.5) | collective-permute-done | bytes 131104 | tf_op jit(solution)/shard_map/ppermute | solution.py:30
  41.0 1.7 %collective-permute-done.6.d_ref = bf16[128,512]{1,0:T(8,128)(2,1)S(1)} collective-permute-done((bf16[128,512]{1,0:T(8,128)(2,1)S(1)}, bf16[128,512]{1,0:T(8,128)(2,1)S(1)}, u32[]{:S(2)}, u32[]{:S(2)}) %collective-permute-start.6) | collective-permute-done | bytes 131104 | tf_op jit(solution)/shard_map/ppermute | solution.py:30
  42.7 0.6 second_sum.1
  43.3 2.8 %collective-permute-start.9 = (bf16[128,512]{1,0:T(8,128)(2,1)S(1)}, bf16[128,512]{1,0:T(8,128)(2,1)S(1)}, u32[]{:S(2)}, u32[]{:S(2)}) collective-permute-start(bf16[128,512]{1,0:T(8,128)(2,1)S(1)} %second_sum.1), channel_id=1, source_target_pairs={{0,24},{1,25},{2,26},{3,27},{4,7},{5,6},{6,5},{7,4},{8,16},{9,17},... | collective-permute-start | bytes 393224 | tf_op jit(solution)/shard_map/ppermute | solution.py:30
  46.8 2.6 %collective-permute-done.9 = bf16[128,512]{1,0:T(8,128)(2,1)S(1)} collective-permute-done((bf16[128,512]{1,0:T(8,128)(2,1)S(1)}, bf16[128,512]{1,0:T(8,128)(2,1)S(1)}, u32[]{:S(2)}, u32[]{:S(2)}) %collective-permute-start.9) | collective-permute-done | bytes 131104 | tf_op jit(solution)/shard_map/ppermute | solution.py:30
  49.5 2.0 %collective-permute-done.8 = bf16[128,512]{1,0:T(8,128)(2,1)S(1)} collective-permute-done((bf16[128,512]{1,0:T(8,128)(2,1)S(1)}, bf16[128,512]{1,0:T(8,128)(2,1)S(1)}, u32[]{:S(2)}, u32[]{:S(2)}) %collective-permute-start.8) | collective-permute-done | bytes 131104 | tf_op jit(solution)/shard_map/ppermute | solution.py:30
  52.1 2.7 %collective-permute-start.10 = (bf16[512,512]{1,0:T(8,128)(2,1)S(1)}, bf16[512,512]{1,0:T(8,128)(2,1)S(1)}, u32[]{:S(2)}, u32[]{:S(2)}) collective-permute-start(bf16[512,512]{1,0:T(8,128)(2,1)S(1)} %pad_maximum_fusion.m0.refs_0_.refs_1_), channel_id=1, source_target_pairs={{0,1},{1,0},{2,3},{3,2},{4,12},{5,13},{6,14},{7,15},{8,9},{9,8},{1... | collective-permute-start | bytes 1572872 | tf_op jit(solution)/shard_map/ppermute | solution.py:30
  54.8 11.9 %collective-permute-done.12.m3.refs_3_.refs_4_ = bf16[512,512]{1,0:T(8,128)(2,1)S(1)} collective-permute-done((bf16[512,512]{1,0:T(8,128)(2,1)S(1)}, bf16[512,512]{1,0:T(8,128)(2,1)S(1)}, u32[]{:S(2)}, u32[]{:S(2)}) %collective-permute-start.12) | collective-permute-done | bytes 524320 | tf_op jit(solution)/shard_map/ppermute | solution.py:30
  66.7 0.6 collective-permute-done.10.m1.refs_1_.refs_2_
  67.4 1.3 first_left.1
  68.6 5.0 %collective-permute-start.13 = (f32[32,1024]{1,0:T(8,128)S(1)}, f32[32,1024]{1,0:T(8,128)S(1)}, u32[]{:S(2)}, u32[]{:S(2)}) collective-permute-start(f32[32,1024]{1,0:T(8,128)S(1)} %get-tuple-element.51), channel_id=1, source_target_pairs={{0,4},{4,0},{8,12},{12,8},{16,20},{20,16},{24,28},{28,24},{32,36},... | collective-permute-start | bytes 393224 | tf_op jit(solution)/shard_map/ppermute | solution.py:249
  73.6 1.0 collective-permute-done.13
  74.8 3.1 %collective-permute-start.14 = (f32[32,1024]{1,0:T(8,128)S(1)}, f32[32,1024]{1,0:T(8,128)S(1)}, u32[]{:S(2)}, u32[]{:S(2)}) collective-permute-start(f32[32,1024]{1,0:T(8,128)S(1)} %add.48), channel_id=1, source_target_pairs={{0,32},{1,33},{2,34},{3,35},{4,36},{5,37},{6,38},{7,39},{8,40},{9,... | collective-permute-start | bytes 393224 | tf_op jit(solution)/shard_map/ppermute | solution.py:30
  77.9 5.8 %collective-permute-done.16 = f32[32,1024]{1,0:T(8,128)S(1)} collective-permute-done((f32[32,1024]{1,0:T(8,128)S(1)}, f32[32,1024]{1,0:T(8,128)S(1)}, u32[]{:S(2)}, u32[]{:S(2)}) %collective-permute-start.16) | collective-permute-done | bytes 131104 | tf_op jit(solution)/shard_map/ppermute | solution.py:30
  83.8 1.5 collective-permute-start.17
  85.3 1.0 collective-permute-done.17.oth_in
  86.3 1.7 %next_left.3 = (f32[32,2048]{1,0:T(8,128)S(1)}, f32[32,1024]{1,0:T(8,128)S(1)}, f32[32,1024]{1,0:T(8,128)S(1)}) custom-call(s32[3]{0:T(128)S(1)} %pad_add_fusion.place_ref, f32[32,1024]{1,0:T(8,128)S(1)} %add_add_fusion.3.own_in, f32[32,1024]{1,0:T(8,128)S(1)} %collective-permute-done.17.oth_in, bf16[512,512]{1,0:T(8,128)(2,1)S(1)} %pad_maximum_fusion.m0.refs_0_.refs_1_, ...), custom_call_target="tpu_custom_call" | custom-call | tf_op jit(solution)/shard_map/next_left/pallas_call | solution.py:95
  88.0 0.4 collective-permute-start.18
  88.4 1.0 collective-permute-done.18
  89.4 0.8 collective-permute-start.21
  90.6 2.2 %collective-permute-start.19 = (f32[32,1024]{1,0:T(8,128)S(1)}, f32[32,1024]{1,0:T(8,128)S(1)}, u32[]{:S(2)}, u32[]{:S(2)}) collective-permute-start(f32[32,1024]{1,0:T(8,128)S(1)} %add.52), channel_id=1, source_target_pairs={{0,32},{1,33},{2,34},{3,35},{4,36},{5,37},{6,38},{7,39},{8,40},{9,... | collective-permute-start | bytes 393224 | tf_op jit(solution)/shard_map/ppermute | solution.py:30
  92.8 5.0 %inverse_of.3.refs_0_ = f32[32,32]{1,0:T(8,128)S(1)} custom-call(s32[3]{0:T(128)S(1)} %pad_add_fusion.place_ref, f32[32,2048]{1,0:T(8,128)S(1)} %get-tuple-element.54.left_ref), custom_call_target="tpu_custom_call" | custom-call | tf_op jit(solution)/shard_map/inverse_of/pallas_call | solution.py:95
  98.2 0.4 collective-permute-done.19
  98.7 1.5 collective-permute-start.22
  100.2 1.0 collective-permute-done.22.oth_in
  101.2 2.0 %next_left.4 = (f32[32,2048]{1,0:T(8,128)S(1)}, f32[32,1024]{1,0:T(8,128)S(1)}, f32[32,1024]{1,0:T(8,128)S(1)}) custom-call(s32[3]{0:T(128)S(1)} %pad_add_fusion.place_ref, f32[32,1024]{1,0:T(8,128)S(1)} %add_add_fusion.2.own_in, f32[32,1024]{1,0:T(8,128)S(1)} %collective-permute-done.22.oth_in, f32[32,32]{1,0:T(8,128)S(1)} %inverse_of.3.refs_0_, ...), custom_call_target="tpu_custom_call" | custom-call | tf_op jit(solution)/shard_map/next_left/pallas_call | solution.py:95
  103.2 0.4 collective-permute-start.23
  103.6 1.0 collective-permute-done.23
  104.6 0.8 collective-permute-start.26
  105.8 2.2 %collective-permute-start.24 = (f32[32,1024]{1,0:T(8,128)S(1)}, f32[32,1024]{1,0:T(8,128)S(1)}, u32[]{:S(2)}, u32[]{:S(2)}) collective-permute-start(f32[32,1024]{1,0:T(8,128)S(1)} %add.56), channel_id=1, source_target_pairs={{0,32},{1,33},{2,34},{3,35},{4,36},{5,37},{6,38},{7,39},{8,40},{9,... | collective-permute-start | bytes 393224 | tf_op jit(solution)/shard_map/ppermute | solution.py:30
  108.0 5.0 %inverse_of.4.refs_0_ = f32[32,32]{1,0:T(8,128)S(1)} custom-call(s32[3]{0:T(128)S(1)} %pad_add_fusion.place_ref, f32[32,2048]{1,0:T(8,128)S(1)} %get-tuple-element.62.left_ref), custom_call_target="tpu_custom_call" | custom-call | tf_op jit(solution)/shard_map/inverse_of/pallas_call | solution.py:95
  112.9 0.4 collective-permute-done.26
  113.4 0.4 collective-permute-done.24
  113.8 1.7 %collective-permute-start.27 = (f32[32,1024]{1,0:T(8,128)S(1)}, f32[32,1024]{1,0:T(8,128)S(1)}, u32[]{:S(2)}, u32[]{:S(2)}) collective-permute-start(f32[32,1024]{1,0:T(8,128)S(1)} %add_add_fusion.1.own_in), channel_id=1, source_target_pairs={{0,4},{4,0},{8,12},{12,8},{16,20},{20,16},{24,28},{28,24},{32,36},... | collective-permute-start | bytes 393224 | tf_op jit(solution)/shard_map/ppermute | solution.py:255
  115.6 1.0 collective-permute-done.27.oth_in
  116.6 2.0 %next_left.5 = (f32[32,2048]{1,0:T(8,128)S(1)}, f32[32,1024]{1,0:T(8,128)S(1)}, f32[32,1024]{1,0:T(8,128)S(1)}) custom-call(s32[3]{0:T(128)S(1)} %pad_add_fusion.place_ref, f32[32,1024]{1,0:T(8,128)S(1)} %add_add_fusion.1.own_in, f32[32,1024]{1,0:T(8,128)S(1)} %collective-permute-done.27.oth_in, f32[32,32]{1,0:T(8,128)S(1)} %inverse_of.4.refs_0_, ...), custom_call_target="tpu_custom_call" | custom-call | tf_op jit(solution)/shard_map/next_left/pallas_call | solution.py:95
  118.6 0.4 collective-permute-start.28
  119.0 1.0 collective-permute-done.28
  120.0 0.8 collective-permute-start.31
  121.1 2.2 %collective-permute-start.29 = (f32[32,1024]{1,0:T(8,128)S(1)}, f32[32,1024]{1,0:T(8,128)S(1)}, u32[]{:S(2)}, u32[]{:S(2)}) collective-permute-start(f32[32,1024]{1,0:T(8,128)S(1)} %add.60), channel_id=1, source_target_pairs={{0,32},{1,33},{2,34},{3,35},{4,36},{5,37},{6,38},{7,39},{8,40},{9,... | collective-permute-start | bytes 393224 | tf_op jit(solution)/shard_map/ppermute | solution.py:30
  123.3 5.0 %inverse_of.5.inv_ref = f32[32,32]{1,0:T(8,128)S(1)} custom-call(s32[3]{0:T(128)S(1)} %pad_add_fusion.place_ref, f32[32,2048]{1,0:T(8,128)S(1)} %get-tuple-element.70.left_ref), custom_call_target="tpu_custom_call" | custom-call | tf_op jit(solution)/shard_map/inverse_of/pallas_call | solution.py:95
  128.7 0.4 collective-permute-done.29
  129.2 1.5 collective-permute-start.32
  130.8 1.0 collective-permute-done.32.oth_in
  131.7 6.2 %last_right.1 = (bf16[32,512]{1,0:T(8,128)(2,1)S(1)}, f32[32,512]{1,0:T(8,128)S(1)}) custom-call(s32[3]{0:T(128)S(1)} %pad_add_fusion.place_ref, f32[32,1024]{1,0:T(8,128)S(1)} %add_add_fusion.own_in, f32[32,1024]{1,0:T(8,128)S(1)} %collective-permute-done.32.oth_in, f32[32,32]{1,0:T(8,128)S(1)} %inverse_of.5.inv_ref, ...), custom_call_target="tpu_custom_call" | custom-call | tf_op jit(solution)/shard_map/last_right/pallas_call | solution.py:95
  138.0 0.4 collective-permute-start.33
  138.4 0.9 collective-permute-done.33
  139.3 0.7 collective-permute-start.36
  140.4 2.2 %collective-permute-start.34 = (f32[64,512]{1,0:T(8,128)S(1)}, f32[64,512]{1,0:T(8,128)S(1)}, u32[]{:S(2)}, u32[]{:S(2)}) collective-permute-start(f32[64,512]{1,0:T(8,128)S(1)} %constant_dynamic-update-slice_fusion.r0), channel_id=1, source_target_pairs={{0,32},{1,33},{2,34},{3,35},{4,36},{5,37},{6,38},{7,39},{8,40},{9,... | collective-permute-start | bytes 393224 | tf_op jit(solution)/shard_map/ppermute | solution.py:30
  142.6 5.4 %collective-permute-done.36.r3 = f32[64,512]{1,0:T(8,128)S(1)} collective-permute-done((f32[64,512]{1,0:T(8,128)S(1)}, f32[64,512]{1,0:T(8,128)S(1)}, u32[]{:S(2)}, u32[]{:S(2)}) %collective-permute-start.36) | collective-permute-done | bytes 131104 | tf_op jit(solution)/shard_map/ppermute | solution.py:30
  148.4 8.2 %finish.1 = (f32[512,4096]{1,0:T(8,128)}, f32[512,4096]{1,0:T(8,128)}, f32[32,4096]{1,0:T(8,128)}) custom-call(s32[3]{0:T(128)S(1)} %pad_add_fusion.place_ref, bf16[32,512]{1,0:T(8,128)(2,1)S(1)} %get-tuple-element.76.o_ref, f32[64,512]{1,0:T(8,128)S(1)} %constant_dynamic-update-slice_fusion.r0, f32[64,512]{1,0:T(8,128)S(1)} %collective-permute-done.34.r1, ...), custom_call_target="tpu_custom_call" | custom-call | tf_op jit(solution)/shard_map/finish/pallas_call | solution.py:279
  (38 shorter events, 4.6 us)
Async XLA Ops:
  3.7 5.4 %collective-permute-start = (bf16[512,2048]{1,0:T(8,128)(2,1)S(1)}, bf16[512,2048]{1,0:T(8,128)(2,1)}, u32[]{:S(2)}, u32[]{:S(2)}) collective-permute-start(bf16[512,2048]{1,0:T(8,128)(2,1)S(1)} %half_of_memory.3.other_ref), channel_id=1, source_target_pairs={{0,4},{4,0},{8,12},{12,8},{16,20},{20,16},{24,28},{28,24},{32,36},... | collective-permute-start | bytes 6291464 | tf_op jit(solution)/shard_map/ppermute | solution.py:315
  8.4 59.0 %copy-start = (f32[4096,32]{0,1:T(8,128)S(1)}, f32[4096,32]{0,1:T(8,128)}, u32[]{:S(2)}) copy-start(f32[4096,32]{0,1:T(8,128)} %param.5) | copy-start | bytes 1572868
  12.7 8.4 %collective-permute-start.1 = (bf16[4,128,512]{2,1,0:T(8,128)(2,1)S(1)}, bf16[4,128,512]{2,1,0:T(8,128)(2,1)S(1)}, u32[]{:S(2)}, u32[]{:S(2)}) collective-permute-start(bf16[4,128,512]{2,1,0:T(8,128)(2,1)S(1)} %get-tuple-element.43), channel_id=1, source_target_pairs={{0,32},{1,33},{2,34},{3,35},{4,12},{5,13},{6,14},{7,15},{8,40},{9,... | collective-permute-start | bytes 1572872 | tf_op jit(solution)/shard_map/ppermute | solution.py:30
  14.1 15.0 %collective-permute-start.2 = (bf16[4,128,512]{2,1,0:T(8,128)(2,1)S(1)}, bf16[4,128,512]{2,1,0:T(8,128)(2,1)S(1)}, u32[]{:S(2)}, u32[]{:S(2)}) collective-permute-start(bf16[4,128,512]{2,1,0:T(8,128)(2,1)S(1)} %get-tuple-element.44), channel_id=1, source_target_pairs={{0,64},{1,65},{2,66},{3,67},{4,20},{5,21},{6,22},{7,23},{8,72},{9,... | collective-permute-start | bytes 1572872 | tf_op jit(solution)/shard_map/ppermute | solution.py:30
  16.6 15.2 %collective-permute-start.3 = (bf16[4,128,512]{2,1,0:T(8,128)(2,1)S(1)}, bf16[4,128,512]{2,1,0:T(8,128)(2,1)S(1)}, u32[]{:S(2)}, u32[]{:S(2)}) collective-permute-start(bf16[4,128,512]{2,1,0:T(8,128)(2,1)S(1)} %get-tuple-element.45), channel_id=1, source_target_pairs={{0,96},{1,97},{2,98},{3,99},{4,28},{5,29},{6,30},{7,31},{8,104},{9... | collective-permute-start | bytes 1572872 | tf_op jit(solution)/shard_map/ppermute | solution.py:30
  32.5 4.7 %collective-permute-start.4 = (bf16[128,512]{1,0:T(8,128)(2,1)S(1)}, bf16[128,512]{1,0:T(8,128)(2,1)S(1)}, u32[]{:S(2)}, u32[]{:S(2)}) collective-permute-start(bf16[128,512]{1,0:T(8,128)(2,1)S(1)} %get-tuple-element.47), channel_id=1, source_target_pairs={{0,8},{1,9},{2,10},{3,11},{4,36},{5,37},{6,38},{7,39},{8,0},{9,1},... | collective-permute-start | bytes 393224 | tf_op jit(solution)/shard_map/ppermute | solution.py:30
  33.9 7.1 %collective-permute-start.5 = (bf16[128,512]{1,0:T(8,128)(2,1)S(1)}, bf16[128,512]{1,0:T(8,128)(2,1)S(1)}, u32[]{:S(2)}, u32[]{:S(2)}) collective-permute-start(bf16[128,512]{1,0:T(8,128)(2,1)S(1)} %get-tuple-element.48), channel_id=1, source_target_pairs={{0,16},{1,17},{2,18},{3,19},{4,68},{5,69},{6,70},{7,71},{8,24},{9,... | collective-permute-start | bytes 393224 | tf_op jit(solution)/shard_map/ppermute | solution.py:30
  37.3 5.5 %collective-permute-start.6 = (bf16[128,512]{1,0:T(8,128)(2,1)S(1)}, bf16[128,512]{1,0:T(8,128)(2,1)S(1)}, u32[]{:S(2)}, u32[]{:S(2)}) collective-permute-start(bf16[128,512]{1,0:T(8,128)(2,1)S(1)} %get-tuple-element.49), channel_id=1, source_target_pairs={{0,24},{1,25},{2,26},{3,27},{4,100},{5,101},{6,102},{7,103},{8,16}... | collective-permute-start | bytes 393224 | tf_op jit(solution)/shard_map/ppermute | solution.py:30
  43.3 6.1 %collective-permute-start.9 = (bf16[128,512]{1,0:T(8,128)(2,1)S(1)}, bf16[128,512]{1,0:T(8,128)(2,1)S(1)}, u32[]{:S(2)}, u32[]{:S(2)}) collective-permute-start(bf16[128,512]{1,0:T(8,128)(2,1)S(1)} %second_sum.1), channel_id=1, source_target_pairs={{0,24},{1,25},{2,26},{3,27},{4,7},{5,6},{6,5},{7,4},{8,16},{9,17},... | collective-permute-start | bytes 393224 | tf_op jit(solution)/shard_map/ppermute | solution.py:30
  46.1 5.3 %collective-permute-start.8 = (bf16[128,512]{1,0:T(8,128)(2,1)S(1)}, bf16[128,512]{1,0:T(8,128)(2,1)S(1)}, u32[]{:S(2)}, u32[]{:S(2)}) collective-permute-start(bf16[128,512]{1,0:T(8,128)(2,1)S(1)} %second_sum.1), channel_id=1, source_target_pairs={{0,16},{1,17},{2,18},{3,19},{4,6},{5,7},{6,4},{7,5},{8,24},{9,25},... | collective-permute-start | bytes 393224 | tf_op jit(solution)/shard_map/ppermute | solution.py:30
  46.5 5.0 %collective-permute-start.7 = (bf16[128,512]{1,0:T(8,128)(2,1)S(1)}, bf16[128,512]{1,0:T(8,128)(2,1)S(1)}, u32[]{:S(2)}, u32[]{:S(2)}) collective-permute-start(bf16[128,512]{1,0:T(8,128)(2,1)S(1)} %second_sum.1), channel_id=1, source_target_pairs={{0,8},{1,9},{2,10},{3,11},{4,5},{5,4},{6,7},{7,6},{8,0},{9,1},{10,... | collective-permute-start | bytes 393224 | tf_op jit(solution)/shard_map/ppermute | solution.py:30
  51.5 15.2 %collective-permute-start.12 = (bf16[512,512]{1,0:T(8,128)(2,1)S(1)}, bf16[512,512]{1,0:T(8,128)(2,1)S(1)}, u32[]{:S(2)}, u32[]{:S(2)}) collective-permute-start(bf16[512,512]{1,0:T(8,128)(2,1)S(1)} %pad_maximum_fusion.m0.refs_0_.refs_1_), channel_id=1, source_target_pairs={{0,3},{1,2},{2,1},{3,0},{4,28},{5,29},{6,30},{7,31},{8,11},{9,10},... | collective-permute-start | bytes 1572872 | tf_op jit(solution)/shard_map/ppermute | solution.py:30
  51.8 15.0 %collective-permute-start.11 = (bf16[512,512]{1,0:T(8,128)(2,1)S(1)}, bf16[512,512]{1,0:T(8,128)(2,1)S(1)}, u32[]{:S(2)}, u32[]{:S(2)}) collective-permute-start(bf16[512,512]{1,0:T(8,128)(2,1)S(1)} %pad_maximum_fusion.m0.refs_0_.refs_1_), channel_id=1, source_target_pairs={{0,2},{1,3},{2,0},{3,1},{4,20},{5,21},{6,22},{7,23},{8,10},{9,11},... | collective-permute-start | bytes 1572872 | tf_op jit(solution)/shard_map/ppermute | solution.py:30
  52.1 15.3 %collective-permute-start.10 = (bf16[512,512]{1,0:T(8,128)(2,1)S(1)}, bf16[512,512]{1,0:T(8,128)(2,1)S(1)}, u32[]{:S(2)}, u32[]{:S(2)}) collective-permute-start(bf16[512,512]{1,0:T(8,128)(2,1)S(1)} %pad_maximum_fusion.m0.refs_0_.refs_1_), channel_id=1, source_target_pairs={{0,1},{1,0},{2,3},{3,2},{4,12},{5,13},{6,14},{7,15},{8,9},{9,8},{1... | collective-permute-start | bytes 1572872 | tf_op jit(solution)/shard_map/ppermute | solution.py:30
  68.6 6.0 %collective-permute-start.13 = (f32[32,1024]{1,0:T(8,128)S(1)}, f32[32,1024]{1,0:T(8,128)S(1)}, u32[]{:S(2)}, u32[]{:S(2)}) collective-permute-start(f32[32,1024]{1,0:T(8,128)S(1)} %get-tuple-element.51), channel_id=1, source_target_pairs={{0,4},{4,0},{8,12},{12,8},{16,20},{20,16},{24,28},{28,24},{32,36},... | collective-permute-start | bytes 393224 | tf_op jit(solution)/shard_map/ppermute | solution.py:249
  74.6 9.2 %collective-permute-start.16 = (f32[32,1024]{1,0:T(8,128)S(1)}, f32[32,1024]{1,0:T(8,128)S(1)}, u32[]{:S(2)}, u32[]{:S(2)}) collective-permute-start(f32[32,1024]{1,0:T(8,128)S(1)} %add.48), channel_id=1, source_target_pairs={{0,96},{1,97},{2,98},{3,99},{4,100},{5,101},{6,102},{7,103},{8,104... | collective-permute-start | bytes 393224 | tf_op jit(solution)/shard_map/ppermute | solution.py:30
  74.7 9.1 %collective-permute-start.15 = (f32[32,1024]{1,0:T(8,128)S(1)}, f32[32,1024]{1,0:T(8,128)S(1)}, u32[]{:S(2)}, u32[]{:S(2)}) collective-permute-start(f32[32,1024]{1,0:T(8,128)S(1)} %add.48), channel_id=1, source_target_pairs={{0,64},{1,65},{2,66},{3,67},{4,68},{5,69},{6,70},{7,71},{8,72},{9,... | collective-permute-start | bytes 393224 | tf_op jit(solution)/shard_map/ppermute | solution.py:30
  74.8 9.0 %collective-permute-start.14 = (f32[32,1024]{1,0:T(8,128)S(1)}, f32[32,1024]{1,0:T(8,128)S(1)}, u32[]{:S(2)}, u32[]{:S(2)}) collective-permute-start(f32[32,1024]{1,0:T(8,128)S(1)} %add.48), channel_id=1, source_target_pairs={{0,32},{1,33},{2,34},{3,35},{4,36},{5,37},{6,38},{7,39},{8,40},{9,... | collective-permute-start | bytes 393224 | tf_op jit(solution)/shard_map/ppermute | solution.py:30
  83.8 2.5 %collective-permute-start.17 = (f32[32,1024]{1,0:T(8,128)S(1)}, f32[32,1024]{1,0:T(8,128)S(1)}, u32[]{:S(2)}, u32[]{:S(2)}) collective-permute-start(f32[32,1024]{1,0:T(8,128)S(1)} %add_add_fusion.3.own_in), channel_id=1, source_target_pairs={{0,4},{4,0},{8,12},{12,8},{16,20},{20,16},{24,28},{28,24},{32,36},... | collective-permute-start | bytes 393224 | tf_op jit(solution)/shard_map/ppermute | solution.py:255
  88.0 1.4 collective-permute-start.18
  89.4 8.7 %collective-permute-start.21 = (f32[32,1024]{1,0:T(8,128)S(1)}, f32[32,1024]{1,0:T(8,128)S(1)}, u32[]{:S(2)}, u32[]{:S(2)}) collective-permute-start(f32[32,1024]{1,0:T(8,128)S(1)} %add.52), channel_id=1, source_target_pairs={{0,96},{1,97},{2,98},{3,99},{4,100},{5,101},{6,102},{7,103},{8,104... | collective-permute-start | bytes 393224 | tf_op jit(solution)/shard_map/ppermute | solution.py:30
  90.2 8.0 %collective-permute-start.20 = (f32[32,1024]{1,0:T(8,128)S(1)}, f32[32,1024]{1,0:T(8,128)S(1)}, u32[]{:S(2)}, u32[]{:S(2)}) collective-permute-start(f32[32,1024]{1,0:T(8,128)S(1)} %add.52), channel_id=1, source_target_pairs={{0,64},{1,65},{2,66},{3,67},{4,68},{5,69},{6,70},{7,71},{8,72},{9,... | collective-permute-start | bytes 393224 | tf_op jit(solution)/shard_map/ppermute | solution.py:30
  90.6 8.0 %collective-permute-start.19 = (f32[32,1024]{1,0:T(8,128)S(1)}, f32[32,1024]{1,0:T(8,128)S(1)}, u32[]{:S(2)}, u32[]{:S(2)}) collective-permute-start(f32[32,1024]{1,0:T(8,128)S(1)} %add.52), channel_id=1, source_target_pairs={{0,32},{1,33},{2,34},{3,35},{4,36},{5,37},{6,38},{7,39},{8,40},{9,... | collective-permute-start | bytes 393224 | tf_op jit(solution)/shard_map/ppermute | solution.py:30
  98.7 2.5 %collective-permute-start.22 = (f32[32,1024]{1,0:T(8,128)S(1)}, f32[32,1024]{1,0:T(8,128)S(1)}, u32[]{:S(2)}, u32[]{:S(2)}) collective-permute-start(f32[32,1024]{1,0:T(8,128)S(1)} %add_add_fusion.2.own_in), channel_id=1, source_target_pairs={{0,4},{4,0},{8,12},{12,8},{16,20},{20,16},{24,28},{28,24},{32,36},... | collective-permute-start | bytes 393224 | tf_op jit(solution)/shard_map/ppermute | solution.py:255
  103.2 1.4 collective-permute-start.23
  104.6 8.7 %collective-permute-start.26 = (f32[32,1024]{1,0:T(8,128)S(1)}, f32[32,1024]{1,0:T(8,128)S(1)}, u32[]{:S(2)}, u32[]{:S(2)}) collective-permute-start(f32[32,1024]{1,0:T(8,128)S(1)} %add.56), channel_id=1, source_target_pairs={{0,96},{1,97},{2,98},{3,99},{4,100},{5,101},{6,102},{7,103},{8,104... | collective-permute-start | bytes 393224 | tf_op jit(solution)/shard_map/ppermute | solution.py:30
  105.4 8.0 %collective-permute-start.25 = (f32[32,1024]{1,0:T(8,128)S(1)}, f32[32,1024]{1,0:T(8,128)S(1)}, u32[]{:S(2)}, u32[]{:S(2)}) collective-permute-start(f32[32,1024]{1,0:T(8,128)S(1)} %add.56), channel_id=1, source_target_pairs={{0,64},{1,65},{2,66},{3,67},{4,68},{5,69},{6,70},{7,71},{8,72},{9,... | collective-permute-start | bytes 393224 | tf_op jit(solution)/shard_map/ppermute | solution.py:30
  105.8 8.0 %collective-permute-start.24 = (f32[32,1024]{1,0:T(8,128)S(1)}, f32[32,1024]{1,0:T(8,128)S(1)}, u32[]{:S(2)}, u32[]{:S(2)}) collective-permute-start(f32[32,1024]{1,0:T(8,128)S(1)} %add.56), channel_id=1, source_target_pairs={{0,32},{1,33},{2,34},{3,35},{4,36},{5,37},{6,38},{7,39},{8,40},{9,... | collective-permute-start | bytes 393224 | tf_op jit(solution)/shard_map/ppermute | solution.py:30
  113.8 2.7 %collective-permute-start.27 = (f32[32,1024]{1,0:T(8,128)S(1)}, f32[32,1024]{1,0:T(8,128)S(1)}, u32[]{:S(2)}, u32[]{:S(2)}) collective-permute-start(f32[32,1024]{1,0:T(8,128)S(1)} %add_add_fusion.1.own_in), channel_id=1, source_target_pairs={{0,4},{4,0},{8,12},{12,8},{16,20},{20,16},{24,28},{28,24},{32,36},... | collective-permute-start | bytes 393224 | tf_op jit(solution)/shard_map/ppermute | solution.py:255
  118.6 1.4 collective-permute-start.28
  120.0 8.7 %collective-permute-start.31 = (f32[32,1024]{1,0:T(8,128)S(1)}, f32[32,1024]{1,0:T(8,128)S(1)}, u32[]{:S(2)}, u32[]{:S(2)}) collective-permute-start(f32[32,1024]{1,0:T(8,128)S(1)} %add.60), channel_id=1, source_target_pairs={{0,96},{1,97},{2,98},{3,99},{4,100},{5,101},{6,102},{7,103},{8,104... | collective-permute-start | bytes 393224 | tf_op jit(solution)/shard_map/ppermute | solution.py:30
  120.8 8.0 %collective-permute-start.30 = (f32[32,1024]{1,0:T(8,128)S(1)}, f32[32,1024]{1,0:T(8,128)S(1)}, u32[]{:S(2)}, u32[]{:S(2)}) collective-permute-start(f32[32,1024]{1,0:T(8,128)S(1)} %add.60), channel_id=1, source_target_pairs={{0,64},{1,65},{2,66},{3,67},{4,68},{5,69},{6,70},{7,71},{8,72},{9,... | collective-permute-start | bytes 393224 | tf_op jit(solution)/shard_map/ppermute | solution.py:30
  121.1 8.0 %collective-permute-start.29 = (f32[32,1024]{1,0:T(8,128)S(1)}, f32[32,1024]{1,0:T(8,128)S(1)}, u32[]{:S(2)}, u32[]{:S(2)}) collective-permute-start(f32[32,1024]{1,0:T(8,128)S(1)} %add.60), channel_id=1, source_target_pairs={{0,32},{1,33},{2,34},{3,35},{4,36},{5,37},{6,38},{7,39},{8,40},{9,... | collective-permute-start | bytes 393224 | tf_op jit(solution)/shard_map/ppermute | solution.py:30
  129.2 2.5 %collective-permute-start.32 = (f32[32,1024]{1,0:T(8,128)S(1)}, f32[32,1024]{1,0:T(8,128)S(1)}, u32[]{:S(2)}, u32[]{:S(2)}) collective-permute-start(f32[32,1024]{1,0:T(8,128)S(1)} %add_add_fusion.own_in), channel_id=1, source_target_pairs={{0,4},{4,0},{8,12},{12,8},{16,20},{20,16},{24,28},{28,24},{32,36},... | collective-permute-start | bytes 393224 | tf_op jit(solution)/shard_map/ppermute | solution.py:255
  138.0 1.3 collective-permute-start.33
  139.3 8.7 %collective-permute-start.36 = (f32[64,512]{1,0:T(8,128)S(1)}, f32[64,512]{1,0:T(8,128)S(1)}, u32[]{:S(2)}, u32[]{:S(2)}) collective-permute-start(f32[64,512]{1,0:T(8,128)S(1)} %constant_dynamic-update-slice_fusion.r0), channel_id=1, source_target_pairs={{0,96},{1,97},{2,98},{3,99},{4,100},{5,101},{6,102},{7,103},{8,104... | collective-permute-start | bytes 393224 | tf_op jit(solution)/shard_map/ppermute | solution.py:30
  140.0 8.0 %collective-permute-start.35 = (f32[64,512]{1,0:T(8,128)S(1)}, f32[64,512]{1,0:T(8,128)S(1)}, u32[]{:S(2)}, u32[]{:S(2)}) collective-permute-start(f32[64,512]{1,0:T(8,128)S(1)} %constant_dynamic-update-slice_fusion.r0), channel_id=1, source_target_pairs={{0,64},{1,65},{2,66},{3,67},{4,68},{5,69},{6,70},{7,71},{8,72},{9,... | collective-permute-start | bytes 393224 | tf_op jit(solution)/shard_map/ppermute | solution.py:30
  140.4 8.0 %collective-permute-start.34 = (f32[64,512]{1,0:T(8,128)S(1)}, f32[64,512]{1,0:T(8,128)S(1)}, u32[]{:S(2)}, u32[]{:S(2)}) collective-permute-start(f32[64,512]{1,0:T(8,128)S(1)} %constant_dynamic-update-slice_fusion.r0), channel_id=1, source_target_pairs={{0,32},{1,33},{2,34},{3,35},{4,36},{5,37},{6,38},{7,39},{8,40},{9,... | collective-permute-start | bytes 393224 | tf_op jit(solution)/shard_map/ppermute | solution.py:30

commit v3 on v2

--- a/solution.py
+++ b/solution.py
@@ -16,6 +16,7 @@
 ROWS_OWN = ROWS // N_OWNER
 PIECE = ROWS_OWN // 4
 MID = ROWS // 2
+PANEL = 8
 BF = jnp.bfloat16
 F32 = jnp.float32
 HIGHEST = lax.Precision.HIGHEST
@@ -42,61 +43,51 @@
     return pltpu.CompilerParams(vmem_limit_bytes=48 * 1024 * 1024, **kw)
 
 
+SCALARS = pl.BlockSpec(memory_space=pltpu.SMEM)
+WHOLE = pl.BlockSpec(memory_space=pltpu.VMEM)
+HBM = pl.BlockSpec(memory_space=pl.ANY)
+
+
 def half_of_memory(grad, error, which):
-    def body(which_ref, g_ref, e_ref, o_ref):
-        o_ref[...] = (g_ref[...].astype(F32) + e_ref[...].astype(F32)).astype(BF)
-
-    steps = 4
-    rows = ROWS_OWN // steps
-    spec = pl.BlockSpec((rows, HALF), lambda i, w: (i, w[0]))
+    chunks = 8
+    rows = ROWS_OWN // chunks
+
+    def body(which_ref, g_hbm, e_hbm, o_ref, g_ref, e_ref, sems):
+        cols = cut(which_ref[0], HALF)
+        copies = []
+        for i in range(chunks):
+            part = pl.ds(i * rows, rows)
+            pair = [
+                pltpu.make_async_copy(src.at[part, cols], dst.at[part, :], sems.at[n, i])
+                for n, (src, dst) in enumerate(((g_hbm, g_ref), (e_hbm, e_ref)))
+            ]
+            for copy in pair:
+                copy.start()
+            copies.append(pair)
+        for i, pair in enumerate(copies):
+            for copy in pair:
+                copy.wait()
+            part = pl.ds(i * rows, rows)
+            o_ref[part, :] = (g_ref[part, :].astype(F32) + e_ref[part, :].astype(F32)).astype(BF)
+
     return pl.pallas_call(
         body,
-        grid_spec=pltpu.PrefetchScalarGridSpec(
-            num_scalar_prefetch=1,
-            grid=(steps,),
-            in_specs=[spec, spec],
-            out_specs=pl.BlockSpec((rows, HALF), lambda i, w: (i, 0)),
-        ),
+        in_specs=[SCALARS, HBM, HBM],
+        out_specs=WHOLE,
+        scratch_shapes=[pltpu.VMEM((ROWS_OWN, HALF), BF)] * 2 + [pltpu.SemaphoreType.DMA((2, chunks))],
         out_shape=jax.ShapeDtypeStruct((ROWS_OWN, HALF), BF),
         compiler_params=params(),
         name="half_of_memory",
     )(which, grad, error)
 
 
-def pair_sum(place, mine, received):
-    def body(place_ref, *refs):
-        for k in range(4):
-            refs[8 + k][0] = (refs[k][...].astype(F32) + refs[4 + k][...].astype(F32)).astype(BF)
-
-    def index(j, p, k):
-        first = p[2] == 0
-        return jnp.where(first, j, p[1] ^ k), jnp.where(first, p[0] ^ k, j)
-
-    cuts = [pl.BlockSpec((PIECE, COLS), lambda j, p, k=k: index(j, p, k)) for k in range(4)]
-    return pl.pallas_call(
-        body,
-        grid_spec=pltpu.PrefetchScalarGridSpec(
-            num_scalar_prefetch=1,
-            grid=(4,),
-            in_specs=cuts + cuts,
-            out_specs=[pl.BlockSpec((1, PIECE, COLS), lambda j, p: (j, 0, 0))] * 4,
-        ),
-        out_shape=[jax.ShapeDtypeStruct((4, PIECE, COLS), BF)] * 4,
-        compiler_params=params(),
-        name="pair_sum",
-    )(place, *[mine] * 4, *[received] * 4)
-
-
-SCALARS = pl.BlockSpec(memory_space=pltpu.SMEM)
-WHOLE = pl.BlockSpec(memory_space=pltpu.VMEM)
-
-
-def call(body, name, out_shape, place, *arrays):
+def call(body, name, out_shape, place, *arrays, scratch=()):
     return pl.pallas_call(
         body,
         in_specs=[SCALARS] + [WHOLE] * len(arrays),
         out_specs=jax.tree.map(lambda s: WHOLE, out_shape),
         out_shape=out_shape,
+        scratch_shapes=scratch,
         compiler_params=params(),
         name=name,
     )(place, *arrays)
@@ -104,6 +95,18 @@
 
 def cut(index, size):
     return pl.ds(pl.multiple_of(index * size, size), size)
+
+
+def pair_sum(place, mine, received):
+    def body(place_ref, a_ref, b_ref, *out):
+        first = place_ref[2] == 0
+        for k in range(4):
+            for j in range(4):
+                rows = cut(jnp.where(first, j, place_ref[1] ^ k), PIECE)
+                cols = cut(jnp.where(first, place_ref[0] ^ k, j), COLS)
+                out[k][j] = a_ref[rows, cols] + b_ref[rows, cols]
+
+    return call(body, "pair_sum", [jax.ShapeDtypeStruct((4, PIECE, COLS), BF)] * 4, place, mine, received)
 
 
 def first_sum(place, parts):
@@ -126,6 +129,41 @@
     return call(body, "second_sum", jax.ShapeDtypeStruct((PIECE, COLS), BF), place, *parts)
 
 
+def early_left(place, warm_t, pairs):
+    def body(place_ref, warm_ref, *refs):
+        pairs, (own_ref, oth_ref, sum_ref) = refs[:4], refs[4:]
+        core = place_ref[2]
+        sum_ref[...] = jnp.zeros((RANK, ROWS_OWN), F32)
+        for k in range(4):
+            for j in range(4):
+                rows = cut(jnp.where(core == 0, j, place_ref[1] ^ k), PIECE)
+                group = jnp.where(core == 0, place_ref[0] ^ k, j)
+                right = warm_ref[:, cut(core * 4 + group, COLS)].astype(BF)
+                sum_ref[:, rows] += dot(right, pairs[k][j], ((1,), (1,)))
+        own_ref[...] = sum_ref[:, cut(core, ROWS_OWN // 2)]
+        oth_ref[...] = sum_ref[:, cut(1 - core, ROWS_OWN // 2)]
+
+    shapes = [jax.ShapeDtypeStruct((RANK, ROWS_OWN // 2), F32)] * 2
+    scratch = [pltpu.VMEM((RANK, ROWS_OWN), F32)]
+    return call(body, "early_left", shapes, place, warm_t, *pairs, scratch=scratch)
+
+
+def assemble_left(place, own, oth):
+    def body(place_ref, own_ref, oth_ref, o_ref, sum_ref):
+        core, half = place_ref[2], ROWS_OWN // 2
+        for y in range(4):
+            rows = slice(y * RANK, (y + 1) * RANK)
+            sum_ref[:, cut(2 * y + core, half)] = own_ref[rows, :]
+            sum_ref[:, cut(2 * y + 1 - core, half)] = oth_ref[rows, :]
+        for y in range(4):
+            for x in range(4):
+                i = 4 * y + x
+                o_ref[:, i * PIECE : (i + 1) * PIECE] = sum_ref[:, cut(4 * y + (place_ref[1] ^ x), PIECE)]
+
+    shape = jax.ShapeDtypeStruct((RANK, ROWS), F32)
+    return call(body, "assemble_left", shape, place, own, oth, scratch=[pltpu.VMEM((RANK, ROWS), F32)])
+
+
 def thirds(x):
     high = x.astype(BF)
     rest = x - high.astype(F32)
@@ -186,10 +224,14 @@
     trace = jnp.sum(jnp.where(row == lane, wide, 0.0), keepdims=True)
     shift = 1e-06 * (trace / RANK)
     work = wide + jnp.where(row == lane, shift, 0.0) + jnp.where(row + RANK == lane, 1.0, 0.0)
-    for k in range(RANK - 1):
-        col = jnp.broadcast_to(work[:, k : k + 1], (RANK, 128))
-        factor = jnp.where(row > k, col / col[k : k + 1, :], 0.0)
-        work = work - factor * work[k : k + 1, :]
+    for start in range(0, RANK, PANEL):
+        cols = [jnp.broadcast_to(work[:, start + j : start + j + 1], (RANK, 128)) for j in range(PANEL)]
+        for j in range(PANEL):
+            k = start + j
+            factor = jnp.where(row > k, cols[j] * (1.0 / cols[j][k : k + 1, :]), 0.0)
+            work = work - factor * work[k : k + 1, :]
+            for i in range(j + 1, PANEL):
+                cols[i] = cols[i] - factor * cols[i][k : k + 1, :]
     pivot = jnp.sum(jnp.where(row == lane, work, 0.0), axis=1, keepdims=True)
     return work[:, RANK : 2 * RANK] * lax.rsqrt(pivot)
 
@@ -197,13 +239,14 @@
 HALVES = [jax.ShapeDtypeStruct((RANK, MID), F32)] * 2
 
 
-def first_left(place, right_t, m):
-    def body(place_ref, r_ref, m0, m1, m2, m3, own_ref, oth_ref):
-        cols = cut(place_ref[2] * 4 + place_ref[0], COLS)
-        left = times_m_t(r_ref[:, cols].astype(BF), (m0, m1, m2, m3))
-        store_halves(place_ref, left, own_ref, oth_ref)
-
-    return call(body, "first_left", HALVES, place, right_t, *m)
+def second_left(place, left, inverse, m):
+    def body(place_ref, left_ref, inv_ref, *refs):
+        m_refs, (own_ref, oth_ref) = refs[:4], refs[4:]
+        ortho = dot(inv_ref[...], left_ref[...], ((1,), (0,)), HIGHEST).astype(BF)
+        right = times_m(reorder(ortho, place_ref), m_refs) * (1.0 / N_DP)
+        store_halves(place_ref, times_m_t(right.astype(BF), m_refs), own_ref, oth_ref)
+
+    return call(body, "second_left", HALVES, place, left, inverse, *m)
 
 
 def next_left(place, own, oth, inverse, m):
@@ -255,55 +298,55 @@
     return own, lax.ppermute(own, "dp", CORE), beside
 
 
-def finish(place, ortho, rights, mine, other):
-    def body(place_ref, o_ref, r0, r1, r2, r3, mine_ref, other_ref, up_ref, err_ref, right_ref):
-        step = pl.program_id(0)
-        left = jnp.concatenate([o_ref[...]] * 3, axis=0)
-        for j in range(2):
-            for k, ref in enumerate((r0, r1, r2, r3)):
-
-                @pl.when(step == 4 * j + k)
-                def _():
-                    right = ref[j * RANK : (j + 1) * RANK, :]
-                    right_ref[...] = right
-                    update = dot(left, thirds(right), ((0,), (0,)))
-                    up_ref[...] = update
-                    memory = (mine_ref, other_ref)[j][...].astype(F32)
-                    err_ref[...] = memory - update
-
-    def group(s, p):
-        return (s % 4) ^ p[0]
-
-    whole = pl.BlockSpec((2 * RANK, COLS), lambda s, p: (0, 0))
-    out_block = lambda s, p: (0, ((s // 4) ^ p[2]) * 4 + group(s, p))
+def columns_of(place, ortho):
+    def body(place_ref, o_ref, out_ref):
+        wide = jnp.concatenate([o_ref[...].astype(F32)] * 3 + [jnp.zeros((RANK, ROWS_OWN), F32)], axis=0)
+        out_ref[...] = wide.T.astype(BF)
+
+    return call(body, "columns_of", jax.ShapeDtypeStruct((ROWS_OWN, 4 * RANK), BF), place, ortho)
+
+
+def finish(place, ortho, rights, mine, other, outs, name):
+    keys = list(rights)
+    count, kept = len(keys), len(outs)
+
+    def body(place_ref, o_ref, *refs):
+        rights, memory, refs = refs[:count], refs[count : count + 2], refs[count + 2 + kept :]
+        up_hbm, err_hbm, right_hbm, up_ref, err_ref, sems = refs
+        copies = []
+
+        def send(i, n, source, target):
+            copies.append(pltpu.make_async_copy(source, target, sems.at[i, n]))
+            copies[-1].start()
+
+        for n, ((k, j), ref) in enumerate(zip(keys, rights)):
+            z = place_ref[0] ^ k
+            cols = cut((place_ref[2] ^ j) * 4 + z, COLS)
+            wide = jnp.concatenate([thirds(ref[...]), jnp.zeros((RANK, COLS), BF)], axis=0)
+            update = dot(o_ref[...], wide, ((1,), (0,)))
+            up_ref[n] = update
+            send(0, n, up_ref.at[n], up_hbm.at[:, cols])
+            err_ref[n] = memory[j][:, cut(z, COLS)].astype(F32) - update
+            send(1, n, err_ref.at[n], err_hbm.at[:, cols])
+            send(2, n, ref, right_hbm.at[:, cols])
+        for copy in copies:
+            copy.wait()
+
+    blocks = pltpu.VMEM((count, ROWS_OWN, COLS), F32)
     return pl.pallas_call(
         body,
-        grid_spec=pltpu.PrefetchScalarGridSpec(
-            num_scalar_prefetch=1,
-            grid=(8,),
-            in_specs=[
-                pl.BlockSpec((RANK, ROWS_OWN), lambda s, p: (0, 0)),
-                whole,
-                whole,
-                whole,
-                whole,
-                pl.BlockSpec((ROWS_OWN, COLS), lambda s, p: (0, group(jnp.minimum(s, 3), p))),
-                pl.BlockSpec((ROWS_OWN, COLS), lambda s, p: (0, group(jnp.maximum(s, 4), p))),
-            ],
-            out_specs=[
-                pl.BlockSpec((ROWS_OWN, COLS), out_block),
-                pl.BlockSpec((ROWS_OWN, COLS), out_block),
-                pl.BlockSpec((RANK, COLS), out_block),
-            ],
-        ),
+        in_specs=[SCALARS] + [WHOLE] * (count + 3) + [HBM] * kept,
+        out_specs=[HBM] * 3,
+        scratch_shapes=[blocks, blocks, pltpu.SemaphoreType.DMA((3, count))],
         out_shape=(
             jax.ShapeDtypeStruct((ROWS_OWN, W), F32),
             jax.ShapeDtypeStruct((ROWS_OWN, W), F32),
             jax.ShapeDtypeStruct((RANK, W), F32),
         ),
+        input_output_aliases={count + 4 + i: i for i in range(kept)},
         compiler_params=params(),
-        name="finish",
-    )(place, ortho, *rights, mine, other)
+        name=name,
+    )(place, ortho, *rights.values(), mine, other, *outs)
 
 
 def per_device(grad, error, warm_right):
@@ -314,18 +357,33 @@
     other = half_of_memory(grad[0], error[0], (1 - core)[None])
     received = lax.ppermute(other, "dp", CORE)
     mine = half_of_memory(grad[0], error[0], core[None])
-    pairs = exchange(pair_sum(place, mine, received), "z", "x")
-    piece = second_sum(place, exchange(first_sum(place, pairs), "x", "z"))
-    m = spread(jnp.concatenate(spread(piece, "x", "y"), axis=0), "y", "x")
-
-    own, oth, inverse = sum_over_group(*first_left(place, warm_right.T, m))
-    for step in range(ITERS - 1):
+    pairs = pair_sum(place, mine, received)
+    early, passed = early_left(place, warm_right.T, pairs)
+    early = early + lax.ppermute(passed, "dp", CORE)
+    parts, early = lax.optimization_barrier((exchange(pairs, "z", "x"), spread(early, "x", "x")))
+    early = (early[0] + early[1]) + (early[2] + early[3])
+    parts = exchange(first_sum(place, parts), "x", "z")
+    parts, early = lax.optimization_barrier((parts, spread(early, "y", "y")))
+    m, early = lax.optimization_barrier((spread(second_sum(place, parts), "x", "y"), early))
+    early = spread(jnp.concatenate(early, axis=0), "z", "z")
+    early = (early[0] + early[1]) + (early[2] + early[3])
+    left = assemble_left(place, early, lax.ppermute(early, "dp", CORE))
+    m = spread(jnp.concatenate(m, axis=0), "y", "x")
+    m, left, inverse = lax.optimization_barrier((m, left, inverse_of(place, left)))
+
+    own, oth, inverse = sum_over_group(*second_left(place, left, inverse, m))
+    for step in range(ITERS - 2):
         left, own, oth = next_left(place, own, oth, inverse, m)
         own, oth, inverse = sum_over_group(own, oth, inverse_of(place, left))
     ortho, right = last_right(place, own, oth, inverse, m)
 
-    pair = jnp.concatenate([right, lax.ppermute(right, "dp", CORE)], axis=0)
-    update, new_error, right_t = finish(place, ortho, spread(pair, "z", "z"), mine, other)
+    ortho = columns_of(place, ortho)
+    near = {(0, 0): right, (0, 1): lax.ppermute(right, "dp", CORE)}
+    outs = finish(place, ortho, near, mine, other, [], "finish_near")
+    rights, outs = lax.optimization_barrier((spread(right, "z", "z"), outs))
+    far = {(k, 0): rights[k] for k in (1, 2, 3)}
+    far.update({(k, 1): lax.ppermute(rights[k], "dp", CORE) for k in (1, 2, 3)})
+    update, new_error, right_t = finish(place, ortho, far, mine, other, outs, "finish_far")
     return update, new_error[None], right_t.T
 
 

time: 157 us -> 142 us (0.904)
  Pallas kernels: 47.4 us -> 33.7 us
  waiting for transfers between devices: 61.5 us -> 49.1 us
  starting transfers between devices: 46.6 us -> 57.1 us
    ppermute x27 -> x33, waiting for transfers between devices: 51.9 us -> 38.9 us  [along(): return lax.ppermute(array, ('dp', 'owner'), pairs)]
    pallas_call x10 -> x13, Pallas kernels: 29.5 us -> 20.5 us  [call(): pl.pallas_call(body, in_specs=[SCALARS] + [WHOLE] * len(arrays), out_spec...]
    ppermute x1 -> x6, starting transfers between devices: 0.44 us -> 8.31 us  [the longest x1 4.07 us: per_device(): left = assemble_left(place, early, lax.ppermute(early, 'dp', CORE))]
    ppermute x27 -> x33, starting transfers between devices: 32.1 us -> 38.9 us  [along(): return lax.ppermute(array, ('dp', 'owner'), pairs)]
    pallas_call x4, Pallas kernels: 17.9 us -> 13.2 us  [the longest x2 8.54 us: finish(): pl.pallas_call(body, in_specs=[SCALARS] + [WHOLE] * (count + 3) + [HBM] *...]
    ppermute x4 -> x3, starting transfers between devices: 6.29 us -> 3.64 us  [sum_over_group(): own = own + lax.ppermute(oth, 'dp', CORE)]
    ppermute x1 -> x6, waiting for transfers between devices: 0.9 us -> 2.75 us  [the longest x1 0.99 us: per_device(): left = assemble_left(place, early, lax.ppermute(early, 'dp', CORE))]
    ppermute x4 -> x3, starting transfers between devices: 6.32 us -> 4.77 us  [sum_over_group(): return (own, lax.ppermute(own, 'dp', CORE), beside)]
  transfers between devices with their start and end apart: 37 -> 46, of which waited for: 28 -> 26; matrix products, arithmetic and copies ran while one was open for 0% -> 0% of each run, Pallas kernels for 11% -> 10%
where the time goes in v3:
time: 142 us; the launch traced here: 141 us
  starting transfers between devices  57.1 us (40%)
  waiting for transfers between devices  49.1 us (35%)
  Pallas kernels  33.7 us (24%)
    ppermute x33, waiting for transfers between devices, along(): return lax.ppermute(array, ('dp', 'owner'), pairs)  38.9 us
    ppermute x33, starting transfers between devices, along(): return lax.ppermute(array, ('dp', 'owner'), pairs)  38.9 us
    pallas_call x13, Pallas kernels, call(): pl.pallas_call(body, in_specs=[SCALARS] + [WHOLE] * len(arrays), out_spec...  20.5 us
    pallas_call x2, Pallas kernels, finish(): pl.pallas_call(body, in_specs=[SCALARS] + [WHOLE] * (count + 3) + [HBM] *...  8.54 us
    ppermute x3, starting transfers between devices, sum_over_group(): return (own, lax.ppermute(own, 'dp', CORE), beside)  4.77 us
    pallas_call x2, Pallas kernels, half_of_memory(): pl.pallas_call(body, in_specs=[SCALARS, HBM, HBM], out_specs=WHOLE, scrat...  4.67 us
    ppermute x1, starting transfers between devices, per_device(): left = assemble_left(place, early, lax.ppermute(early, 'dp', CORE))  4.07 us
    ppermute x3, starting transfers between devices, sum_over_group(): own = own + lax.ppermute(oth, 'dp', CORE)  3.64 us
  transfers between devices with their start and end apart: 46, of which 26 were waited for; matrix products, arithmetic and copies ran while one was open for 0% of the time, Pallas kernels for 10%

profile of v3, /device:TPU:1, one launch (start us, length us, event | category | flops | bytes accessed | tf_op | source)
XLA Modules:
  0.0 141.4 jit_solution(17876859818600163193)
XLA Ops:
  0.6 2.3 %half_of_memory.3.refs_3_.refs_7_ = bf16[512,2048]{1,0:T(8,128)(2,1)S(1)} custom-call(s32[1]{0:T(128)} %bitcast.5.which_ref, bf16[512,4096]{1,0:T(8,128)(2,1)} %bitcast.10, bf16[512,4096]{1,0:T(8,128)(2,1)} %bitcast.12), custom_call_target="tpu_custom_call" | custom-call | tf_op jit(solution)/shard_map/half_of_memory/pallas_call | solution.py:73
  3.0 1.5 %collective-permute-start = (bf16[512,2048]{1,0:T(8,128)(2,1)S(1)}, bf16[512,2048]{1,0:T(8,128)(2,1)}, u32[]{:S(2)}, u32[]{:S(2)}) collective-permute-start(bf16[512,2048]{1,0:T(8,128)(2,1)S(1)} %half_of_memory.3.refs_3_.refs_7_), channel_id=1, source_target_pairs={{0,4},{4,0},{8,12},{12,8},{16,20},{20,16},{24,28},{28,24},{32,36},... | collective-permute-start | bytes 6291464 | tf_op jit(solution)/shard_map/ppermute | solution.py:358
  4.5 2.3 %half_of_memory.2.a_ref.refs_2_.refs_6_ = bf16[512,2048]{1,0:T(8,128)(2,1)S(1)} custom-call(s32[1]{0:T(128)} %bitcast.2.which_ref, bf16[512,4096]{1,0:T(8,128)(2,1)} %bitcast.11, bf16[512,4096]{1,0:T(8,128)(2,1)} %bitcast.13), custom_call_target="tpu_custom_call" | custom-call | tf_op jit(solution)/shard_map/half_of_memory/pallas_call | solution.py:73
  6.9 1.5 %collective-permute-done.b_ref = bf16[512,2048]{1,0:T(8,128)(2,1)} collective-permute-done((bf16[512,2048]{1,0:T(8,128)(2,1)S(1)}, bf16[512,2048]{1,0:T(8,128)(2,1)}, u32[]{:S(2)}, u32[]{:S(2)}) %collective-permute-start) | collective-permute-done | bytes 2097184 | tf_op jit(solution)/shard_map/ppermute | solution.py:358
  8.4 1.9 %pair_sum.1 = (bf16[4,128,512]{2,1,0:T(8,128)(2,1)S(1)}, bf16[4,128,512]{2,1,0:T(8,128)(2,1)S(1)}, bf16[4,128,512]{2,1,0:T(8,128)(2,1)S(1)}, bf16[4,128,512]{2,1,0:T(8,128)(2,1)S(1)}) custom-call(s32[3]{0:T(128)S(1)} %pad_add_fusion.place_ref, bf16[512,2048]{1,0:T(8,128)(2,1)S(1)} %half_of_memory.2.a_ref.refs_2_.refs_6_, ...), custom_call_target="tpu_custom_call" | custom-call | tf_op jit(solution)/shard_map/pair_sum/pallas_call | solution.py:85
  10.3 1.4 collective-permute-start.1
  11.7 2.5 %collective-permute-start.2 = (bf16[4,128,512]{2,1,0:T(8,128)(2,1)S(1)}, bf16[4,128,512]{2,1,0:T(8,128)(2,1)S(1)}, u32[]{:S(2)}, u32[]{:S(2)}) collective-permute-start(bf16[4,128,512]{2,1,0:T(8,128)(2,1)S(1)} %get-tuple-element.77.refs_2_), channel_id=1, source_target_pairs={{0,64},{1,65},{2,66},{3,67},{4,20},{5,21},{6,22},{7,23},{8,72},{9,... | collective-permute-start | bytes 1572872 | tf_op jit(solution)/shard_map/ppermute | solution.py:31
  14.2 1.4 early_left.1
  15.6 2.2 %collective-permute-start.4 = (f32[32,256]{1,0:T(8,128)S(1)}, f32[32,256]{1,0:T(8,128)S(1)}, u32[]{:S(2)}, u32[]{:S(2)}) collective-permute-start(f32[32,256]{1,0:T(8,128)S(1)} %get-tuple-element.80), channel_id=1, source_target_pairs={{0,4},{4,0},{8,12},{12,8},{16,20},{20,16},{24,28},{28,24},{32,36},... | collective-permute-start | bytes 98312 | tf_op jit(solution)/shard_map/ppermute | solution.py:362
  17.8 0.9 collective-permute-done.4
  18.7 2.5 %collective-permute-start.7 = (f32[32,256]{1,0:T(8,128)S(1)}, f32[32,256]{1,0:T(8,128)S(1)}, u32[]{:S(2)}, u32[]{:S(2)}) collective-permute-start(f32[32,256]{1,0:T(8,128)S(1)} %add.57), channel_id=1, source_target_pairs={{0,24},{1,25},{2,26},{3,27},{4,28},{5,29},{6,30},{7,31},{8,16},{9,... | collective-permute-start | bytes 98312 | tf_op jit(solution)/shard_map/ppermute | solution.py:31
  21.7 9.0 %collective-permute-done.7 = f32[32,256]{1,0:T(8,128)S(1)} collective-permute-done((f32[32,256]{1,0:T(8,128)S(1)}, f32[32,256]{1,0:T(8,128)S(1)}, u32[]{:S(2)}, u32[]{:S(2)}) %collective-permute-start.7) | collective-permute-done | bytes 32800 | tf_op jit(solution)/shard_map/ppermute | solution.py:31
  30.7 2.8 %collective-permute-done.5 = f32[32,256]{1,0:T(8,128)S(1)} collective-permute-done((f32[32,256]{1,0:T(8,128)S(1)}, f32[32,256]{1,0:T(8,128)S(1)}, u32[]{:S(2)}, u32[]{:S(2)}) %collective-permute-start.5) | collective-permute-done | bytes 32800 | tf_op jit(solution)/shard_map/ppermute | solution.py:31
  33.5 0.8 first_sum.1
  34.3 1.4 %collective-permute-start.8 = (bf16[128,512]{1,0:T(8,128)(2,1)S(1)}, bf16[128,512]{1,0:T(8,128)(2,1)S(1)}, u32[]{:S(2)}, u32[]{:S(2)}) collective-permute-start(bf16[128,512]{1,0:T(8,128)(2,1)S(1)} %get-tuple-element.86), channel_id=1, source_target_pairs={{0,8},{1,9},{2,10},{3,11},{4,36},{5,37},{6,38},{7,39},{8,0},{9,1},... | collective-permute-start | bytes 393224 | tf_op jit(solution)/shard_map/ppermute | solution.py:31
  35.7 3.3 %collective-permute-start.9 = (bf16[128,512]{1,0:T(8,128)(2,1)S(1)}, bf16[128,512]{1,0:T(8,128)(2,1)S(1)}, u32[]{:S(2)}, u32[]{:S(2)}) collective-permute-start(bf16[128,512]{1,0:T(8,128)(2,1)S(1)} %get-tuple-element.87), channel_id=1, source_target_pairs={{0,16},{1,17},{2,18},{3,19},{4,68},{5,69},{6,70},{7,71},{8,24},{9,... | collective-permute-start | bytes 393224 | tf_op jit(solution)/shard_map/ppermute | solution.py:31
  39.0 2.8 %collective-permute-start.13 = (f32[32,256]{1,0:T(8,128)S(1)}, f32[32,256]{1,0:T(8,128)S(1)}, u32[]{:S(2)}, u32[]{:S(2)}) collective-permute-start(f32[32,256]{1,0:T(8,128)S(1)} %add_add_fusion.4), channel_id=1, source_target_pairs={{0,3},{1,2},{2,1},{3,0},{4,7},{5,6},{6,5},{7,4},{8,11},{9,10},{10,... | collective-permute-start | bytes 98312 | tf_op jit(solution)/shard_map/ppermute | solution.py:31
  42.2 1.1 collective-permute-done.13
  43.4 2.9 %collective-permute-done.12 = f32[32,256]{1,0:T(8,128)S(1)} collective-permute-done((f32[32,256]{1,0:T(8,128)S(1)}, f32[32,256]{1,0:T(8,128)S(1)}, u32[]{:S(2)}, u32[]{:S(2)}) %collective-permute-start.12) | collective-permute-done | bytes 32800 | tf_op jit(solution)/shard_map/ppermute | solution.py:31
  47.0 3.6 %collective-permute-start.16 = (bf16[128,512]{1,0:T(8,128)(2,1)S(1)}, bf16[128,512]{1,0:T(8,128)(2,1)S(1)}, u32[]{:S(2)}, u32[]{:S(2)}) collective-permute-start(bf16[128,512]{1,0:T(8,128)(2,1)S(1)} %second_sum.1), channel_id=1, source_target_pairs={{0,24},{1,25},{2,26},{3,27},{4,7},{5,6},{6,5},{7,4},{8,16},{9,17},... | collective-permute-start | bytes 393224 | tf_op jit(solution)/shard_map/ppermute | solution.py:31
  50.6 0.7 collective-permute-start.14
  51.3 2.6 %collective-permute-done.16 = bf16[128,512]{1,0:T(8,128)(2,1)S(1)} collective-permute-done((bf16[128,512]{1,0:T(8,128)(2,1)S(1)}, bf16[128,512]{1,0:T(8,128)(2,1)S(1)}, u32[]{:S(2)}, u32[]{:S(2)}) %collective-permute-start.16) | collective-permute-done | bytes 131104 | tf_op jit(solution)/shard_map/ppermute | solution.py:31
  53.9 2.3 %collective-permute-done.15 = bf16[128,512]{1,0:T(8,128)(2,1)S(1)} collective-permute-done((bf16[128,512]{1,0:T(8,128)(2,1)S(1)}, bf16[128,512]{1,0:T(8,128)(2,1)S(1)}, u32[]{:S(2)}, u32[]{:S(2)}) %collective-permute-start.15) | collective-permute-done | bytes 131104 | tf_op jit(solution)/shard_map/ppermute | solution.py:31
  56.2 1.4 %collective-permute-start.22 = (f32[128,256]{1,0:T(8,128)S(1)}, f32[128,256]{1,0:T(8,128)S(1)}, u32[]{:S(2)}, u32[]{:S(2)}) collective-permute-start(f32[128,256]{1,0:T(8,128)S(1)} %constant_dynamic-update-slice_fusion.4), channel_id=1, source_target_pairs={{0,96},{1,97},{2,98},{3,99},{4,100},{5,101},{6,102},{7,103},{8,104... | collective-permute-start | bytes 393224 | tf_op jit(solution)/shard_map/ppermute | solution.py:31
  58.0 2.4 %collective-permute-start.18 = (bf16[512,512]{1,0:T(8,128)(2,1)S(1)}, bf16[512,512]{1,0:T(8,128)(2,1)S(1)}, u32[]{:S(2)}, u32[]{:S(2)}) collective-permute-start(bf16[512,512]{1,0:T(8,128)(2,1)S(1)} %constant_dynamic-update-slice_fusion.refs_0_.refs_1_.m0), channel_id=1, source_target_pairs={{0,2},{1,3},{2,0},{3,1},{4,20},{5,21},{6,22},{7,23},{8,10},{9,11},... | collective-permute-start | bytes 1572872 | tf_op jit(solution)/shard_map/ppermute | solution.py:31
  60.4 0.7 collective-permute-start.17
  61.4 1.6 %collective-permute-start.20 = (f32[128,256]{1,0:T(8,128)S(1)}, f32[128,256]{1,0:T(8,128)S(1)}, u32[]{:S(2)}, u32[]{:S(2)}) collective-permute-start(f32[128,256]{1,0:T(8,128)S(1)} %constant_dynamic-update-slice_fusion.4), channel_id=1, source_target_pairs={{0,32},{1,33},{2,34},{3,35},{4,36},{5,37},{6,38},{7,39},{8,40},{9,... | collective-permute-start | bytes 393224 | tf_op jit(solution)/shard_map/ppermute | solution.py:31
  63.0 3.4 %collective-permute-done.21 = f32[128,256]{1,0:T(8,128)S(1)} collective-permute-done((f32[128,256]{1,0:T(8,128)S(1)}, f32[128,256]{1,0:T(8,128)S(1)}, u32[]{:S(2)}, u32[]{:S(2)}) %collective-permute-start.21) | collective-permute-done | bytes 131104 | tf_op jit(solution)/shard_map/ppermute | solution.py:31
  66.4 0.8 collective-permute-done.20
  67.3 4.1 %collective-permute-start.23 = (f32[128,256]{1,0:T(8,128)S(1)}, f32[128,256]{1,0:T(8,128)S(1)}, u32[]{:S(2)}, u32[]{:S(2)}) collective-permute-start(f32[128,256]{1,0:T(8,128)S(1)} %add_add_fusion.3.own_ref), channel_id=1, source_target_pairs={{0,4},{4,0},{8,12},{12,8},{16,20},{20,16},{24,28},{28,24},{32,36},... | collective-permute-start | bytes 393224 | tf_op jit(solution)/shard_map/ppermute | solution.py:370
  71.3 1.0 collective-permute-done.23.oth_ref
  72.9 1.9 %inverse_of.3.inv_ref = f32[32,32]{1,0:T(8,128)S(1)} custom-call(s32[3]{0:T(128)S(1)} %pad_add_fusion.place_ref, f32[32,2048]{1,0:T(8,128)S(1)} %assemble_left.1.left_ref), custom_call_target="tpu_custom_call" | custom-call | tf_op jit(solution)/shard_map/inverse_of/pallas_call | solution.py:85
  74.9 1.9 %second_left.1 = (f32[32,1024]{1,0:T(8,128)S(1)}, f32[32,1024]{1,0:T(8,128)S(1)}) custom-call(s32[3]{0:T(128)S(1)} %pad_add_fusion.place_ref, f32[32,2048]{1,0:T(8,128)S(1)} %assemble_left.1.left_ref, f32[32,32]{1,0:T(8,128)S(1)} %inverse_of.3.inv_ref, bf16[512,512]{1,0:T(8,128)(2,1)S(1)} %constant_dynamic-update-slice_fusion.refs_0_.refs_1_.m0, ...), custom_call_target="tpu_custom_call" | custom-call | tf_op jit(solution)/shard_map/second_left/pallas_call | solution.py:85
  76.8 2.8 %collective-permute-start.24 = (f32[32,1024]{1,0:T(8,128)S(1)}, f32[32,1024]{1,0:T(8,128)S(1)}, u32[]{:S(2)}, u32[]{:S(2)}) collective-permute-start(f32[32,1024]{1,0:T(8,128)S(1)} %get-tuple-element.116), channel_id=1, source_target_pairs={{0,4},{4,0},{8,12},{12,8},{16,20},{20,16},{24,28},{28,24},{32,36},... | collective-permute-start | bytes 393224 | tf_op jit(solution)/shard_map/ppermute | solution.py:292
  79.6 1.0 collective-permute-done.24
  80.7 1.3 collective-permute-start.26
  82.0 1.9 %collective-permute-start.25 = (f32[32,1024]{1,0:T(8,128)S(1)}, f32[32,1024]{1,0:T(8,128)S(1)}, u32[]{:S(2)}, u32[]{:S(2)}) collective-permute-start(f32[32,1024]{1,0:T(8,128)S(1)} %add.64), channel_id=1, source_target_pairs={{0,32},{1,33},{2,34},{3,35},{4,36},{5,37},{6,38},{7,39},{8,40},{9,... | collective-permute-start | bytes 393224 | tf_op jit(solution)/shard_map/ppermute | solution.py:31
  83.9 5.8 %collective-permute-done.27 = f32[32,1024]{1,0:T(8,128)S(1)} collective-permute-done((f32[32,1024]{1,0:T(8,128)S(1)}, f32[32,1024]{1,0:T(8,128)S(1)}, u32[]{:S(2)}, u32[]{:S(2)}) %collective-permute-start.27) | collective-permute-done | bytes 131104 | tf_op jit(solution)/shard_map/ppermute | solution.py:31
  89.8 1.7 %collective-permute-start.28 = (f32[32,1024]{1,0:T(8,128)S(1)}, f32[32,1024]{1,0:T(8,128)S(1)}, u32[]{:S(2)}, u32[]{:S(2)}) collective-permute-start(f32[32,1024]{1,0:T(8,128)S(1)} %add_add_fusion.2.own_in), channel_id=1, source_target_pairs={{0,4},{4,0},{8,12},{12,8},{16,20},{20,16},{24,28},{28,24},{32,36},... | collective-permute-start | bytes 393224 | tf_op jit(solution)/shard_map/ppermute | solution.py:298
  91.5 1.0 collective-permute-done.28.oth_in
  92.5 1.7 %next_left.2 = (f32[32,2048]{1,0:T(8,128)S(1)}, f32[32,1024]{1,0:T(8,128)S(1)}, f32[32,1024]{1,0:T(8,128)S(1)}) custom-call(s32[3]{0:T(128)S(1)} %pad_add_fusion.place_ref, f32[32,1024]{1,0:T(8,128)S(1)} %add_add_fusion.2.own_in, f32[32,1024]{1,0:T(8,128)S(1)} %collective-permute-done.28.oth_in, ...), custom_call_target="tpu_custom_call" | custom-call | tf_op jit(solution)/shard_map/next_left/pallas_call | solution.py:85
  94.6 1.0 collective-permute-done.29
  95.6 0.8 collective-permute-start.32
  97.0 1.9 %collective-permute-start.30 = (f32[32,1024]{1,0:T(8,128)S(1)}, f32[32,1024]{1,0:T(8,128)S(1)}, u32[]{:S(2)}, u32[]{:S(2)}) collective-permute-start(f32[32,1024]{1,0:T(8,128)S(1)} %add.68), channel_id=1, source_target_pairs={{0,32},{1,33},{2,34},{3,35},{4,36},{5,37},{6,38},{7,39},{8,40},{9,... | collective-permute-start | bytes 393224 | tf_op jit(solution)/shard_map/ppermute | solution.py:31
  99.0 1.9 %inverse_of.4.refs_0_ = f32[32,32]{1,0:T(8,128)S(1)} custom-call(s32[3]{0:T(128)S(1)} %pad_add_fusion.place_ref, f32[32,2048]{1,0:T(8,128)S(1)} %get-tuple-element.119.left_ref), custom_call_target="tpu_custom_call" | custom-call | tf_op jit(solution)/shard_map/inverse_of/pallas_call | solution.py:85
  100.9 3.5 %collective-permute-done.32 = f32[32,1024]{1,0:T(8,128)S(1)} collective-permute-done((f32[32,1024]{1,0:T(8,128)S(1)}, f32[32,1024]{1,0:T(8,128)S(1)}, u32[]{:S(2)}, u32[]{:S(2)}) %collective-permute-start.32) | collective-permute-done | bytes 131104 | tf_op jit(solution)/shard_map/ppermute | solution.py:31
  104.8 1.5 %collective-permute-start.33 = (f32[32,1024]{1,0:T(8,128)S(1)}, f32[32,1024]{1,0:T(8,128)S(1)}, u32[]{:S(2)}, u32[]{:S(2)}) collective-permute-start(f32[32,1024]{1,0:T(8,128)S(1)} %add_add_fusion.1.own_in), channel_id=1, source_target_pairs={{0,4},{4,0},{8,12},{12,8},{16,20},{20,16},{24,28},{28,24},{32,36},... | collective-permute-start | bytes 393224 | tf_op jit(solution)/shard_map/ppermute | solution.py:298
  106.4 1.0 collective-permute-done.33.oth_in
  107.4 2.0 %next_left.3 = (f32[32,2048]{1,0:T(8,128)S(1)}, f32[32,1024]{1,0:T(8,128)S(1)}, f32[32,1024]{1,0:T(8,128)S(1)}) custom-call(s32[3]{0:T(128)S(1)} %pad_add_fusion.place_ref, f32[32,1024]{1,0:T(8,128)S(1)} %add_add_fusion.1.own_in, f32[32,1024]{1,0:T(8,128)S(1)} %collective-permute-done.33.oth_in, f32[32,32]{1,0:T(8,128)S(1)} %inverse_of.4.refs_0_, ...), custom_call_target="tpu_custom_call" | custom-call | tf_op jit(solution)/shard_map/next_left/pallas_call | solution.py:85
  109.8 1.0 collective-permute-done.34
  110.8 0.8 collective-permute-start.37
  112.2 1.9 %collective-permute-start.35 = (f32[32,1024]{1,0:T(8,128)S(1)}, f32[32,1024]{1,0:T(8,128)S(1)}, u32[]{:S(2)}, u32[]{:S(2)}) collective-permute-start(f32[32,1024]{1,0:T(8,128)S(1)} %add.72), channel_id=1, source_target_pairs={{0,32},{1,33},{2,34},{3,35},{4,36},{5,37},{6,38},{7,39},{8,40},{9,... | collective-permute-start | bytes 393224 | tf_op jit(solution)/shard_map/ppermute | solution.py:31
  114.2 1.9 %inverse_of.5.inv_ref = f32[32,32]{1,0:T(8,128)S(1)} custom-call(s32[3]{0:T(128)S(1)} %pad_add_fusion.place_ref, f32[32,2048]{1,0:T(8,128)S(1)} %get-tuple-element.127.left_ref), custom_call_target="tpu_custom_call" | custom-call | tf_op jit(solution)/shard_map/inverse_of/pallas_call | solution.py:85
  116.1 3.5 %collective-permute-done.37 = f32[32,1024]{1,0:T(8,128)S(1)} collective-permute-done((f32[32,1024]{1,0:T(8,128)S(1)}, f32[32,1024]{1,0:T(8,128)S(1)}, u32[]{:S(2)}, u32[]{:S(2)}) %collective-permute-start.37) | collective-permute-done | bytes 131104 | tf_op jit(solution)/shard_map/ppermute | solution.py:31
  120.0 1.5 %collective-permute-start.38 = (f32[32,1024]{1,0:T(8,128)S(1)}, f32[32,1024]{1,0:T(8,128)S(1)}, u32[]{:S(2)}, u32[]{:S(2)}) collective-permute-start(f32[32,1024]{1,0:T(8,128)S(1)} %add_add_fusion.own_in), channel_id=1, source_target_pairs={{0,4},{4,0},{8,12},{12,8},{16,20},{20,16},{24,28},{28,24},{32,36},... | collective-permute-start | bytes 393224 | tf_op jit(solution)/shard_map/ppermute | solution.py:298
  121.6 1.0 collective-permute-done.38.oth_in
  122.6 3.2 %last_right.1 = (bf16[32,512]{1,0:T(8,128)(2,1)S(1)}, f32[32,512]{1,0:T(8,128)S(1)}) custom-call(s32[3]{0:T(128)S(1)} %pad_add_fusion.place_ref, f32[32,1024]{1,0:T(8,128)S(1)} %add_add_fusion.own_in, f32[32,1024]{1,0:T(8,128)S(1)} %collective-permute-done.38.oth_in, f32[32,32]{1,0:T(8,128)S(1)} %inverse_of.5.inv_ref, ...), custom_call_target="tpu_custom_call" | custom-call | tf_op jit(solution)/shard_map/last_right/pallas_call | solution.py:85
  126.2 0.7 collective-permute-start.41
  126.9 0.6 collective-permute-start.40
  127.5 1.9 %collective-permute-start.39 = (f32[32,512]{1,0:T(8,128)S(1)}, f32[32,512]{1,0:T(8,128)S(1)}, u32[]{:S(2)}, u32[]{:S(2)}) collective-permute-start(f32[32,512]{1,0:T(8,128)S(1)} %get-tuple-element.134.refs_0_), channel_id=1, source_target_pairs={{0,32},{1,33},{2,34},{3,35},{4,36},{5,37},{6,38},{7,39},{8,40},{9,... | collective-permute-start | bytes 196616 | tf_op jit(solution)/shard_map/ppermute | solution.py:31
  129.5 0.6 columns_of.1.o_ref
  130.1 2.9 %finish_near.1 = (f32[512,4096]{1,0:T(8,128)}, f32[512,4096]{1,0:T(8,128)}, f32[32,4096]{1,0:T(8,128)}) custom-call(s32[3]{0:T(128)S(1)} %pad_add_fusion.place_ref, bf16[512,128]{1,0:T(8,128)(2,1)S(1)} %columns_of.1.o_ref, f32[32,512]{1,0:T(8,128)S(1)} %get-tuple-element.134.refs_0_, f32[32,512]{1,0:T(8,128)S(1)} %collective-permute-done.42.refs_1_, ...), custom_call_target="tpu_custom_call" | custom-call | tf_op jit(solution)/shard_map/finish_near/pallas_call | solution.py:336
  133.1 1.1 collective-permute-start.43
  135.6 5.6 %finish_far.1 = (f32[512,4096]{1,0:T(8,128)}, f32[512,4096]{1,0:T(8,128)}, f32[32,4096]{1,0:T(8,128)}) custom-call(s32[3]{0:T(128)S(1)} %pad_add_fusion.place_ref, bf16[512,128]{1,0:T(8,128)(2,1)S(1)} %columns_of.1.o_ref, f32[32,512]{1,0:T(8,128)S(1)} %collective-permute-done.39.refs_0_, ...), custom_call_target="tpu_custom_call", output_to_operand_aliasing={{0}: (10, {}), {1}: (11, {}), {2}: (12, {})} | custom-call | tf_op jit(solution)/shard_map/finish_far/pallas_call | solution.py:336
  (65 shorter events, 8.3 us)
Async XLA Ops:
  3.0 5.4 %collective-permute-start = (bf16[512,2048]{1,0:T(8,128)(2,1)S(1)}, bf16[512,2048]{1,0:T(8,128)(2,1)}, u32[]{:S(2)}, u32[]{:S(2)}) collective-permute-start(bf16[512,2048]{1,0:T(8,128)(2,1)S(1)} %half_of_memory.3.refs_3_.refs_7_), channel_id=1, source_target_pairs={{0,4},{4,0},{8,12},{12,8},{16,20},{20,16},{24,28},{28,24},{32,36},... | collective-permute-start | bytes 6291464 | tf_op jit(solution)/shard_map/ppermute | solution.py:358
  6.8 7.4 %copy-start = (f32[4096,32]{0,1:T(8,128)S(1)}, f32[4096,32]{0,1:T(8,128)}, u32[]{:S(2)}) copy-start(f32[4096,32]{0,1:T(8,128)} %param.5) | copy-start | bytes 1572868
  10.3 23.2 %collective-permute-start.1 = (bf16[4,128,512]{2,1,0:T(8,128)(2,1)S(1)}, bf16[4,128,512]{2,1,0:T(8,128)(2,1)S(1)}, u32[]{:S(2)}, u32[]{:S(2)}) collective-permute-start(bf16[4,128,512]{2,1,0:T(8,128)(2,1)S(1)} %get-tuple-element.76.refs_1_), channel_id=1, source_target_pairs={{0,32},{1,33},{2,34},{3,35},{4,12},{5,13},{6,14},{7,15},{8,40},{9,... | collective-permute-start | bytes 1572872 | tf_op jit(solution)/shard_map/ppermute | solution.py:31
  11.7 21.8 %collective-permute-start.2 = (bf16[4,128,512]{2,1,0:T(8,128)(2,1)S(1)}, bf16[4,128,512]{2,1,0:T(8,128)(2,1)S(1)}, u32[]{:S(2)}, u32[]{:S(2)}) collective-permute-start(bf16[4,128,512]{2,1,0:T(8,128)(2,1)S(1)} %get-tuple-element.77.refs_2_), channel_id=1, source_target_pairs={{0,64},{1,65},{2,66},{3,67},{4,20},{5,21},{6,22},{7,23},{8,72},{9,... | collective-permute-start | bytes 1572872 | tf_op jit(solution)/shard_map/ppermute | solution.py:31
  14.1 19.3 %collective-permute-start.3 = (bf16[4,128,512]{2,1,0:T(8,128)(2,1)S(1)}, bf16[4,128,512]{2,1,0:T(8,128)(2,1)S(1)}, u32[]{:S(2)}, u32[]{:S(2)}) collective-permute-start(bf16[4,128,512]{2,1,0:T(8,128)(2,1)S(1)} %get-tuple-element.78.refs_3_), channel_id=1, source_target_pairs={{0,96},{1,97},{2,98},{3,99},{4,28},{5,29},{6,30},{7,31},{8,104},{9... | collective-permute-start | bytes 1572872 | tf_op jit(solution)/shard_map/ppermute | solution.py:31
  15.6 3.1 %collective-permute-start.4 = (f32[32,256]{1,0:T(8,128)S(1)}, f32[32,256]{1,0:T(8,128)S(1)}, u32[]{:S(2)}, u32[]{:S(2)}) collective-permute-start(f32[32,256]{1,0:T(8,128)S(1)} %get-tuple-element.80), channel_id=1, source_target_pairs={{0,4},{4,0},{8,12},{12,8},{16,20},{20,16},{24,28},{28,24},{32,36},... | collective-permute-start | bytes 98312 | tf_op jit(solution)/shard_map/ppermute | solution.py:362
  18.7 12.0 %collective-permute-start.7 = (f32[32,256]{1,0:T(8,128)S(1)}, f32[32,256]{1,0:T(8,128)S(1)}, u32[]{:S(2)}, u32[]{:S(2)}) collective-permute-start(f32[32,256]{1,0:T(8,128)S(1)} %add.57), channel_id=1, source_target_pairs={{0,24},{1,25},{2,26},{3,27},{4,28},{5,29},{6,30},{7,31},{8,16},{9,... | collective-permute-start | bytes 98312 | tf_op jit(solution)/shard_map/ppermute | solution.py:31
  21.1 9.5 %collective-permute-start.6 = (f32[32,256]{1,0:T(8,128)S(1)}, f32[32,256]{1,0:T(8,128)S(1)}, u32[]{:S(2)}, u32[]{:S(2)}) collective-permute-start(f32[32,256]{1,0:T(8,128)S(1)} %add.57), channel_id=1, source_target_pairs={{0,16},{1,17},{2,18},{3,19},{4,20},{5,21},{6,22},{7,23},{8,24},{9,... | collective-permute-start | bytes 98312 | tf_op jit(solution)/shard_map/ppermute | solution.py:31
  30.7 2.8 %collective-permute-start.5 = (f32[32,256]{1,0:T(8,128)S(1)}, f32[32,256]{1,0:T(8,128)S(1)}, u32[]{:S(2)}, u32[]{:S(2)}) collective-permute-start(f32[32,256]{1,0:T(8,128)S(1)} %add.57), channel_id=1, source_target_pairs={{0,8},{1,9},{2,10},{3,11},{4,12},{5,13},{6,14},{7,15},{8,0},{9,1},... | collective-permute-start | bytes 98312 | tf_op jit(solution)/shard_map/ppermute | solution.py:31
  34.3 12.1 %collective-permute-start.8 = (bf16[128,512]{1,0:T(8,128)(2,1)S(1)}, bf16[128,512]{1,0:T(8,128)(2,1)S(1)}, u32[]{:S(2)}, u32[]{:S(2)}) collective-permute-start(bf16[128,512]{1,0:T(8,128)(2,1)S(1)} %get-tuple-element.86), channel_id=1, source_target_pairs={{0,8},{1,9},{2,10},{3,11},{4,36},{5,37},{6,38},{7,39},{8,0},{9,1},... | collective-permute-start | bytes 393224 | tf_op jit(solution)/shard_map/ppermute | solution.py:31
  35.7 10.7 %collective-permute-start.9 = (bf16[128,512]{1,0:T(8,128)(2,1)S(1)}, bf16[128,512]{1,0:T(8,128)(2,1)S(1)}, u32[]{:S(2)}, u32[]{:S(2)}) collective-permute-start(bf16[128,512]{1,0:T(8,128)(2,1)S(1)} %get-tuple-element.87), channel_id=1, source_target_pairs={{0,16},{1,17},{2,18},{3,19},{4,68},{5,69},{6,70},{7,71},{8,24},{9,... | collective-permute-start | bytes 393224 | tf_op jit(solution)/shard_map/ppermute | solution.py:31
  39.0 7.4 %collective-permute-start.10 = (bf16[128,512]{1,0:T(8,128)(2,1)S(1)}, bf16[128,512]{1,0:T(8,128)(2,1)S(1)}, u32[]{:S(2)}, u32[]{:S(2)}) collective-permute-start(bf16[128,512]{1,0:T(8,128)(2,1)S(1)} %get-tuple-element.88), channel_id=1, source_target_pairs={{0,24},{1,25},{2,26},{3,27},{4,100},{5,101},{6,102},{7,103},{8,16}... | collective-permute-start | bytes 393224 | tf_op jit(solution)/shard_map/ppermute | solution.py:31
  39.0 4.2 %collective-permute-start.13 = (f32[32,256]{1,0:T(8,128)S(1)}, f32[32,256]{1,0:T(8,128)S(1)}, u32[]{:S(2)}, u32[]{:S(2)}) collective-permute-start(f32[32,256]{1,0:T(8,128)S(1)} %add_add_fusion.4), channel_id=1, source_target_pairs={{0,3},{1,2},{2,1},{3,0},{4,7},{5,6},{6,5},{7,4},{8,11},{9,10},{10,... | collective-permute-start | bytes 98312 | tf_op jit(solution)/shard_map/ppermute | solution.py:31
  41.8 4.5 %collective-permute-start.12 = (f32[32,256]{1,0:T(8,128)S(1)}, f32[32,256]{1,0:T(8,128)S(1)}, u32[]{:S(2)}, u32[]{:S(2)}) collective-permute-start(f32[32,256]{1,0:T(8,128)S(1)} %add_add_fusion.4), channel_id=1, source_target_pairs={{0,2},{1,3},{2,0},{3,1},{4,6},{5,7},{6,4},{7,5},{8,10},{9,11},{10,... | collective-permute-start | bytes 98312 | tf_op jit(solution)/shard_map/ppermute | solution.py:31
  43.3 3.1 %collective-permute-start.11 = (f32[32,256]{1,0:T(8,128)S(1)}, f32[32,256]{1,0:T(8,128)S(1)}, u32[]{:S(2)}, u32[]{:S(2)}) collective-permute-start(f32[32,256]{1,0:T(8,128)S(1)} %add_add_fusion.4), channel_id=1, source_target_pairs={{0,1},{1,0},{2,3},{3,2},{4,5},{5,4},{6,7},{7,6},{8,9},{9,8},{10,11... | collective-permute-start | bytes 98312 | tf_op jit(solution)/shard_map/ppermute | solution.py:31
  47.0 6.9 %collective-permute-start.16 = (bf16[128,512]{1,0:T(8,128)(2,1)S(1)}, bf16[128,512]{1,0:T(8,128)(2,1)S(1)}, u32[]{:S(2)}, u32[]{:S(2)}) collective-permute-start(bf16[128,512]{1,0:T(8,128)(2,1)S(1)} %second_sum.1), channel_id=1, source_target_pairs={{0,24},{1,25},{2,26},{3,27},{4,7},{5,6},{6,5},{7,4},{8,16},{9,17},... | collective-permute-start | bytes 393224 | tf_op jit(solution)/shard_map/ppermute | solution.py:31
  50.6 5.6 %collective-permute-start.15 = (bf16[128,512]{1,0:T(8,128)(2,1)S(1)}, bf16[128,512]{1,0:T(8,128)(2,1)S(1)}, u32[]{:S(2)}, u32[]{:S(2)}) collective-permute-start(bf16[128,512]{1,0:T(8,128)(2,1)S(1)} %second_sum.1), channel_id=1, source_target_pairs={{0,16},{1,17},{2,18},{3,19},{4,6},{5,7},{6,4},{7,5},{8,24},{9,25},... | collective-permute-start | bytes 393224 | tf_op jit(solution)/shard_map/ppermute | solution.py:31
  50.6 5.6 %collective-permute-start.14 = (bf16[128,512]{1,0:T(8,128)(2,1)S(1)}, bf16[128,512]{1,0:T(8,128)(2,1)S(1)}, u32[]{:S(2)}, u32[]{:S(2)}) collective-permute-start(bf16[128,512]{1,0:T(8,128)(2,1)S(1)} %second_sum.1), channel_id=1, source_target_pairs={{0,8},{1,9},{2,10},{3,11},{4,5},{5,4},{6,7},{7,6},{8,0},{9,1},{10,... | collective-permute-start | bytes 393224 | tf_op jit(solution)/shard_map/ppermute | solution.py:31
  56.2 5.1 %collective-permute-start.22 = (f32[128,256]{1,0:T(8,128)S(1)}, f32[128,256]{1,0:T(8,128)S(1)}, u32[]{:S(2)}, u32[]{:S(2)}) collective-permute-start(f32[128,256]{1,0:T(8,128)S(1)} %constant_dynamic-update-slice_fusion.4), channel_id=1, source_target_pairs={{0,96},{1,97},{2,98},{3,99},{4,100},{5,101},{6,102},{7,103},{8,104... | collective-permute-start | bytes 393224 | tf_op jit(solution)/shard_map/ppermute | solution.py:31
  57.8 17.1 %collective-permute-start.19 = (bf16[512,512]{1,0:T(8,128)(2,1)S(1)}, bf16[512,512]{1,0:T(8,128)(2,1)S(1)}, u32[]{:S(2)}, u32[]{:S(2)}) collective-permute-start(bf16[512,512]{1,0:T(8,128)(2,1)S(1)} %constant_dynamic-update-slice_fusion.refs_0_.refs_1_.m0), channel_id=1, source_target_pairs={{0,3},{1,2},{2,1},{3,0},{4,28},{5,29},{6,30},{7,31},{8,11},{9,10},... | collective-permute-start | bytes 1572872 | tf_op jit(solution)/shard_map/ppermute | solution.py:31
  58.0 16.8 %collective-permute-start.18 = (bf16[512,512]{1,0:T(8,128)(2,1)S(1)}, bf16[512,512]{1,0:T(8,128)(2,1)S(1)}, u32[]{:S(2)}, u32[]{:S(2)}) collective-permute-start(bf16[512,512]{1,0:T(8,128)(2,1)S(1)} %constant_dynamic-update-slice_fusion.refs_0_.refs_1_.m0), channel_id=1, source_target_pairs={{0,2},{1,3},{2,0},{3,1},{4,20},{5,21},{6,22},{7,23},{8,10},{9,11},... | collective-permute-start | bytes 1572872 | tf_op jit(solution)/shard_map/ppermute | solution.py:31
  60.4 14.5 %collective-permute-start.17 = (bf16[512,512]{1,0:T(8,128)(2,1)S(1)}, bf16[512,512]{1,0:T(8,128)(2,1)S(1)}, u32[]{:S(2)}, u32[]{:S(2)}) collective-permute-start(bf16[512,512]{1,0:T(8,128)(2,1)S(1)} %constant_dynamic-update-slice_fusion.refs_0_.refs_1_.m0), channel_id=1, source_target_pairs={{0,1},{1,0},{2,3},{3,2},{4,12},{5,13},{6,14},{7,15},{8,9},{9,8},{1... | collective-permute-start | bytes 1572872 | tf_op jit(solution)/shard_map/ppermute | solution.py:31
  61.1 5.3 %collective-permute-start.21 = (f32[128,256]{1,0:T(8,128)S(1)}, f32[128,256]{1,0:T(8,128)S(1)}, u32[]{:S(2)}, u32[]{:S(2)}) collective-permute-start(f32[128,256]{1,0:T(8,128)S(1)} %constant_dynamic-update-slice_fusion.4), channel_id=1, source_target_pairs={{0,64},{1,65},{2,66},{3,67},{4,68},{5,69},{6,70},{7,71},{8,72},{9,... | collective-permute-start | bytes 393224 | tf_op jit(solution)/shard_map/ppermute | solution.py:31
  61.4 5.9 %collective-permute-start.20 = (f32[128,256]{1,0:T(8,128)S(1)}, f32[128,256]{1,0:T(8,128)S(1)}, u32[]{:S(2)}, u32[]{:S(2)}) collective-permute-start(f32[128,256]{1,0:T(8,128)S(1)} %constant_dynamic-update-slice_fusion.4), channel_id=1, source_target_pairs={{0,32},{1,33},{2,34},{3,35},{4,36},{5,37},{6,38},{7,39},{8,40},{9,... | collective-permute-start | bytes 393224 | tf_op jit(solution)/shard_map/ppermute | solution.py:31
  67.3 5.1 %collective-permute-start.23 = (f32[128,256]{1,0:T(8,128)S(1)}, f32[128,256]{1,0:T(8,128)S(1)}, u32[]{:S(2)}, u32[]{:S(2)}) collective-permute-start(f32[128,256]{1,0:T(8,128)S(1)} %add_add_fusion.3.own_ref), channel_id=1, source_target_pairs={{0,4},{4,0},{8,12},{12,8},{16,20},{20,16},{24,28},{28,24},{32,36},... | collective-permute-start | bytes 393224 | tf_op jit(solution)/shard_map/ppermute | solution.py:370
  76.8 3.7 %collective-permute-start.24 = (f32[32,1024]{1,0:T(8,128)S(1)}, f32[32,1024]{1,0:T(8,128)S(1)}, u32[]{:S(2)}, u32[]{:S(2)}) collective-permute-start(f32[32,1024]{1,0:T(8,128)S(1)} %get-tuple-element.116), channel_id=1, source_target_pairs={{0,4},{4,0},{8,12},{12,8},{16,20},{20,16},{24,28},{28,24},{32,36},... | collective-permute-start | bytes 393224 | tf_op jit(solution)/shard_map/ppermute | solution.py:292
  80.6 9.2 %collective-permute-start.27 = (f32[32,1024]{1,0:T(8,128)S(1)}, f32[32,1024]{1,0:T(8,128)S(1)}, u32[]{:S(2)}, u32[]{:S(2)}) collective-permute-start(f32[32,1024]{1,0:T(8,128)S(1)} %add.64), channel_id=1, source_target_pairs={{0,96},{1,97},{2,98},{3,99},{4,100},{5,101},{6,102},{7,103},{8,104... | collective-permute-start | bytes 393224 | tf_op jit(solution)/shard_map/ppermute | solution.py:31
  80.7 9.1 %collective-permute-start.26 = (f32[32,1024]{1,0:T(8,128)S(1)}, f32[32,1024]{1,0:T(8,128)S(1)}, u32[]{:S(2)}, u32[]{:S(2)}) collective-permute-start(f32[32,1024]{1,0:T(8,128)S(1)} %add.64), channel_id=1, source_target_pairs={{0,64},{1,65},{2,66},{3,67},{4,68},{5,69},{6,70},{7,71},{8,72},{9,... | collective-permute-start | bytes 393224 | tf_op jit(solution)/shard_map/ppermute | solution.py:31
  82.0 7.8 %collective-permute-start.25 = (f32[32,1024]{1,0:T(8,128)S(1)}, f32[32,1024]{1,0:T(8,128)S(1)}, u32[]{:S(2)}, u32[]{:S(2)}) collective-permute-start(f32[32,1024]{1,0:T(8,128)S(1)} %add.64), channel_id=1, source_target_pairs={{0,32},{1,33},{2,34},{3,35},{4,36},{5,37},{6,38},{7,39},{8,40},{9,... | collective-permute-start | bytes 393224 | tf_op jit(solution)/shard_map/ppermute | solution.py:31
  89.8 2.7 %collective-permute-start.28 = (f32[32,1024]{1,0:T(8,128)S(1)}, f32[32,1024]{1,0:T(8,128)S(1)}, u32[]{:S(2)}, u32[]{:S(2)}) collective-permute-start(f32[32,1024]{1,0:T(8,128)S(1)} %add_add_fusion.2.own_in), channel_id=1, source_target_pairs={{0,4},{4,0},{8,12},{12,8},{16,20},{20,16},{24,28},{28,24},{32,36},... | collective-permute-start | bytes 393224 | tf_op jit(solution)/shard_map/ppermute | solution.py:298
  94.2 1.4 %collective-permute-start.29 = (f32[32,1024]{1,0:T(8,128)S(1)}, f32[32,1024]{1,0:T(8,128)S(1)}, u32[]{:S(2)}, u32[]{:S(2)}) collective-permute-start(f32[32,1024]{1,0:T(8,128)S(1)} %get-tuple-element.118), channel_id=1, source_target_pairs={{0,4},{4,0},{8,12},{12,8},{16,20},{20,16},{24,28},{28,24},{32,36},... | collective-permute-start | bytes 393224 | tf_op jit(solution)/shard_map/ppermute | solution.py:292
  95.6 8.7 %collective-permute-start.32 = (f32[32,1024]{1,0:T(8,128)S(1)}, f32[32,1024]{1,0:T(8,128)S(1)}, u32[]{:S(2)}, u32[]{:S(2)}) collective-permute-start(f32[32,1024]{1,0:T(8,128)S(1)} %add.68), channel_id=1, source_target_pairs={{0,96},{1,97},{2,98},{3,99},{4,100},{5,101},{6,102},{7,103},{8,104... | collective-permute-start | bytes 393224 | tf_op jit(solution)/shard_map/ppermute | solution.py:31
  96.4 7.9 %collective-permute-start.31 = (f32[32,1024]{1,0:T(8,128)S(1)}, f32[32,1024]{1,0:T(8,128)S(1)}, u32[]{:S(2)}, u32[]{:S(2)}) collective-permute-start(f32[32,1024]{1,0:T(8,128)S(1)} %add.68), channel_id=1, source_target_pairs={{0,64},{1,65},{2,66},{3,67},{4,68},{5,69},{6,70},{7,71},{8,72},{9,... | collective-permute-start | bytes 393224 | tf_op jit(solution)/shard_map/ppermute | solution.py:31
  97.0 7.8 %collective-permute-start.30 = (f32[32,1024]{1,0:T(8,128)S(1)}, f32[32,1024]{1,0:T(8,128)S(1)}, u32[]{:S(2)}, u32[]{:S(2)}) collective-permute-start(f32[32,1024]{1,0:T(8,128)S(1)} %add.68), channel_id=1, source_target_pairs={{0,32},{1,33},{2,34},{3,35},{4,36},{5,37},{6,38},{7,39},{8,40},{9,... | collective-permute-start | bytes 393224 | tf_op jit(solution)/shard_map/ppermute | solution.py:31
  104.8 2.5 %collective-permute-start.33 = (f32[32,1024]{1,0:T(8,128)S(1)}, f32[32,1024]{1,0:T(8,128)S(1)}, u32[]{:S(2)}, u32[]{:S(2)}) collective-permute-start(f32[32,1024]{1,0:T(8,128)S(1)} %add_add_fusion.1.own_in), channel_id=1, source_target_pairs={{0,4},{4,0},{8,12},{12,8},{16,20},{20,16},{24,28},{28,24},{32,36},... | collective-permute-start | bytes 393224 | tf_op jit(solution)/shard_map/ppermute | solution.py:298
  109.4 1.4 %collective-permute-start.34 = (f32[32,1024]{1,0:T(8,128)S(1)}, f32[32,1024]{1,0:T(8,128)S(1)}, u32[]{:S(2)}, u32[]{:S(2)}) collective-permute-start(f32[32,1024]{1,0:T(8,128)S(1)} %get-tuple-element.126), channel_id=1, source_target_pairs={{0,4},{4,0},{8,12},{12,8},{16,20},{20,16},{24,28},{28,24},{32,36},... | collective-permute-start | bytes 393224 | tf_op jit(solution)/shard_map/ppermute | solution.py:292
  110.8 8.7 %collective-permute-start.37 = (f32[32,1024]{1,0:T(8,128)S(1)}, f32[32,1024]{1,0:T(8,128)S(1)}, u32[]{:S(2)}, u32[]{:S(2)}) collective-permute-start(f32[32,1024]{1,0:T(8,128)S(1)} %add.72), channel_id=1, source_target_pairs={{0,96},{1,97},{2,98},{3,99},{4,100},{5,101},{6,102},{7,103},{8,104... | collective-permute-start | bytes 393224 | tf_op jit(solution)/shard_map/ppermute | solution.py:31
  111.6 8.0 %collective-permute-start.36 = (f32[32,1024]{1,0:T(8,128)S(1)}, f32[32,1024]{1,0:T(8,128)S(1)}, u32[]{:S(2)}, u32[]{:S(2)}) collective-permute-start(f32[32,1024]{1,0:T(8,128)S(1)} %add.72), channel_id=1, source_target_pairs={{0,64},{1,65},{2,66},{3,67},{4,68},{5,69},{6,70},{7,71},{8,72},{9,... | collective-permute-start | bytes 393224 | tf_op jit(solution)/shard_map/ppermute | solution.py:31
  112.2 7.8 %collective-permute-start.35 = (f32[32,1024]{1,0:T(8,128)S(1)}, f32[32,1024]{1,0:T(8,128)S(1)}, u32[]{:S(2)}, u32[]{:S(2)}) collective-permute-start(f32[32,1024]{1,0:T(8,128)S(1)} %add.72), channel_id=1, source_target_pairs={{0,32},{1,33},{2,34},{3,35},{4,36},{5,37},{6,38},{7,39},{8,40},{9,... | collective-permute-start | bytes 393224 | tf_op jit(solution)/shard_map/ppermute | solution.py:31
  120.0 2.5 %collective-permute-start.38 = (f32[32,1024]{1,0:T(8,128)S(1)}, f32[32,1024]{1,0:T(8,128)S(1)}, u32[]{:S(2)}, u32[]{:S(2)}) collective-permute-start(f32[32,1024]{1,0:T(8,128)S(1)} %add_add_fusion.own_in), channel_id=1, source_target_pairs={{0,4},{4,0},{8,12},{12,8},{16,20},{20,16},{24,28},{28,24},{32,36},... | collective-permute-start | bytes 393224 | tf_op jit(solution)/shard_map/ppermute | solution.py:298
  125.8 4.3 %collective-permute-start.42 = (f32[32,512]{1,0:T(8,128)S(1)}, f32[32,512]{1,0:T(8,128)S(1)}, u32[]{:S(2)}, u32[]{:S(2)}) collective-permute-start(f32[32,512]{1,0:T(8,128)S(1)} %get-tuple-element.134.refs_0_), channel_id=1, source_target_pairs={{0,4},{4,0},{8,12},{12,8},{16,20},{20,16},{24,28},{28,24},{32,36},... | collective-permute-start | bytes 196616 | tf_op jit(solution)/shard_map/ppermute | solution.py:381
  126.2 6.8 %collective-permute-start.41 = (f32[32,512]{1,0:T(8,128)S(1)}, f32[32,512]{1,0:T(8,128)S(1)}, u32[]{:S(2)}, u32[]{:S(2)}) collective-permute-start(f32[32,512]{1,0:T(8,128)S(1)} %get-tuple-element.134.refs_0_), channel_id=1, source_target_pairs={{0,96},{1,97},{2,98},{3,99},{4,100},{5,101},{6,102},{7,103},{8,104... | collective-permute-start | bytes 196616 | tf_op jit(solution)/shard_map/ppermute | solution.py:31
  126.9 6.1 %collective-permute-start.40 = (f32[32,512]{1,0:T(8,128)S(1)}, f32[32,512]{1,0:T(8,128)S(1)}, u32[]{:S(2)}, u32[]{:S(2)}) collective-permute-start(f32[32,512]{1,0:T(8,128)S(1)} %get-tuple-element.134.refs_0_), channel_id=1, source_target_pairs={{0,64},{1,65},{2,66},{3,67},{4,68},{5,69},{6,70},{7,71},{8,72},{9,... | collective-permute-start | bytes 196616 | tf_op jit(solution)/shard_map/ppermute | solution.py:31
  127.5 5.5 %collective-permute-start.39 = (f32[32,512]{1,0:T(8,128)S(1)}, f32[32,512]{1,0:T(8,128)S(1)}, u32[]{:S(2)}, u32[]{:S(2)}) collective-permute-start(f32[32,512]{1,0:T(8,128)S(1)} %get-tuple-element.134.refs_0_), channel_id=1, source_target_pairs={{0,32},{1,33},{2,34},{3,35},{4,36},{5,37},{6,38},{7,39},{8,40},{9,... | collective-permute-start | bytes 196616 | tf_op jit(solution)/shard_map/ppermute | solution.py:31
  133.1 2.0 %collective-permute-start.43 = (f32[32,512]{1,0:T(8,128)S(1)}, f32[32,512]{1,0:T(8,128)S(1)}, u32[]{:S(2)}, u32[]{:S(2)}) collective-permute-start(f32[32,512]{1,0:T(8,128)S(1)} %collective-permute-done.39.refs_0_), channel_id=1, source_target_pairs={{0,4},{4,0},{8,12},{12,8},{16,20},{20,16},{24,28},{28,24},{32,36},... | collective-permute-start | bytes 196616 | tf_op jit(solution)/shard_map/ppermute | solution.py:385
  134.1 1.3 collective-permute-start.44
  134.2 1.3 collective-permute-start.45

commit v4 on v3

--- a/solution.py
+++ b/solution.py
@@ -46,6 +46,7 @@
 SCALARS = pl.BlockSpec(memory_space=pltpu.SMEM)
 WHOLE = pl.BlockSpec(memory_space=pltpu.VMEM)
 HBM = pl.BlockSpec(memory_space=pl.ANY)
+SMALL = pl.CostEstimate(flops=1000, bytes_accessed=1000, transcendentals=0)
 
 
 def half_of_memory(grad, error, which):
@@ -81,13 +82,14 @@
     )(which, grad, error)
 
 
-def call(body, name, out_shape, place, *arrays, scratch=()):
+def call(body, name, out_shape, place, *arrays, scratch=(), cost=None):
     return pl.pallas_call(
         body,
         in_specs=[SCALARS] + [WHOLE] * len(arrays),
         out_specs=jax.tree.map(lambda s: WHOLE, out_shape),
         out_shape=out_shape,
         scratch_shapes=scratch,
+        cost_estimate=cost,
         compiler_params=params(),
         name=name,
     )(place, *arrays)
@@ -148,6 +150,22 @@
     return call(body, "early_left", shapes, place, warm_t, *pairs, scratch=scratch)
 
 
+def stack_early(place, parts, after):
+    def body(place_ref, a_ref, b_ref, c_ref, d_ref, after_ref, o_ref):
+        for i, ref in enumerate((a_ref, b_ref, c_ref, d_ref)):
+            o_ref[i * RANK : (i + 1) * RANK, :] = ref[...]
+
+    return pl.pallas_call(
+        body,
+        in_specs=[SCALARS] + [WHOLE] * 4 + [HBM],
+        out_specs=WHOLE,
+        out_shape=jax.ShapeDtypeStruct((4 * RANK, ROWS_OWN // 2), F32),
+        cost_estimate=SMALL,
+        compiler_params=params(),
+        name="stack_early",
+    )(place, *parts, after)
+
+
 def assemble_left(place, own, oth):
     def body(place_ref, own_ref, oth_ref, o_ref, sum_ref):
         core, half = place_ref[2], ROWS_OWN // 2
@@ -161,7 +179,7 @@
                 o_ref[:, i * PIECE : (i + 1) * PIECE] = sum_ref[:, cut(4 * y + (place_ref[1] ^ x), PIECE)]
 
     shape = jax.ShapeDtypeStruct((RANK, ROWS), F32)
-    return call(body, "assemble_left", shape, place, own, oth, scratch=[pltpu.VMEM((RANK, ROWS), F32)])
+    return call(body, "assemble_left", shape, place, own, oth, scratch=[pltpu.VMEM((RANK, ROWS), F32)], cost=SMALL)
 
 
 def thirds(x):
@@ -239,31 +257,27 @@
 HALVES = [jax.ShapeDtypeStruct((RANK, MID), F32)] * 2
 
 
-def second_left(place, left, inverse, m):
-    def body(place_ref, left_ref, inv_ref, *refs):
-        m_refs, (own_ref, oth_ref) = refs[:4], refs[4:]
-        ortho = dot(inv_ref[...], left_ref[...], ((1,), (0,)), HIGHEST).astype(BF)
-        right = times_m(reorder(ortho, place_ref), m_refs) * (1.0 / N_DP)
-        store_halves(place_ref, times_m_t(right.astype(BF), m_refs), own_ref, oth_ref)
-
-    return call(body, "second_left", HALVES, place, left, inverse, *m)
+def from_left(place_ref, left, m_refs, own_ref, oth_ref):
+    right = add_thirds(times_m(thirds(reorder(left, place_ref)), m_refs))
+    store_halves(place_ref, add_thirds(times_m_t(thirds(right), m_refs)), own_ref, oth_ref)
+
+
+def second_left(place, left, m):
+    def body(place_ref, left_ref, m0, m1, m2, m3, own_ref, oth_ref):
+        from_left(place_ref, left_ref[...], (m0, m1, m2, m3), own_ref, oth_ref)
+
+    return call(body, "second_left", HALVES, place, left, *m)
 
 
 def next_left(place, own, oth, inverse, m):
-    def body(place_ref, own_in, oth_in, *refs):
+    def body(place_ref, own_in, oth_in, inv_ref, m0, m1, m2, m3, left_ref, own_ref, oth_ref):
         left = load_halves(place_ref, own_in, oth_in)
-        if inverse is not None:
-            left = dot(refs[0][...], left, ((1,), (0,)), HIGHEST) * (1.0 / N_DP)
-            refs = refs[1:]
-        m_refs, (left_ref, own_ref, oth_ref) = refs[:4], refs[4:]
+        left = dot(inv_ref[...], left, ((1,), (0,)), HIGHEST) * (1.0 / N_DP)
         left_ref[...] = left
-        right = add_thirds(times_m(thirds(reorder(left, place_ref)), m_refs))
-        following = add_thirds(times_m_t(thirds(right), m_refs))
-        store_halves(place_ref, following, own_ref, oth_ref)
+        from_left(place_ref, left, (m0, m1, m2, m3), own_ref, oth_ref)
 
     shapes = [jax.ShapeDtypeStruct((RANK, ROWS), F32)] + HALVES
-    extra = [] if inverse is None else [inverse]
-    return call(body, "next_left", shapes, place, own, oth, *extra, *m)
+    return call(body, "next_left", shapes, place, own, oth, inverse, *m)
 
 
 def inverse_of(place, left):
@@ -271,21 +285,22 @@
         left = left_ref[...]
         o_ref[...] = inverse_factor(dot(left, left, ((1,), (1,)), HIGHEST))
 
-    return call(body, "inverse_of", jax.ShapeDtypeStruct((RANK, RANK), F32), place, left)
+    return call(body, "inverse_of", jax.ShapeDtypeStruct((RANK, RANK), F32), place, left, cost=SMALL)
 
 
 def last_right(place, own, oth, inverse, m):
-    def body(place_ref, own_in, oth_in, inv_ref, m0, m1, m2, m3, ortho_ref, right_ref):
+    def body(place_ref, own_in, oth_in, inv_ref, m0, m1, m2, m3, right_ref, left_ref, out_ref):
         left = load_halves(place_ref, own_in, oth_in)
         left = dot(inv_ref[...], left, ((1,), (0,)), HIGHEST) * (1.0 / N_DP)
-        gram = dot(left, left, ((1,), (1,)), HIGHEST)
-        ortho = dot(inverse_factor(gram), left, ((1,), (0,)), HIGHEST).astype(BF)
+        raw = add_thirds(times_m(thirds(reorder(left, place_ref)), (m0, m1, m2, m3)))
+        inverse = inverse_factor(dot(left, left, ((1,), (1,)), HIGHEST))
+        right_ref[...] = dot(inverse, raw, ((1,), (0,)), HIGHEST) * (1.0 / N_DP)
         for k in range(4):
-            ortho_ref[:, cut(place_ref[1] ^ k, PIECE)] = ortho[:, k * PIECE : (k + 1) * PIECE]
-        right_ref[...] = times_m(reorder(ortho, place_ref), (m0, m1, m2, m3)) * (1.0 / N_DP)
-
-    shapes = [jax.ShapeDtypeStruct((RANK, ROWS_OWN), BF), jax.ShapeDtypeStruct((RANK, COLS), F32)]
-    return call(body, "last_right", shapes, place, own, oth, inverse, *m)
+            left_ref[:, cut(place_ref[1] ^ k, PIECE)] = left[:, k * PIECE : (k + 1) * PIECE]
+        out_ref[...] = inverse
+
+    shapes = [(RANK, COLS), (RANK, ROWS_OWN), (RANK, RANK)]
+    return call(body, "last_right", [jax.ShapeDtypeStruct(s, F32) for s in shapes], place, own, oth, inverse, *m)
 
 
 def sum_over_group(own, oth, beside=None):
@@ -298,12 +313,13 @@
     return own, lax.ppermute(own, "dp", CORE), beside
 
 
-def columns_of(place, ortho):
-    def body(place_ref, o_ref, out_ref):
-        wide = jnp.concatenate([o_ref[...].astype(F32)] * 3 + [jnp.zeros((RANK, ROWS_OWN), F32)], axis=0)
+def columns_of(place, left, inverse):
+    def body(place_ref, left_ref, inv_ref, out_ref):
+        ortho = dot(inv_ref[...], left_ref[...], ((1,), (0,)), HIGHEST)
+        wide = jnp.concatenate([ortho] * 3 + [jnp.zeros((RANK, ROWS_OWN), F32)], axis=0)
         out_ref[...] = wide.T.astype(BF)
 
-    return call(body, "columns_of", jax.ShapeDtypeStruct((ROWS_OWN, 4 * RANK), BF), place, ortho)
+    return call(body, "columns_of", jax.ShapeDtypeStruct((ROWS_OWN, 4 * RANK), BF), place, left, inverse)
 
 
 def finish(place, ortho, rights, mine, other, outs, name):
@@ -360,24 +376,25 @@
     pairs = pair_sum(place, mine, received)
     early, passed = early_left(place, warm_right.T, pairs)
     early = early + lax.ppermute(passed, "dp", CORE)
-    parts, early = lax.optimization_barrier((exchange(pairs, "z", "x"), spread(early, "x", "x")))
-    early = (early[0] + early[1]) + (early[2] + early[3])
-    parts = exchange(first_sum(place, parts), "x", "z")
-    parts, early = lax.optimization_barrier((parts, spread(early, "y", "y")))
-    m, early = lax.optimization_barrier((spread(second_sum(place, parts), "x", "y"), early))
-    early = spread(jnp.concatenate(early, axis=0), "z", "z")
+    parts, early = lax.optimization_barrier((exchange(pairs, "z", "x"), spread(early, "y", "y")))
+    rows = first_sum(place, parts)
+    early = spread(stack_early(place, early, rows[0]), "z", "x")
+    parts, early = lax.optimization_barrier((exchange(rows, "x", "z"), early))
+    piece = second_sum(place, parts)
+    early = spread((early[0] + early[1]) + (early[2] + early[3]), "x", "z")
+    m = jnp.concatenate(spread(piece, "x", "y"), axis=0)
     early = (early[0] + early[1]) + (early[2] + early[3])
     left = assemble_left(place, early, lax.ppermute(early, "dp", CORE))
-    m = spread(jnp.concatenate(m, axis=0), "y", "x")
-    m, left, inverse = lax.optimization_barrier((m, left, inverse_of(place, left)))
-
-    own, oth, inverse = sum_over_group(*second_left(place, left, inverse, m))
+    m = spread(m, "y", "x")
+    m, left = lax.optimization_barrier((m, left))
+
+    own, oth, inverse = sum_over_group(*second_left(place, left, m), inverse_of(place, left))
     for step in range(ITERS - 2):
         left, own, oth = next_left(place, own, oth, inverse, m)
         own, oth, inverse = sum_over_group(own, oth, inverse_of(place, left))
-    ortho, right = last_right(place, own, oth, inverse, m)
-
-    ortho = columns_of(place, ortho)
+    right, left, inverse = last_right(place, own, oth, inverse, m)
+
+    ortho = columns_of(place, left, inverse)
     near = {(0, 0): right, (0, 1): lax.ppermute(right, "dp", CORE)}
     outs = finish(place, ortho, near, mine, other, [], "finish_near")
     rights, outs = lax.optimization_barrier((spread(right, "z", "z"), outs))

time: 142 us -> 138 us (0.972)
  waiting for transfers between devices: 49.1 us -> 42.1 us
  starting transfers between devices: 57.1 us -> 60.2 us
    ppermute x33, waiting for transfers between devices: 38.9 us -> 32 us  [along(): return lax.ppermute(array, ('dp', 'owner'), pairs)]
    ppermute x1, starting transfers between devices: 4.07 us -> 9.85 us  [per_device(): left = assemble_left(place, early, lax.ppermute(early, 'dp', CORE))]
    ppermute x3, starting transfers between devices: 3.64 us -> 1.32 us  [sum_over_group(): own = own + lax.ppermute(oth, 'dp', CORE)]
  transfers between devices with their start and end apart: 46 -> 46, of which waited for: 26 -> 29; matrix products, arithmetic and copies ran while one was open for 0% -> 0% of each run, Pallas kernels for 10% -> 10%
where the time goes in v4:
time: 138 us
  starting transfers between devices  60.2 us (44%)
  waiting for transfers between devices  42.1 us (31%)
  Pallas kernels  34.1 us (25%)
    ppermute x33, starting transfers between devices, along(): return lax.ppermute(array, ('dp', 'owner'), pairs)  38.5 us
    ppermute x33, waiting for transfers between devices, along(): return lax.ppermute(array, ('dp', 'owner'), pairs)  32 us
    pallas_call x13, Pallas kernels, call(): pl.pallas_call(body, in_specs=[SCALARS] + [WHOLE] * len(arrays), out_spec...  20.3 us
    ppermute x1, starting transfers between devices, per_device(): left = assemble_left(place, early, lax.ppermute(early, 'dp', CORE))  9.85 us
    pallas_call x2, Pallas kernels, finish(): pl.pallas_call(body, in_specs=[SCALARS] + [WHOLE] * (count + 3) + [HBM] *...  8.54 us
    ppermute x3, starting transfers between devices, sum_over_group(): return (own, lax.ppermute(own, 'dp', CORE), beside)  4.81 us
    pallas_call x2, Pallas kernels, half_of_memory(): pl.pallas_call(body, in_specs=[SCALARS, HBM, HBM], out_specs=WHOLE, scrat...  4.67 us
    ppermute x3, waiting for transfers between devices, sum_over_group(): own = own + lax.ppermute(oth, 'dp', CORE)  2.96 us
  transfers between devices with their start and end apart: 46, of which 29 were waited for; matrix products, arithmetic and copies ran while one was open for 0% of the time, Pallas kernels for 10%

profile of v4, /device:TPU:1, one launch (start us, length us, event | category | flops | bytes accessed | tf_op | source)
XLA Modules:
  0.0 137.8 jit_solution(15858348604356097496)
XLA Ops:
  0.6 2.3 %half_of_memory.3.refs_3_.refs_7_ = bf16[512,2048]{1,0:T(8,128)(2,1)S(1)} custom-call(s32[1]{0:T(128)} %bitcast.5.which_ref, bf16[512,4096]{1,0:T(8,128)(2,1)} %bitcast.10, bf16[512,4096]{1,0:T(8,128)(2,1)} %bitcast.12), custom_call_target="tpu_custom_call" | custom-call | tf_op jit(solution)/shard_map/half_of_memory/pallas_call | solution.py:74
  3.0 1.5 %collective-permute-start = (bf16[512,2048]{1,0:T(8,128)(2,1)S(1)}, bf16[512,2048]{1,0:T(8,128)(2,1)}, u32[]{:S(2)}, u32[]{:S(2)}) collective-permute-start(bf16[512,2048]{1,0:T(8,128)(2,1)S(1)} %half_of_memory.3.refs_3_.refs_7_), channel_id=1, source_target_pairs={{0,4},{4,0},{8,12},{12,8},{16,20},{20,16},{24,28},{28,24},{32,36},... | collective-permute-start | bytes 6291464 | tf_op jit(solution)/shard_map/ppermute | solution.py:374
  4.5 2.3 %half_of_memory.2.a_ref.refs_2_.refs_6_ = bf16[512,2048]{1,0:T(8,128)(2,1)S(1)} custom-call(s32[1]{0:T(128)} %bitcast.2.which_ref, bf16[512,4096]{1,0:T(8,128)(2,1)} %bitcast.11, bf16[512,4096]{1,0:T(8,128)(2,1)} %bitcast.13), custom_call_target="tpu_custom_call" | custom-call | tf_op jit(solution)/shard_map/half_of_memory/pallas_call | solution.py:74
  6.9 1.5 %collective-permute-done.b_ref = bf16[512,2048]{1,0:T(8,128)(2,1)} collective-permute-done((bf16[512,2048]{1,0:T(8,128)(2,1)S(1)}, bf16[512,2048]{1,0:T(8,128)(2,1)}, u32[]{:S(2)}, u32[]{:S(2)}) %collective-permute-start) | collective-permute-done | bytes 2097184 | tf_op jit(solution)/shard_map/ppermute | solution.py:374
  8.4 1.9 %pair_sum.1 = (bf16[4,128,512]{2,1,0:T(8,128)(2,1)S(1)}, bf16[4,128,512]{2,1,0:T(8,128)(2,1)S(1)}, bf16[4,128,512]{2,1,0:T(8,128)(2,1)S(1)}, bf16[4,128,512]{2,1,0:T(8,128)(2,1)S(1)}) custom-call(s32[3]{0:T(128)S(1)} %pad_add_fusion.place_ref, bf16[512,2048]{1,0:T(8,128)(2,1)S(1)} %half_of_memory.2.a_ref.refs_2_.refs_6_, ...), custom_call_target="tpu_custom_call" | custom-call | tf_op jit(solution)/shard_map/pair_sum/pallas_call | solution.py:86
  10.3 1.4 collective-permute-start.1
  11.7 2.5 %collective-permute-start.2 = (bf16[4,128,512]{2,1,0:T(8,128)(2,1)S(1)}, bf16[4,128,512]{2,1,0:T(8,128)(2,1)S(1)}, u32[]{:S(2)}, u32[]{:S(2)}) collective-permute-start(bf16[4,128,512]{2,1,0:T(8,128)(2,1)S(1)} %get-tuple-element.74.refs_2_), channel_id=1, source_target_pairs={{0,64},{1,65},{2,66},{3,67},{4,20},{5,21},{6,22},{7,23},{8,72},{9,... | collective-permute-start | bytes 1572872 | tf_op jit(solution)/shard_map/ppermute | solution.py:31
  14.2 1.4 early_left.1
  15.6 2.2 %collective-permute-start.4 = (f32[32,256]{1,0:T(8,128)S(1)}, f32[32,256]{1,0:T(8,128)S(1)}, u32[]{:S(2)}, u32[]{:S(2)}) collective-permute-start(f32[32,256]{1,0:T(8,128)S(1)} %get-tuple-element.77), channel_id=1, source_target_pairs={{0,4},{4,0},{8,12},{12,8},{16,20},{20,16},{24,28},{28,24},{32,36},... | collective-permute-start | bytes 98312 | tf_op jit(solution)/shard_map/ppermute | solution.py:378
  17.8 0.9 collective-permute-done.4
  18.7 2.7 %collective-permute-start.7 = (f32[32,256]{1,0:T(8,128)S(1)}, f32[32,256]{1,0:T(8,128)S(1)}, u32[]{:S(2)}, u32[]{:S(2)}) collective-permute-start(f32[32,256]{1,0:T(8,128)S(1)} %add.57.a_ref), channel_id=1, source_target_pairs={{0,3},{1,2},{2,1},{3,0},{4,7},{5,6},{6,5},{7,4},{8,11},{9,10},{10,... | collective-permute-start | bytes 98312 | tf_op jit(solution)/shard_map/ppermute | solution.py:31
  21.8 1.2 collective-permute-done.7.d_ref
  23.0 2.9 %collective-permute-done.6.c_ref = f32[32,256]{1,0:T(8,128)S(1)} collective-permute-done((f32[32,256]{1,0:T(8,128)S(1)}, f32[32,256]{1,0:T(8,128)S(1)}, u32[]{:S(2)}, u32[]{:S(2)}) %collective-permute-start.6) | collective-permute-done | bytes 32800 | tf_op jit(solution)/shard_map/ppermute | solution.py:31
  26.6 2.6 %collective-permute-done.3.refs_3_ = bf16[4,128,512]{2,1,0:T(8,128)(2,1)S(1)} collective-permute-done((bf16[4,128,512]{2,1,0:T(8,128)(2,1)S(1)}, bf16[4,128,512]{2,1,0:T(8,128)(2,1)S(1)}, u32[]{:S(2)}, u32[]{:S(2)}) %collective-permute-start.3) | collective-permute-done | bytes 524320 | tf_op jit(solution)/shard_map/ppermute | solution.py:31
  29.3 0.8 first_sum.1
  30.1 1.4 %collective-permute-start.8 = (bf16[128,512]{1,0:T(8,128)(2,1)S(1)}, bf16[128,512]{1,0:T(8,128)(2,1)S(1)}, u32[]{:S(2)}, u32[]{:S(2)}) collective-permute-start(bf16[128,512]{1,0:T(8,128)(2,1)S(1)} %get-tuple-element.83), channel_id=1, source_target_pairs={{0,8},{1,9},{2,10},{3,11},{4,36},{5,37},{6,38},{7,39},{8,0},{9,1},... | collective-permute-start | bytes 393224 | tf_op jit(solution)/shard_map/ppermute | solution.py:31
  31.5 3.3 %collective-permute-start.9 = (bf16[128,512]{1,0:T(8,128)(2,1)S(1)}, bf16[128,512]{1,0:T(8,128)(2,1)S(1)}, u32[]{:S(2)}, u32[]{:S(2)}) collective-permute-start(bf16[128,512]{1,0:T(8,128)(2,1)S(1)} %get-tuple-element.84), channel_id=1, source_target_pairs={{0,16},{1,17},{2,18},{3,19},{4,68},{5,69},{6,70},{7,71},{8,24},{9,... | collective-permute-start | bytes 393224 | tf_op jit(solution)/shard_map/ppermute | solution.py:31
  36.3 2.4 %collective-permute-start.11 = (f32[128,256]{1,0:T(8,128)S(1)}, f32[128,256]{1,0:T(8,128)S(1)}, u32[]{:S(2)}, u32[]{:S(2)}) collective-permute-start(f32[128,256]{1,0:T(8,128)S(1)} %stack_early.1), channel_id=1, source_target_pairs={{0,32},{1,33},{2,34},{3,35},{4,12},{5,13},{6,14},{7,15},{8,40},{9,... | collective-permute-start | bytes 393224 | tf_op jit(solution)/shard_map/ppermute | solution.py:31
  38.7 1.6 %collective-permute-done.10.d_ref = bf16[128,512]{1,0:T(8,128)(2,1)S(1)} collective-permute-done((bf16[128,512]{1,0:T(8,128)(2,1)S(1)}, bf16[128,512]{1,0:T(8,128)(2,1)S(1)}, u32[]{:S(2)}, u32[]{:S(2)}) %collective-permute-start.10) | collective-permute-done | bytes 131104 | tf_op jit(solution)/shard_map/ppermute | solution.py:31
  40.3 3.9 %collective-permute-done.13 = f32[128,256]{1,0:T(8,128)S(1)} collective-permute-done((f32[128,256]{1,0:T(8,128)S(1)}, f32[128,256]{1,0:T(8,128)S(1)}, u32[]{:S(2)}, u32[]{:S(2)}) %collective-permute-start.13) | collective-permute-done | bytes 131104 | tf_op jit(solution)/shard_map/ppermute | solution.py:31
  44.8 2.8 %collective-permute-start.16 = (bf16[128,512]{1,0:T(8,128)(2,1)S(1)}, bf16[128,512]{1,0:T(8,128)(2,1)S(1)}, u32[]{:S(2)}, u32[]{:S(2)}) collective-permute-start(bf16[128,512]{1,0:T(8,128)(2,1)S(1)} %second_sum.1), channel_id=1, source_target_pairs={{0,24},{1,25},{2,26},{3,27},{4,7},{5,6},{6,5},{7,4},{8,16},{9,17},... | collective-permute-start | bytes 393224 | tf_op jit(solution)/shard_map/ppermute | solution.py:31
  48.3 1.4 %collective-permute-start.22 = (f32[128,256]{1,0:T(8,128)S(1)}, f32[128,256]{1,0:T(8,128)S(1)}, u32[]{:S(2)}, u32[]{:S(2)}) collective-permute-start(f32[128,256]{1,0:T(8,128)S(1)} %add_add_fusion.4), channel_id=1, source_target_pairs={{0,24},{1,25},{2,26},{3,27},{4,100},{5,101},{6,102},{7,103},{8,16}... | collective-permute-start | bytes 393224 | tf_op jit(solution)/shard_map/ppermute | solution.py:31
  49.7 1.2 collective-permute-done.16
  50.9 2.0 %collective-permute-done.15 = bf16[128,512]{1,0:T(8,128)(2,1)S(1)} collective-permute-done((bf16[128,512]{1,0:T(8,128)(2,1)S(1)}, bf16[128,512]{1,0:T(8,128)(2,1)S(1)}, u32[]{:S(2)}, u32[]{:S(2)}) %collective-permute-start.15) | collective-permute-done | bytes 131104 | tf_op jit(solution)/shard_map/ppermute | solution.py:31
  53.9 2.4 %collective-permute-start.17 = (bf16[512,512]{1,0:T(8,128)(2,1)S(1)}, bf16[512,512]{1,0:T(8,128)(2,1)S(1)}, u32[]{:S(2)}, u32[]{:S(2)}) collective-permute-start(bf16[512,512]{1,0:T(8,128)(2,1)S(1)} %pad_maximum_fusion.m0), channel_id=1, source_target_pairs={{0,1},{1,0},{2,3},{3,2},{4,12},{5,13},{6,14},{7,15},{8,9},{9,8},{1... | collective-permute-start | bytes 1572872 | tf_op jit(solution)/shard_map/ppermute | solution.py:31
  56.6 1.6 %collective-permute-start.20 = (f32[128,256]{1,0:T(8,128)S(1)}, f32[128,256]{1,0:T(8,128)S(1)}, u32[]{:S(2)}, u32[]{:S(2)}) collective-permute-start(f32[128,256]{1,0:T(8,128)S(1)} %add_add_fusion.4), channel_id=1, source_target_pairs={{0,8},{1,9},{2,10},{3,11},{4,36},{5,37},{6,38},{7,39},{8,0},{9,1},... | collective-permute-start | bytes 393224 | tf_op jit(solution)/shard_map/ppermute | solution.py:31
  58.2 3.4 %collective-permute-done.21 = f32[128,256]{1,0:T(8,128)S(1)} collective-permute-done((f32[128,256]{1,0:T(8,128)S(1)}, f32[128,256]{1,0:T(8,128)S(1)}, u32[]{:S(2)}, u32[]{:S(2)}) %collective-permute-start.21) | collective-permute-done | bytes 131104 | tf_op jit(solution)/shard_map/ppermute | solution.py:31
  62.3 9.9 %collective-permute-start.23 = (f32[128,256]{1,0:T(8,128)S(1)}, f32[128,256]{1,0:T(8,128)S(1)}, u32[]{:S(2)}, u32[]{:S(2)}) collective-permute-start(f32[128,256]{1,0:T(8,128)S(1)} %add_add_fusion.3.own_ref), channel_id=1, source_target_pairs={{0,4},{4,0},{8,12},{12,8},{16,20},{20,16},{24,28},{28,24},{32,36},... | collective-permute-start | bytes 393224 | tf_op jit(solution)/shard_map/ppermute | solution.py:387
  72.2 1.0 collective-permute-done.23.oth_ref
  73.8 1.7 %second_left.1 = (f32[32,1024]{1,0:T(8,128)S(1)}, f32[32,1024]{1,0:T(8,128)S(1)}) custom-call(s32[3]{0:T(128)S(1)} %pad_add_fusion.place_ref, f32[32,2048]{1,0:T(8,128)S(1)} %assemble_left.1.left_ref, bf16[512,512]{1,0:T(8,128)(2,1)S(1)} %pad_maximum_fusion.m0, bf16[512,512]{1,0:T(8,128)(2,1)S(1)} %collective-permute-done.17.m1, ...), custom_call_target="tpu_custom_call" | custom-call | tf_op jit(solution)/shard_map/second_left/pallas_call | solution.py:86
  75.9 1.0 collective-permute-done.24
  76.9 0.9 collective-permute-start.27
  77.9 1.1 collective-permute-start.26
  79.0 1.2 collective-permute-start.25
  80.3 1.9 %inverse_of.3.inv_ref = f32[32,32]{1,0:T(8,128)S(1)} custom-call(s32[3]{0:T(128)S(1)} %pad_add_fusion.place_ref, f32[32,2048]{1,0:T(8,128)S(1)} %assemble_left.1.left_ref), custom_call_target="tpu_custom_call" | custom-call | flops 1000 | bytes 1000 | tf_op jit(solution)/shard_map/inverse_of/pallas_call | solution.py:86
  82.2 3.3 %collective-permute-done.27 = f32[32,1024]{1,0:T(8,128)S(1)} collective-permute-done((f32[32,1024]{1,0:T(8,128)S(1)}, f32[32,1024]{1,0:T(8,128)S(1)}, u32[]{:S(2)}, u32[]{:S(2)}) %collective-permute-start.27) | collective-permute-done | bytes 131104 | tf_op jit(solution)/shard_map/ppermute | solution.py:31
  86.2 1.7 %collective-permute-start.28 = (f32[32,1024]{1,0:T(8,128)S(1)}, f32[32,1024]{1,0:T(8,128)S(1)}, u32[]{:S(2)}, u32[]{:S(2)}) collective-permute-start(f32[32,1024]{1,0:T(8,128)S(1)} %add_add_fusion.2.own_in), channel_id=1, source_target_pairs={{0,4},{4,0},{8,12},{12,8},{16,20},{20,16},{24,28},{28,24},{32,36},... | collective-permute-start | bytes 393224 | tf_op jit(solution)/shard_map/ppermute | solution.py:313
  87.9 1.0 collective-permute-done.28.oth_in
  88.9 2.0 %next_left.2 = (f32[32,2048]{1,0:T(8,128)S(1)}, f32[32,1024]{1,0:T(8,128)S(1)}, f32[32,1024]{1,0:T(8,128)S(1)}) custom-call(s32[3]{0:T(128)S(1)} %pad_add_fusion.place_ref, f32[32,1024]{1,0:T(8,128)S(1)} %add_add_fusion.2.own_in, f32[32,1024]{1,0:T(8,128)S(1)} %collective-permute-done.28.oth_in, f32[32,32]{1,0:T(8,128)S(1)} %inverse_of.3.inv_ref, ...), custom_call_target="tpu_custom_call" | custom-call | tf_op jit(solution)/shard_map/next_left/pallas_call | solution.py:86
  91.3 1.0 collective-permute-done.29
  92.3 0.9 collective-permute-start.32
  93.2 1.1 collective-permute-start.31
  94.3 1.3 collective-permute-start.30
  95.6 1.9 %inverse_of.4.inv_ref = f32[32,32]{1,0:T(8,128)S(1)} custom-call(s32[3]{0:T(128)S(1)} %pad_add_fusion.place_ref, f32[32,2048]{1,0:T(8,128)S(1)} %get-tuple-element.112.left_ref), custom_call_target="tpu_custom_call" | custom-call | flops 1000 | bytes 1000 | tf_op jit(solution)/shard_map/inverse_of/pallas_call | solution.py:86
  97.6 3.3 %collective-permute-done.32 = f32[32,1024]{1,0:T(8,128)S(1)} collective-permute-done((f32[32,1024]{1,0:T(8,128)S(1)}, f32[32,1024]{1,0:T(8,128)S(1)}, u32[]{:S(2)}, u32[]{:S(2)}) %collective-permute-start.32) | collective-permute-done | bytes 131104 | tf_op jit(solution)/shard_map/ppermute | solution.py:31
  101.5 1.5 %collective-permute-start.33 = (f32[32,1024]{1,0:T(8,128)S(1)}, f32[32,1024]{1,0:T(8,128)S(1)}, u32[]{:S(2)}, u32[]{:S(2)}) collective-permute-start(f32[32,1024]{1,0:T(8,128)S(1)} %add_add_fusion.1.own_in), channel_id=1, source_target_pairs={{0,4},{4,0},{8,12},{12,8},{16,20},{20,16},{24,28},{28,24},{32,36},... | collective-permute-start | bytes 393224 | tf_op jit(solution)/shard_map/ppermute | solution.py:313
  103.1 1.0 collective-permute-done.33.oth_in
  104.1 2.0 %next_left.3 = (f32[32,2048]{1,0:T(8,128)S(1)}, f32[32,1024]{1,0:T(8,128)S(1)}, f32[32,1024]{1,0:T(8,128)S(1)}) custom-call(s32[3]{0:T(128)S(1)} %pad_add_fusion.place_ref, f32[32,1024]{1,0:T(8,128)S(1)} %add_add_fusion.1.own_in, f32[32,1024]{1,0:T(8,128)S(1)} %collective-permute-done.33.oth_in, f32[32,32]{1,0:T(8,128)S(1)} %inverse_of.4.inv_ref, ...), custom_call_target="tpu_custom_call" | custom-call | tf_op jit(solution)/shard_map/next_left/pallas_call | solution.py:86
  106.5 1.0 collective-permute-done.34
  107.5 0.9 collective-permute-start.37
  108.4 1.1 collective-permute-start.36
  109.5 1.3 collective-permute-start.35
  110.8 1.9 %inverse_of.5.inv_ref = f32[32,32]{1,0:T(8,128)S(1)} custom-call(s32[3]{0:T(128)S(1)} %pad_add_fusion.place_ref, f32[32,2048]{1,0:T(8,128)S(1)} %get-tuple-element.120.left_ref), custom_call_target="tpu_custom_call" | custom-call | flops 1000 | bytes 1000 | tf_op jit(solution)/shard_map/inverse_of/pallas_call | solution.py:86
  112.8 3.3 %collective-permute-done.37 = f32[32,1024]{1,0:T(8,128)S(1)} collective-permute-done((f32[32,1024]{1,0:T(8,128)S(1)}, f32[32,1024]{1,0:T(8,128)S(1)}, u32[]{:S(2)}, u32[]{:S(2)}) %collective-permute-start.37) | collective-permute-done | bytes 131104 | tf_op jit(solution)/shard_map/ppermute | solution.py:31
  116.7 1.5 %collective-permute-start.38 = (f32[32,1024]{1,0:T(8,128)S(1)}, f32[32,1024]{1,0:T(8,128)S(1)}, u32[]{:S(2)}, u32[]{:S(2)}) collective-permute-start(f32[32,1024]{1,0:T(8,128)S(1)} %add_add_fusion.own_in), channel_id=1, source_target_pairs={{0,4},{4,0},{8,12},{12,8},{16,20},{20,16},{24,28},{28,24},{32,36},... | collective-permute-start | bytes 393224 | tf_op jit(solution)/shard_map/ppermute | solution.py:313
  118.3 1.0 collective-permute-done.38.oth_in
  119.3 2.8 %last_right.1 = (f32[32,512]{1,0:T(8,128)S(1)}, f32[32,512]{1,0:T(8,128)S(1)}, f32[32,32]{1,0:T(8,128)S(1)}) custom-call(s32[3]{0:T(128)S(1)} %pad_add_fusion.place_ref, f32[32,1024]{1,0:T(8,128)S(1)} %add_add_fusion.own_in, f32[32,1024]{1,0:T(8,128)S(1)} %collective-permute-done.38.oth_in, f32[32,32]{1,0:T(8,128)S(1)} %inverse_of.5.inv_ref, ...), custom_call_target="tpu_custom_call" | custom-call | tf_op jit(solution)/shard_map/last_right/pallas_call | solution.py:86
  122.5 0.8 collective-permute-start.41
  123.3 1.0 collective-permute-start.40
  124.4 1.4 %collective-permute-start.39 = (f32[32,512]{1,0:T(8,128)S(1)}, f32[32,512]{1,0:T(8,128)S(1)}, u32[]{:S(2)}, u32[]{:S(2)}) collective-permute-start(f32[32,512]{1,0:T(8,128)S(1)} %get-tuple-element.128.refs_0_), channel_id=1, source_target_pairs={{0,32},{1,33},{2,34},{3,35},{4,36},{5,37},{6,38},{7,39},{8,40},{9,... | collective-permute-start | bytes 196616 | tf_op jit(solution)/shard_map/ppermute | solution.py:31
  125.7 0.8 columns_of.1.o_ref
  126.6 2.9 %finish_near.1 = (f32[512,4096]{1,0:T(8,128)}, f32[512,4096]{1,0:T(8,128)}, f32[32,4096]{1,0:T(8,128)}) custom-call(s32[3]{0:T(128)S(1)} %pad_add_fusion.place_ref, bf16[512,128]{1,0:T(8,128)(2,1)S(1)} %columns_of.1.o_ref, f32[32,512]{1,0:T(8,128)S(1)} %get-tuple-element.128.refs_0_, f32[32,512]{1,0:T(8,128)S(1)} %collective-permute-done.42.refs_1_, ...), custom_call_target="tpu_custom_call" | custom-call | tf_op jit(solution)/shard_map/finish_near/pallas_call | solution.py:352
  129.5 1.1 collective-permute-start.43
  132.0 5.6 %finish_far.1 = (f32[512,4096]{1,0:T(8,128)}, f32[512,4096]{1,0:T(8,128)}, f32[32,4096]{1,0:T(8,128)}) custom-call(s32[3]{0:T(128)S(1)} %pad_add_fusion.place_ref, bf16[512,128]{1,0:T(8,128)(2,1)S(1)} %columns_of.1.o_ref, f32[32,512]{1,0:T(8,128)S(1)} %collective-permute-done.39.refs_0_, ...), custom_call_target="tpu_custom_call", output_to_operand_aliasing={{0}: (10, {}), {1}: (11, {}), {2}: (12, {})} | custom-call | tf_op jit(solution)/shard_map/finish_far/pallas_call | solution.py:352
  (59 shorter events, 11.7 us)
Async XLA Ops:
  3.0 5.4 %collective-permute-start = (bf16[512,2048]{1,0:T(8,128)(2,1)S(1)}, bf16[512,2048]{1,0:T(8,128)(2,1)}, u32[]{:S(2)}, u32[]{:S(2)}) collective-permute-start(bf16[512,2048]{1,0:T(8,128)(2,1)S(1)} %half_of_memory.3.refs_3_.refs_7_), channel_id=1, source_target_pairs={{0,4},{4,0},{8,12},{12,8},{16,20},{20,16},{24,28},{28,24},{32,36},... | collective-permute-start | bytes 6291464 | tf_op jit(solution)/shard_map/ppermute | solution.py:374
  6.8 7.4 %copy-start = (f32[4096,32]{0,1:T(8,128)S(1)}, f32[4096,32]{0,1:T(8,128)}, u32[]{:S(2)}) copy-start(f32[4096,32]{0,1:T(8,128)} %param.5) | copy-start | bytes 1572868
  10.3 15.8 %collective-permute-start.1 = (bf16[4,128,512]{2,1,0:T(8,128)(2,1)S(1)}, bf16[4,128,512]{2,1,0:T(8,128)(2,1)S(1)}, u32[]{:S(2)}, u32[]{:S(2)}) collective-permute-start(bf16[4,128,512]{2,1,0:T(8,128)(2,1)S(1)} %get-tuple-element.73.refs_1_), channel_id=1, source_target_pairs={{0,32},{1,33},{2,34},{3,35},{4,12},{5,13},{6,14},{7,15},{8,40},{9,... | collective-permute-start | bytes 1572872 | tf_op jit(solution)/shard_map/ppermute | solution.py:31
  11.7 15.0 %collective-permute-start.2 = (bf16[4,128,512]{2,1,0:T(8,128)(2,1)S(1)}, bf16[4,128,512]{2,1,0:T(8,128)(2,1)S(1)}, u32[]{:S(2)}, u32[]{:S(2)}) collective-permute-start(bf16[4,128,512]{2,1,0:T(8,128)(2,1)S(1)} %get-tuple-element.74.refs_2_), channel_id=1, source_target_pairs={{0,64},{1,65},{2,66},{3,67},{4,20},{5,21},{6,22},{7,23},{8,72},{9,... | collective-permute-start | bytes 1572872 | tf_op jit(solution)/shard_map/ppermute | solution.py:31
  14.1 15.2 %collective-permute-start.3 = (bf16[4,128,512]{2,1,0:T(8,128)(2,1)S(1)}, bf16[4,128,512]{2,1,0:T(8,128)(2,1)S(1)}, u32[]{:S(2)}, u32[]{:S(2)}) collective-permute-start(bf16[4,128,512]{2,1,0:T(8,128)(2,1)S(1)} %get-tuple-element.75.refs_3_), channel_id=1, source_target_pairs={{0,96},{1,97},{2,98},{3,99},{4,28},{5,29},{6,30},{7,31},{8,104},{9... | collective-permute-start | bytes 1572872 | tf_op jit(solution)/shard_map/ppermute | solution.py:31
  15.6 3.1 %collective-permute-start.4 = (f32[32,256]{1,0:T(8,128)S(1)}, f32[32,256]{1,0:T(8,128)S(1)}, u32[]{:S(2)}, u32[]{:S(2)}) collective-permute-start(f32[32,256]{1,0:T(8,128)S(1)} %get-tuple-element.77), channel_id=1, source_target_pairs={{0,4},{4,0},{8,12},{12,8},{16,20},{20,16},{24,28},{28,24},{32,36},... | collective-permute-start | bytes 98312 | tf_op jit(solution)/shard_map/ppermute | solution.py:378
  18.7 4.3 %collective-permute-start.7 = (f32[32,256]{1,0:T(8,128)S(1)}, f32[32,256]{1,0:T(8,128)S(1)}, u32[]{:S(2)}, u32[]{:S(2)}) collective-permute-start(f32[32,256]{1,0:T(8,128)S(1)} %add.57.a_ref), channel_id=1, source_target_pairs={{0,3},{1,2},{2,1},{3,0},{4,7},{5,6},{6,5},{7,4},{8,11},{9,10},{10,... | collective-permute-start | bytes 98312 | tf_op jit(solution)/shard_map/ppermute | solution.py:31
  21.4 4.6 %collective-permute-start.6 = (f32[32,256]{1,0:T(8,128)S(1)}, f32[32,256]{1,0:T(8,128)S(1)}, u32[]{:S(2)}, u32[]{:S(2)}) collective-permute-start(f32[32,256]{1,0:T(8,128)S(1)} %add.57.a_ref), channel_id=1, source_target_pairs={{0,2},{1,3},{2,0},{3,1},{4,6},{5,7},{6,4},{7,5},{8,10},{9,11},{10,... | collective-permute-start | bytes 98312 | tf_op jit(solution)/shard_map/ppermute | solution.py:31
  23.0 3.1 %collective-permute-start.5 = (f32[32,256]{1,0:T(8,128)S(1)}, f32[32,256]{1,0:T(8,128)S(1)}, u32[]{:S(2)}, u32[]{:S(2)}) collective-permute-start(f32[32,256]{1,0:T(8,128)S(1)} %add.57.a_ref), channel_id=1, source_target_pairs={{0,1},{1,0},{2,3},{3,2},{4,5},{5,4},{6,7},{7,6},{8,9},{9,8},{10,11... | collective-permute-start | bytes 98312 | tf_op jit(solution)/shard_map/ppermute | solution.py:31
  30.1 6.2 %collective-permute-start.8 = (bf16[128,512]{1,0:T(8,128)(2,1)S(1)}, bf16[128,512]{1,0:T(8,128)(2,1)S(1)}, u32[]{:S(2)}, u32[]{:S(2)}) collective-permute-start(bf16[128,512]{1,0:T(8,128)(2,1)S(1)} %get-tuple-element.83), channel_id=1, source_target_pairs={{0,8},{1,9},{2,10},{3,11},{4,36},{5,37},{6,38},{7,39},{8,0},{9,1},... | collective-permute-start | bytes 393224 | tf_op jit(solution)/shard_map/ppermute | solution.py:31
  31.5 7.2 %collective-permute-start.9 = (bf16[128,512]{1,0:T(8,128)(2,1)S(1)}, bf16[128,512]{1,0:T(8,128)(2,1)S(1)}, u32[]{:S(2)}, u32[]{:S(2)}) collective-permute-start(bf16[128,512]{1,0:T(8,128)(2,1)S(1)} %get-tuple-element.84), channel_id=1, source_target_pairs={{0,16},{1,17},{2,18},{3,19},{4,68},{5,69},{6,70},{7,71},{8,24},{9,... | collective-permute-start | bytes 393224 | tf_op jit(solution)/shard_map/ppermute | solution.py:31
  34.8 5.5 %collective-permute-start.10 = (bf16[128,512]{1,0:T(8,128)(2,1)S(1)}, bf16[128,512]{1,0:T(8,128)(2,1)S(1)}, u32[]{:S(2)}, u32[]{:S(2)}) collective-permute-start(bf16[128,512]{1,0:T(8,128)(2,1)S(1)} %get-tuple-element.85), channel_id=1, source_target_pairs={{0,24},{1,25},{2,26},{3,27},{4,100},{5,101},{6,102},{7,103},{8,16}... | collective-permute-start | bytes 393224 | tf_op jit(solution)/shard_map/ppermute | solution.py:31
  35.4 8.8 %collective-permute-start.13 = (f32[128,256]{1,0:T(8,128)S(1)}, f32[128,256]{1,0:T(8,128)S(1)}, u32[]{:S(2)}, u32[]{:S(2)}) collective-permute-start(f32[128,256]{1,0:T(8,128)S(1)} %stack_early.1), channel_id=1, source_target_pairs={{0,96},{1,97},{2,98},{3,99},{4,28},{5,29},{6,30},{7,31},{8,104},{9... | collective-permute-start | bytes 393224 | tf_op jit(solution)/shard_map/ppermute | solution.py:31
  35.9 8.2 %collective-permute-start.12 = (f32[128,256]{1,0:T(8,128)S(1)}, f32[128,256]{1,0:T(8,128)S(1)}, u32[]{:S(2)}, u32[]{:S(2)}) collective-permute-start(f32[128,256]{1,0:T(8,128)S(1)} %stack_early.1), channel_id=1, source_target_pairs={{0,64},{1,65},{2,66},{3,67},{4,20},{5,21},{6,22},{7,23},{8,72},{9,... | collective-permute-start | bytes 393224 | tf_op jit(solution)/shard_map/ppermute | solution.py:31
  36.3 7.9 %collective-permute-start.11 = (f32[128,256]{1,0:T(8,128)S(1)}, f32[128,256]{1,0:T(8,128)S(1)}, u32[]{:S(2)}, u32[]{:S(2)}) collective-permute-start(f32[128,256]{1,0:T(8,128)S(1)} %stack_early.1), channel_id=1, source_target_pairs={{0,32},{1,33},{2,34},{3,35},{4,12},{5,13},{6,14},{7,15},{8,40},{9,... | collective-permute-start | bytes 393224 | tf_op jit(solution)/shard_map/ppermute | solution.py:31
  44.8 6.1 %collective-permute-start.16 = (bf16[128,512]{1,0:T(8,128)(2,1)S(1)}, bf16[128,512]{1,0:T(8,128)(2,1)S(1)}, u32[]{:S(2)}, u32[]{:S(2)}) collective-permute-start(bf16[128,512]{1,0:T(8,128)(2,1)S(1)} %second_sum.1), channel_id=1, source_target_pairs={{0,24},{1,25},{2,26},{3,27},{4,7},{5,6},{6,5},{7,4},{8,16},{9,17},... | collective-permute-start | bytes 393224 | tf_op jit(solution)/shard_map/ppermute | solution.py:31
  47.6 5.3 %collective-permute-start.15 = (bf16[128,512]{1,0:T(8,128)(2,1)S(1)}, bf16[128,512]{1,0:T(8,128)(2,1)S(1)}, u32[]{:S(2)}, u32[]{:S(2)}) collective-permute-start(bf16[128,512]{1,0:T(8,128)(2,1)S(1)} %second_sum.1), channel_id=1, source_target_pairs={{0,16},{1,17},{2,18},{3,19},{4,6},{5,7},{6,4},{7,5},{8,24},{9,25},... | collective-permute-start | bytes 393224 | tf_op jit(solution)/shard_map/ppermute | solution.py:31
  48.0 5.0 %collective-permute-start.14 = (bf16[128,512]{1,0:T(8,128)(2,1)S(1)}, bf16[128,512]{1,0:T(8,128)(2,1)S(1)}, u32[]{:S(2)}, u32[]{:S(2)}) collective-permute-start(bf16[128,512]{1,0:T(8,128)(2,1)S(1)} %second_sum.1), channel_id=1, source_target_pairs={{0,8},{1,9},{2,10},{3,11},{4,5},{5,4},{6,7},{7,6},{8,0},{9,1},{10,... | collective-permute-start | bytes 393224 | tf_op jit(solution)/shard_map/ppermute | solution.py:31
  48.3 8.2 %collective-permute-start.22 = (f32[128,256]{1,0:T(8,128)S(1)}, f32[128,256]{1,0:T(8,128)S(1)}, u32[]{:S(2)}, u32[]{:S(2)}) collective-permute-start(f32[128,256]{1,0:T(8,128)S(1)} %add_add_fusion.4), channel_id=1, source_target_pairs={{0,24},{1,25},{2,26},{3,27},{4,100},{5,101},{6,102},{7,103},{8,16}... | collective-permute-start | bytes 393224 | tf_op jit(solution)/shard_map/ppermute | solution.py:31
  53.0 20.8 %collective-permute-start.19 = (bf16[512,512]{1,0:T(8,128)(2,1)S(1)}, bf16[512,512]{1,0:T(8,128)(2,1)S(1)}, u32[]{:S(2)}, u32[]{:S(2)}) collective-permute-start(bf16[512,512]{1,0:T(8,128)(2,1)S(1)} %pad_maximum_fusion.m0), channel_id=1, source_target_pairs={{0,3},{1,2},{2,1},{3,0},{4,28},{5,29},{6,30},{7,31},{8,11},{9,10},... | collective-permute-start | bytes 1572872 | tf_op jit(solution)/shard_map/ppermute | solution.py:31
  53.4 20.3 %collective-permute-start.18 = (bf16[512,512]{1,0:T(8,128)(2,1)S(1)}, bf16[512,512]{1,0:T(8,128)(2,1)S(1)}, u32[]{:S(2)}, u32[]{:S(2)}) collective-permute-start(bf16[512,512]{1,0:T(8,128)(2,1)S(1)} %pad_maximum_fusion.m0), channel_id=1, source_target_pairs={{0,2},{1,3},{2,0},{3,1},{4,20},{5,21},{6,22},{7,23},{8,10},{9,11},... | collective-permute-start | bytes 1572872 | tf_op jit(solution)/shard_map/ppermute | solution.py:31
  53.9 19.8 %collective-permute-start.17 = (bf16[512,512]{1,0:T(8,128)(2,1)S(1)}, bf16[512,512]{1,0:T(8,128)(2,1)S(1)}, u32[]{:S(2)}, u32[]{:S(2)}) collective-permute-start(bf16[512,512]{1,0:T(8,128)(2,1)S(1)} %pad_maximum_fusion.m0), channel_id=1, source_target_pairs={{0,1},{1,0},{2,3},{3,2},{4,12},{5,13},{6,14},{7,15},{8,9},{9,8},{1... | collective-permute-start | bytes 1572872 | tf_op jit(solution)/shard_map/ppermute | solution.py:31
  56.3 5.3 %collective-permute-start.21 = (f32[128,256]{1,0:T(8,128)S(1)}, f32[128,256]{1,0:T(8,128)S(1)}, u32[]{:S(2)}, u32[]{:S(2)}) collective-permute-start(f32[128,256]{1,0:T(8,128)S(1)} %add_add_fusion.4), channel_id=1, source_target_pairs={{0,16},{1,17},{2,18},{3,19},{4,68},{5,69},{6,70},{7,71},{8,24},{9,... | collective-permute-start | bytes 393224 | tf_op jit(solution)/shard_map/ppermute | solution.py:31
  56.6 5.7 %collective-permute-start.20 = (f32[128,256]{1,0:T(8,128)S(1)}, f32[128,256]{1,0:T(8,128)S(1)}, u32[]{:S(2)}, u32[]{:S(2)}) collective-permute-start(f32[128,256]{1,0:T(8,128)S(1)} %add_add_fusion.4), channel_id=1, source_target_pairs={{0,8},{1,9},{2,10},{3,11},{4,36},{5,37},{6,38},{7,39},{8,0},{9,1},... | collective-permute-start | bytes 393224 | tf_op jit(solution)/shard_map/ppermute | solution.py:31
  62.3 10.8 %collective-permute-start.23 = (f32[128,256]{1,0:T(8,128)S(1)}, f32[128,256]{1,0:T(8,128)S(1)}, u32[]{:S(2)}, u32[]{:S(2)}) collective-permute-start(f32[128,256]{1,0:T(8,128)S(1)} %add_add_fusion.3.own_ref), channel_id=1, source_target_pairs={{0,4},{4,0},{8,12},{12,8},{16,20},{20,16},{24,28},{28,24},{32,36},... | collective-permute-start | bytes 393224 | tf_op jit(solution)/shard_map/ppermute | solution.py:387
  75.5 1.4 %collective-permute-start.24 = (f32[32,1024]{1,0:T(8,128)S(1)}, f32[32,1024]{1,0:T(8,128)S(1)}, u32[]{:S(2)}, u32[]{:S(2)}) collective-permute-start(f32[32,1024]{1,0:T(8,128)S(1)} %get-tuple-element.104), channel_id=1, source_target_pairs={{0,4},{4,0},{8,12},{12,8},{16,20},{20,16},{24,28},{28,24},{32,36},... | collective-permute-start | bytes 393224 | tf_op jit(solution)/shard_map/ppermute | solution.py:307
  76.9 8.6 %collective-permute-start.27 = (f32[32,1024]{1,0:T(8,128)S(1)}, f32[32,1024]{1,0:T(8,128)S(1)}, u32[]{:S(2)}, u32[]{:S(2)}) collective-permute-start(f32[32,1024]{1,0:T(8,128)S(1)} %add.64), channel_id=1, source_target_pairs={{0,96},{1,97},{2,98},{3,99},{4,100},{5,101},{6,102},{7,103},{8,104... | collective-permute-start | bytes 393224 | tf_op jit(solution)/shard_map/ppermute | solution.py:31
  77.9 7.6 %collective-permute-start.26 = (f32[32,1024]{1,0:T(8,128)S(1)}, f32[32,1024]{1,0:T(8,128)S(1)}, u32[]{:S(2)}, u32[]{:S(2)}) collective-permute-start(f32[32,1024]{1,0:T(8,128)S(1)} %add.64), channel_id=1, source_target_pairs={{0,64},{1,65},{2,66},{3,67},{4,68},{5,69},{6,70},{7,71},{8,72},{9,... | collective-permute-start | bytes 393224 | tf_op jit(solution)/shard_map/ppermute | solution.py:31
  79.0 7.1 %collective-permute-start.25 = (f32[32,1024]{1,0:T(8,128)S(1)}, f32[32,1024]{1,0:T(8,128)S(1)}, u32[]{:S(2)}, u32[]{:S(2)}) collective-permute-start(f32[32,1024]{1,0:T(8,128)S(1)} %add.64), channel_id=1, source_target_pairs={{0,32},{1,33},{2,34},{3,35},{4,36},{5,37},{6,38},{7,39},{8,40},{9,... | collective-permute-start | bytes 393224 | tf_op jit(solution)/shard_map/ppermute | solution.py:31
  86.2 2.7 %collective-permute-start.28 = (f32[32,1024]{1,0:T(8,128)S(1)}, f32[32,1024]{1,0:T(8,128)S(1)}, u32[]{:S(2)}, u32[]{:S(2)}) collective-permute-start(f32[32,1024]{1,0:T(8,128)S(1)} %add_add_fusion.2.own_in), channel_id=1, source_target_pairs={{0,4},{4,0},{8,12},{12,8},{16,20},{20,16},{24,28},{28,24},{32,36},... | collective-permute-start | bytes 393224 | tf_op jit(solution)/shard_map/ppermute | solution.py:313
  90.9 1.4 %collective-permute-start.29 = (f32[32,1024]{1,0:T(8,128)S(1)}, f32[32,1024]{1,0:T(8,128)S(1)}, u32[]{:S(2)}, u32[]{:S(2)}) collective-permute-start(f32[32,1024]{1,0:T(8,128)S(1)} %get-tuple-element.111), channel_id=1, source_target_pairs={{0,4},{4,0},{8,12},{12,8},{16,20},{20,16},{24,28},{28,24},{32,36},... | collective-permute-start | bytes 393224 | tf_op jit(solution)/shard_map/ppermute | solution.py:307
  92.3 8.6 %collective-permute-start.32 = (f32[32,1024]{1,0:T(8,128)S(1)}, f32[32,1024]{1,0:T(8,128)S(1)}, u32[]{:S(2)}, u32[]{:S(2)}) collective-permute-start(f32[32,1024]{1,0:T(8,128)S(1)} %add.68), channel_id=1, source_target_pairs={{0,96},{1,97},{2,98},{3,99},{4,100},{5,101},{6,102},{7,103},{8,104... | collective-permute-start | bytes 393224 | tf_op jit(solution)/shard_map/ppermute | solution.py:31
  93.2 7.6 %collective-permute-start.31 = (f32[32,1024]{1,0:T(8,128)S(1)}, f32[32,1024]{1,0:T(8,128)S(1)}, u32[]{:S(2)}, u32[]{:S(2)}) collective-permute-start(f32[32,1024]{1,0:T(8,128)S(1)} %add.68), channel_id=1, source_target_pairs={{0,64},{1,65},{2,66},{3,67},{4,68},{5,69},{6,70},{7,71},{8,72},{9,... | collective-permute-start | bytes 393224 | tf_op jit(solution)/shard_map/ppermute | solution.py:31
  94.3 7.1 %collective-permute-start.30 = (f32[32,1024]{1,0:T(8,128)S(1)}, f32[32,1024]{1,0:T(8,128)S(1)}, u32[]{:S(2)}, u32[]{:S(2)}) collective-permute-start(f32[32,1024]{1,0:T(8,128)S(1)} %add.68), channel_id=1, source_target_pairs={{0,32},{1,33},{2,34},{3,35},{4,36},{5,37},{6,38},{7,39},{8,40},{9,... | collective-permute-start | bytes 393224 | tf_op jit(solution)/shard_map/ppermute | solution.py:31
  101.5 2.5 %collective-permute-start.33 = (f32[32,1024]{1,0:T(8,128)S(1)}, f32[32,1024]{1,0:T(8,128)S(1)}, u32[]{:S(2)}, u32[]{:S(2)}) collective-permute-start(f32[32,1024]{1,0:T(8,128)S(1)} %add_add_fusion.1.own_in), channel_id=1, source_target_pairs={{0,4},{4,0},{8,12},{12,8},{16,20},{20,16},{24,28},{28,24},{32,36},... | collective-permute-start | bytes 393224 | tf_op jit(solution)/shard_map/ppermute | solution.py:313
  106.1 1.4 %collective-permute-start.34 = (f32[32,1024]{1,0:T(8,128)S(1)}, f32[32,1024]{1,0:T(8,128)S(1)}, u32[]{:S(2)}, u32[]{:S(2)}) collective-permute-start(f32[32,1024]{1,0:T(8,128)S(1)} %get-tuple-element.119), channel_id=1, source_target_pairs={{0,4},{4,0},{8,12},{12,8},{16,20},{20,16},{24,28},{28,24},{32,36},... | collective-permute-start | bytes 393224 | tf_op jit(solution)/shard_map/ppermute | solution.py:307
  107.5 8.6 %collective-permute-start.37 = (f32[32,1024]{1,0:T(8,128)S(1)}, f32[32,1024]{1,0:T(8,128)S(1)}, u32[]{:S(2)}, u32[]{:S(2)}) collective-permute-start(f32[32,1024]{1,0:T(8,128)S(1)} %add.72), channel_id=1, source_target_pairs={{0,96},{1,97},{2,98},{3,99},{4,100},{5,101},{6,102},{7,103},{8,104... | collective-permute-start | bytes 393224 | tf_op jit(solution)/shard_map/ppermute | solution.py:31
  108.4 7.6 %collective-permute-start.36 = (f32[32,1024]{1,0:T(8,128)S(1)}, f32[32,1024]{1,0:T(8,128)S(1)}, u32[]{:S(2)}, u32[]{:S(2)}) collective-permute-start(f32[32,1024]{1,0:T(8,128)S(1)} %add.72), channel_id=1, source_target_pairs={{0,64},{1,65},{2,66},{3,67},{4,68},{5,69},{6,70},{7,71},{8,72},{9,... | collective-permute-start | bytes 393224 | tf_op jit(solution)/shard_map/ppermute | solution.py:31
  109.5 7.2 %collective-permute-start.35 = (f32[32,1024]{1,0:T(8,128)S(1)}, f32[32,1024]{1,0:T(8,128)S(1)}, u32[]{:S(2)}, u32[]{:S(2)}) collective-permute-start(f32[32,1024]{1,0:T(8,128)S(1)} %add.72), channel_id=1, source_target_pairs={{0,32},{1,33},{2,34},{3,35},{4,36},{5,37},{6,38},{7,39},{8,40},{9,... | collective-permute-start | bytes 393224 | tf_op jit(solution)/shard_map/ppermute | solution.py:31
  116.7 2.5 %collective-permute-start.38 = (f32[32,1024]{1,0:T(8,128)S(1)}, f32[32,1024]{1,0:T(8,128)S(1)}, u32[]{:S(2)}, u32[]{:S(2)}) collective-permute-start(f32[32,1024]{1,0:T(8,128)S(1)} %add_add_fusion.own_in), channel_id=1, source_target_pairs={{0,4},{4,0},{8,12},{12,8},{16,20},{20,16},{24,28},{28,24},{32,36},... | collective-permute-start | bytes 393224 | tf_op jit(solution)/shard_map/ppermute | solution.py:313
  122.1 4.5 %collective-permute-start.42 = (f32[32,512]{1,0:T(8,128)S(1)}, f32[32,512]{1,0:T(8,128)S(1)}, u32[]{:S(2)}, u32[]{:S(2)}) collective-permute-start(f32[32,512]{1,0:T(8,128)S(1)} %get-tuple-element.128.refs_0_), channel_id=1, source_target_pairs={{0,4},{4,0},{8,12},{12,8},{16,20},{20,16},{24,28},{28,24},{32,36},... | collective-permute-start | bytes 196616 | tf_op jit(solution)/shard_map/ppermute | solution.py:398
  122.5 7.0 %collective-permute-start.41 = (f32[32,512]{1,0:T(8,128)S(1)}, f32[32,512]{1,0:T(8,128)S(1)}, u32[]{:S(2)}, u32[]{:S(2)}) collective-permute-start(f32[32,512]{1,0:T(8,128)S(1)} %get-tuple-element.128.refs_0_), channel_id=1, source_target_pairs={{0,96},{1,97},{2,98},{3,99},{4,100},{5,101},{6,102},{7,103},{8,104... | collective-permute-start | bytes 196616 | tf_op jit(solution)/shard_map/ppermute | solution.py:31
  123.3 6.2 %collective-permute-start.40 = (f32[32,512]{1,0:T(8,128)S(1)}, f32[32,512]{1,0:T(8,128)S(1)}, u32[]{:S(2)}, u32[]{:S(2)}) collective-permute-start(f32[32,512]{1,0:T(8,128)S(1)} %get-tuple-element.128.refs_0_), channel_id=1, source_target_pairs={{0,64},{1,65},{2,66},{3,67},{4,68},{5,69},{6,70},{7,71},{8,72},{9,... | collective-permute-start | bytes 196616 | tf_op jit(solution)/shard_map/ppermute | solution.py:31
  124.4 5.2 %collective-permute-start.39 = (f32[32,512]{1,0:T(8,128)S(1)}, f32[32,512]{1,0:T(8,128)S(1)}, u32[]{:S(2)}, u32[]{:S(2)}) collective-permute-start(f32[32,512]{1,0:T(8,128)S(1)} %get-tuple-element.128.refs_0_), channel_id=1, source_target_pairs={{0,32},{1,33},{2,34},{3,35},{4,36},{5,37},{6,38},{7,39},{8,40},{9,... | collective-permute-start | bytes 196616 | tf_op jit(solution)/shard_map/ppermute | solution.py:31
  129.5 2.0 %collective-permute-start.43 = (f32[32,512]{1,0:T(8,128)S(1)}, f32[32,512]{1,0:T(8,128)S(1)}, u32[]{:S(2)}, u32[]{:S(2)}) collective-permute-start(f32[32,512]{1,0:T(8,128)S(1)} %collective-permute-done.39.refs_0_), channel_id=1, source_target_pairs={{0,4},{4,0},{8,12},{12,8},{16,20},{20,16},{24,28},{28,24},{32,36},... | collective-permute-start | bytes 196616 | tf_op jit(solution)/shard_map/ppermute | solution.py:402
  130.6 1.3 collective-permute-start.44
  130.7 1.3 collective-permute-start.45

commit v5 on v4

--- a/solution.py
+++ b/solution.py
@@ -150,20 +150,12 @@
     return call(body, "early_left", shapes, place, warm_t, *pairs, scratch=scratch)
 
 
-def stack_early(place, parts, after):
-    def body(place_ref, a_ref, b_ref, c_ref, d_ref, after_ref, o_ref):
+def stack_early(place, parts):
+    def body(place_ref, a_ref, b_ref, c_ref, d_ref, o_ref):
         for i, ref in enumerate((a_ref, b_ref, c_ref, d_ref)):
             o_ref[i * RANK : (i + 1) * RANK, :] = ref[...]
 
-    return pl.pallas_call(
-        body,
-        in_specs=[SCALARS] + [WHOLE] * 4 + [HBM],
-        out_specs=WHOLE,
-        out_shape=jax.ShapeDtypeStruct((4 * RANK, ROWS_OWN // 2), F32),
-        cost_estimate=SMALL,
-        compiler_params=params(),
-        name="stack_early",
-    )(place, *parts, after)
+    return call(body, "stack_early", jax.ShapeDtypeStruct((4 * RANK, ROWS_OWN // 2), F32), place, *parts)
 
 
 def assemble_left(place, own, oth):
@@ -294,13 +286,13 @@
         left = dot(inv_ref[...], left, ((1,), (0,)), HIGHEST) * (1.0 / N_DP)
         raw = add_thirds(times_m(thirds(reorder(left, place_ref)), (m0, m1, m2, m3)))
         inverse = inverse_factor(dot(left, left, ((1,), (1,)), HIGHEST))
-        right_ref[...] = dot(inverse, raw, ((1,), (0,)), HIGHEST) * (1.0 / N_DP)
+        right_ref[...] = (dot(inverse, raw, ((1,), (0,)), HIGHEST) * (1.0 / N_DP)).astype(BF)
         for k in range(4):
             left_ref[:, cut(place_ref[1] ^ k, PIECE)] = left[:, k * PIECE : (k + 1) * PIECE]
         out_ref[...] = inverse
 
-    shapes = [(RANK, COLS), (RANK, ROWS_OWN), (RANK, RANK)]
-    return call(body, "last_right", [jax.ShapeDtypeStruct(s, F32) for s in shapes], place, own, oth, inverse, *m)
+    shapes = [((RANK, COLS), BF), ((RANK, ROWS_OWN), F32), ((RANK, RANK), F32)]
+    return call(body, "last_right", [jax.ShapeDtypeStruct(*s) for s in shapes], place, own, oth, inverse, *m)
 
 
 def sum_over_group(own, oth, beside=None):
@@ -315,11 +307,9 @@
 
 def columns_of(place, left, inverse):
     def body(place_ref, left_ref, inv_ref, out_ref):
-        ortho = dot(inv_ref[...], left_ref[...], ((1,), (0,)), HIGHEST)
-        wide = jnp.concatenate([ortho] * 3 + [jnp.zeros((RANK, ROWS_OWN), F32)], axis=0)
-        out_ref[...] = wide.T.astype(BF)
-
-    return call(body, "columns_of", jax.ShapeDtypeStruct((ROWS_OWN, 4 * RANK), BF), place, left, inverse)
+        out_ref[...] = dot(inv_ref[...], left_ref[...], ((1,), (0,)), HIGHEST).T.astype(BF)
+
+    return call(body, "columns_of", jax.ShapeDtypeStruct((ROWS_OWN, RANK), BF), place, left, inverse)
 
 
 def finish(place, ortho, rights, mine, other, outs, name):
@@ -328,7 +318,7 @@
 
     def body(place_ref, o_ref, *refs):
         rights, memory, refs = refs[:count], refs[count : count + 2], refs[count + 2 + kept :]
-        up_hbm, err_hbm, right_hbm, up_ref, err_ref, sems = refs
+        up_hbm, err_hbm, right_hbm, up_ref, err_ref, right_ref, sems = refs
         copies = []
 
         def send(i, n, source, target):
@@ -338,13 +328,13 @@
         for n, ((k, j), ref) in enumerate(zip(keys, rights)):
             z = place_ref[0] ^ k
             cols = cut((place_ref[2] ^ j) * 4 + z, COLS)
-            wide = jnp.concatenate([thirds(ref[...]), jnp.zeros((RANK, COLS), BF)], axis=0)
-            update = dot(o_ref[...], wide, ((1,), (0,)))
+            update = dot(o_ref[...], ref[...], ((1,), (0,)))
             up_ref[n] = update
             send(0, n, up_ref.at[n], up_hbm.at[:, cols])
             err_ref[n] = memory[j][:, cut(z, COLS)].astype(F32) - update
             send(1, n, err_ref.at[n], err_hbm.at[:, cols])
-            send(2, n, ref, right_hbm.at[:, cols])
+            right_ref[n] = ref[...].astype(F32)
+            send(2, n, right_ref.at[n], right_hbm.at[:, cols])
         for copy in copies:
             copy.wait()
 
@@ -353,7 +343,7 @@
         body,
         in_specs=[SCALARS] + [WHOLE] * (count + 3) + [HBM] * kept,
         out_specs=[HBM] * 3,
-        scratch_shapes=[blocks, blocks, pltpu.SemaphoreType.DMA((3, count))],
+        scratch_shapes=[blocks, blocks, pltpu.VMEM((count, RANK, COLS), F32), pltpu.SemaphoreType.DMA((3, count))],
         out_shape=(
             jax.ShapeDtypeStruct((ROWS_OWN, W), F32),
             jax.ShapeDtypeStruct((ROWS_OWN, W), F32),
@@ -376,9 +366,10 @@
     pairs = pair_sum(place, mine, received)
     early, passed = early_left(place, warm_right.T, pairs)
     early = early + lax.ppermute(passed, "dp", CORE)
-    parts, early = lax.optimization_barrier((exchange(pairs, "z", "x"), spread(early, "y", "y")))
+    early = stack_early(place, spread(early, "y", "y"))
+    parts, early = lax.optimization_barrier((exchange(pairs, "z", "x"), early))
     rows = first_sum(place, parts)
-    early = spread(stack_early(place, early, rows[0]), "z", "x")
+    early = spread(early, "z", "x")
     parts, early = lax.optimization_barrier((exchange(rows, "x", "z"), early))
     piece = second_sum(place, parts)
     early = spread((early[0] + early[1]) + (early[2] + early[3]), "x", "z")

time: 138 us -> 137 us (level)
  waiting for transfers between devices: 42.1 us -> 40 us
    ppermute x33, waiting for transfers between devices: 32 us -> 29.9 us  [along(): return lax.ppermute(array, ('dp', 'owner'), pairs)]
    ppermute x33, starting transfers between devices: 38.5 us -> 40.5 us  [along(): return lax.ppermute(array, ('dp', 'owner'), pairs)]
    pallas_call x13 -> x14, Pallas kernels: 20.3 us -> 20.9 us  [call(): pl.pallas_call(body, in_specs=[SCALARS] + [WHOLE] * len(arrays), out_spec...]
  transfers between devices with their start and end apart: 46 -> 46, of which waited for: 29 -> 30; matrix products, arithmetic and copies ran while one was open for 0% -> 0% of each run, Pallas kernels for 10% -> 10%
where the time goes in v5:
time: 137 us
  starting transfers between devices  61.5 us (45%)
  waiting for transfers between devices  40 us (29%)
  Pallas kernels  34.1 us (25%)
    ppermute x33, starting transfers between devices, along(): return lax.ppermute(array, ('dp', 'owner'), pairs)  40.5 us
    ppermute x33, waiting for transfers between devices, along(): return lax.ppermute(array, ('dp', 'owner'), pairs)  29.9 us
    pallas_call x14, Pallas kernels, call(): pl.pallas_call(body, in_specs=[SCALARS] + [WHOLE] * len(arrays), out_spec...  20.9 us
    ppermute x1, starting transfers between devices, per_device(): left = assemble_left(place, early, lax.ppermute(early, 'dp', CORE))  8.81 us
    pallas_call x2, Pallas kernels, finish(): pl.pallas_call(body, in_specs=[SCALARS] + [WHOLE] * (count + 3) + [HBM] *...  8.53 us
    ppermute x3, starting transfers between devices, sum_over_group(): return (own, lax.ppermute(own, 'dp', CORE), beside)  4.81 us
    pallas_call x2, Pallas kernels, half_of_memory(): pl.pallas_call(body, in_specs=[SCALARS, HBM, HBM], out_specs=WHOLE, scrat...  4.67 us
    ppermute x3, waiting for transfers between devices, sum_over_group(): return (own, lax.ppermute(own, 'dp', CORE), beside)  2.96 us
  transfers between devices with their start and end apart: 46, of which 30 were waited for; matrix products, arithmetic and copies ran while one was open for 0% of the time, Pallas kernels for 10%

profile of v5, /device:TPU:1, one launch (start us, length us, event | category | flops | bytes accessed | tf_op | source)
XLA Modules:
  0.0 137.0 jit_solution(13497395276682562606)
XLA Ops:
  0.6 2.3 %half_of_memory.3.refs_3_.refs_7_ = bf16[512,2048]{1,0:T(8,128)(2,1)S(1)} custom-call(s32[1]{0:T(128)} %bitcast.5.which_ref, bf16[512,4096]{1,0:T(8,128)(2,1)} %bitcast.10, bf16[512,4096]{1,0:T(8,128)(2,1)} %bitcast.12), custom_call_target="tpu_custom_call" | custom-call | tf_op jit(solution)/shard_map/half_of_memory/pallas_call | solution.py:74
  3.0 1.5 %collective-permute-start = (bf16[512,2048]{1,0:T(8,128)(2,1)S(1)}, bf16[512,2048]{1,0:T(8,128)(2,1)}, u32[]{:S(2)}, u32[]{:S(2)}) collective-permute-start(bf16[512,2048]{1,0:T(8,128)(2,1)S(1)} %half_of_memory.3.refs_3_.refs_7_), channel_id=1, source_target_pairs={{0,4},{4,0},{8,12},{12,8},{16,20},{20,16},{24,28},{28,24},{32,36},... | collective-permute-start | bytes 6291464 | tf_op jit(solution)/shard_map/ppermute | solution.py:364
  4.5 2.3 %half_of_memory.2.a_ref.refs_2_.refs_6_ = bf16[512,2048]{1,0:T(8,128)(2,1)S(1)} custom-call(s32[1]{0:T(128)} %bitcast.2.which_ref, bf16[512,4096]{1,0:T(8,128)(2,1)} %bitcast.11, bf16[512,4096]{1,0:T(8,128)(2,1)} %bitcast.13), custom_call_target="tpu_custom_call" | custom-call | tf_op jit(solution)/shard_map/half_of_memory/pallas_call | solution.py:74
  6.9 1.5 %collective-permute-done.b_ref = bf16[512,2048]{1,0:T(8,128)(2,1)} collective-permute-done((bf16[512,2048]{1,0:T(8,128)(2,1)S(1)}, bf16[512,2048]{1,0:T(8,128)(2,1)}, u32[]{:S(2)}, u32[]{:S(2)}) %collective-permute-start) | collective-permute-done | bytes 2097184 | tf_op jit(solution)/shard_map/ppermute | solution.py:364
  8.4 1.9 %pair_sum.1 = (bf16[4,128,512]{2,1,0:T(8,128)(2,1)S(1)}, bf16[4,128,512]{2,1,0:T(8,128)(2,1)S(1)}, bf16[4,128,512]{2,1,0:T(8,128)(2,1)S(1)}, bf16[4,128,512]{2,1,0:T(8,128)(2,1)S(1)}) custom-call(s32[3]{0:T(128)S(1)} %pad_add_fusion.place_ref, bf16[512,2048]{1,0:T(8,128)(2,1)S(1)} %half_of_memory.2.a_ref.refs_2_.refs_6_, ...), custom_call_target="tpu_custom_call" | custom-call | tf_op jit(solution)/shard_map/pair_sum/pallas_call | solution.py:86
  10.3 1.4 %collective-permute-start.1 = (bf16[4,128,512]{2,1,0:T(8,128)(2,1)S(1)}, bf16[4,128,512]{2,1,0:T(8,128)(2,1)S(1)}, u32[]{:S(2)}, u32[]{:S(2)}) collective-permute-start(bf16[4,128,512]{2,1,0:T(8,128)(2,1)S(1)} %get-tuple-element.70.refs_1_), channel_id=1, source_target_pairs={{0,32},{1,33},{2,34},{3,35},{4,12},{5,13},{6,14},{7,15},{8,40},{9,... | collective-permute-start | bytes 1572872 | tf_op jit(solution)/shard_map/ppermute | solution.py:31
  11.7 2.5 %collective-permute-start.2 = (bf16[4,128,512]{2,1,0:T(8,128)(2,1)S(1)}, bf16[4,128,512]{2,1,0:T(8,128)(2,1)S(1)}, u32[]{:S(2)}, u32[]{:S(2)}) collective-permute-start(bf16[4,128,512]{2,1,0:T(8,128)(2,1)S(1)} %get-tuple-element.71.refs_2_), channel_id=1, source_target_pairs={{0,64},{1,65},{2,66},{3,67},{4,20},{5,21},{6,22},{7,23},{8,72},{9,... | collective-permute-start | bytes 1572872 | tf_op jit(solution)/shard_map/ppermute | solution.py:31
  14.2 1.4 early_left.1
  15.6 2.2 %collective-permute-start.4 = (f32[32,256]{1,0:T(8,128)S(1)}, f32[32,256]{1,0:T(8,128)S(1)}, u32[]{:S(2)}, u32[]{:S(2)}) collective-permute-start(f32[32,256]{1,0:T(8,128)S(1)} %get-tuple-element.74), channel_id=1, source_target_pairs={{0,4},{4,0},{8,12},{12,8},{16,20},{20,16},{24,28},{28,24},{32,36},... | collective-permute-start | bytes 98312 | tf_op jit(solution)/shard_map/ppermute | solution.py:368
  17.8 0.9 collective-permute-done.4
  18.7 2.7 %collective-permute-start.7 = (f32[32,256]{1,0:T(8,128)S(1)}, f32[32,256]{1,0:T(8,128)S(1)}, u32[]{:S(2)}, u32[]{:S(2)}) collective-permute-start(f32[32,256]{1,0:T(8,128)S(1)} %add.57.a_ref), channel_id=1, source_target_pairs={{0,3},{1,2},{2,1},{3,0},{4,7},{5,6},{6,5},{7,4},{8,11},{9,10},{10,... | collective-permute-start | bytes 98312 | tf_op jit(solution)/shard_map/ppermute | solution.py:31
  21.8 1.2 collective-permute-done.7.d_ref
  23.0 2.9 %collective-permute-done.6.c_ref = f32[32,256]{1,0:T(8,128)S(1)} collective-permute-done((f32[32,256]{1,0:T(8,128)S(1)}, f32[32,256]{1,0:T(8,128)S(1)}, u32[]{:S(2)}, u32[]{:S(2)}) %collective-permute-start.6) | collective-permute-done | bytes 32800 | tf_op jit(solution)/shard_map/ppermute | solution.py:31
  26.6 2.6 %collective-permute-done.3.refs_3_ = bf16[4,128,512]{2,1,0:T(8,128)(2,1)S(1)} collective-permute-done((bf16[4,128,512]{2,1,0:T(8,128)(2,1)S(1)}, bf16[4,128,512]{2,1,0:T(8,128)(2,1)S(1)}, u32[]{:S(2)}, u32[]{:S(2)}) %collective-permute-start.3) | collective-permute-done | bytes 524320 | tf_op jit(solution)/shard_map/ppermute | solution.py:31
  30.1 1.4 %collective-permute-start.8 = (bf16[128,512]{1,0:T(8,128)(2,1)S(1)}, bf16[128,512]{1,0:T(8,128)(2,1)S(1)}, u32[]{:S(2)}, u32[]{:S(2)}) collective-permute-start(bf16[128,512]{1,0:T(8,128)(2,1)S(1)} %get-tuple-element.80), channel_id=1, source_target_pairs={{0,8},{1,9},{2,10},{3,11},{4,36},{5,37},{6,38},{7,39},{8,0},{9,1},... | collective-permute-start | bytes 393224 | tf_op jit(solution)/shard_map/ppermute | solution.py:31
  31.5 3.3 %collective-permute-start.9 = (bf16[128,512]{1,0:T(8,128)(2,1)S(1)}, bf16[128,512]{1,0:T(8,128)(2,1)S(1)}, u32[]{:S(2)}, u32[]{:S(2)}) collective-permute-start(bf16[128,512]{1,0:T(8,128)(2,1)S(1)} %get-tuple-element.81), channel_id=1, source_target_pairs={{0,16},{1,17},{2,18},{3,19},{4,68},{5,69},{6,70},{7,71},{8,24},{9,... | collective-permute-start | bytes 393224 | tf_op jit(solution)/shard_map/ppermute | solution.py:31
  35.6 2.4 %collective-permute-start.11 = (f32[128,256]{1,0:T(8,128)S(1)}, f32[128,256]{1,0:T(8,128)S(1)}, u32[]{:S(2)}, u32[]{:S(2)}) collective-permute-start(f32[128,256]{1,0:T(8,128)S(1)} %stack_early.1), channel_id=1, source_target_pairs={{0,32},{1,33},{2,34},{3,35},{4,12},{5,13},{6,14},{7,15},{8,40},{9,... | collective-permute-start | bytes 393224 | tf_op jit(solution)/shard_map/ppermute | solution.py:31
  38.6 1.4 %collective-permute-done.10.d_ref = bf16[128,512]{1,0:T(8,128)(2,1)S(1)} collective-permute-done((bf16[128,512]{1,0:T(8,128)(2,1)S(1)}, bf16[128,512]{1,0:T(8,128)(2,1)S(1)}, u32[]{:S(2)}, u32[]{:S(2)}) %collective-permute-start.10) | collective-permute-done | bytes 131104 | tf_op jit(solution)/shard_map/ppermute | solution.py:31
  40.0 2.6 %collective-permute-done.13 = f32[128,256]{1,0:T(8,128)S(1)} collective-permute-done((f32[128,256]{1,0:T(8,128)S(1)}, f32[128,256]{1,0:T(8,128)S(1)}, u32[]{:S(2)}, u32[]{:S(2)}) %collective-permute-start.13) | collective-permute-done | bytes 131104 | tf_op jit(solution)/shard_map/ppermute | solution.py:31
  43.7 2.8 %collective-permute-start.16 = (bf16[128,512]{1,0:T(8,128)(2,1)S(1)}, bf16[128,512]{1,0:T(8,128)(2,1)S(1)}, u32[]{:S(2)}, u32[]{:S(2)}) collective-permute-start(bf16[128,512]{1,0:T(8,128)(2,1)S(1)} %second_sum.1), channel_id=1, source_target_pairs={{0,24},{1,25},{2,26},{3,27},{4,7},{5,6},{6,5},{7,4},{8,16},{9,17},... | collective-permute-start | bytes 393224 | tf_op jit(solution)/shard_map/ppermute | solution.py:31
  47.2 2.4 %collective-permute-start.22 = (f32[128,256]{1,0:T(8,128)S(1)}, f32[128,256]{1,0:T(8,128)S(1)}, u32[]{:S(2)}, u32[]{:S(2)}) collective-permute-start(f32[128,256]{1,0:T(8,128)S(1)} %add_add_fusion.4), channel_id=1, source_target_pairs={{0,24},{1,25},{2,26},{3,27},{4,100},{5,101},{6,102},{7,103},{8,16}... | collective-permute-start | bytes 393224 | tf_op jit(solution)/shard_map/ppermute | solution.py:31
  49.8 2.0 %collective-permute-done.15 = bf16[128,512]{1,0:T(8,128)(2,1)S(1)} collective-permute-done((bf16[128,512]{1,0:T(8,128)(2,1)S(1)}, bf16[128,512]{1,0:T(8,128)(2,1)S(1)}, u32[]{:S(2)}, u32[]{:S(2)}) %collective-permute-start.15) | collective-permute-done | bytes 131104 | tf_op jit(solution)/shard_map/ppermute | solution.py:31
  51.9 1.5 %collective-permute-start.19 = (bf16[512,512]{1,0:T(8,128)(2,1)S(1)}, bf16[512,512]{1,0:T(8,128)(2,1)S(1)}, u32[]{:S(2)}, u32[]{:S(2)}) collective-permute-start(bf16[512,512]{1,0:T(8,128)(2,1)S(1)} %pad_maximum_fusion.m0), channel_id=1, source_target_pairs={{0,3},{1,2},{2,1},{3,0},{4,28},{5,29},{6,30},{7,31},{8,11},{9,10},... | collective-permute-start | bytes 1572872 | tf_op jit(solution)/shard_map/ppermute | solution.py:31
  53.9 1.3 collective-permute-start.17
  55.2 0.8 collective-permute-start.21
  56.1 2.1 %collective-permute-start.20 = (f32[128,256]{1,0:T(8,128)S(1)}, f32[128,256]{1,0:T(8,128)S(1)}, u32[]{:S(2)}, u32[]{:S(2)}) collective-permute-start(f32[128,256]{1,0:T(8,128)S(1)} %add_add_fusion.4), channel_id=1, source_target_pairs={{0,8},{1,9},{2,10},{3,11},{4,36},{5,37},{6,38},{7,39},{8,0},{9,1},... | collective-permute-start | bytes 393224 | tf_op jit(solution)/shard_map/ppermute | solution.py:31
  58.2 2.4 %collective-permute-done.21 = f32[128,256]{1,0:T(8,128)S(1)} collective-permute-done((f32[128,256]{1,0:T(8,128)S(1)}, f32[128,256]{1,0:T(8,128)S(1)}, u32[]{:S(2)}, u32[]{:S(2)}) %collective-permute-start.21) | collective-permute-done | bytes 131104 | tf_op jit(solution)/shard_map/ppermute | solution.py:31
  60.5 1.7 %collective-permute-done.20 = f32[128,256]{1,0:T(8,128)S(1)} collective-permute-done((f32[128,256]{1,0:T(8,128)S(1)}, f32[128,256]{1,0:T(8,128)S(1)}, u32[]{:S(2)}, u32[]{:S(2)}) %collective-permute-start.20) | collective-permute-done | bytes 131104 | tf_op jit(solution)/shard_map/ppermute | solution.py:31
  62.2 8.8 %collective-permute-start.23 = (f32[128,256]{1,0:T(8,128)S(1)}, f32[128,256]{1,0:T(8,128)S(1)}, u32[]{:S(2)}, u32[]{:S(2)}) collective-permute-start(f32[128,256]{1,0:T(8,128)S(1)} %add_add_fusion.3.own_ref), channel_id=1, source_target_pairs={{0,4},{4,0},{8,12},{12,8},{16,20},{20,16},{24,28},{28,24},{32,36},... | collective-permute-start | bytes 393224 | tf_op jit(solution)/shard_map/ppermute | solution.py:378
  71.1 1.0 collective-permute-done.23.oth_ref
  72.7 1.7 %second_left.1 = (f32[32,1024]{1,0:T(8,128)S(1)}, f32[32,1024]{1,0:T(8,128)S(1)}) custom-call(s32[3]{0:T(128)S(1)} %pad_add_fusion.place_ref, f32[32,2048]{1,0:T(8,128)S(1)} %assemble_left.1.left_ref, bf16[512,512]{1,0:T(8,128)(2,1)S(1)} %pad_maximum_fusion.m0, bf16[512,512]{1,0:T(8,128)(2,1)S(1)} %collective-permute-done.17.m1, ...), custom_call_target="tpu_custom_call" | custom-call | tf_op jit(solution)/shard_map/second_left/pallas_call | solution.py:86
  75.2 1.0 collective-permute-done.24
  76.2 1.1 collective-permute-start.27
  77.2 1.2 collective-permute-start.26
  78.5 1.0 collective-permute-start.25
  79.5 1.9 %inverse_of.3.inv_ref = f32[32,32]{1,0:T(8,128)S(1)} custom-call(s32[3]{0:T(128)S(1)} %pad_add_fusion.place_ref, f32[32,2048]{1,0:T(8,128)S(1)} %assemble_left.1.left_ref), custom_call_target="tpu_custom_call" | custom-call | flops 1000 | bytes 1000 | tf_op jit(solution)/shard_map/inverse_of/pallas_call | solution.py:86
  81.4 3.2 %collective-permute-done.27 = f32[32,1024]{1,0:T(8,128)S(1)} collective-permute-done((f32[32,1024]{1,0:T(8,128)S(1)}, f32[32,1024]{1,0:T(8,128)S(1)}, u32[]{:S(2)}, u32[]{:S(2)}) %collective-permute-start.27) | collective-permute-done | bytes 131104 | tf_op jit(solution)/shard_map/ppermute | solution.py:31
  85.4 1.7 %collective-permute-start.28 = (f32[32,1024]{1,0:T(8,128)S(1)}, f32[32,1024]{1,0:T(8,128)S(1)}, u32[]{:S(2)}, u32[]{:S(2)}) collective-permute-start(f32[32,1024]{1,0:T(8,128)S(1)} %add_add_fusion.2.own_in), channel_id=1, source_target_pairs={{0,4},{4,0},{8,12},{12,8},{16,20},{20,16},{24,28},{28,24},{32,36},... | collective-permute-start | bytes 393224 | tf_op jit(solution)/shard_map/ppermute | solution.py:305
  87.1 1.0 collective-permute-done.28.oth_in
  88.1 2.0 %next_left.2 = (f32[32,2048]{1,0:T(8,128)S(1)}, f32[32,1024]{1,0:T(8,128)S(1)}, f32[32,1024]{1,0:T(8,128)S(1)}) custom-call(s32[3]{0:T(128)S(1)} %pad_add_fusion.place_ref, f32[32,1024]{1,0:T(8,128)S(1)} %add_add_fusion.2.own_in, f32[32,1024]{1,0:T(8,128)S(1)} %collective-permute-done.28.oth_in, f32[32,32]{1,0:T(8,128)S(1)} %inverse_of.3.inv_ref, ...), custom_call_target="tpu_custom_call" | custom-call | tf_op jit(solution)/shard_map/next_left/pallas_call | solution.py:86
  90.5 1.0 collective-permute-done.29
  91.5 1.1 collective-permute-start.32
  92.6 1.2 collective-permute-start.31
  93.8 1.1 collective-permute-start.30
  94.9 1.9 %inverse_of.4.inv_ref = f32[32,32]{1,0:T(8,128)S(1)} custom-call(s32[3]{0:T(128)S(1)} %pad_add_fusion.place_ref, f32[32,2048]{1,0:T(8,128)S(1)} %get-tuple-element.106.left_ref), custom_call_target="tpu_custom_call" | custom-call | flops 1000 | bytes 1000 | tf_op jit(solution)/shard_map/inverse_of/pallas_call | solution.py:86
  96.8 3.2 %collective-permute-done.32 = f32[32,1024]{1,0:T(8,128)S(1)} collective-permute-done((f32[32,1024]{1,0:T(8,128)S(1)}, f32[32,1024]{1,0:T(8,128)S(1)}, u32[]{:S(2)}, u32[]{:S(2)}) %collective-permute-start.32) | collective-permute-done | bytes 131104 | tf_op jit(solution)/shard_map/ppermute | solution.py:31
  100.7 1.5 %collective-permute-start.33 = (f32[32,1024]{1,0:T(8,128)S(1)}, f32[32,1024]{1,0:T(8,128)S(1)}, u32[]{:S(2)}, u32[]{:S(2)}) collective-permute-start(f32[32,1024]{1,0:T(8,128)S(1)} %add_add_fusion.1.own_in), channel_id=1, source_target_pairs={{0,4},{4,0},{8,12},{12,8},{16,20},{20,16},{24,28},{28,24},{32,36},... | collective-permute-start | bytes 393224 | tf_op jit(solution)/shard_map/ppermute | solution.py:305
  102.3 1.0 collective-permute-done.33.oth_in
  103.3 2.0 %next_left.3 = (f32[32,2048]{1,0:T(8,128)S(1)}, f32[32,1024]{1,0:T(8,128)S(1)}, f32[32,1024]{1,0:T(8,128)S(1)}) custom-call(s32[3]{0:T(128)S(1)} %pad_add_fusion.place_ref, f32[32,1024]{1,0:T(8,128)S(1)} %add_add_fusion.1.own_in, f32[32,1024]{1,0:T(8,128)S(1)} %collective-permute-done.33.oth_in, f32[32,32]{1,0:T(8,128)S(1)} %inverse_of.4.inv_ref, ...), custom_call_target="tpu_custom_call" | custom-call | tf_op jit(solution)/shard_map/next_left/pallas_call | solution.py:86
  105.7 1.0 collective-permute-done.34
  106.7 1.1 collective-permute-start.37
  107.8 1.1 collective-permute-start.36
  108.9 1.1 collective-permute-start.35
  110.1 1.9 %inverse_of.5.inv_ref = f32[32,32]{1,0:T(8,128)S(1)} custom-call(s32[3]{0:T(128)S(1)} %pad_add_fusion.place_ref, f32[32,2048]{1,0:T(8,128)S(1)} %get-tuple-element.114.left_ref), custom_call_target="tpu_custom_call" | custom-call | flops 1000 | bytes 1000 | tf_op jit(solution)/shard_map/inverse_of/pallas_call | solution.py:86
  112.0 3.2 %collective-permute-done.37 = f32[32,1024]{1,0:T(8,128)S(1)} collective-permute-done((f32[32,1024]{1,0:T(8,128)S(1)}, f32[32,1024]{1,0:T(8,128)S(1)}, u32[]{:S(2)}, u32[]{:S(2)}) %collective-permute-start.37) | collective-permute-done | bytes 131104 | tf_op jit(solution)/shard_map/ppermute | solution.py:31
  115.9 1.5 %collective-permute-start.38 = (f32[32,1024]{1,0:T(8,128)S(1)}, f32[32,1024]{1,0:T(8,128)S(1)}, u32[]{:S(2)}, u32[]{:S(2)}) collective-permute-start(f32[32,1024]{1,0:T(8,128)S(1)} %add_add_fusion.own_in), channel_id=1, source_target_pairs={{0,4},{4,0},{8,12},{12,8},{16,20},{20,16},{24,28},{28,24},{32,36},... | collective-permute-start | bytes 393224 | tf_op jit(solution)/shard_map/ppermute | solution.py:305
  117.5 1.0 collective-permute-done.38.oth_in
  118.5 2.8 %last_right.1 = (bf16[32,512]{1,0:T(8,128)(2,1)S(1)}, f32[32,512]{1,0:T(8,128)S(1)}, f32[32,32]{1,0:T(8,128)S(1)}) custom-call(s32[3]{0:T(128)S(1)} %pad_add_fusion.place_ref, f32[32,1024]{1,0:T(8,128)S(1)} %add_add_fusion.own_in, f32[32,1024]{1,0:T(8,128)S(1)} %collective-permute-done.38.oth_in, f32[32,32]{1,0:T(8,128)S(1)} %inverse_of.5.inv_ref, ...), custom_call_target="tpu_custom_call" | custom-call | tf_op jit(solution)/shard_map/last_right/pallas_call | solution.py:86
  121.7 1.0 collective-permute-start.41
  122.7 1.1 collective-permute-start.40
  123.8 1.2 collective-permute-start.39
  125.8 2.9 %finish_near.1 = (f32[512,4096]{1,0:T(8,128)}, f32[512,4096]{1,0:T(8,128)}, f32[32,4096]{1,0:T(8,128)}) custom-call(s32[3]{0:T(128)S(1)} %pad_add_fusion.place_ref, bf16[512,32]{1,0:T(8,128)(2,1)S(1)} %columns_of.1.o_ref, bf16[32,512]{1,0:T(8,128)(2,1)S(1)} %get-tuple-element.122.refs_0_, bf16[32,512]{1,0:T(8,128)(2,1)S(1)} %collective-permute-done.42.refs_1_, ...), custom_call_target="tpu_custom_call" | custom-call | tf_op jit(solution)/shard_map/finish_near/pallas_call | solution.py:342
  128.7 1.1 collective-permute-start.43
  131.2 5.6 %finish_far.1 = (f32[512,4096]{1,0:T(8,128)}, f32[512,4096]{1,0:T(8,128)}, f32[32,4096]{1,0:T(8,128)}) custom-call(s32[3]{0:T(128)S(1)} %pad_add_fusion.place_ref, bf16[512,32]{1,0:T(8,128)(2,1)S(1)} %columns_of.1.o_ref, bf16[32,512]{1,0:T(8,128)(2,1)S(1)} %collective-permute-done.39.refs_0_, ...), custom_call_target="tpu_custom_call", output_to_operand_aliasing={{0}: (10, {}), {1}: (11, {}), {2}: (12, {})} | custom-call | tf_op jit(solution)/shard_map/finish_far/pallas_call | solution.py:342
  (59 shorter events, 13.2 us)
Async XLA Ops:
  3.0 5.4 %collective-permute-start = (bf16[512,2048]{1,0:T(8,128)(2,1)S(1)}, bf16[512,2048]{1,0:T(8,128)(2,1)}, u32[]{:S(2)}, u32[]{:S(2)}) collective-permute-start(bf16[512,2048]{1,0:T(8,128)(2,1)S(1)} %half_of_memory.3.refs_3_.refs_7_), channel_id=1, source_target_pairs={{0,4},{4,0},{8,12},{12,8},{16,20},{20,16},{24,28},{28,24},{32,36},... | collective-permute-start | bytes 6291464 | tf_op jit(solution)/shard_map/ppermute | solution.py:364
  6.8 7.4 %copy-start = (f32[4096,32]{0,1:T(8,128)S(1)}, f32[4096,32]{0,1:T(8,128)}, u32[]{:S(2)}) copy-start(f32[4096,32]{0,1:T(8,128)} %param.5) | copy-start | bytes 1572868
  10.3 16.3 %collective-permute-start.1 = (bf16[4,128,512]{2,1,0:T(8,128)(2,1)S(1)}, bf16[4,128,512]{2,1,0:T(8,128)(2,1)S(1)}, u32[]{:S(2)}, u32[]{:S(2)}) collective-permute-start(bf16[4,128,512]{2,1,0:T(8,128)(2,1)S(1)} %get-tuple-element.70.refs_1_), channel_id=1, source_target_pairs={{0,32},{1,33},{2,34},{3,35},{4,12},{5,13},{6,14},{7,15},{8,40},{9,... | collective-permute-start | bytes 1572872 | tf_op jit(solution)/shard_map/ppermute | solution.py:31
  11.7 15.0 %collective-permute-start.2 = (bf16[4,128,512]{2,1,0:T(8,128)(2,1)S(1)}, bf16[4,128,512]{2,1,0:T(8,128)(2,1)S(1)}, u32[]{:S(2)}, u32[]{:S(2)}) collective-permute-start(bf16[4,128,512]{2,1,0:T(8,128)(2,1)S(1)} %get-tuple-element.71.refs_2_), channel_id=1, source_target_pairs={{0,64},{1,65},{2,66},{3,67},{4,20},{5,21},{6,22},{7,23},{8,72},{9,... | collective-permute-start | bytes 1572872 | tf_op jit(solution)/shard_map/ppermute | solution.py:31
  14.1 15.2 %collective-permute-start.3 = (bf16[4,128,512]{2,1,0:T(8,128)(2,1)S(1)}, bf16[4,128,512]{2,1,0:T(8,128)(2,1)S(1)}, u32[]{:S(2)}, u32[]{:S(2)}) collective-permute-start(bf16[4,128,512]{2,1,0:T(8,128)(2,1)S(1)} %get-tuple-element.72.refs_3_), channel_id=1, source_target_pairs={{0,96},{1,97},{2,98},{3,99},{4,28},{5,29},{6,30},{7,31},{8,104},{9... | collective-permute-start | bytes 1572872 | tf_op jit(solution)/shard_map/ppermute | solution.py:31
  15.6 3.1 %collective-permute-start.4 = (f32[32,256]{1,0:T(8,128)S(1)}, f32[32,256]{1,0:T(8,128)S(1)}, u32[]{:S(2)}, u32[]{:S(2)}) collective-permute-start(f32[32,256]{1,0:T(8,128)S(1)} %get-tuple-element.74), channel_id=1, source_target_pairs={{0,4},{4,0},{8,12},{12,8},{16,20},{20,16},{24,28},{28,24},{32,36},... | collective-permute-start | bytes 98312 | tf_op jit(solution)/shard_map/ppermute | solution.py:368
  18.7 4.3 %collective-permute-start.7 = (f32[32,256]{1,0:T(8,128)S(1)}, f32[32,256]{1,0:T(8,128)S(1)}, u32[]{:S(2)}, u32[]{:S(2)}) collective-permute-start(f32[32,256]{1,0:T(8,128)S(1)} %add.57.a_ref), channel_id=1, source_target_pairs={{0,3},{1,2},{2,1},{3,0},{4,7},{5,6},{6,5},{7,4},{8,11},{9,10},{10,... | collective-permute-start | bytes 98312 | tf_op jit(solution)/shard_map/ppermute | solution.py:31
  21.4 4.6 %collective-permute-start.6 = (f32[32,256]{1,0:T(8,128)S(1)}, f32[32,256]{1,0:T(8,128)S(1)}, u32[]{:S(2)}, u32[]{:S(2)}) collective-permute-start(f32[32,256]{1,0:T(8,128)S(1)} %add.57.a_ref), channel_id=1, source_target_pairs={{0,2},{1,3},{2,0},{3,1},{4,6},{5,7},{6,4},{7,5},{8,10},{9,11},{10,... | collective-permute-start | bytes 98312 | tf_op jit(solution)/shard_map/ppermute | solution.py:31
  23.0 3.1 %collective-permute-start.5 = (f32[32,256]{1,0:T(8,128)S(1)}, f32[32,256]{1,0:T(8,128)S(1)}, u32[]{:S(2)}, u32[]{:S(2)}) collective-permute-start(f32[32,256]{1,0:T(8,128)S(1)} %add.57.a_ref), channel_id=1, source_target_pairs={{0,1},{1,0},{2,3},{3,2},{4,5},{5,4},{6,7},{7,6},{8,9},{9,8},{10,11... | collective-permute-start | bytes 98312 | tf_op jit(solution)/shard_map/ppermute | solution.py:31
  30.1 5.5 %collective-permute-start.8 = (bf16[128,512]{1,0:T(8,128)(2,1)S(1)}, bf16[128,512]{1,0:T(8,128)(2,1)S(1)}, u32[]{:S(2)}, u32[]{:S(2)}) collective-permute-start(bf16[128,512]{1,0:T(8,128)(2,1)S(1)} %get-tuple-element.80), channel_id=1, source_target_pairs={{0,8},{1,9},{2,10},{3,11},{4,36},{5,37},{6,38},{7,39},{8,0},{9,1},... | collective-permute-start | bytes 393224 | tf_op jit(solution)/shard_map/ppermute | solution.py:31
  31.5 7.1 %collective-permute-start.9 = (bf16[128,512]{1,0:T(8,128)(2,1)S(1)}, bf16[128,512]{1,0:T(8,128)(2,1)S(1)}, u32[]{:S(2)}, u32[]{:S(2)}) collective-permute-start(bf16[128,512]{1,0:T(8,128)(2,1)S(1)} %get-tuple-element.81), channel_id=1, source_target_pairs={{0,16},{1,17},{2,18},{3,19},{4,68},{5,69},{6,70},{7,71},{8,24},{9,... | collective-permute-start | bytes 393224 | tf_op jit(solution)/shard_map/ppermute | solution.py:31
  34.8 5.2 %collective-permute-start.10 = (bf16[128,512]{1,0:T(8,128)(2,1)S(1)}, bf16[128,512]{1,0:T(8,128)(2,1)S(1)}, u32[]{:S(2)}, u32[]{:S(2)}) collective-permute-start(bf16[128,512]{1,0:T(8,128)(2,1)S(1)} %get-tuple-element.82), channel_id=1, source_target_pairs={{0,24},{1,25},{2,26},{3,27},{4,100},{5,101},{6,102},{7,103},{8,16}... | collective-permute-start | bytes 393224 | tf_op jit(solution)/shard_map/ppermute | solution.py:31
  34.8 7.7 %collective-permute-start.13 = (f32[128,256]{1,0:T(8,128)S(1)}, f32[128,256]{1,0:T(8,128)S(1)}, u32[]{:S(2)}, u32[]{:S(2)}) collective-permute-start(f32[128,256]{1,0:T(8,128)S(1)} %stack_early.1), channel_id=1, source_target_pairs={{0,96},{1,97},{2,98},{3,99},{4,28},{5,29},{6,30},{7,31},{8,104},{9... | collective-permute-start | bytes 393224 | tf_op jit(solution)/shard_map/ppermute | solution.py:31
  35.3 7.2 %collective-permute-start.12 = (f32[128,256]{1,0:T(8,128)S(1)}, f32[128,256]{1,0:T(8,128)S(1)}, u32[]{:S(2)}, u32[]{:S(2)}) collective-permute-start(f32[128,256]{1,0:T(8,128)S(1)} %stack_early.1), channel_id=1, source_target_pairs={{0,64},{1,65},{2,66},{3,67},{4,20},{5,21},{6,22},{7,23},{8,72},{9,... | collective-permute-start | bytes 393224 | tf_op jit(solution)/shard_map/ppermute | solution.py:31
  35.6 7.5 %collective-permute-start.11 = (f32[128,256]{1,0:T(8,128)S(1)}, f32[128,256]{1,0:T(8,128)S(1)}, u32[]{:S(2)}, u32[]{:S(2)}) collective-permute-start(f32[128,256]{1,0:T(8,128)S(1)} %stack_early.1), channel_id=1, source_target_pairs={{0,32},{1,33},{2,34},{3,35},{4,12},{5,13},{6,14},{7,15},{8,40},{9,... | collective-permute-start | bytes 393224 | tf_op jit(solution)/shard_map/ppermute | solution.py:31
  43.7 6.1 %collective-permute-start.16 = (bf16[128,512]{1,0:T(8,128)(2,1)S(1)}, bf16[128,512]{1,0:T(8,128)(2,1)S(1)}, u32[]{:S(2)}, u32[]{:S(2)}) collective-permute-start(bf16[128,512]{1,0:T(8,128)(2,1)S(1)} %second_sum.1), channel_id=1, source_target_pairs={{0,24},{1,25},{2,26},{3,27},{4,7},{5,6},{6,5},{7,4},{8,16},{9,17},... | collective-permute-start | bytes 393224 | tf_op jit(solution)/shard_map/ppermute | solution.py:31
  46.5 5.3 %collective-permute-start.15 = (bf16[128,512]{1,0:T(8,128)(2,1)S(1)}, bf16[128,512]{1,0:T(8,128)(2,1)S(1)}, u32[]{:S(2)}, u32[]{:S(2)}) collective-permute-start(bf16[128,512]{1,0:T(8,128)(2,1)S(1)} %second_sum.1), channel_id=1, source_target_pairs={{0,16},{1,17},{2,18},{3,19},{4,6},{5,7},{6,4},{7,5},{8,24},{9,25},... | collective-permute-start | bytes 393224 | tf_op jit(solution)/shard_map/ppermute | solution.py:31
  46.9 5.0 %collective-permute-start.14 = (bf16[128,512]{1,0:T(8,128)(2,1)S(1)}, bf16[128,512]{1,0:T(8,128)(2,1)S(1)}, u32[]{:S(2)}, u32[]{:S(2)}) collective-permute-start(bf16[128,512]{1,0:T(8,128)(2,1)S(1)} %second_sum.1), channel_id=1, source_target_pairs={{0,8},{1,9},{2,10},{3,11},{4,5},{5,4},{6,7},{7,6},{8,0},{9,1},{10,... | collective-permute-start | bytes 393224 | tf_op jit(solution)/shard_map/ppermute | solution.py:31
  47.2 8.8 %collective-permute-start.22 = (f32[128,256]{1,0:T(8,128)S(1)}, f32[128,256]{1,0:T(8,128)S(1)}, u32[]{:S(2)}, u32[]{:S(2)}) collective-permute-start(f32[128,256]{1,0:T(8,128)S(1)} %add_add_fusion.4), channel_id=1, source_target_pairs={{0,24},{1,25},{2,26},{3,27},{4,100},{5,101},{6,102},{7,103},{8,16}... | collective-permute-start | bytes 393224 | tf_op jit(solution)/shard_map/ppermute | solution.py:31
  51.9 20.8 %collective-permute-start.19 = (bf16[512,512]{1,0:T(8,128)(2,1)S(1)}, bf16[512,512]{1,0:T(8,128)(2,1)S(1)}, u32[]{:S(2)}, u32[]{:S(2)}) collective-permute-start(bf16[512,512]{1,0:T(8,128)(2,1)S(1)} %pad_maximum_fusion.m0), channel_id=1, source_target_pairs={{0,3},{1,2},{2,1},{3,0},{4,28},{5,29},{6,30},{7,31},{8,11},{9,10},... | collective-permute-start | bytes 1572872 | tf_op jit(solution)/shard_map/ppermute | solution.py:31
  53.4 19.3 %collective-permute-start.18 = (bf16[512,512]{1,0:T(8,128)(2,1)S(1)}, bf16[512,512]{1,0:T(8,128)(2,1)S(1)}, u32[]{:S(2)}, u32[]{:S(2)}) collective-permute-start(bf16[512,512]{1,0:T(8,128)(2,1)S(1)} %pad_maximum_fusion.m0), channel_id=1, source_target_pairs={{0,2},{1,3},{2,0},{3,1},{4,20},{5,21},{6,22},{7,23},{8,10},{9,11},... | collective-permute-start | bytes 1572872 | tf_op jit(solution)/shard_map/ppermute | solution.py:31
  53.9 18.7 %collective-permute-start.17 = (bf16[512,512]{1,0:T(8,128)(2,1)S(1)}, bf16[512,512]{1,0:T(8,128)(2,1)S(1)}, u32[]{:S(2)}, u32[]{:S(2)}) collective-permute-start(bf16[512,512]{1,0:T(8,128)(2,1)S(1)} %pad_maximum_fusion.m0), channel_id=1, source_target_pairs={{0,1},{1,0},{2,3},{3,2},{4,12},{5,13},{6,14},{7,15},{8,9},{9,8},{1... | collective-permute-start | bytes 1572872 | tf_op jit(solution)/shard_map/ppermute | solution.py:31
  55.2 5.3 %collective-permute-start.21 = (f32[128,256]{1,0:T(8,128)S(1)}, f32[128,256]{1,0:T(8,128)S(1)}, u32[]{:S(2)}, u32[]{:S(2)}) collective-permute-start(f32[128,256]{1,0:T(8,128)S(1)} %add_add_fusion.4), channel_id=1, source_target_pairs={{0,16},{1,17},{2,18},{3,19},{4,68},{5,69},{6,70},{7,71},{8,24},{9,... | collective-permute-start | bytes 393224 | tf_op jit(solution)/shard_map/ppermute | solution.py:31
  56.1 6.2 %collective-permute-start.20 = (f32[128,256]{1,0:T(8,128)S(1)}, f32[128,256]{1,0:T(8,128)S(1)}, u32[]{:S(2)}, u32[]{:S(2)}) collective-permute-start(f32[128,256]{1,0:T(8,128)S(1)} %add_add_fusion.4), channel_id=1, source_target_pairs={{0,8},{1,9},{2,10},{3,11},{4,36},{5,37},{6,38},{7,39},{8,0},{9,1},... | collective-permute-start | bytes 393224 | tf_op jit(solution)/shard_map/ppermute | solution.py:31
  62.2 9.8 %collective-permute-start.23 = (f32[128,256]{1,0:T(8,128)S(1)}, f32[128,256]{1,0:T(8,128)S(1)}, u32[]{:S(2)}, u32[]{:S(2)}) collective-permute-start(f32[128,256]{1,0:T(8,128)S(1)} %add_add_fusion.3.own_ref), channel_id=1, source_target_pairs={{0,4},{4,0},{8,12},{12,8},{16,20},{20,16},{24,28},{28,24},{32,36},... | collective-permute-start | bytes 393224 | tf_op jit(solution)/shard_map/ppermute | solution.py:378
  74.4 1.8 %collective-permute-start.24 = (f32[32,1024]{1,0:T(8,128)S(1)}, f32[32,1024]{1,0:T(8,128)S(1)}, u32[]{:S(2)}, u32[]{:S(2)}) collective-permute-start(f32[32,1024]{1,0:T(8,128)S(1)} %get-tuple-element.98), channel_id=1, source_target_pairs={{0,4},{4,0},{8,12},{12,8},{16,20},{20,16},{24,28},{28,24},{32,36},... | collective-permute-start | bytes 393224 | tf_op jit(solution)/shard_map/ppermute | solution.py:299
  76.2 8.4 %collective-permute-start.27 = (f32[32,1024]{1,0:T(8,128)S(1)}, f32[32,1024]{1,0:T(8,128)S(1)}, u32[]{:S(2)}, u32[]{:S(2)}) collective-permute-start(f32[32,1024]{1,0:T(8,128)S(1)} %add.64), channel_id=1, source_target_pairs={{0,96},{1,97},{2,98},{3,99},{4,100},{5,101},{6,102},{7,103},{8,104... | collective-permute-start | bytes 393224 | tf_op jit(solution)/shard_map/ppermute | solution.py:31
  77.2 7.4 %collective-permute-start.26 = (f32[32,1024]{1,0:T(8,128)S(1)}, f32[32,1024]{1,0:T(8,128)S(1)}, u32[]{:S(2)}, u32[]{:S(2)}) collective-permute-start(f32[32,1024]{1,0:T(8,128)S(1)} %add.64), channel_id=1, source_target_pairs={{0,64},{1,65},{2,66},{3,67},{4,68},{5,69},{6,70},{7,71},{8,72},{9,... | collective-permute-start | bytes 393224 | tf_op jit(solution)/shard_map/ppermute | solution.py:31
  78.5 6.9 %collective-permute-start.25 = (f32[32,1024]{1,0:T(8,128)S(1)}, f32[32,1024]{1,0:T(8,128)S(1)}, u32[]{:S(2)}, u32[]{:S(2)}) collective-permute-start(f32[32,1024]{1,0:T(8,128)S(1)} %add.64), channel_id=1, source_target_pairs={{0,32},{1,33},{2,34},{3,35},{4,36},{5,37},{6,38},{7,39},{8,40},{9,... | collective-permute-start | bytes 393224 | tf_op jit(solution)/shard_map/ppermute | solution.py:31
  85.4 2.7 %collective-permute-start.28 = (f32[32,1024]{1,0:T(8,128)S(1)}, f32[32,1024]{1,0:T(8,128)S(1)}, u32[]{:S(2)}, u32[]{:S(2)}) collective-permute-start(f32[32,1024]{1,0:T(8,128)S(1)} %add_add_fusion.2.own_in), channel_id=1, source_target_pairs={{0,4},{4,0},{8,12},{12,8},{16,20},{20,16},{24,28},{28,24},{32,36},... | collective-permute-start | bytes 393224 | tf_op jit(solution)/shard_map/ppermute | solution.py:305
  90.1 1.4 %collective-permute-start.29 = (f32[32,1024]{1,0:T(8,128)S(1)}, f32[32,1024]{1,0:T(8,128)S(1)}, u32[]{:S(2)}, u32[]{:S(2)}) collective-permute-start(f32[32,1024]{1,0:T(8,128)S(1)} %get-tuple-element.105), channel_id=1, source_target_pairs={{0,4},{4,0},{8,12},{12,8},{16,20},{20,16},{24,28},{28,24},{32,36},... | collective-permute-start | bytes 393224 | tf_op jit(solution)/shard_map/ppermute | solution.py:299
  91.5 8.4 %collective-permute-start.32 = (f32[32,1024]{1,0:T(8,128)S(1)}, f32[32,1024]{1,0:T(8,128)S(1)}, u32[]{:S(2)}, u32[]{:S(2)}) collective-permute-start(f32[32,1024]{1,0:T(8,128)S(1)} %add.68), channel_id=1, source_target_pairs={{0,96},{1,97},{2,98},{3,99},{4,100},{5,101},{6,102},{7,103},{8,104... | collective-permute-start | bytes 393224 | tf_op jit(solution)/shard_map/ppermute | solution.py:31
  92.6 7.4 %collective-permute-start.31 = (f32[32,1024]{1,0:T(8,128)S(1)}, f32[32,1024]{1,0:T(8,128)S(1)}, u32[]{:S(2)}, u32[]{:S(2)}) collective-permute-start(f32[32,1024]{1,0:T(8,128)S(1)} %add.68), channel_id=1, source_target_pairs={{0,64},{1,65},{2,66},{3,67},{4,68},{5,69},{6,70},{7,71},{8,72},{9,... | collective-permute-start | bytes 393224 | tf_op jit(solution)/shard_map/ppermute | solution.py:31
  93.8 6.9 %collective-permute-start.30 = (f32[32,1024]{1,0:T(8,128)S(1)}, f32[32,1024]{1,0:T(8,128)S(1)}, u32[]{:S(2)}, u32[]{:S(2)}) collective-permute-start(f32[32,1024]{1,0:T(8,128)S(1)} %add.68), channel_id=1, source_target_pairs={{0,32},{1,33},{2,34},{3,35},{4,36},{5,37},{6,38},{7,39},{8,40},{9,... | collective-permute-start | bytes 393224 | tf_op jit(solution)/shard_map/ppermute | solution.py:31
  100.7 2.5 %collective-permute-start.33 = (f32[32,1024]{1,0:T(8,128)S(1)}, f32[32,1024]{1,0:T(8,128)S(1)}, u32[]{:S(2)}, u32[]{:S(2)}) collective-permute-start(f32[32,1024]{1,0:T(8,128)S(1)} %add_add_fusion.1.own_in), channel_id=1, source_target_pairs={{0,4},{4,0},{8,12},{12,8},{16,20},{20,16},{24,28},{28,24},{32,36},... | collective-permute-start | bytes 393224 | tf_op jit(solution)/shard_map/ppermute | solution.py:305
  105.3 1.4 %collective-permute-start.34 = (f32[32,1024]{1,0:T(8,128)S(1)}, f32[32,1024]{1,0:T(8,128)S(1)}, u32[]{:S(2)}, u32[]{:S(2)}) collective-permute-start(f32[32,1024]{1,0:T(8,128)S(1)} %get-tuple-element.113), channel_id=1, source_target_pairs={{0,4},{4,0},{8,12},{12,8},{16,20},{20,16},{24,28},{28,24},{32,36},... | collective-permute-start | bytes 393224 | tf_op jit(solution)/shard_map/ppermute | solution.py:299
  106.7 8.4 %collective-permute-start.37 = (f32[32,1024]{1,0:T(8,128)S(1)}, f32[32,1024]{1,0:T(8,128)S(1)}, u32[]{:S(2)}, u32[]{:S(2)}) collective-permute-start(f32[32,1024]{1,0:T(8,128)S(1)} %add.72), channel_id=1, source_target_pairs={{0,96},{1,97},{2,98},{3,99},{4,100},{5,101},{6,102},{7,103},{8,104... | collective-permute-start | bytes 393224 | tf_op jit(solution)/shard_map/ppermute | solution.py:31
  107.8 7.4 %collective-permute-start.36 = (f32[32,1024]{1,0:T(8,128)S(1)}, f32[32,1024]{1,0:T(8,128)S(1)}, u32[]{:S(2)}, u32[]{:S(2)}) collective-permute-start(f32[32,1024]{1,0:T(8,128)S(1)} %add.72), channel_id=1, source_target_pairs={{0,64},{1,65},{2,66},{3,67},{4,68},{5,69},{6,70},{7,71},{8,72},{9,... | collective-permute-start | bytes 393224 | tf_op jit(solution)/shard_map/ppermute | solution.py:31
  108.9 7.0 %collective-permute-start.35 = (f32[32,1024]{1,0:T(8,128)S(1)}, f32[32,1024]{1,0:T(8,128)S(1)}, u32[]{:S(2)}, u32[]{:S(2)}) collective-permute-start(f32[32,1024]{1,0:T(8,128)S(1)} %add.72), channel_id=1, source_target_pairs={{0,32},{1,33},{2,34},{3,35},{4,36},{5,37},{6,38},{7,39},{8,40},{9,... | collective-permute-start | bytes 393224 | tf_op jit(solution)/shard_map/ppermute | solution.py:31
  115.9 2.5 %collective-permute-start.38 = (f32[32,1024]{1,0:T(8,128)S(1)}, f32[32,1024]{1,0:T(8,128)S(1)}, u32[]{:S(2)}, u32[]{:S(2)}) collective-permute-start(f32[32,1024]{1,0:T(8,128)S(1)} %add_add_fusion.own_in), channel_id=1, source_target_pairs={{0,4},{4,0},{8,12},{12,8},{16,20},{20,16},{24,28},{28,24},{32,36},... | collective-permute-start | bytes 393224 | tf_op jit(solution)/shard_map/ppermute | solution.py:305
  121.3 4.5 %collective-permute-start.42 = (bf16[32,512]{1,0:T(8,128)(2,1)S(1)}, bf16[32,512]{1,0:T(8,128)(2,1)S(1)}, u32[]{:S(2)}, u32[]{:S(2)}) collective-permute-start(bf16[32,512]{1,0:T(8,128)(2,1)S(1)} %get-tuple-element.122.refs_0_), channel_id=1, source_target_pairs={{0,4},{4,0},{8,12},{12,8},{16,20},{20,16},{24,28},{28,24},{32,36},... | collective-permute-start | bytes 98312 | tf_op jit(solution)/shard_map/ppermute | solution.py:389
  121.7 7.0 %collective-permute-start.41 = (bf16[32,512]{1,0:T(8,128)(2,1)S(1)}, bf16[32,512]{1,0:T(8,128)(2,1)S(1)}, u32[]{:S(2)}, u32[]{:S(2)}) collective-permute-start(bf16[32,512]{1,0:T(8,128)(2,1)S(1)} %get-tuple-element.122.refs_0_), channel_id=1, source_target_pairs={{0,96},{1,97},{2,98},{3,99},{4,100},{5,101},{6,102},{7,103},{8,104... | collective-permute-start | bytes 98312 | tf_op jit(solution)/shard_map/ppermute | solution.py:31
  122.7 6.0 %collective-permute-start.40 = (bf16[32,512]{1,0:T(8,128)(2,1)S(1)}, bf16[32,512]{1,0:T(8,128)(2,1)S(1)}, u32[]{:S(2)}, u32[]{:S(2)}) collective-permute-start(bf16[32,512]{1,0:T(8,128)(2,1)S(1)} %get-tuple-element.122.refs_0_), channel_id=1, source_target_pairs={{0,64},{1,65},{2,66},{3,67},{4,68},{5,69},{6,70},{7,71},{8,72},{9,... | collective-permute-start | bytes 98312 | tf_op jit(solution)/shard_map/ppermute | solution.py:31
  123.8 4.9 %collective-permute-start.39 = (bf16[32,512]{1,0:T(8,128)(2,1)S(1)}, bf16[32,512]{1,0:T(8,128)(2,1)S(1)}, u32[]{:S(2)}, u32[]{:S(2)}) collective-permute-start(bf16[32,512]{1,0:T(8,128)(2,1)S(1)} %get-tuple-element.122.refs_0_), channel_id=1, source_target_pairs={{0,32},{1,33},{2,34},{3,35},{4,36},{5,37},{6,38},{7,39},{8,40},{9,... | collective-permute-start | bytes 98312 | tf_op jit(solution)/shard_map/ppermute | solution.py:31
  128.7 1.9 %collective-permute-start.43 = (bf16[32,512]{1,0:T(8,128)(2,1)S(1)}, bf16[32,512]{1,0:T(8,128)(2,1)S(1)}, u32[]{:S(2)}, u32[]{:S(2)}) collective-permute-start(bf16[32,512]{1,0:T(8,128)(2,1)S(1)} %collective-permute-done.39.refs_0_), channel_id=1, source_target_pairs={{0,4},{4,0},{8,12},{12,8},{16,20},{20,16},{24,28},{28,24},{32,36},... | collective-permute-start | bytes 98312 | tf_op jit(solution)/shard_map/ppermute | solution.py:393
  129.8 1.2 collective-permute-start.44
  129.9 1.3 collective-permute-start.45

commit v6 on v5

--- a/solution.py
+++ b/solution.py
@@ -16,7 +16,7 @@
 ROWS_OWN = ROWS // N_OWNER
 PIECE = ROWS_OWN // 4
 MID = ROWS // 2
-PANEL = 8
+PANEL = 16
 BF = jnp.bfloat16
 F32 = jnp.float32
 HIGHEST = lax.Precision.HIGHEST
@@ -158,22 +158,6 @@
     return call(body, "stack_early", jax.ShapeDtypeStruct((4 * RANK, ROWS_OWN // 2), F32), place, *parts)
 
 
-def assemble_left(place, own, oth):
-    def body(place_ref, own_ref, oth_ref, o_ref, sum_ref):
-        core, half = place_ref[2], ROWS_OWN // 2
-        for y in range(4):
-            rows = slice(y * RANK, (y + 1) * RANK)
-            sum_ref[:, cut(2 * y + core, half)] = own_ref[rows, :]
-            sum_ref[:, cut(2 * y + 1 - core, half)] = oth_ref[rows, :]
-        for y in range(4):
-            for x in range(4):
-                i = 4 * y + x
-                o_ref[:, i * PIECE : (i + 1) * PIECE] = sum_ref[:, cut(4 * y + (place_ref[1] ^ x), PIECE)]
-
-    shape = jax.ShapeDtypeStruct((RANK, ROWS), F32)
-    return call(body, "assemble_left", shape, place, own, oth, scratch=[pltpu.VMEM((RANK, ROWS), F32)], cost=SMALL)
-
-
 def thirds(x):
     high = x.astype(BF)
     rest = x - high.astype(F32)
@@ -254,11 +238,20 @@
     store_halves(place_ref, add_thirds(times_m_t(thirds(right), m_refs)), own_ref, oth_ref)
 
 
-def second_left(place, left, m):
-    def body(place_ref, left_ref, m0, m1, m2, m3, own_ref, oth_ref):
+def second_left(place, own, oth, m):
+    def body(place_ref, own_in, oth_in, m0, m1, m2, m3, left_ref, own_ref, oth_ref, sum_ref):
+        core, half = place_ref[2], ROWS_OWN // 2
+        for y in range(4):
+            rows = slice(y * RANK, (y + 1) * RANK)
+            sum_ref[:, cut(2 * y + core, half)] = own_in[rows, :]
+            sum_ref[:, cut(2 * y + 1 - core, half)] = oth_in[rows, :]
+        for i in range(16):
+            source = cut(i // 4 * 4 + (place_ref[1] ^ (i % 4)), PIECE)
+            left_ref[:, i * PIECE : (i + 1) * PIECE] = sum_ref[:, source]
         from_left(place_ref, left_ref[...], (m0, m1, m2, m3), own_ref, oth_ref)
 
-    return call(body, "second_left", HALVES, place, left, *m)
+    shapes = [jax.ShapeDtypeStruct((RANK, ROWS), F32)] + HALVES
+    return call(body, "second_left", shapes, place, own, oth, *m, scratch=[pltpu.VMEM((RANK, ROWS), F32)])
 
 
 def next_left(place, own, oth, inverse, m):
@@ -305,20 +298,19 @@
     return own, lax.ppermute(own, "dp", CORE), beside
 
 
-def columns_of(place, left, inverse):
-    def body(place_ref, left_ref, inv_ref, out_ref):
-        out_ref[...] = dot(inv_ref[...], left_ref[...], ((1,), (0,)), HIGHEST).T.astype(BF)
-
-    return call(body, "columns_of", jax.ShapeDtypeStruct((ROWS_OWN, RANK), BF), place, left, inverse)
-
-
 def finish(place, ortho, rights, mine, other, outs, name):
     keys = list(rights)
-    count, kept = len(keys), len(outs)
-
-    def body(place_ref, o_ref, *refs):
+    count, kept, made = len(keys), len(outs), len(ortho) == 2
+
+    def body(place_ref, *refs):
+        ortho_refs, refs = refs[: len(ortho)], refs[len(ortho) :]
         rights, memory, refs = refs[:count], refs[count : count + 2], refs[count + 2 + kept :]
-        up_hbm, err_hbm, right_hbm, up_ref, err_ref, right_ref, sems = refs
+        up_hbm, err_hbm, right_hbm = refs[:3]
+        up_ref, err_ref, right_ref, sems = refs[-4:]
+        o_ref = ortho_refs[0]
+        if made:
+            o_ref = refs[3]
+            o_ref[...] = dot(ortho_refs[1][...], ortho_refs[0][...], ((1,), (0,)), HIGHEST).T.astype(BF)
         copies = []
 
         def send(i, n, source, target):
@@ -341,18 +333,19 @@
     blocks = pltpu.VMEM((count, ROWS_OWN, COLS), F32)
     return pl.pallas_call(
         body,
-        in_specs=[SCALARS] + [WHOLE] * (count + 3) + [HBM] * kept,
-        out_specs=[HBM] * 3,
+        in_specs=[SCALARS] + [WHOLE] * (len(ortho) + count + 2) + [HBM] * kept,
+        out_specs=[HBM] * 3 + [WHOLE] * made,
         scratch_shapes=[blocks, blocks, pltpu.VMEM((count, RANK, COLS), F32), pltpu.SemaphoreType.DMA((3, count))],
         out_shape=(
             jax.ShapeDtypeStruct((ROWS_OWN, W), F32),
             jax.ShapeDtypeStruct((ROWS_OWN, W), F32),
             jax.ShapeDtypeStruct((RANK, W), F32),
-        ),
+        )
+        + (jax.ShapeDtypeStruct((ROWS_OWN, RANK), BF),) * made,
         input_output_aliases={count + 4 + i: i for i in range(kept)},
         compiler_params=params(),
         name=name,
-    )(place, ortho, *rights.values(), mine, other, *outs)
+    )(place, *ortho, *rights.values(), mine, other, *outs)
 
 
 def per_device(grad, error, warm_right):
@@ -375,23 +368,23 @@
     early = spread((early[0] + early[1]) + (early[2] + early[3]), "x", "z")
     m = jnp.concatenate(spread(piece, "x", "y"), axis=0)
     early = (early[0] + early[1]) + (early[2] + early[3])
-    left = assemble_left(place, early, lax.ppermute(early, "dp", CORE))
+    passed = lax.ppermute(early, "dp", CORE)
     m = spread(m, "y", "x")
-    m, left = lax.optimization_barrier((m, left))
-
-    own, oth, inverse = sum_over_group(*second_left(place, left, m), inverse_of(place, left))
+    m, early, passed = lax.optimization_barrier((m, early, passed))
+
+    left, own, oth = second_left(place, early, passed, m)
+    own, oth, inverse = sum_over_group(own, oth, inverse_of(place, left))
     for step in range(ITERS - 2):
         left, own, oth = next_left(place, own, oth, inverse, m)
         own, oth, inverse = sum_over_group(own, oth, inverse_of(place, left))
     right, left, inverse = last_right(place, own, oth, inverse, m)
 
-    ortho = columns_of(place, left, inverse)
     near = {(0, 0): right, (0, 1): lax.ppermute(right, "dp", CORE)}
-    outs = finish(place, ortho, near, mine, other, [], "finish_near")
+    *outs, ortho = finish(place, [left, inverse], near, mine, other, [], "finish_near")
     rights, outs = lax.optimization_barrier((spread(right, "z", "z"), outs))
     far = {(k, 0): rights[k] for k in (1, 2, 3)}
     far.update({(k, 1): lax.ppermute(rights[k], "dp", CORE) for k in (1, 2, 3)})
-    update, new_error, right_t = finish(place, ortho, far, mine, other, outs, "finish_far")
+    update, new_error, right_t = finish(place, [ortho], far, mine, other, outs, "finish_far")
     return update, new_error[None], right_t.T
 
 

time: 137 us -> 136 us (level)
  Pallas kernels: 34.1 us -> 32.2 us
    pallas_call x14 -> x12, Pallas kernels: 20.9 us -> 18.7 us  [call(): pl.pallas_call(body, in_specs=[SCALARS] + [WHOLE] * len(arrays), out_spec...]
  transfers between devices with their start and end apart: 46 -> 46, of which waited for: 30 -> 30; matrix products, arithmetic and copies ran while one was open for 0% -> 0% of each run, Pallas kernels for 10% -> 9%
where the time goes in v6:
time: 136 us
  starting transfers between devices  62.1 us (46%)
  waiting for transfers between devices  40.6 us (30%)
  Pallas kernels  32.2 us (24%)
    ppermute x33, starting transfers between devices, along(): return lax.ppermute(array, ('dp', 'owner'), pairs)  40.5 us
    ppermute x33, waiting for transfers between devices, along(): return lax.ppermute(array, ('dp', 'owner'), pairs)  30.5 us
    pallas_call x12, Pallas kernels, call(): pl.pallas_call(body, in_specs=[SCALARS] + [WHOLE] * len(arrays), out_spec...  18.7 us
    ppermute x1, starting transfers between devices, per_device(): passed = lax.ppermute(early, 'dp', CORE)  8.81 us
    pallas_call x2, Pallas kernels, finish(): pl.pallas_call(body, in_specs=[SCALARS] + [WHOLE] * (len(ortho) + count +...  8.78 us
    ppermute x3, starting transfers between devices, sum_over_group(): return (own, lax.ppermute(own, 'dp', CORE), beside)  4.81 us
    pallas_call x2, Pallas kernels, half_of_memory(): pl.pallas_call(body, in_specs=[SCALARS, HBM, HBM], out_specs=WHOLE, scrat...  4.67 us
    ppermute x3, waiting for transfers between devices, sum_over_group(): own = own + lax.ppermute(oth, 'dp', CORE)  2.96 us
  transfers between devices with their start and end apart: 46, of which 30 were waited for; matrix products, arithmetic and copies ran while one was open for 0% of the time, Pallas kernels for 9%

profile of v6, /device:TPU:1, one launch (start us, length us, event | category | flops | bytes accessed | tf_op | source)
XLA Modules:
  0.0 136.2 jit_solution(11191159448258175975)
XLA Ops:
  0.6 2.3 %half_of_memory.3.refs_5_.refs_8_ = bf16[512,2048]{1,0:T(8,128)(2,1)S(1)} custom-call(s32[1]{0:T(128)} %bitcast.5.which_ref, bf16[512,4096]{1,0:T(8,128)(2,1)} %bitcast.10, bf16[512,4096]{1,0:T(8,128)(2,1)} %bitcast.12), custom_call_target="tpu_custom_call" | custom-call | tf_op jit(solution)/shard_map/half_of_memory/pallas_call | solution.py:74
  3.0 1.5 %collective-permute-start = (bf16[512,2048]{1,0:T(8,128)(2,1)S(1)}, bf16[512,2048]{1,0:T(8,128)(2,1)}, u32[]{:S(2)}, u32[]{:S(2)}) collective-permute-start(bf16[512,2048]{1,0:T(8,128)(2,1)S(1)} %half_of_memory.3.refs_5_.refs_8_), channel_id=1, source_target_pairs={{0,4},{4,0},{8,12},{12,8},{16,20},{20,16},{24,28},{28,24},{32,36},... | collective-permute-start | bytes 6291464 | tf_op jit(solution)/shard_map/ppermute | solution.py:357
  4.5 2.3 %half_of_memory.2.a_ref.refs_4_.refs_7_ = bf16[512,2048]{1,0:T(8,128)(2,1)S(1)} custom-call(s32[1]{0:T(128)} %bitcast.2.which_ref, bf16[512,4096]{1,0:T(8,128)(2,1)} %bitcast.11, bf16[512,4096]{1,0:T(8,128)(2,1)} %bitcast.13), custom_call_target="tpu_custom_call" | custom-call | tf_op jit(solution)/shard_map/half_of_memory/pallas_call | solution.py:74
  6.9 1.5 %collective-permute-done.b_ref = bf16[512,2048]{1,0:T(8,128)(2,1)} collective-permute-done((bf16[512,2048]{1,0:T(8,128)(2,1)S(1)}, bf16[512,2048]{1,0:T(8,128)(2,1)}, u32[]{:S(2)}, u32[]{:S(2)}) %collective-permute-start) | collective-permute-done | bytes 2097184 | tf_op jit(solution)/shard_map/ppermute | solution.py:357
  8.4 1.9 %pair_sum.1 = (bf16[4,128,512]{2,1,0:T(8,128)(2,1)S(1)}, bf16[4,128,512]{2,1,0:T(8,128)(2,1)S(1)}, bf16[4,128,512]{2,1,0:T(8,128)(2,1)S(1)}, bf16[4,128,512]{2,1,0:T(8,128)(2,1)S(1)}) custom-call(s32[3]{0:T(128)S(1)} %pad_add_fusion.place_ref, bf16[512,2048]{1,0:T(8,128)(2,1)S(1)} %half_of_memory.2.a_ref.refs_4_.refs_7_, ...), custom_call_target="tpu_custom_call" | custom-call | tf_op jit(solution)/shard_map/pair_sum/pallas_call | solution.py:86
  10.3 1.4 %collective-permute-start.1 = (bf16[4,128,512]{2,1,0:T(8,128)(2,1)S(1)}, bf16[4,128,512]{2,1,0:T(8,128)(2,1)S(1)}, u32[]{:S(2)}, u32[]{:S(2)}) collective-permute-start(bf16[4,128,512]{2,1,0:T(8,128)(2,1)S(1)} %get-tuple-element.73.refs_1_), channel_id=1, source_target_pairs={{0,32},{1,33},{2,34},{3,35},{4,12},{5,13},{6,14},{7,15},{8,40},{9,... | collective-permute-start | bytes 1572872 | tf_op jit(solution)/shard_map/ppermute | solution.py:31
  11.7 2.5 %collective-permute-start.2 = (bf16[4,128,512]{2,1,0:T(8,128)(2,1)S(1)}, bf16[4,128,512]{2,1,0:T(8,128)(2,1)S(1)}, u32[]{:S(2)}, u32[]{:S(2)}) collective-permute-start(bf16[4,128,512]{2,1,0:T(8,128)(2,1)S(1)} %get-tuple-element.74.refs_2_), channel_id=1, source_target_pairs={{0,64},{1,65},{2,66},{3,67},{4,20},{5,21},{6,22},{7,23},{8,72},{9,... | collective-permute-start | bytes 1572872 | tf_op jit(solution)/shard_map/ppermute | solution.py:31
  14.2 1.4 early_left.1
  15.6 2.2 %collective-permute-start.4 = (f32[32,256]{1,0:T(8,128)S(1)}, f32[32,256]{1,0:T(8,128)S(1)}, u32[]{:S(2)}, u32[]{:S(2)}) collective-permute-start(f32[32,256]{1,0:T(8,128)S(1)} %get-tuple-element.77), channel_id=1, source_target_pairs={{0,4},{4,0},{8,12},{12,8},{16,20},{20,16},{24,28},{28,24},{32,36},... | collective-permute-start | bytes 98312 | tf_op jit(solution)/shard_map/ppermute | solution.py:361
  17.8 0.9 collective-permute-done.4
  18.7 2.7 %collective-permute-start.7 = (f32[32,256]{1,0:T(8,128)S(1)}, f32[32,256]{1,0:T(8,128)S(1)}, u32[]{:S(2)}, u32[]{:S(2)}) collective-permute-start(f32[32,256]{1,0:T(8,128)S(1)} %add.57.a_ref), channel_id=1, source_target_pairs={{0,3},{1,2},{2,1},{3,0},{4,7},{5,6},{6,5},{7,4},{8,11},{9,10},{10,... | collective-permute-start | bytes 98312 | tf_op jit(solution)/shard_map/ppermute | solution.py:31
  21.8 1.2 collective-permute-done.7.d_ref
  23.0 2.9 %collective-permute-done.6.c_ref = f32[32,256]{1,0:T(8,128)S(1)} collective-permute-done((f32[32,256]{1,0:T(8,128)S(1)}, f32[32,256]{1,0:T(8,128)S(1)}, u32[]{:S(2)}, u32[]{:S(2)}) %collective-permute-start.6) | collective-permute-done | bytes 32800 | tf_op jit(solution)/shard_map/ppermute | solution.py:31
  26.6 2.6 %collective-permute-done.3.refs_3_ = bf16[4,128,512]{2,1,0:T(8,128)(2,1)S(1)} collective-permute-done((bf16[4,128,512]{2,1,0:T(8,128)(2,1)S(1)}, bf16[4,128,512]{2,1,0:T(8,128)(2,1)S(1)}, u32[]{:S(2)}, u32[]{:S(2)}) %collective-permute-start.3) | collective-permute-done | bytes 524320 | tf_op jit(solution)/shard_map/ppermute | solution.py:31
  30.1 1.4 %collective-permute-start.8 = (bf16[128,512]{1,0:T(8,128)(2,1)S(1)}, bf16[128,512]{1,0:T(8,128)(2,1)S(1)}, u32[]{:S(2)}, u32[]{:S(2)}) collective-permute-start(bf16[128,512]{1,0:T(8,128)(2,1)S(1)} %get-tuple-element.83), channel_id=1, source_target_pairs={{0,8},{1,9},{2,10},{3,11},{4,36},{5,37},{6,38},{7,39},{8,0},{9,1},... | collective-permute-start | bytes 393224 | tf_op jit(solution)/shard_map/ppermute | solution.py:31
  31.5 3.3 %collective-permute-start.9 = (bf16[128,512]{1,0:T(8,128)(2,1)S(1)}, bf16[128,512]{1,0:T(8,128)(2,1)S(1)}, u32[]{:S(2)}, u32[]{:S(2)}) collective-permute-start(bf16[128,512]{1,0:T(8,128)(2,1)S(1)} %get-tuple-element.84), channel_id=1, source_target_pairs={{0,16},{1,17},{2,18},{3,19},{4,68},{5,69},{6,70},{7,71},{8,24},{9,... | collective-permute-start | bytes 393224 | tf_op jit(solution)/shard_map/ppermute | solution.py:31
  35.6 2.4 %collective-permute-start.11 = (f32[128,256]{1,0:T(8,128)S(1)}, f32[128,256]{1,0:T(8,128)S(1)}, u32[]{:S(2)}, u32[]{:S(2)}) collective-permute-start(f32[128,256]{1,0:T(8,128)S(1)} %stack_early.1), channel_id=1, source_target_pairs={{0,32},{1,33},{2,34},{3,35},{4,12},{5,13},{6,14},{7,15},{8,40},{9,... | collective-permute-start | bytes 393224 | tf_op jit(solution)/shard_map/ppermute | solution.py:31
  38.6 1.4 %collective-permute-done.10.d_ref = bf16[128,512]{1,0:T(8,128)(2,1)S(1)} collective-permute-done((bf16[128,512]{1,0:T(8,128)(2,1)S(1)}, bf16[128,512]{1,0:T(8,128)(2,1)S(1)}, u32[]{:S(2)}, u32[]{:S(2)}) %collective-permute-start.10) | collective-permute-done | bytes 131104 | tf_op jit(solution)/shard_map/ppermute | solution.py:31
  40.0 2.6 %collective-permute-done.13 = f32[128,256]{1,0:T(8,128)S(1)} collective-permute-done((f32[128,256]{1,0:T(8,128)S(1)}, f32[128,256]{1,0:T(8,128)S(1)}, u32[]{:S(2)}, u32[]{:S(2)}) %collective-permute-start.13) | collective-permute-done | bytes 131104 | tf_op jit(solution)/shard_map/ppermute | solution.py:31
  43.7 2.8 %collective-permute-start.16 = (bf16[128,512]{1,0:T(8,128)(2,1)S(1)}, bf16[128,512]{1,0:T(8,128)(2,1)S(1)}, u32[]{:S(2)}, u32[]{:S(2)}) collective-permute-start(bf16[128,512]{1,0:T(8,128)(2,1)S(1)} %second_sum.1), channel_id=1, source_target_pairs={{0,24},{1,25},{2,26},{3,27},{4,7},{5,6},{6,5},{7,4},{8,16},{9,17},... | collective-permute-start | bytes 393224 | tf_op jit(solution)/shard_map/ppermute | solution.py:31
  47.2 2.4 %collective-permute-start.22 = (f32[128,256]{1,0:T(8,128)S(1)}, f32[128,256]{1,0:T(8,128)S(1)}, u32[]{:S(2)}, u32[]{:S(2)}) collective-permute-start(f32[128,256]{1,0:T(8,128)S(1)} %add_add_fusion.4), channel_id=1, source_target_pairs={{0,24},{1,25},{2,26},{3,27},{4,100},{5,101},{6,102},{7,103},{8,16}... | collective-permute-start | bytes 393224 | tf_op jit(solution)/shard_map/ppermute | solution.py:31
  49.8 2.0 %collective-permute-done.15 = bf16[128,512]{1,0:T(8,128)(2,1)S(1)} collective-permute-done((bf16[128,512]{1,0:T(8,128)(2,1)S(1)}, bf16[128,512]{1,0:T(8,128)(2,1)S(1)}, u32[]{:S(2)}, u32[]{:S(2)}) %collective-permute-start.15) | collective-permute-done | bytes 131104 | tf_op jit(solution)/shard_map/ppermute | solution.py:31
  51.9 1.5 %collective-permute-start.19 = (bf16[512,512]{1,0:T(8,128)(2,1)S(1)}, bf16[512,512]{1,0:T(8,128)(2,1)S(1)}, u32[]{:S(2)}, u32[]{:S(2)}) collective-permute-start(bf16[512,512]{1,0:T(8,128)(2,1)S(1)} %pad_maximum_fusion.m0), channel_id=1, source_target_pairs={{0,3},{1,2},{2,1},{3,0},{4,28},{5,29},{6,30},{7,31},{8,11},{9,10},... | collective-permute-start | bytes 1572872 | tf_op jit(solution)/shard_map/ppermute | solution.py:31
  53.9 1.3 collective-permute-start.17
  56.1 2.1 %collective-permute-start.20 = (f32[128,256]{1,0:T(8,128)S(1)}, f32[128,256]{1,0:T(8,128)S(1)}, u32[]{:S(2)}, u32[]{:S(2)}) collective-permute-start(f32[128,256]{1,0:T(8,128)S(1)} %add_add_fusion.4), channel_id=1, source_target_pairs={{0,8},{1,9},{2,10},{3,11},{4,36},{5,37},{6,38},{7,39},{8,0},{9,1},... | collective-permute-start | bytes 393224 | tf_op jit(solution)/shard_map/ppermute | solution.py:31
  58.2 2.4 %collective-permute-done.21 = f32[128,256]{1,0:T(8,128)S(1)} collective-permute-done((f32[128,256]{1,0:T(8,128)S(1)}, f32[128,256]{1,0:T(8,128)S(1)}, u32[]{:S(2)}, u32[]{:S(2)}) %collective-permute-start.21) | collective-permute-done | bytes 131104 | tf_op jit(solution)/shard_map/ppermute | solution.py:31
  60.5 1.7 %collective-permute-done.20 = f32[128,256]{1,0:T(8,128)S(1)} collective-permute-done((f32[128,256]{1,0:T(8,128)S(1)}, f32[128,256]{1,0:T(8,128)S(1)}, u32[]{:S(2)}, u32[]{:S(2)}) %collective-permute-start.20) | collective-permute-done | bytes 131104 | tf_op jit(solution)/shard_map/ppermute | solution.py:31
  62.2 8.8 %collective-permute-start.23 = (f32[128,256]{1,0:T(8,128)S(1)}, f32[128,256]{1,0:T(8,128)S(1)}, u32[]{:S(2)}, u32[]{:S(2)}) collective-permute-start(f32[128,256]{1,0:T(8,128)S(1)} %add_add_fusion.3.own_in), channel_id=1, source_target_pairs={{0,4},{4,0},{8,12},{12,8},{16,20},{20,16},{24,28},{28,24},{32,36},... | collective-permute-start | bytes 393224 | tf_op jit(solution)/shard_map/ppermute | solution.py:371
  71.1 1.0 collective-permute-done.23.oth_in
  72.1 1.7 %second_left.1 = (f32[32,2048]{1,0:T(8,128)S(1)}, f32[32,1024]{1,0:T(8,128)S(1)}, f32[32,1024]{1,0:T(8,128)S(1)}) custom-call(s32[3]{0:T(128)S(1)} %pad_add_fusion.place_ref, f32[128,256]{1,0:T(8,128)S(1)} %add_add_fusion.3.own_in, f32[128,256]{1,0:T(8,128)S(1)} %collective-permute-done.23.oth_in, bf16[512,512]{1,0:T(8,128)(2,1)S(1)} %pad_maximum_fusion.m0, ...), custom_call_target="tpu_custom_call" | custom-call | tf_op jit(solution)/shard_map/second_left/pallas_call | solution.py:86
  73.8 1.4 %collective-permute-start.24 = (f32[32,1024]{1,0:T(8,128)S(1)}, f32[32,1024]{1,0:T(8,128)S(1)}, u32[]{:S(2)}, u32[]{:S(2)}) collective-permute-start(f32[32,1024]{1,0:T(8,128)S(1)} %get-tuple-element.102), channel_id=1, source_target_pairs={{0,4},{4,0},{8,12},{12,8},{16,20},{20,16},{24,28},{28,24},{32,36},... | collective-permute-start | bytes 393224 | tf_op jit(solution)/shard_map/ppermute | solution.py:292
  75.2 1.0 collective-permute-done.24
  76.2 1.1 collective-permute-start.27
  77.3 1.1 collective-permute-start.26
  78.4 1.1 collective-permute-start.25
  79.5 1.7 %inverse_of.3.inv_ref = f32[32,32]{1,0:T(8,128)S(1)} custom-call(s32[3]{0:T(128)S(1)} %pad_add_fusion.place_ref, f32[32,2048]{1,0:T(8,128)S(1)} %get-tuple-element.103.left_ref), custom_call_target="tpu_custom_call" | custom-call | flops 1000 | bytes 1000 | tf_op jit(solution)/shard_map/inverse_of/pallas_call | solution.py:86
  81.3 3.4 %collective-permute-done.27 = f32[32,1024]{1,0:T(8,128)S(1)} collective-permute-done((f32[32,1024]{1,0:T(8,128)S(1)}, f32[32,1024]{1,0:T(8,128)S(1)}, u32[]{:S(2)}, u32[]{:S(2)}) %collective-permute-start.27) | collective-permute-done | bytes 131104 | tf_op jit(solution)/shard_map/ppermute | solution.py:31
  85.4 1.7 %collective-permute-start.28 = (f32[32,1024]{1,0:T(8,128)S(1)}, f32[32,1024]{1,0:T(8,128)S(1)}, u32[]{:S(2)}, u32[]{:S(2)}) collective-permute-start(f32[32,1024]{1,0:T(8,128)S(1)} %add_add_fusion.2.own_in), channel_id=1, source_target_pairs={{0,4},{4,0},{8,12},{12,8},{16,20},{20,16},{24,28},{28,24},{32,36},... | collective-permute-start | bytes 393224 | tf_op jit(solution)/shard_map/ppermute | solution.py:298
  87.1 1.0 collective-permute-done.28.oth_in
  88.1 2.0 %next_left.2 = (f32[32,2048]{1,0:T(8,128)S(1)}, f32[32,1024]{1,0:T(8,128)S(1)}, f32[32,1024]{1,0:T(8,128)S(1)}) custom-call(s32[3]{0:T(128)S(1)} %pad_add_fusion.place_ref, f32[32,1024]{1,0:T(8,128)S(1)} %add_add_fusion.2.own_in, f32[32,1024]{1,0:T(8,128)S(1)} %collective-permute-done.28.oth_in, f32[32,32]{1,0:T(8,128)S(1)} %inverse_of.3.inv_ref, ...), custom_call_target="tpu_custom_call" | custom-call | tf_op jit(solution)/shard_map/next_left/pallas_call | solution.py:86
  90.5 1.0 collective-permute-done.29
  91.6 1.1 collective-permute-start.32
  92.6 1.1 collective-permute-start.31
  93.7 1.2 collective-permute-start.30
  94.9 1.7 %inverse_of.4.inv_ref = f32[32,32]{1,0:T(8,128)S(1)} custom-call(s32[3]{0:T(128)S(1)} %pad_add_fusion.place_ref, f32[32,2048]{1,0:T(8,128)S(1)} %get-tuple-element.111.left_ref), custom_call_target="tpu_custom_call" | custom-call | flops 1000 | bytes 1000 | tf_op jit(solution)/shard_map/inverse_of/pallas_call | solution.py:86
  96.6 3.4 %collective-permute-done.32 = f32[32,1024]{1,0:T(8,128)S(1)} collective-permute-done((f32[32,1024]{1,0:T(8,128)S(1)}, f32[32,1024]{1,0:T(8,128)S(1)}, u32[]{:S(2)}, u32[]{:S(2)}) %collective-permute-start.32) | collective-permute-done | bytes 131104 | tf_op jit(solution)/shard_map/ppermute | solution.py:31
  100.8 1.5 %collective-permute-start.33 = (f32[32,1024]{1,0:T(8,128)S(1)}, f32[32,1024]{1,0:T(8,128)S(1)}, u32[]{:S(2)}, u32[]{:S(2)}) collective-permute-start(f32[32,1024]{1,0:T(8,128)S(1)} %add_add_fusion.1.own_in), channel_id=1, source_target_pairs={{0,4},{4,0},{8,12},{12,8},{16,20},{20,16},{24,28},{28,24},{32,36},... | collective-permute-start | bytes 393224 | tf_op jit(solution)/shard_map/ppermute | solution.py:298
  102.3 1.0 collective-permute-done.33.oth_in
  103.3 2.0 %next_left.3 = (f32[32,2048]{1,0:T(8,128)S(1)}, f32[32,1024]{1,0:T(8,128)S(1)}, f32[32,1024]{1,0:T(8,128)S(1)}) custom-call(s32[3]{0:T(128)S(1)} %pad_add_fusion.place_ref, f32[32,1024]{1,0:T(8,128)S(1)} %add_add_fusion.1.own_in, f32[32,1024]{1,0:T(8,128)S(1)} %collective-permute-done.33.oth_in, f32[32,32]{1,0:T(8,128)S(1)} %inverse_of.4.inv_ref, ...), custom_call_target="tpu_custom_call" | custom-call | tf_op jit(solution)/shard_map/next_left/pallas_call | solution.py:86
  105.7 1.0 collective-permute-done.34
  106.7 1.1 collective-permute-start.37
  107.8 1.1 collective-permute-start.36
  108.9 1.2 collective-permute-start.35
  110.1 1.7 %inverse_of.5.inv_ref = f32[32,32]{1,0:T(8,128)S(1)} custom-call(s32[3]{0:T(128)S(1)} %pad_add_fusion.place_ref, f32[32,2048]{1,0:T(8,128)S(1)} %get-tuple-element.119.left_ref), custom_call_target="tpu_custom_call" | custom-call | flops 1000 | bytes 1000 | tf_op jit(solution)/shard_map/inverse_of/pallas_call | solution.py:86
  111.8 3.4 %collective-permute-done.37 = f32[32,1024]{1,0:T(8,128)S(1)} collective-permute-done((f32[32,1024]{1,0:T(8,128)S(1)}, f32[32,1024]{1,0:T(8,128)S(1)}, u32[]{:S(2)}, u32[]{:S(2)}) %collective-permute-start.37) | collective-permute-done | bytes 131104 | tf_op jit(solution)/shard_map/ppermute | solution.py:31
  115.9 1.5 %collective-permute-start.38 = (f32[32,1024]{1,0:T(8,128)S(1)}, f32[32,1024]{1,0:T(8,128)S(1)}, u32[]{:S(2)}, u32[]{:S(2)}) collective-permute-start(f32[32,1024]{1,0:T(8,128)S(1)} %add_add_fusion.own_in), channel_id=1, source_target_pairs={{0,4},{4,0},{8,12},{12,8},{16,20},{20,16},{24,28},{28,24},{32,36},... | collective-permute-start | bytes 393224 | tf_op jit(solution)/shard_map/ppermute | solution.py:298
  117.5 1.0 collective-permute-done.38.oth_in
  118.5 2.6 %last_right.1 = (bf16[32,512]{1,0:T(8,128)(2,1)S(1)}, f32[32,512]{1,0:T(8,128)S(1)}, f32[32,32]{1,0:T(8,128)S(1)}) custom-call(s32[3]{0:T(128)S(1)} %pad_add_fusion.place_ref, f32[32,1024]{1,0:T(8,128)S(1)} %add_add_fusion.own_in, f32[32,1024]{1,0:T(8,128)S(1)} %collective-permute-done.38.oth_in, f32[32,32]{1,0:T(8,128)S(1)} %inverse_of.5.inv_ref, ...), custom_call_target="tpu_custom_call" | custom-call | tf_op jit(solution)/shard_map/last_right/pallas_call | solution.py:86
  121.5 1.0 collective-permute-start.42
  122.5 1.0 collective-permute-start.41
  123.5 1.3 collective-permute-start.40
  124.8 3.2 %finish_near.1 = (f32[512,4096]{1,0:T(8,128)}, f32[512,4096]{1,0:T(8,128)}, f32[32,4096]{1,0:T(8,128)}, bf16[512,32]{1,0:T(8,128)(2,1)S(1)}) custom-call(s32[3]{0:T(128)S(1)} %pad_add_fusion.place_ref, f32[32,512]{1,0:T(8,128)S(1)} %get-tuple-element.125.refs_0_, f32[32,32]{1,0:T(8,128)S(1)} %get-tuple-element.126.refs_1_, ...), custom_call_target="tpu_custom_call" | custom-call | tf_op jit(solution)/shard_map/finish_near/pallas_call | solution.py:334
  128.0 1.1 collective-permute-start.43
  130.4 5.6 %finish_far.1 = (f32[512,4096]{1,0:T(8,128)}, f32[512,4096]{1,0:T(8,128)}, f32[32,4096]{1,0:T(8,128)}) custom-call(s32[3]{0:T(128)S(1)} %pad_add_fusion.place_ref, bf16[512,32]{1,0:T(8,128)(2,1)S(1)} %get-tuple-element.128.refs_0_, ...), custom_call_target="tpu_custom_call", output_to_operand_aliasing={{0}: (10, {}), {1}: (11, {}), {2}: (12, {})} | custom-call | tf_op jit(solution)/shard_map/finish_far/pallas_call | solution.py:334
  (57 shorter events, 11.9 us)
Async XLA Ops:
  3.0 5.4 %collective-permute-start = (bf16[512,2048]{1,0:T(8,128)(2,1)S(1)}, bf16[512,2048]{1,0:T(8,128)(2,1)}, u32[]{:S(2)}, u32[]{:S(2)}) collective-permute-start(bf16[512,2048]{1,0:T(8,128)(2,1)S(1)} %half_of_memory.3.refs_5_.refs_8_), channel_id=1, source_target_pairs={{0,4},{4,0},{8,12},{12,8},{16,20},{20,16},{24,28},{28,24},{32,36},... | collective-permute-start | bytes 6291464 | tf_op jit(solution)/shard_map/ppermute | solution.py:357
  6.8 7.4 %copy-start = (f32[4096,32]{0,1:T(8,128)S(1)}, f32[4096,32]{0,1:T(8,128)}, u32[]{:S(2)}) copy-start(f32[4096,32]{0,1:T(8,128)} %param.5) | copy-start | bytes 1572868
  10.3 16.3 %collective-permute-start.1 = (bf16[4,128,512]{2,1,0:T(8,128)(2,1)S(1)}, bf16[4,128,512]{2,1,0:T(8,128)(2,1)S(1)}, u32[]{:S(2)}, u32[]{:S(2)}) collective-permute-start(bf16[4,128,512]{2,1,0:T(8,128)(2,1)S(1)} %get-tuple-element.73.refs_1_), channel_id=1, source_target_pairs={{0,32},{1,33},{2,34},{3,35},{4,12},{5,13},{6,14},{7,15},{8,40},{9,... | collective-permute-start | bytes 1572872 | tf_op jit(solution)/shard_map/ppermute | solution.py:31
  11.7 15.0 %collective-permute-start.2 = (bf16[4,128,512]{2,1,0:T(8,128)(2,1)S(1)}, bf16[4,128,512]{2,1,0:T(8,128)(2,1)S(1)}, u32[]{:S(2)}, u32[]{:S(2)}) collective-permute-start(bf16[4,128,512]{2,1,0:T(8,128)(2,1)S(1)} %get-tuple-element.74.refs_2_), channel_id=1, source_target_pairs={{0,64},{1,65},{2,66},{3,67},{4,20},{5,21},{6,22},{7,23},{8,72},{9,... | collective-permute-start | bytes 1572872 | tf_op jit(solution)/shard_map/ppermute | solution.py:31
  14.1 15.2 %collective-permute-start.3 = (bf16[4,128,512]{2,1,0:T(8,128)(2,1)S(1)}, bf16[4,128,512]{2,1,0:T(8,128)(2,1)S(1)}, u32[]{:S(2)}, u32[]{:S(2)}) collective-permute-start(bf16[4,128,512]{2,1,0:T(8,128)(2,1)S(1)} %get-tuple-element.75.refs_3_), channel_id=1, source_target_pairs={{0,96},{1,97},{2,98},{3,99},{4,28},{5,29},{6,30},{7,31},{8,104},{9... | collective-permute-start | bytes 1572872 | tf_op jit(solution)/shard_map/ppermute | solution.py:31
  15.6 3.1 %collective-permute-start.4 = (f32[32,256]{1,0:T(8,128)S(1)}, f32[32,256]{1,0:T(8,128)S(1)}, u32[]{:S(2)}, u32[]{:S(2)}) collective-permute-start(f32[32,256]{1,0:T(8,128)S(1)} %get-tuple-element.77), channel_id=1, source_target_pairs={{0,4},{4,0},{8,12},{12,8},{16,20},{20,16},{24,28},{28,24},{32,36},... | collective-permute-start | bytes 98312 | tf_op jit(solution)/shard_map/ppermute | solution.py:361
  18.7 4.3 %collective-permute-start.7 = (f32[32,256]{1,0:T(8,128)S(1)}, f32[32,256]{1,0:T(8,128)S(1)}, u32[]{:S(2)}, u32[]{:S(2)}) collective-permute-start(f32[32,256]{1,0:T(8,128)S(1)} %add.57.a_ref), channel_id=1, source_target_pairs={{0,3},{1,2},{2,1},{3,0},{4,7},{5,6},{6,5},{7,4},{8,11},{9,10},{10,... | collective-permute-start | bytes 98312 | tf_op jit(solution)/shard_map/ppermute | solution.py:31
  21.4 4.6 %collective-permute-start.6 = (f32[32,256]{1,0:T(8,128)S(1)}, f32[32,256]{1,0:T(8,128)S(1)}, u32[]{:S(2)}, u32[]{:S(2)}) collective-permute-start(f32[32,256]{1,0:T(8,128)S(1)} %add.57.a_ref), channel_id=1, source_target_pairs={{0,2},{1,3},{2,0},{3,1},{4,6},{5,7},{6,4},{7,5},{8,10},{9,11},{10,... | collective-permute-start | bytes 98312 | tf_op jit(solution)/shard_map/ppermute | solution.py:31
  23.0 3.1 %collective-permute-start.5 = (f32[32,256]{1,0:T(8,128)S(1)}, f32[32,256]{1,0:T(8,128)S(1)}, u32[]{:S(2)}, u32[]{:S(2)}) collective-permute-start(f32[32,256]{1,0:T(8,128)S(1)} %add.57.a_ref), channel_id=1, source_target_pairs={{0,1},{1,0},{2,3},{3,2},{4,5},{5,4},{6,7},{7,6},{8,9},{9,8},{10,11... | collective-permute-start | bytes 98312 | tf_op jit(solution)/shard_map/ppermute | solution.py:31
  30.1 5.5 %collective-permute-start.8 = (bf16[128,512]{1,0:T(8,128)(2,1)S(1)}, bf16[128,512]{1,0:T(8,128)(2,1)S(1)}, u32[]{:S(2)}, u32[]{:S(2)}) collective-permute-start(bf16[128,512]{1,0:T(8,128)(2,1)S(1)} %get-tuple-element.83), channel_id=1, source_target_pairs={{0,8},{1,9},{2,10},{3,11},{4,36},{5,37},{6,38},{7,39},{8,0},{9,1},... | collective-permute-start | bytes 393224 | tf_op jit(solution)/shard_map/ppermute | solution.py:31
  31.5 7.1 %collective-permute-start.9 = (bf16[128,512]{1,0:T(8,128)(2,1)S(1)}, bf16[128,512]{1,0:T(8,128)(2,1)S(1)}, u32[]{:S(2)}, u32[]{:S(2)}) collective-permute-start(bf16[128,512]{1,0:T(8,128)(2,1)S(1)} %get-tuple-element.84), channel_id=1, source_target_pairs={{0,16},{1,17},{2,18},{3,19},{4,68},{5,69},{6,70},{7,71},{8,24},{9,... | collective-permute-start | bytes 393224 | tf_op jit(solution)/shard_map/ppermute | solution.py:31
  34.8 5.2 %collective-permute-start.10 = (bf16[128,512]{1,0:T(8,128)(2,1)S(1)}, bf16[128,512]{1,0:T(8,128)(2,1)S(1)}, u32[]{:S(2)}, u32[]{:S(2)}) collective-permute-start(bf16[128,512]{1,0:T(8,128)(2,1)S(1)} %get-tuple-element.85), channel_id=1, source_target_pairs={{0,24},{1,25},{2,26},{3,27},{4,100},{5,101},{6,102},{7,103},{8,16}... | collective-permute-start | bytes 393224 | tf_op jit(solution)/shard_map/ppermute | solution.py:31
  34.8 7.7 %collective-permute-start.13 = (f32[128,256]{1,0:T(8,128)S(1)}, f32[128,256]{1,0:T(8,128)S(1)}, u32[]{:S(2)}, u32[]{:S(2)}) collective-permute-start(f32[128,256]{1,0:T(8,128)S(1)} %stack_early.1), channel_id=1, source_target_pairs={{0,96},{1,97},{2,98},{3,99},{4,28},{5,29},{6,30},{7,31},{8,104},{9... | collective-permute-start | bytes 393224 | tf_op jit(solution)/shard_map/ppermute | solution.py:31
  35.3 7.2 %collective-permute-start.12 = (f32[128,256]{1,0:T(8,128)S(1)}, f32[128,256]{1,0:T(8,128)S(1)}, u32[]{:S(2)}, u32[]{:S(2)}) collective-permute-start(f32[128,256]{1,0:T(8,128)S(1)} %stack_early.1), channel_id=1, source_target_pairs={{0,64},{1,65},{2,66},{3,67},{4,20},{5,21},{6,22},{7,23},{8,72},{9,... | collective-permute-start | bytes 393224 | tf_op jit(solution)/shard_map/ppermute | solution.py:31
  35.6 7.5 %collective-permute-start.11 = (f32[128,256]{1,0:T(8,128)S(1)}, f32[128,256]{1,0:T(8,128)S(1)}, u32[]{:S(2)}, u32[]{:S(2)}) collective-permute-start(f32[128,256]{1,0:T(8,128)S(1)} %stack_early.1), channel_id=1, source_target_pairs={{0,32},{1,33},{2,34},{3,35},{4,12},{5,13},{6,14},{7,15},{8,40},{9,... | collective-permute-start | bytes 393224 | tf_op jit(solution)/shard_map/ppermute | solution.py:31
  43.7 6.1 %collective-permute-start.16 = (bf16[128,512]{1,0:T(8,128)(2,1)S(1)}, bf16[128,512]{1,0:T(8,128)(2,1)S(1)}, u32[]{:S(2)}, u32[]{:S(2)}) collective-permute-start(bf16[128,512]{1,0:T(8,128)(2,1)S(1)} %second_sum.1), channel_id=1, source_target_pairs={{0,24},{1,25},{2,26},{3,27},{4,7},{5,6},{6,5},{7,4},{8,16},{9,17},... | collective-permute-start | bytes 393224 | tf_op jit(solution)/shard_map/ppermute | solution.py:31
  46.5 5.3 %collective-permute-start.15 = (bf16[128,512]{1,0:T(8,128)(2,1)S(1)}, bf16[128,512]{1,0:T(8,128)(2,1)S(1)}, u32[]{:S(2)}, u32[]{:S(2)}) collective-permute-start(bf16[128,512]{1,0:T(8,128)(2,1)S(1)} %second_sum.1), channel_id=1, source_target_pairs={{0,16},{1,17},{2,18},{3,19},{4,6},{5,7},{6,4},{7,5},{8,24},{9,25},... | collective-permute-start | bytes 393224 | tf_op jit(solution)/shard_map/ppermute | solution.py:31
  46.9 5.0 %collective-permute-start.14 = (bf16[128,512]{1,0:T(8,128)(2,1)S(1)}, bf16[128,512]{1,0:T(8,128)(2,1)S(1)}, u32[]{:S(2)}, u32[]{:S(2)}) collective-permute-start(bf16[128,512]{1,0:T(8,128)(2,1)S(1)} %second_sum.1), channel_id=1, source_target_pairs={{0,8},{1,9},{2,10},{3,11},{4,5},{5,4},{6,7},{7,6},{8,0},{9,1},{10,... | collective-permute-start | bytes 393224 | tf_op jit(solution)/shard_map/ppermute | solution.py:31
  47.2 8.8 %collective-permute-start.22 = (f32[128,256]{1,0:T(8,128)S(1)}, f32[128,256]{1,0:T(8,128)S(1)}, u32[]{:S(2)}, u32[]{:S(2)}) collective-permute-start(f32[128,256]{1,0:T(8,128)S(1)} %add_add_fusion.4), channel_id=1, source_target_pairs={{0,24},{1,25},{2,26},{3,27},{4,100},{5,101},{6,102},{7,103},{8,16}... | collective-permute-start | bytes 393224 | tf_op jit(solution)/shard_map/ppermute | solution.py:31
  51.9 20.2 %collective-permute-start.19 = (bf16[512,512]{1,0:T(8,128)(2,1)S(1)}, bf16[512,512]{1,0:T(8,128)(2,1)S(1)}, u32[]{:S(2)}, u32[]{:S(2)}) collective-permute-start(bf16[512,512]{1,0:T(8,128)(2,1)S(1)} %pad_maximum_fusion.m0), channel_id=1, source_target_pairs={{0,3},{1,2},{2,1},{3,0},{4,28},{5,29},{6,30},{7,31},{8,11},{9,10},... | collective-permute-start | bytes 1572872 | tf_op jit(solution)/shard_map/ppermute | solution.py:31
  53.4 18.7 %collective-permute-start.18 = (bf16[512,512]{1,0:T(8,128)(2,1)S(1)}, bf16[512,512]{1,0:T(8,128)(2,1)S(1)}, u32[]{:S(2)}, u32[]{:S(2)}) collective-permute-start(bf16[512,512]{1,0:T(8,128)(2,1)S(1)} %pad_maximum_fusion.m0), channel_id=1, source_target_pairs={{0,2},{1,3},{2,0},{3,1},{4,20},{5,21},{6,22},{7,23},{8,10},{9,11},... | collective-permute-start | bytes 1572872 | tf_op jit(solution)/shard_map/ppermute | solution.py:31
  53.9 18.1 %collective-permute-start.17 = (bf16[512,512]{1,0:T(8,128)(2,1)S(1)}, bf16[512,512]{1,0:T(8,128)(2,1)S(1)}, u32[]{:S(2)}, u32[]{:S(2)}) collective-permute-start(bf16[512,512]{1,0:T(8,128)(2,1)S(1)} %pad_maximum_fusion.m0), channel_id=1, source_target_pairs={{0,1},{1,0},{2,3},{3,2},{4,12},{5,13},{6,14},{7,15},{8,9},{9,8},{1... | collective-permute-start | bytes 1572872 | tf_op jit(solution)/shard_map/ppermute | solution.py:31
  55.2 5.3 %collective-permute-start.21 = (f32[128,256]{1,0:T(8,128)S(1)}, f32[128,256]{1,0:T(8,128)S(1)}, u32[]{:S(2)}, u32[]{:S(2)}) collective-permute-start(f32[128,256]{1,0:T(8,128)S(1)} %add_add_fusion.4), channel_id=1, source_target_pairs={{0,16},{1,17},{2,18},{3,19},{4,68},{5,69},{6,70},{7,71},{8,24},{9,... | collective-permute-start | bytes 393224 | tf_op jit(solution)/shard_map/ppermute | solution.py:31
  56.1 6.2 %collective-permute-start.20 = (f32[128,256]{1,0:T(8,128)S(1)}, f32[128,256]{1,0:T(8,128)S(1)}, u32[]{:S(2)}, u32[]{:S(2)}) collective-permute-start(f32[128,256]{1,0:T(8,128)S(1)} %add_add_fusion.4), channel_id=1, source_target_pairs={{0,8},{1,9},{2,10},{3,11},{4,36},{5,37},{6,38},{7,39},{8,0},{9,1},... | collective-permute-start | bytes 393224 | tf_op jit(solution)/shard_map/ppermute | solution.py:31
  62.2 9.8 %collective-permute-start.23 = (f32[128,256]{1,0:T(8,128)S(1)}, f32[128,256]{1,0:T(8,128)S(1)}, u32[]{:S(2)}, u32[]{:S(2)}) collective-permute-start(f32[128,256]{1,0:T(8,128)S(1)} %add_add_fusion.3.own_in), channel_id=1, source_target_pairs={{0,4},{4,0},{8,12},{12,8},{16,20},{20,16},{24,28},{28,24},{32,36},... | collective-permute-start | bytes 393224 | tf_op jit(solution)/shard_map/ppermute | solution.py:371
  73.8 2.4 %collective-permute-start.24 = (f32[32,1024]{1,0:T(8,128)S(1)}, f32[32,1024]{1,0:T(8,128)S(1)}, u32[]{:S(2)}, u32[]{:S(2)}) collective-permute-start(f32[32,1024]{1,0:T(8,128)S(1)} %get-tuple-element.102), channel_id=1, source_target_pairs={{0,4},{4,0},{8,12},{12,8},{16,20},{20,16},{24,28},{28,24},{32,36},... | collective-permute-start | bytes 393224 | tf_op jit(solution)/shard_map/ppermute | solution.py:292
  76.2 8.4 %collective-permute-start.27 = (f32[32,1024]{1,0:T(8,128)S(1)}, f32[32,1024]{1,0:T(8,128)S(1)}, u32[]{:S(2)}, u32[]{:S(2)}) collective-permute-start(f32[32,1024]{1,0:T(8,128)S(1)} %add.64), channel_id=1, source_target_pairs={{0,96},{1,97},{2,98},{3,99},{4,100},{5,101},{6,102},{7,103},{8,104... | collective-permute-start | bytes 393224 | tf_op jit(solution)/shard_map/ppermute | solution.py:31
  77.3 7.4 %collective-permute-start.26 = (f32[32,1024]{1,0:T(8,128)S(1)}, f32[32,1024]{1,0:T(8,128)S(1)}, u32[]{:S(2)}, u32[]{:S(2)}) collective-permute-start(f32[32,1024]{1,0:T(8,128)S(1)} %add.64), channel_id=1, source_target_pairs={{0,64},{1,65},{2,66},{3,67},{4,68},{5,69},{6,70},{7,71},{8,72},{9,... | collective-permute-start | bytes 393224 | tf_op jit(solution)/shard_map/ppermute | solution.py:31
  78.4 7.0 %collective-permute-start.25 = (f32[32,1024]{1,0:T(8,128)S(1)}, f32[32,1024]{1,0:T(8,128)S(1)}, u32[]{:S(2)}, u32[]{:S(2)}) collective-permute-start(f32[32,1024]{1,0:T(8,128)S(1)} %add.64), channel_id=1, source_target_pairs={{0,32},{1,33},{2,34},{3,35},{4,36},{5,37},{6,38},{7,39},{8,40},{9,... | collective-permute-start | bytes 393224 | tf_op jit(solution)/shard_map/ppermute | solution.py:31
  85.4 2.7 %collective-permute-start.28 = (f32[32,1024]{1,0:T(8,128)S(1)}, f32[32,1024]{1,0:T(8,128)S(1)}, u32[]{:S(2)}, u32[]{:S(2)}) collective-permute-start(f32[32,1024]{1,0:T(8,128)S(1)} %add_add_fusion.2.own_in), channel_id=1, source_target_pairs={{0,4},{4,0},{8,12},{12,8},{16,20},{20,16},{24,28},{28,24},{32,36},... | collective-permute-start | bytes 393224 | tf_op jit(solution)/shard_map/ppermute | solution.py:298
  90.1 1.4 %collective-permute-start.29 = (f32[32,1024]{1,0:T(8,128)S(1)}, f32[32,1024]{1,0:T(8,128)S(1)}, u32[]{:S(2)}, u32[]{:S(2)}) collective-permute-start(f32[32,1024]{1,0:T(8,128)S(1)} %get-tuple-element.110), channel_id=1, source_target_pairs={{0,4},{4,0},{8,12},{12,8},{16,20},{20,16},{24,28},{28,24},{32,36},... | collective-permute-start | bytes 393224 | tf_op jit(solution)/shard_map/ppermute | solution.py:292
  91.6 8.4 %collective-permute-start.32 = (f32[32,1024]{1,0:T(8,128)S(1)}, f32[32,1024]{1,0:T(8,128)S(1)}, u32[]{:S(2)}, u32[]{:S(2)}) collective-permute-start(f32[32,1024]{1,0:T(8,128)S(1)} %add.68), channel_id=1, source_target_pairs={{0,96},{1,97},{2,98},{3,99},{4,100},{5,101},{6,102},{7,103},{8,104... | collective-permute-start | bytes 393224 | tf_op jit(solution)/shard_map/ppermute | solution.py:31
  92.6 7.4 %collective-permute-start.31 = (f32[32,1024]{1,0:T(8,128)S(1)}, f32[32,1024]{1,0:T(8,128)S(1)}, u32[]{:S(2)}, u32[]{:S(2)}) collective-permute-start(f32[32,1024]{1,0:T(8,128)S(1)} %add.68), channel_id=1, source_target_pairs={{0,64},{1,65},{2,66},{3,67},{4,68},{5,69},{6,70},{7,71},{8,72},{9,... | collective-permute-start | bytes 393224 | tf_op jit(solution)/shard_map/ppermute | solution.py:31
  93.7 7.0 %collective-permute-start.30 = (f32[32,1024]{1,0:T(8,128)S(1)}, f32[32,1024]{1,0:T(8,128)S(1)}, u32[]{:S(2)}, u32[]{:S(2)}) collective-permute-start(f32[32,1024]{1,0:T(8,128)S(1)} %add.68), channel_id=1, source_target_pairs={{0,32},{1,33},{2,34},{3,35},{4,36},{5,37},{6,38},{7,39},{8,40},{9,... | collective-permute-start | bytes 393224 | tf_op jit(solution)/shard_map/ppermute | solution.py:31
  100.8 2.5 %collective-permute-start.33 = (f32[32,1024]{1,0:T(8,128)S(1)}, f32[32,1024]{1,0:T(8,128)S(1)}, u32[]{:S(2)}, u32[]{:S(2)}) collective-permute-start(f32[32,1024]{1,0:T(8,128)S(1)} %add_add_fusion.1.own_in), channel_id=1, source_target_pairs={{0,4},{4,0},{8,12},{12,8},{16,20},{20,16},{24,28},{28,24},{32,36},... | collective-permute-start | bytes 393224 | tf_op jit(solution)/shard_map/ppermute | solution.py:298
  105.3 1.4 %collective-permute-start.34 = (f32[32,1024]{1,0:T(8,128)S(1)}, f32[32,1024]{1,0:T(8,128)S(1)}, u32[]{:S(2)}, u32[]{:S(2)}) collective-permute-start(f32[32,1024]{1,0:T(8,128)S(1)} %get-tuple-element.118), channel_id=1, source_target_pairs={{0,4},{4,0},{8,12},{12,8},{16,20},{20,16},{24,28},{28,24},{32,36},... | collective-permute-start | bytes 393224 | tf_op jit(solution)/shard_map/ppermute | solution.py:292
  106.7 8.4 %collective-permute-start.37 = (f32[32,1024]{1,0:T(8,128)S(1)}, f32[32,1024]{1,0:T(8,128)S(1)}, u32[]{:S(2)}, u32[]{:S(2)}) collective-permute-start(f32[32,1024]{1,0:T(8,128)S(1)} %add.72), channel_id=1, source_target_pairs={{0,96},{1,97},{2,98},{3,99},{4,100},{5,101},{6,102},{7,103},{8,104... | collective-permute-start | bytes 393224 | tf_op jit(solution)/shard_map/ppermute | solution.py:31
  107.8 7.4 %collective-permute-start.36 = (f32[32,1024]{1,0:T(8,128)S(1)}, f32[32,1024]{1,0:T(8,128)S(1)}, u32[]{:S(2)}, u32[]{:S(2)}) collective-permute-start(f32[32,1024]{1,0:T(8,128)S(1)} %add.72), channel_id=1, source_target_pairs={{0,64},{1,65},{2,66},{3,67},{4,68},{5,69},{6,70},{7,71},{8,72},{9,... | collective-permute-start | bytes 393224 | tf_op jit(solution)/shard_map/ppermute | solution.py:31
  108.9 7.0 %collective-permute-start.35 = (f32[32,1024]{1,0:T(8,128)S(1)}, f32[32,1024]{1,0:T(8,128)S(1)}, u32[]{:S(2)}, u32[]{:S(2)}) collective-permute-start(f32[32,1024]{1,0:T(8,128)S(1)} %add.72), channel_id=1, source_target_pairs={{0,32},{1,33},{2,34},{3,35},{4,36},{5,37},{6,38},{7,39},{8,40},{9,... | collective-permute-start | bytes 393224 | tf_op jit(solution)/shard_map/ppermute | solution.py:31
  115.9 2.5 %collective-permute-start.38 = (f32[32,1024]{1,0:T(8,128)S(1)}, f32[32,1024]{1,0:T(8,128)S(1)}, u32[]{:S(2)}, u32[]{:S(2)}) collective-permute-start(f32[32,1024]{1,0:T(8,128)S(1)} %add_add_fusion.own_in), channel_id=1, source_target_pairs={{0,4},{4,0},{8,12},{12,8},{16,20},{20,16},{24,28},{28,24},{32,36},... | collective-permute-start | bytes 393224 | tf_op jit(solution)/shard_map/ppermute | solution.py:298
  121.1 3.7 %collective-permute-start.39 = (bf16[32,512]{1,0:T(8,128)(2,1)S(1)}, bf16[32,512]{1,0:T(8,128)(2,1)S(1)}, u32[]{:S(2)}, u32[]{:S(2)}) collective-permute-start(bf16[32,512]{1,0:T(8,128)(2,1)S(1)} %get-tuple-element.127.refs_2_), channel_id=1, source_target_pairs={{0,4},{4,0},{8,12},{12,8},{16,20},{20,16},{24,28},{28,24},{32,36},... | collective-permute-start | bytes 98312 | tf_op jit(solution)/shard_map/ppermute | solution.py:382
  121.5 6.4 %collective-permute-start.42 = (bf16[32,512]{1,0:T(8,128)(2,1)S(1)}, bf16[32,512]{1,0:T(8,128)(2,1)S(1)}, u32[]{:S(2)}, u32[]{:S(2)}) collective-permute-start(bf16[32,512]{1,0:T(8,128)(2,1)S(1)} %get-tuple-element.127.refs_2_), channel_id=1, source_target_pairs={{0,96},{1,97},{2,98},{3,99},{4,100},{5,101},{6,102},{7,103},{8,104... | collective-permute-start | bytes 98312 | tf_op jit(solution)/shard_map/ppermute | solution.py:31
  122.5 5.5 %collective-permute-start.41 = (bf16[32,512]{1,0:T(8,128)(2,1)S(1)}, bf16[32,512]{1,0:T(8,128)(2,1)S(1)}, u32[]{:S(2)}, u32[]{:S(2)}) collective-permute-start(bf16[32,512]{1,0:T(8,128)(2,1)S(1)} %get-tuple-element.127.refs_2_), channel_id=1, source_target_pairs={{0,64},{1,65},{2,66},{3,67},{4,68},{5,69},{6,70},{7,71},{8,72},{9,... | collective-permute-start | bytes 98312 | tf_op jit(solution)/shard_map/ppermute | solution.py:31
  123.5 4.5 %collective-permute-start.40 = (bf16[32,512]{1,0:T(8,128)(2,1)S(1)}, bf16[32,512]{1,0:T(8,128)(2,1)S(1)}, u32[]{:S(2)}, u32[]{:S(2)}) collective-permute-start(bf16[32,512]{1,0:T(8,128)(2,1)S(1)} %get-tuple-element.127.refs_2_), channel_id=1, source_target_pairs={{0,32},{1,33},{2,34},{3,35},{4,36},{5,37},{6,38},{7,39},{8,40},{9,... | collective-permute-start | bytes 98312 | tf_op jit(solution)/shard_map/ppermute | solution.py:31
  128.0 1.9 %collective-permute-start.43 = (bf16[32,512]{1,0:T(8,128)(2,1)S(1)}, bf16[32,512]{1,0:T(8,128)(2,1)S(1)}, u32[]{:S(2)}, u32[]{:S(2)}) collective-permute-start(bf16[32,512]{1,0:T(8,128)(2,1)S(1)} %collective-permute-done.40.refs_1_), channel_id=1, source_target_pairs={{0,4},{4,0},{8,12},{12,8},{16,20},{20,16},{24,28},{28,24},{32,36},... | collective-permute-start | bytes 98312 | tf_op jit(solution)/shard_map/ppermute | solution.py:386
  129.1 1.2 collective-permute-start.44
  129.2 1.3 collective-permute-start.45

commit v7 on v6

--- a/solution.py
+++ b/solution.py
@@ -362,10 +362,10 @@
     early = stack_early(place, spread(early, "y", "y"))
     parts, early = lax.optimization_barrier((exchange(pairs, "z", "x"), early))
     rows = first_sum(place, parts)
-    early = spread(early, "z", "x")
+    early = spread(early, "x", "x")
     parts, early = lax.optimization_barrier((exchange(rows, "x", "z"), early))
     piece = second_sum(place, parts)
-    early = spread((early[0] + early[1]) + (early[2] + early[3]), "x", "z")
+    early = spread((early[0] + early[1]) + (early[2] + early[3]), "z", "z")
     m = jnp.concatenate(spread(piece, "x", "y"), axis=0)
     early = (early[0] + early[1]) + (early[2] + early[3])
     passed = lax.ppermute(early, "dp", CORE)

time: 136 us -> 137 us (level)
  starting transfers between devices: 62.1 us -> 64.4 us
  waiting for transfers between devices: 40.6 us -> 39.2 us
    ppermute x1, starting transfers between devices: 8.81 us -> 4.09 us  [per_device(): passed = lax.ppermute(early, 'dp', CORE)]
    ppermute x3, starting transfers between devices: 2.27 us -> 6.18 us  [sum_over_group(): own = own + lax.ppermute(oth, 'dp', CORE)]
    ppermute x33, starting transfers between devices: 40.5 us -> 43.6 us  [along(): return lax.ppermute(array, ('dp', 'owner'), pairs)]
    ppermute x33, waiting for transfers between devices: 30.5 us -> 29.1 us  [along(): return lax.ppermute(array, ('dp', 'owner'), pairs)]
  transfers between devices with their start and end apart: 46 -> 46, of which waited for: 30 -> 29; matrix products, arithmetic and copies ran while one was open for 0% -> 0% of each run, Pallas kernels for 9% -> 9%
where the time goes in v7:
time: 137 us
  starting transfers between devices  64.4 us (47%)
  waiting for transfers between devices  39.2 us (29%)
  Pallas kernels  32.2 us (24%)
    ppermute x33, starting transfers between devices, along(): return lax.ppermute(array, ('dp', 'owner'), pairs)  43.6 us
    ppermute x33, waiting for transfers between devices, along(): return lax.ppermute(array, ('dp', 'owner'), pairs)  29.1 us
    pallas_call x12, Pallas kernels, call(): pl.pallas_call(body, in_specs=[SCALARS] + [WHOLE] * len(arrays), out_spec...  18.7 us
    pallas_call x2, Pallas kernels, finish(): pl.pallas_call(body, in_specs=[SCALARS] + [WHOLE] * (len(ortho) + count +...  8.78 us
    ppermute x3, starting transfers between devices, sum_over_group(): own = own + lax.ppermute(oth, 'dp', CORE)  6.18 us
    ppermute x3, starting transfers between devices, sum_over_group(): return (own, lax.ppermute(own, 'dp', CORE), beside)  4.81 us
    pallas_call x2, Pallas kernels, half_of_memory(): pl.pallas_call(body, in_specs=[SCALARS, HBM, HBM], out_specs=WHOLE, scrat...  4.67 us
    ppermute x1, starting transfers between devices, per_device(): passed = lax.ppermute(early, 'dp', CORE)  4.09 us
  transfers between devices with their start and end apart: 46, of which 29 were waited for; matrix products, arithmetic and copies ran while one was open for 0% of the time, Pallas kernels for 9%

profile of v7, /device:TPU:1, one launch (start us, length us, event | category | flops | bytes accessed | tf_op | source)
XLA Modules:
  0.0 137.1 jit_solution(12612143498359012958)
XLA Ops:
  0.6 2.3 %half_of_memory.3.refs_5_.refs_8_ = bf16[512,2048]{1,0:T(8,128)(2,1)S(1)} custom-call(s32[1]{0:T(128)} %bitcast.5.which_ref, bf16[512,4096]{1,0:T(8,128)(2,1)} %bitcast.10, bf16[512,4096]{1,0:T(8,128)(2,1)} %bitcast.12), custom_call_target="tpu_custom_call" | custom-call | tf_op jit(solution)/shard_map/half_of_memory/pallas_call | solution.py:74
  3.0 1.5 %collective-permute-start = (bf16[512,2048]{1,0:T(8,128)(2,1)S(1)}, bf16[512,2048]{1,0:T(8,128)(2,1)}, u32[]{:S(2)}, u32[]{:S(2)}) collective-permute-start(bf16[512,2048]{1,0:T(8,128)(2,1)S(1)} %half_of_memory.3.refs_5_.refs_8_), channel_id=1, source_target_pairs={{0,4},{4,0},{8,12},{12,8},{16,20},{20,16},{24,28},{28,24},{32,36},... | collective-permute-start | bytes 6291464 | tf_op jit(solution)/shard_map/ppermute | solution.py:357
  4.5 2.3 %half_of_memory.2.a_ref.refs_4_.refs_7_ = bf16[512,2048]{1,0:T(8,128)(2,1)S(1)} custom-call(s32[1]{0:T(128)} %bitcast.2.which_ref, bf16[512,4096]{1,0:T(8,128)(2,1)} %bitcast.11, bf16[512,4096]{1,0:T(8,128)(2,1)} %bitcast.13), custom_call_target="tpu_custom_call" | custom-call | tf_op jit(solution)/shard_map/half_of_memory/pallas_call | solution.py:74
  6.9 1.5 %collective-permute-done.b_ref = bf16[512,2048]{1,0:T(8,128)(2,1)} collective-permute-done((bf16[512,2048]{1,0:T(8,128)(2,1)S(1)}, bf16[512,2048]{1,0:T(8,128)(2,1)}, u32[]{:S(2)}, u32[]{:S(2)}) %collective-permute-start) | collective-permute-done | bytes 2097184 | tf_op jit(solution)/shard_map/ppermute | solution.py:357
  8.4 1.9 %pair_sum.1 = (bf16[4,128,512]{2,1,0:T(8,128)(2,1)S(1)}, bf16[4,128,512]{2,1,0:T(8,128)(2,1)S(1)}, bf16[4,128,512]{2,1,0:T(8,128)(2,1)S(1)}, bf16[4,128,512]{2,1,0:T(8,128)(2,1)S(1)}) custom-call(s32[3]{0:T(128)S(1)} %pad_add_fusion.place_ref, bf16[512,2048]{1,0:T(8,128)(2,1)S(1)} %half_of_memory.2.a_ref.refs_4_.refs_7_, ...), custom_call_target="tpu_custom_call" | custom-call | tf_op jit(solution)/shard_map/pair_sum/pallas_call | solution.py:86
  10.3 1.4 %collective-permute-start.1 = (bf16[4,128,512]{2,1,0:T(8,128)(2,1)S(1)}, bf16[4,128,512]{2,1,0:T(8,128)(2,1)S(1)}, u32[]{:S(2)}, u32[]{:S(2)}) collective-permute-start(bf16[4,128,512]{2,1,0:T(8,128)(2,1)S(1)} %get-tuple-element.73.refs_1_), channel_id=1, source_target_pairs={{0,32},{1,33},{2,34},{3,35},{4,12},{5,13},{6,14},{7,15},{8,40},{9,... | collective-permute-start | bytes 1572872 | tf_op jit(solution)/shard_map/ppermute | solution.py:31
  11.7 2.5 %collective-permute-start.2 = (bf16[4,128,512]{2,1,0:T(8,128)(2,1)S(1)}, bf16[4,128,512]{2,1,0:T(8,128)(2,1)S(1)}, u32[]{:S(2)}, u32[]{:S(2)}) collective-permute-start(bf16[4,128,512]{2,1,0:T(8,128)(2,1)S(1)} %get-tuple-element.74.refs_2_), channel_id=1, source_target_pairs={{0,64},{1,65},{2,66},{3,67},{4,20},{5,21},{6,22},{7,23},{8,72},{9,... | collective-permute-start | bytes 1572872 | tf_op jit(solution)/shard_map/ppermute | solution.py:31
  14.2 1.4 early_left.1
  15.6 2.2 %collective-permute-start.4 = (f32[32,256]{1,0:T(8,128)S(1)}, f32[32,256]{1,0:T(8,128)S(1)}, u32[]{:S(2)}, u32[]{:S(2)}) collective-permute-start(f32[32,256]{1,0:T(8,128)S(1)} %get-tuple-element.77), channel_id=1, source_target_pairs={{0,4},{4,0},{8,12},{12,8},{16,20},{20,16},{24,28},{28,24},{32,36},... | collective-permute-start | bytes 98312 | tf_op jit(solution)/shard_map/ppermute | solution.py:361
  17.8 0.9 collective-permute-done.4
  18.7 2.7 %collective-permute-start.7 = (f32[32,256]{1,0:T(8,128)S(1)}, f32[32,256]{1,0:T(8,128)S(1)}, u32[]{:S(2)}, u32[]{:S(2)}) collective-permute-start(f32[32,256]{1,0:T(8,128)S(1)} %add.57.a_ref), channel_id=1, source_target_pairs={{0,3},{1,2},{2,1},{3,0},{4,7},{5,6},{6,5},{7,4},{8,11},{9,10},{10,... | collective-permute-start | bytes 98312 | tf_op jit(solution)/shard_map/ppermute | solution.py:31
  21.8 1.2 collective-permute-done.7.d_ref
  23.0 2.9 %collective-permute-done.6.c_ref = f32[32,256]{1,0:T(8,128)S(1)} collective-permute-done((f32[32,256]{1,0:T(8,128)S(1)}, f32[32,256]{1,0:T(8,128)S(1)}, u32[]{:S(2)}, u32[]{:S(2)}) %collective-permute-start.6) | collective-permute-done | bytes 32800 | tf_op jit(solution)/shard_map/ppermute | solution.py:31
  26.6 2.6 %collective-permute-done.3.refs_3_ = bf16[4,128,512]{2,1,0:T(8,128)(2,1)S(1)} collective-permute-done((bf16[4,128,512]{2,1,0:T(8,128)(2,1)S(1)}, bf16[4,128,512]{2,1,0:T(8,128)(2,1)S(1)}, u32[]{:S(2)}, u32[]{:S(2)}) %collective-permute-start.3) | collective-permute-done | bytes 524320 | tf_op jit(solution)/shard_map/ppermute | solution.py:31
  29.3 0.8 first_sum.1
  30.1 1.4 %collective-permute-start.8 = (bf16[128,512]{1,0:T(8,128)(2,1)S(1)}, bf16[128,512]{1,0:T(8,128)(2,1)S(1)}, u32[]{:S(2)}, u32[]{:S(2)}) collective-permute-start(bf16[128,512]{1,0:T(8,128)(2,1)S(1)} %get-tuple-element.83), channel_id=1, source_target_pairs={{0,8},{1,9},{2,10},{3,11},{4,36},{5,37},{6,38},{7,39},{8,0},{9,1},... | collective-permute-start | bytes 393224 | tf_op jit(solution)/shard_map/ppermute | solution.py:31
  31.5 3.3 %collective-permute-start.9 = (bf16[128,512]{1,0:T(8,128)(2,1)S(1)}, bf16[128,512]{1,0:T(8,128)(2,1)S(1)}, u32[]{:S(2)}, u32[]{:S(2)}) collective-permute-start(bf16[128,512]{1,0:T(8,128)(2,1)S(1)} %get-tuple-element.84), channel_id=1, source_target_pairs={{0,16},{1,17},{2,18},{3,19},{4,68},{5,69},{6,70},{7,71},{8,24},{9,... | collective-permute-start | bytes 393224 | tf_op jit(solution)/shard_map/ppermute | solution.py:31
  35.6 2.4 %collective-permute-start.11 = (f32[128,256]{1,0:T(8,128)S(1)}, f32[128,256]{1,0:T(8,128)S(1)}, u32[]{:S(2)}, u32[]{:S(2)}) collective-permute-start(f32[128,256]{1,0:T(8,128)S(1)} %stack_early.1), channel_id=1, source_target_pairs={{0,8},{1,9},{2,10},{3,11},{4,12},{5,13},{6,14},{7,15},{8,0},{9,1},... | collective-permute-start | bytes 393224 | tf_op jit(solution)/shard_map/ppermute | solution.py:31
  38.6 1.4 %collective-permute-done.10.d_ref = bf16[128,512]{1,0:T(8,128)(2,1)S(1)} collective-permute-done((bf16[128,512]{1,0:T(8,128)(2,1)S(1)}, bf16[128,512]{1,0:T(8,128)(2,1)S(1)}, u32[]{:S(2)}, u32[]{:S(2)}) %collective-permute-start.10) | collective-permute-done | bytes 131104 | tf_op jit(solution)/shard_map/ppermute | solution.py:31
  40.0 2.6 %collective-permute-done.13 = f32[128,256]{1,0:T(8,128)S(1)} collective-permute-done((f32[128,256]{1,0:T(8,128)S(1)}, f32[128,256]{1,0:T(8,128)S(1)}, u32[]{:S(2)}, u32[]{:S(2)}) %collective-permute-start.13) | collective-permute-done | bytes 131104 | tf_op jit(solution)/shard_map/ppermute | solution.py:31
  43.1 0.6 second_sum.1
  43.7 2.8 %collective-permute-start.16 = (bf16[128,512]{1,0:T(8,128)(2,1)S(1)}, bf16[128,512]{1,0:T(8,128)(2,1)S(1)}, u32[]{:S(2)}, u32[]{:S(2)}) collective-permute-start(bf16[128,512]{1,0:T(8,128)(2,1)S(1)} %second_sum.1), channel_id=1, source_target_pairs={{0,24},{1,25},{2,26},{3,27},{4,7},{5,6},{6,5},{7,4},{8,16},{9,17},... | collective-permute-start | bytes 393224 | tf_op jit(solution)/shard_map/ppermute | solution.py:31
  47.2 3.8 %collective-permute-start.22 = (f32[128,256]{1,0:T(8,128)S(1)}, f32[128,256]{1,0:T(8,128)S(1)}, u32[]{:S(2)}, u32[]{:S(2)}) collective-permute-start(f32[128,256]{1,0:T(8,128)S(1)} %add_add_fusion.4), channel_id=1, source_target_pairs={{0,96},{1,97},{2,98},{3,99},{4,100},{5,101},{6,102},{7,103},{8,104... | collective-permute-start | bytes 393224 | tf_op jit(solution)/shard_map/ppermute | solution.py:31
  51.1 0.8 collective-permute-done.15
  51.9 1.5 %collective-permute-start.19 = (bf16[512,512]{1,0:T(8,128)(2,1)S(1)}, bf16[512,512]{1,0:T(8,128)(2,1)S(1)}, u32[]{:S(2)}, u32[]{:S(2)}) collective-permute-start(bf16[512,512]{1,0:T(8,128)(2,1)S(1)} %pad_maximum_fusion.m0), channel_id=1, source_target_pairs={{0,3},{1,2},{2,1},{3,0},{4,28},{5,29},{6,30},{7,31},{8,11},{9,10},... | collective-permute-start | bytes 1572872 | tf_op jit(solution)/shard_map/ppermute | solution.py:31
  53.4 0.6 collective-permute-start.18
  53.9 1.3 collective-permute-start.17
  55.2 2.4 %collective-permute-start.21 = (f32[128,256]{1,0:T(8,128)S(1)}, f32[128,256]{1,0:T(8,128)S(1)}, u32[]{:S(2)}, u32[]{:S(2)}) collective-permute-start(f32[128,256]{1,0:T(8,128)S(1)} %add_add_fusion.4), channel_id=1, source_target_pairs={{0,64},{1,65},{2,66},{3,67},{4,68},{5,69},{6,70},{7,71},{8,72},{9,... | collective-permute-start | bytes 393224 | tf_op jit(solution)/shard_map/ppermute | solution.py:31
  57.6 2.2 %collective-permute-start.20 = (f32[128,256]{1,0:T(8,128)S(1)}, f32[128,256]{1,0:T(8,128)S(1)}, u32[]{:S(2)}, u32[]{:S(2)}) collective-permute-start(f32[128,256]{1,0:T(8,128)S(1)} %add_add_fusion.4), channel_id=1, source_target_pairs={{0,32},{1,33},{2,34},{3,35},{4,36},{5,37},{6,38},{7,39},{8,40},{9,... | collective-permute-start | bytes 393224 | tf_op jit(solution)/shard_map/ppermute | solution.py:31
  59.9 0.7 collective-permute-done.21
  60.5 3.4 %collective-permute-done.20 = f32[128,256]{1,0:T(8,128)S(1)} collective-permute-done((f32[128,256]{1,0:T(8,128)S(1)}, f32[128,256]{1,0:T(8,128)S(1)}, u32[]{:S(2)}, u32[]{:S(2)}) %collective-permute-start.20) | collective-permute-done | bytes 131104 | tf_op jit(solution)/shard_map/ppermute | solution.py:31
  63.9 4.1 %collective-permute-start.23 = (f32[128,256]{1,0:T(8,128)S(1)}, f32[128,256]{1,0:T(8,128)S(1)}, u32[]{:S(2)}, u32[]{:S(2)}) collective-permute-start(f32[128,256]{1,0:T(8,128)S(1)} %add_add_fusion.3.own_in), channel_id=1, source_target_pairs={{0,4},{4,0},{8,12},{12,8},{16,20},{20,16},{24,28},{28,24},{32,36},... | collective-permute-start | bytes 393224 | tf_op jit(solution)/shard_map/ppermute | solution.py:371
  68.0 1.0 collective-permute-done.23.oth_in
  69.0 1.7 %second_left.1 = (f32[32,2048]{1,0:T(8,128)S(1)}, f32[32,1024]{1,0:T(8,128)S(1)}, f32[32,1024]{1,0:T(8,128)S(1)}) custom-call(s32[3]{0:T(128)S(1)} %pad_add_fusion.place_ref, f32[128,256]{1,0:T(8,128)S(1)} %add_add_fusion.3.own_in, f32[128,256]{1,0:T(8,128)S(1)} %collective-permute-done.23.oth_in, bf16[512,512]{1,0:T(8,128)(2,1)S(1)} %pad_maximum_fusion.m0, ...), custom_call_target="tpu_custom_call" | custom-call | tf_op jit(solution)/shard_map/second_left/pallas_call | solution.py:86
  70.8 5.3 %collective-permute-start.24 = (f32[32,1024]{1,0:T(8,128)S(1)}, f32[32,1024]{1,0:T(8,128)S(1)}, u32[]{:S(2)}, u32[]{:S(2)}) collective-permute-start(f32[32,1024]{1,0:T(8,128)S(1)} %get-tuple-element.102), channel_id=1, source_target_pairs={{0,4},{4,0},{8,12},{12,8},{16,20},{20,16},{24,28},{28,24},{32,36},... | collective-permute-start | bytes 393224 | tf_op jit(solution)/shard_map/ppermute | solution.py:292
  76.1 1.0 collective-permute-done.24
  77.1 0.8 collective-permute-start.27
  78.0 2.4 %collective-permute-start.25 = (f32[32,1024]{1,0:T(8,128)S(1)}, f32[32,1024]{1,0:T(8,128)S(1)}, u32[]{:S(2)}, u32[]{:S(2)}) collective-permute-start(f32[32,1024]{1,0:T(8,128)S(1)} %add.64), channel_id=1, source_target_pairs={{0,32},{1,33},{2,34},{3,35},{4,36},{5,37},{6,38},{7,39},{8,40},{9,... | collective-permute-start | bytes 393224 | tf_op jit(solution)/shard_map/ppermute | solution.py:31
  80.4 1.7 %inverse_of.3.inv_ref = f32[32,32]{1,0:T(8,128)S(1)} custom-call(s32[3]{0:T(128)S(1)} %pad_add_fusion.place_ref, f32[32,2048]{1,0:T(8,128)S(1)} %get-tuple-element.103.left_ref), custom_call_target="tpu_custom_call" | custom-call | flops 1000 | bytes 1000 | tf_op jit(solution)/shard_map/inverse_of/pallas_call | solution.py:86
  82.1 3.6 %collective-permute-done.27 = f32[32,1024]{1,0:T(8,128)S(1)} collective-permute-done((f32[32,1024]{1,0:T(8,128)S(1)}, f32[32,1024]{1,0:T(8,128)S(1)}, u32[]{:S(2)}, u32[]{:S(2)}) %collective-permute-start.27) | collective-permute-done | bytes 131104 | tf_op jit(solution)/shard_map/ppermute | solution.py:31
  86.3 1.7 %collective-permute-start.28 = (f32[32,1024]{1,0:T(8,128)S(1)}, f32[32,1024]{1,0:T(8,128)S(1)}, u32[]{:S(2)}, u32[]{:S(2)}) collective-permute-start(f32[32,1024]{1,0:T(8,128)S(1)} %add_add_fusion.2.own_in), channel_id=1, source_target_pairs={{0,4},{4,0},{8,12},{12,8},{16,20},{20,16},{24,28},{28,24},{32,36},... | collective-permute-start | bytes 393224 | tf_op jit(solution)/shard_map/ppermute | solution.py:298
  88.0 1.0 collective-permute-done.28.oth_in
  89.0 2.0 %next_left.2 = (f32[32,2048]{1,0:T(8,128)S(1)}, f32[32,1024]{1,0:T(8,128)S(1)}, f32[32,1024]{1,0:T(8,128)S(1)}) custom-call(s32[3]{0:T(128)S(1)} %pad_add_fusion.place_ref, f32[32,1024]{1,0:T(8,128)S(1)} %add_add_fusion.2.own_in, f32[32,1024]{1,0:T(8,128)S(1)} %collective-permute-done.28.oth_in, f32[32,32]{1,0:T(8,128)S(1)} %inverse_of.3.inv_ref, ...), custom_call_target="tpu_custom_call" | custom-call | tf_op jit(solution)/shard_map/next_left/pallas_call | solution.py:86
  91.4 1.0 collective-permute-done.29
  92.4 0.8 collective-permute-start.32
  93.6 2.2 %collective-permute-start.30 = (f32[32,1024]{1,0:T(8,128)S(1)}, f32[32,1024]{1,0:T(8,128)S(1)}, u32[]{:S(2)}, u32[]{:S(2)}) collective-permute-start(f32[32,1024]{1,0:T(8,128)S(1)} %add.68), channel_id=1, source_target_pairs={{0,32},{1,33},{2,34},{3,35},{4,36},{5,37},{6,38},{7,39},{8,40},{9,... | collective-permute-start | bytes 393224 | tf_op jit(solution)/shard_map/ppermute | solution.py:31
  95.8 1.7 %inverse_of.4.inv_ref = f32[32,32]{1,0:T(8,128)S(1)} custom-call(s32[3]{0:T(128)S(1)} %pad_add_fusion.place_ref, f32[32,2048]{1,0:T(8,128)S(1)} %get-tuple-element.111.left_ref), custom_call_target="tpu_custom_call" | custom-call | flops 1000 | bytes 1000 | tf_op jit(solution)/shard_map/inverse_of/pallas_call | solution.py:86
  97.5 3.6 %collective-permute-done.32 = f32[32,1024]{1,0:T(8,128)S(1)} collective-permute-done((f32[32,1024]{1,0:T(8,128)S(1)}, f32[32,1024]{1,0:T(8,128)S(1)}, u32[]{:S(2)}, u32[]{:S(2)}) %collective-permute-start.32) | collective-permute-done | bytes 131104 | tf_op jit(solution)/shard_map/ppermute | solution.py:31
  101.6 1.5 %collective-permute-start.33 = (f32[32,1024]{1,0:T(8,128)S(1)}, f32[32,1024]{1,0:T(8,128)S(1)}, u32[]{:S(2)}, u32[]{:S(2)}) collective-permute-start(f32[32,1024]{1,0:T(8,128)S(1)} %add_add_fusion.1.own_in), channel_id=1, source_target_pairs={{0,4},{4,0},{8,12},{12,8},{16,20},{20,16},{24,28},{28,24},{32,36},... | collective-permute-start | bytes 393224 | tf_op jit(solution)/shard_map/ppermute | solution.py:298
  103.2 1.0 collective-permute-done.33.oth_in
  104.2 2.0 %next_left.3 = (f32[32,2048]{1,0:T(8,128)S(1)}, f32[32,1024]{1,0:T(8,128)S(1)}, f32[32,1024]{1,0:T(8,128)S(1)}) custom-call(s32[3]{0:T(128)S(1)} %pad_add_fusion.place_ref, f32[32,1024]{1,0:T(8,128)S(1)} %add_add_fusion.1.own_in, f32[32,1024]{1,0:T(8,128)S(1)} %collective-permute-done.33.oth_in, f32[32,32]{1,0:T(8,128)S(1)} %inverse_of.4.inv_ref, ...), custom_call_target="tpu_custom_call" | custom-call | tf_op jit(solution)/shard_map/next_left/pallas_call | solution.py:86
  106.6 1.0 collective-permute-done.34
  107.6 0.8 collective-permute-start.37
  108.8 2.2 %collective-permute-start.35 = (f32[32,1024]{1,0:T(8,128)S(1)}, f32[32,1024]{1,0:T(8,128)S(1)}, u32[]{:S(2)}, u32[]{:S(2)}) collective-permute-start(f32[32,1024]{1,0:T(8,128)S(1)} %add.72), channel_id=1, source_target_pairs={{0,32},{1,33},{2,34},{3,35},{4,36},{5,37},{6,38},{7,39},{8,40},{9,... | collective-permute-start | bytes 393224 | tf_op jit(solution)/shard_map/ppermute | solution.py:31
  111.0 1.7 %inverse_of.5.inv_ref = f32[32,32]{1,0:T(8,128)S(1)} custom-call(s32[3]{0:T(128)S(1)} %pad_add_fusion.place_ref, f32[32,2048]{1,0:T(8,128)S(1)} %get-tuple-element.119.left_ref), custom_call_target="tpu_custom_call" | custom-call | flops 1000 | bytes 1000 | tf_op jit(solution)/shard_map/inverse_of/pallas_call | solution.py:86
  112.7 3.6 %collective-permute-done.37 = f32[32,1024]{1,0:T(8,128)S(1)} collective-permute-done((f32[32,1024]{1,0:T(8,128)S(1)}, f32[32,1024]{1,0:T(8,128)S(1)}, u32[]{:S(2)}, u32[]{:S(2)}) %collective-permute-start.37) | collective-permute-done | bytes 131104 | tf_op jit(solution)/shard_map/ppermute | solution.py:31
  116.8 1.5 %collective-permute-start.38 = (f32[32,1024]{1,0:T(8,128)S(1)}, f32[32,1024]{1,0:T(8,128)S(1)}, u32[]{:S(2)}, u32[]{:S(2)}) collective-permute-start(f32[32,1024]{1,0:T(8,128)S(1)} %add_add_fusion.own_in), channel_id=1, source_target_pairs={{0,4},{4,0},{8,12},{12,8},{16,20},{20,16},{24,28},{28,24},{32,36},... | collective-permute-start | bytes 393224 | tf_op jit(solution)/shard_map/ppermute | solution.py:298
  118.4 1.0 collective-permute-done.38.oth_in
  119.4 2.6 %last_right.1 = (bf16[32,512]{1,0:T(8,128)(2,1)S(1)}, f32[32,512]{1,0:T(8,128)S(1)}, f32[32,32]{1,0:T(8,128)S(1)}) custom-call(s32[3]{0:T(128)S(1)} %pad_add_fusion.place_ref, f32[32,1024]{1,0:T(8,128)S(1)} %add_add_fusion.own_in, f32[32,1024]{1,0:T(8,128)S(1)} %collective-permute-done.38.oth_in, f32[32,32]{1,0:T(8,128)S(1)} %inverse_of.5.inv_ref, ...), custom_call_target="tpu_custom_call" | custom-call | tf_op jit(solution)/shard_map/last_right/pallas_call | solution.py:86
  122.4 0.7 collective-permute-start.42
  123.5 2.2 %collective-permute-start.40 = (bf16[32,512]{1,0:T(8,128)(2,1)S(1)}, bf16[32,512]{1,0:T(8,128)(2,1)S(1)}, u32[]{:S(2)}, u32[]{:S(2)}) collective-permute-start(bf16[32,512]{1,0:T(8,128)(2,1)S(1)} %get-tuple-element.127.refs_2_), channel_id=1, source_target_pairs={{0,32},{1,33},{2,34},{3,35},{4,36},{5,37},{6,38},{7,39},{8,40},{9,... | collective-permute-start | bytes 98312 | tf_op jit(solution)/shard_map/ppermute | solution.py:31
  125.7 3.2 %finish_near.1 = (f32[512,4096]{1,0:T(8,128)}, f32[512,4096]{1,0:T(8,128)}, f32[32,4096]{1,0:T(8,128)}, bf16[512,32]{1,0:T(8,128)(2,1)S(1)}) custom-call(s32[3]{0:T(128)S(1)} %pad_add_fusion.place_ref, f32[32,512]{1,0:T(8,128)S(1)} %get-tuple-element.125.refs_0_, f32[32,32]{1,0:T(8,128)S(1)} %get-tuple-element.126.refs_1_, ...), custom_call_target="tpu_custom_call" | custom-call | tf_op jit(solution)/shard_map/finish_near/pallas_call | solution.py:334
  128.9 1.1 collective-permute-start.43
  131.3 5.6 %finish_far.1 = (f32[512,4096]{1,0:T(8,128)}, f32[512,4096]{1,0:T(8,128)}, f32[32,4096]{1,0:T(8,128)}) custom-call(s32[3]{0:T(128)S(1)} %pad_add_fusion.place_ref, bf16[512,32]{1,0:T(8,128)(2,1)S(1)} %get-tuple-element.128.refs_0_, ...), custom_call_target="tpu_custom_call", output_to_operand_aliasing={{0}: (10, {}), {1}: (11, {}), {2}: (12, {})} | custom-call | tf_op jit(solution)/shard_map/finish_far/pallas_call | solution.py:334
  (57 shorter events, 9.2 us)
Async XLA Ops:
  3.0 5.4 %collective-permute-start = (bf16[512,2048]{1,0:T(8,128)(2,1)S(1)}, bf16[512,2048]{1,0:T(8,128)(2,1)}, u32[]{:S(2)}, u32[]{:S(2)}) collective-permute-start(bf16[512,2048]{1,0:T(8,128)(2,1)S(1)} %half_of_memory.3.refs_5_.refs_8_), channel_id=1, source_target_pairs={{0,4},{4,0},{8,12},{12,8},{16,20},{20,16},{24,28},{28,24},{32,36},... | collective-permute-start | bytes 6291464 | tf_op jit(solution)/shard_map/ppermute | solution.py:357
  6.8 7.4 %copy-start = (f32[4096,32]{0,1:T(8,128)S(1)}, f32[4096,32]{0,1:T(8,128)}, u32[]{:S(2)}) copy-start(f32[4096,32]{0,1:T(8,128)} %param.5) | copy-start | bytes 1572868
  10.3 16.3 %collective-permute-start.1 = (bf16[4,128,512]{2,1,0:T(8,128)(2,1)S(1)}, bf16[4,128,512]{2,1,0:T(8,128)(2,1)S(1)}, u32[]{:S(2)}, u32[]{:S(2)}) collective-permute-start(bf16[4,128,512]{2,1,0:T(8,128)(2,1)S(1)} %get-tuple-element.73.refs_1_), channel_id=1, source_target_pairs={{0,32},{1,33},{2,34},{3,35},{4,12},{5,13},{6,14},{7,15},{8,40},{9,... | collective-permute-start | bytes 1572872 | tf_op jit(solution)/shard_map/ppermute | solution.py:31
  11.7 15.0 %collective-permute-start.2 = (bf16[4,128,512]{2,1,0:T(8,128)(2,1)S(1)}, bf16[4,128,512]{2,1,0:T(8,128)(2,1)S(1)}, u32[]{:S(2)}, u32[]{:S(2)}) collective-permute-start(bf16[4,128,512]{2,1,0:T(8,128)(2,1)S(1)} %get-tuple-element.74.refs_2_), channel_id=1, source_target_pairs={{0,64},{1,65},{2,66},{3,67},{4,20},{5,21},{6,22},{7,23},{8,72},{9,... | collective-permute-start | bytes 1572872 | tf_op jit(solution)/shard_map/ppermute | solution.py:31
  14.1 15.2 %collective-permute-start.3 = (bf16[4,128,512]{2,1,0:T(8,128)(2,1)S(1)}, bf16[4,128,512]{2,1,0:T(8,128)(2,1)S(1)}, u32[]{:S(2)}, u32[]{:S(2)}) collective-permute-start(bf16[4,128,512]{2,1,0:T(8,128)(2,1)S(1)} %get-tuple-element.75.refs_3_), channel_id=1, source_target_pairs={{0,96},{1,97},{2,98},{3,99},{4,28},{5,29},{6,30},{7,31},{8,104},{9... | collective-permute-start | bytes 1572872 | tf_op jit(solution)/shard_map/ppermute | solution.py:31
  15.6 3.1 %collective-permute-start.4 = (f32[32,256]{1,0:T(8,128)S(1)}, f32[32,256]{1,0:T(8,128)S(1)}, u32[]{:S(2)}, u32[]{:S(2)}) collective-permute-start(f32[32,256]{1,0:T(8,128)S(1)} %get-tuple-element.77), channel_id=1, source_target_pairs={{0,4},{4,0},{8,12},{12,8},{16,20},{20,16},{24,28},{28,24},{32,36},... | collective-permute-start | bytes 98312 | tf_op jit(solution)/shard_map/ppermute | solution.py:361
  18.7 4.3 %collective-permute-start.7 = (f32[32,256]{1,0:T(8,128)S(1)}, f32[32,256]{1,0:T(8,128)S(1)}, u32[]{:S(2)}, u32[]{:S(2)}) collective-permute-start(f32[32,256]{1,0:T(8,128)S(1)} %add.57.a_ref), channel_id=1, source_target_pairs={{0,3},{1,2},{2,1},{3,0},{4,7},{5,6},{6,5},{7,4},{8,11},{9,10},{10,... | collective-permute-start | bytes 98312 | tf_op jit(solution)/shard_map/ppermute | solution.py:31
  21.4 4.6 %collective-permute-start.6 = (f32[32,256]{1,0:T(8,128)S(1)}, f32[32,256]{1,0:T(8,128)S(1)}, u32[]{:S(2)}, u32[]{:S(2)}) collective-permute-start(f32[32,256]{1,0:T(8,128)S(1)} %add.57.a_ref), channel_id=1, source_target_pairs={{0,2},{1,3},{2,0},{3,1},{4,6},{5,7},{6,4},{7,5},{8,10},{9,11},{10,... | collective-permute-start | bytes 98312 | tf_op jit(solution)/shard_map/ppermute | solution.py:31
  23.0 3.1 %collective-permute-start.5 = (f32[32,256]{1,0:T(8,128)S(1)}, f32[32,256]{1,0:T(8,128)S(1)}, u32[]{:S(2)}, u32[]{:S(2)}) collective-permute-start(f32[32,256]{1,0:T(8,128)S(1)} %add.57.a_ref), channel_id=1, source_target_pairs={{0,1},{1,0},{2,3},{3,2},{4,5},{5,4},{6,7},{7,6},{8,9},{9,8},{10,11... | collective-permute-start | bytes 98312 | tf_op jit(solution)/shard_map/ppermute | solution.py:31
  30.1 5.5 %collective-permute-start.8 = (bf16[128,512]{1,0:T(8,128)(2,1)S(1)}, bf16[128,512]{1,0:T(8,128)(2,1)S(1)}, u32[]{:S(2)}, u32[]{:S(2)}) collective-permute-start(bf16[128,512]{1,0:T(8,128)(2,1)S(1)} %get-tuple-element.83), channel_id=1, source_target_pairs={{0,8},{1,9},{2,10},{3,11},{4,36},{5,37},{6,38},{7,39},{8,0},{9,1},... | collective-permute-start | bytes 393224 | tf_op jit(solution)/shard_map/ppermute | solution.py:31
  31.5 7.1 %collective-permute-start.9 = (bf16[128,512]{1,0:T(8,128)(2,1)S(1)}, bf16[128,512]{1,0:T(8,128)(2,1)S(1)}, u32[]{:S(2)}, u32[]{:S(2)}) collective-permute-start(bf16[128,512]{1,0:T(8,128)(2,1)S(1)} %get-tuple-element.84), channel_id=1, source_target_pairs={{0,16},{1,17},{2,18},{3,19},{4,68},{5,69},{6,70},{7,71},{8,24},{9,... | collective-permute-start | bytes 393224 | tf_op jit(solution)/shard_map/ppermute | solution.py:31
  34.8 5.2 %collective-permute-start.10 = (bf16[128,512]{1,0:T(8,128)(2,1)S(1)}, bf16[128,512]{1,0:T(8,128)(2,1)S(1)}, u32[]{:S(2)}, u32[]{:S(2)}) collective-permute-start(bf16[128,512]{1,0:T(8,128)(2,1)S(1)} %get-tuple-element.85), channel_id=1, source_target_pairs={{0,24},{1,25},{2,26},{3,27},{4,100},{5,101},{6,102},{7,103},{8,16}... | collective-permute-start | bytes 393224 | tf_op jit(solution)/shard_map/ppermute | solution.py:31
  34.8 7.7 %collective-permute-start.13 = (f32[128,256]{1,0:T(8,128)S(1)}, f32[128,256]{1,0:T(8,128)S(1)}, u32[]{:S(2)}, u32[]{:S(2)}) collective-permute-start(f32[128,256]{1,0:T(8,128)S(1)} %stack_early.1), channel_id=1, source_target_pairs={{0,24},{1,25},{2,26},{3,27},{4,28},{5,29},{6,30},{7,31},{8,16},{9,... | collective-permute-start | bytes 393224 | tf_op jit(solution)/shard_map/ppermute | solution.py:31
  35.3 7.2 %collective-permute-start.12 = (f32[128,256]{1,0:T(8,128)S(1)}, f32[128,256]{1,0:T(8,128)S(1)}, u32[]{:S(2)}, u32[]{:S(2)}) collective-permute-start(f32[128,256]{1,0:T(8,128)S(1)} %stack_early.1), channel_id=1, source_target_pairs={{0,16},{1,17},{2,18},{3,19},{4,20},{5,21},{6,22},{7,23},{8,24},{9,... | collective-permute-start | bytes 393224 | tf_op jit(solution)/shard_map/ppermute | solution.py:31
  35.6 7.5 %collective-permute-start.11 = (f32[128,256]{1,0:T(8,128)S(1)}, f32[128,256]{1,0:T(8,128)S(1)}, u32[]{:S(2)}, u32[]{:S(2)}) collective-permute-start(f32[128,256]{1,0:T(8,128)S(1)} %stack_early.1), channel_id=1, source_target_pairs={{0,8},{1,9},{2,10},{3,11},{4,12},{5,13},{6,14},{7,15},{8,0},{9,1},... | collective-permute-start | bytes 393224 | tf_op jit(solution)/shard_map/ppermute | solution.py:31
  43.7 7.4 %collective-permute-start.16 = (bf16[128,512]{1,0:T(8,128)(2,1)S(1)}, bf16[128,512]{1,0:T(8,128)(2,1)S(1)}, u32[]{:S(2)}, u32[]{:S(2)}) collective-permute-start(bf16[128,512]{1,0:T(8,128)(2,1)S(1)} %second_sum.1), channel_id=1, source_target_pairs={{0,24},{1,25},{2,26},{3,27},{4,7},{5,6},{6,5},{7,4},{8,16},{9,17},... | collective-permute-start | bytes 393224 | tf_op jit(solution)/shard_map/ppermute | solution.py:31
  46.5 5.3 %collective-permute-start.15 = (bf16[128,512]{1,0:T(8,128)(2,1)S(1)}, bf16[128,512]{1,0:T(8,128)(2,1)S(1)}, u32[]{:S(2)}, u32[]{:S(2)}) collective-permute-start(bf16[128,512]{1,0:T(8,128)(2,1)S(1)} %second_sum.1), channel_id=1, source_target_pairs={{0,16},{1,17},{2,18},{3,19},{4,6},{5,7},{6,4},{7,5},{8,24},{9,25},... | collective-permute-start | bytes 393224 | tf_op jit(solution)/shard_map/ppermute | solution.py:31
  46.9 5.0 %collective-permute-start.14 = (bf16[128,512]{1,0:T(8,128)(2,1)S(1)}, bf16[128,512]{1,0:T(8,128)(2,1)S(1)}, u32[]{:S(2)}, u32[]{:S(2)}) collective-permute-start(bf16[128,512]{1,0:T(8,128)(2,1)S(1)} %second_sum.1), channel_id=1, source_target_pairs={{0,8},{1,9},{2,10},{3,11},{4,5},{5,4},{6,7},{7,6},{8,0},{9,1},{10,... | collective-permute-start | bytes 393224 | tf_op jit(solution)/shard_map/ppermute | solution.py:31
  47.2 10.4 %collective-permute-start.22 = (f32[128,256]{1,0:T(8,128)S(1)}, f32[128,256]{1,0:T(8,128)S(1)}, u32[]{:S(2)}, u32[]{:S(2)}) collective-permute-start(f32[128,256]{1,0:T(8,128)S(1)} %add_add_fusion.4), channel_id=1, source_target_pairs={{0,96},{1,97},{2,98},{3,99},{4,100},{5,101},{6,102},{7,103},{8,104... | collective-permute-start | bytes 393224 | tf_op jit(solution)/shard_map/ppermute | solution.py:31
  51.9 17.1 %collective-permute-start.19 = (bf16[512,512]{1,0:T(8,128)(2,1)S(1)}, bf16[512,512]{1,0:T(8,128)(2,1)S(1)}, u32[]{:S(2)}, u32[]{:S(2)}) collective-permute-start(bf16[512,512]{1,0:T(8,128)(2,1)S(1)} %pad_maximum_fusion.m0), channel_id=1, source_target_pairs={{0,3},{1,2},{2,1},{3,0},{4,28},{5,29},{6,30},{7,31},{8,11},{9,10},... | collective-permute-start | bytes 1572872 | tf_op jit(solution)/shard_map/ppermute | solution.py:31
  53.4 15.6 %collective-permute-start.18 = (bf16[512,512]{1,0:T(8,128)(2,1)S(1)}, bf16[512,512]{1,0:T(8,128)(2,1)S(1)}, u32[]{:S(2)}, u32[]{:S(2)}) collective-permute-start(bf16[512,512]{1,0:T(8,128)(2,1)S(1)} %pad_maximum_fusion.m0), channel_id=1, source_target_pairs={{0,2},{1,3},{2,0},{3,1},{4,20},{5,21},{6,22},{7,23},{8,10},{9,11},... | collective-permute-start | bytes 1572872 | tf_op jit(solution)/shard_map/ppermute | solution.py:31
  53.9 15.1 %collective-permute-start.17 = (bf16[512,512]{1,0:T(8,128)(2,1)S(1)}, bf16[512,512]{1,0:T(8,128)(2,1)S(1)}, u32[]{:S(2)}, u32[]{:S(2)}) collective-permute-start(bf16[512,512]{1,0:T(8,128)(2,1)S(1)} %pad_maximum_fusion.m0), channel_id=1, source_target_pairs={{0,1},{1,0},{2,3},{3,2},{4,12},{5,13},{6,14},{7,15},{8,9},{9,8},{1... | collective-permute-start | bytes 1572872 | tf_op jit(solution)/shard_map/ppermute | solution.py:31
  55.2 5.3 %collective-permute-start.21 = (f32[128,256]{1,0:T(8,128)S(1)}, f32[128,256]{1,0:T(8,128)S(1)}, u32[]{:S(2)}, u32[]{:S(2)}) collective-permute-start(f32[128,256]{1,0:T(8,128)S(1)} %add_add_fusion.4), channel_id=1, source_target_pairs={{0,64},{1,65},{2,66},{3,67},{4,68},{5,69},{6,70},{7,71},{8,72},{9,... | collective-permute-start | bytes 393224 | tf_op jit(solution)/shard_map/ppermute | solution.py:31
  57.6 6.3 %collective-permute-start.20 = (f32[128,256]{1,0:T(8,128)S(1)}, f32[128,256]{1,0:T(8,128)S(1)}, u32[]{:S(2)}, u32[]{:S(2)}) collective-permute-start(f32[128,256]{1,0:T(8,128)S(1)} %add_add_fusion.4), channel_id=1, source_target_pairs={{0,32},{1,33},{2,34},{3,35},{4,36},{5,37},{6,38},{7,39},{8,40},{9,... | collective-permute-start | bytes 393224 | tf_op jit(solution)/shard_map/ppermute | solution.py:31
  63.9 5.1 %collective-permute-start.23 = (f32[128,256]{1,0:T(8,128)S(1)}, f32[128,256]{1,0:T(8,128)S(1)}, u32[]{:S(2)}, u32[]{:S(2)}) collective-permute-start(f32[128,256]{1,0:T(8,128)S(1)} %add_add_fusion.3.own_in), channel_id=1, source_target_pairs={{0,4},{4,0},{8,12},{12,8},{16,20},{20,16},{24,28},{28,24},{32,36},... | collective-permute-start | bytes 393224 | tf_op jit(solution)/shard_map/ppermute | solution.py:371
  70.8 6.3 %collective-permute-start.24 = (f32[32,1024]{1,0:T(8,128)S(1)}, f32[32,1024]{1,0:T(8,128)S(1)}, u32[]{:S(2)}, u32[]{:S(2)}) collective-permute-start(f32[32,1024]{1,0:T(8,128)S(1)} %get-tuple-element.102), channel_id=1, source_target_pairs={{0,4},{4,0},{8,12},{12,8},{16,20},{20,16},{24,28},{28,24},{32,36},... | collective-permute-start | bytes 393224 | tf_op jit(solution)/shard_map/ppermute | solution.py:292
  77.1 8.7 %collective-permute-start.27 = (f32[32,1024]{1,0:T(8,128)S(1)}, f32[32,1024]{1,0:T(8,128)S(1)}, u32[]{:S(2)}, u32[]{:S(2)}) collective-permute-start(f32[32,1024]{1,0:T(8,128)S(1)} %add.64), channel_id=1, source_target_pairs={{0,96},{1,97},{2,98},{3,99},{4,100},{5,101},{6,102},{7,103},{8,104... | collective-permute-start | bytes 393224 | tf_op jit(solution)/shard_map/ppermute | solution.py:31
  77.9 7.9 %collective-permute-start.26 = (f32[32,1024]{1,0:T(8,128)S(1)}, f32[32,1024]{1,0:T(8,128)S(1)}, u32[]{:S(2)}, u32[]{:S(2)}) collective-permute-start(f32[32,1024]{1,0:T(8,128)S(1)} %add.64), channel_id=1, source_target_pairs={{0,64},{1,65},{2,66},{3,67},{4,68},{5,69},{6,70},{7,71},{8,72},{9,... | collective-permute-start | bytes 393224 | tf_op jit(solution)/shard_map/ppermute | solution.py:31
  78.0 8.2 %collective-permute-start.25 = (f32[32,1024]{1,0:T(8,128)S(1)}, f32[32,1024]{1,0:T(8,128)S(1)}, u32[]{:S(2)}, u32[]{:S(2)}) collective-permute-start(f32[32,1024]{1,0:T(8,128)S(1)} %add.64), channel_id=1, source_target_pairs={{0,32},{1,33},{2,34},{3,35},{4,36},{5,37},{6,38},{7,39},{8,40},{9,... | collective-permute-start | bytes 393224 | tf_op jit(solution)/shard_map/ppermute | solution.py:31
  86.3 2.7 %collective-permute-start.28 = (f32[32,1024]{1,0:T(8,128)S(1)}, f32[32,1024]{1,0:T(8,128)S(1)}, u32[]{:S(2)}, u32[]{:S(2)}) collective-permute-start(f32[32,1024]{1,0:T(8,128)S(1)} %add_add_fusion.2.own_in), channel_id=1, source_target_pairs={{0,4},{4,0},{8,12},{12,8},{16,20},{20,16},{24,28},{28,24},{32,36},... | collective-permute-start | bytes 393224 | tf_op jit(solution)/shard_map/ppermute | solution.py:298
  91.0 1.4 %collective-permute-start.29 = (f32[32,1024]{1,0:T(8,128)S(1)}, f32[32,1024]{1,0:T(8,128)S(1)}, u32[]{:S(2)}, u32[]{:S(2)}) collective-permute-start(f32[32,1024]{1,0:T(8,128)S(1)} %get-tuple-element.110), channel_id=1, source_target_pairs={{0,4},{4,0},{8,12},{12,8},{16,20},{20,16},{24,28},{28,24},{32,36},... | collective-permute-start | bytes 393224 | tf_op jit(solution)/shard_map/ppermute | solution.py:292
  92.4 8.7 %collective-permute-start.32 = (f32[32,1024]{1,0:T(8,128)S(1)}, f32[32,1024]{1,0:T(8,128)S(1)}, u32[]{:S(2)}, u32[]{:S(2)}) collective-permute-start(f32[32,1024]{1,0:T(8,128)S(1)} %add.68), channel_id=1, source_target_pairs={{0,96},{1,97},{2,98},{3,99},{4,100},{5,101},{6,102},{7,103},{8,104... | collective-permute-start | bytes 393224 | tf_op jit(solution)/shard_map/ppermute | solution.py:31
  93.2 7.9 %collective-permute-start.31 = (f32[32,1024]{1,0:T(8,128)S(1)}, f32[32,1024]{1,0:T(8,128)S(1)}, u32[]{:S(2)}, u32[]{:S(2)}) collective-permute-start(f32[32,1024]{1,0:T(8,128)S(1)} %add.68), channel_id=1, source_target_pairs={{0,64},{1,65},{2,66},{3,67},{4,68},{5,69},{6,70},{7,71},{8,72},{9,... | collective-permute-start | bytes 393224 | tf_op jit(solution)/shard_map/ppermute | solution.py:31
  93.6 8.0 %collective-permute-start.30 = (f32[32,1024]{1,0:T(8,128)S(1)}, f32[32,1024]{1,0:T(8,128)S(1)}, u32[]{:S(2)}, u32[]{:S(2)}) collective-permute-start(f32[32,1024]{1,0:T(8,128)S(1)} %add.68), channel_id=1, source_target_pairs={{0,32},{1,33},{2,34},{3,35},{4,36},{5,37},{6,38},{7,39},{8,40},{9,... | collective-permute-start | bytes 393224 | tf_op jit(solution)/shard_map/ppermute | solution.py:31
  101.6 2.5 %collective-permute-start.33 = (f32[32,1024]{1,0:T(8,128)S(1)}, f32[32,1024]{1,0:T(8,128)S(1)}, u32[]{:S(2)}, u32[]{:S(2)}) collective-permute-start(f32[32,1024]{1,0:T(8,128)S(1)} %add_add_fusion.1.own_in), channel_id=1, source_target_pairs={{0,4},{4,0},{8,12},{12,8},{16,20},{20,16},{24,28},{28,24},{32,36},... | collective-permute-start | bytes 393224 | tf_op jit(solution)/shard_map/ppermute | solution.py:298
  106.2 1.4 %collective-permute-start.34 = (f32[32,1024]{1,0:T(8,128)S(1)}, f32[32,1024]{1,0:T(8,128)S(1)}, u32[]{:S(2)}, u32[]{:S(2)}) collective-permute-start(f32[32,1024]{1,0:T(8,128)S(1)} %get-tuple-element.118), channel_id=1, source_target_pairs={{0,4},{4,0},{8,12},{12,8},{16,20},{20,16},{24,28},{28,24},{32,36},... | collective-permute-start | bytes 393224 | tf_op jit(solution)/shard_map/ppermute | solution.py:292
  107.6 8.7 %collective-permute-start.37 = (f32[32,1024]{1,0:T(8,128)S(1)}, f32[32,1024]{1,0:T(8,128)S(1)}, u32[]{:S(2)}, u32[]{:S(2)}) collective-permute-start(f32[32,1024]{1,0:T(8,128)S(1)} %add.72), channel_id=1, source_target_pairs={{0,96},{1,97},{2,98},{3,99},{4,100},{5,101},{6,102},{7,103},{8,104... | collective-permute-start | bytes 393224 | tf_op jit(solution)/shard_map/ppermute | solution.py:31
  108.4 7.9 %collective-permute-start.36 = (f32[32,1024]{1,0:T(8,128)S(1)}, f32[32,1024]{1,0:T(8,128)S(1)}, u32[]{:S(2)}, u32[]{:S(2)}) collective-permute-start(f32[32,1024]{1,0:T(8,128)S(1)} %add.72), channel_id=1, source_target_pairs={{0,64},{1,65},{2,66},{3,67},{4,68},{5,69},{6,70},{7,71},{8,72},{9,... | collective-permute-start | bytes 393224 | tf_op jit(solution)/shard_map/ppermute | solution.py:31
  108.8 8.0 %collective-permute-start.35 = (f32[32,1024]{1,0:T(8,128)S(1)}, f32[32,1024]{1,0:T(8,128)S(1)}, u32[]{:S(2)}, u32[]{:S(2)}) collective-permute-start(f32[32,1024]{1,0:T(8,128)S(1)} %add.72), channel_id=1, source_target_pairs={{0,32},{1,33},{2,34},{3,35},{4,36},{5,37},{6,38},{7,39},{8,40},{9,... | collective-permute-start | bytes 393224 | tf_op jit(solution)/shard_map/ppermute | solution.py:31
  116.8 2.5 %collective-permute-start.38 = (f32[32,1024]{1,0:T(8,128)S(1)}, f32[32,1024]{1,0:T(8,128)S(1)}, u32[]{:S(2)}, u32[]{:S(2)}) collective-permute-start(f32[32,1024]{1,0:T(8,128)S(1)} %add_add_fusion.own_in), channel_id=1, source_target_pairs={{0,4},{4,0},{8,12},{12,8},{16,20},{20,16},{24,28},{28,24},{32,36},... | collective-permute-start | bytes 393224 | tf_op jit(solution)/shard_map/ppermute | solution.py:298
  122.0 3.7 %collective-permute-start.39 = (bf16[32,512]{1,0:T(8,128)(2,1)S(1)}, bf16[32,512]{1,0:T(8,128)(2,1)S(1)}, u32[]{:S(2)}, u32[]{:S(2)}) collective-permute-start(bf16[32,512]{1,0:T(8,128)(2,1)S(1)} %get-tuple-element.127.refs_2_), channel_id=1, source_target_pairs={{0,4},{4,0},{8,12},{12,8},{16,20},{20,16},{24,28},{28,24},{32,36},... | collective-permute-start | bytes 98312 | tf_op jit(solution)/shard_map/ppermute | solution.py:382
  122.4 6.4 %collective-permute-start.42 = (bf16[32,512]{1,0:T(8,128)(2,1)S(1)}, bf16[32,512]{1,0:T(8,128)(2,1)S(1)}, u32[]{:S(2)}, u32[]{:S(2)}) collective-permute-start(bf16[32,512]{1,0:T(8,128)(2,1)S(1)} %get-tuple-element.127.refs_2_), channel_id=1, source_target_pairs={{0,96},{1,97},{2,98},{3,99},{4,100},{5,101},{6,102},{7,103},{8,104... | collective-permute-start | bytes 98312 | tf_op jit(solution)/shard_map/ppermute | solution.py:31
  123.1 5.7 %collective-permute-start.41 = (bf16[32,512]{1,0:T(8,128)(2,1)S(1)}, bf16[32,512]{1,0:T(8,128)(2,1)S(1)}, u32[]{:S(2)}, u32[]{:S(2)}) collective-permute-start(bf16[32,512]{1,0:T(8,128)(2,1)S(1)} %get-tuple-element.127.refs_2_), channel_id=1, source_target_pairs={{0,64},{1,65},{2,66},{3,67},{4,68},{5,69},{6,70},{7,71},{8,72},{9,... | collective-permute-start | bytes 98312 | tf_op jit(solution)/shard_map/ppermute | solution.py:31
  123.5 5.4 %collective-permute-start.40 = (bf16[32,512]{1,0:T(8,128)(2,1)S(1)}, bf16[32,512]{1,0:T(8,128)(2,1)S(1)}, u32[]{:S(2)}, u32[]{:S(2)}) collective-permute-start(bf16[32,512]{1,0:T(8,128)(2,1)S(1)} %get-tuple-element.127.refs_2_), channel_id=1, source_target_pairs={{0,32},{1,33},{2,34},{3,35},{4,36},{5,37},{6,38},{7,39},{8,40},{9,... | collective-permute-start | bytes 98312 | tf_op jit(solution)/shard_map/ppermute | solution.py:31
  128.9 1.9 %collective-permute-start.43 = (bf16[32,512]{1,0:T(8,128)(2,1)S(1)}, bf16[32,512]{1,0:T(8,128)(2,1)S(1)}, u32[]{:S(2)}, u32[]{:S(2)}) collective-permute-start(bf16[32,512]{1,0:T(8,128)(2,1)S(1)} %collective-permute-done.40.refs_1_), channel_id=1, source_target_pairs={{0,4},{4,0},{8,12},{12,8},{16,20},{20,16},{24,28},{28,24},{32,36},... | collective-permute-start | bytes 98312 | tf_op jit(solution)/shard_map/ppermute | solution.py:386
  130.0 1.2 collective-permute-start.44
  130.0 1.3 collective-permute-start.45
